TPU v7x, 32 devices: a whole 2x2x4 slice. The times are simulated.
32 devices in a mesh: dp: 4 (over y, x), seq: 8 (over z, core).
Axes of the slice: x: 2, y: 2, z: 4, core: 2. Of those that a mesh axis runs over, the one named last changes fastest.
Arguments:
- tokens: bfloat16 [8, 1024, 2048], P('dp', 'seq'), may hold values from -6 to 6
- segment_ids: int32 [8, 1024], P('dp', 'seq'), may hold values from 0 to 4, as said below
- cotangent: bfloat16 [8, 1024, 2048], P('dp', 'seq'), may hold values from -6 to 6
- norm_one: bfloat16 [2048], P(('dp', 'seq')), may hold values from 0.5 to 1.5
- branch_weight: bfloat16 [2048, 2560], P(('dp', 'seq')), may hold values from -0.125 to 0.125
- input_proj: bfloat16 [2048, 2560], P(('dp', 'seq')), may hold values from -0.125 to 0.125
- conv_weight: bfloat16 [4, 2560], P(None, ('dp', 'seq')), may hold values from -3 to 3
- conv_bias: bfloat16 [2560], P(('dp', 'seq')), may hold values from -3 to 3
- rate_weight: bfloat16 [2560, 160], P(('dp', 'seq')), may hold values from -0.5 to 0.5
- igate_weight: bfloat16 [2560, 160], P(('dp', 'seq')), may hold values from -0.5 to 0.5
- rate_bias: bfloat16 [2560], P(('dp', 'seq')), may hold values from -4 to 4
- igate_bias: bfloat16 [2560], P(('dp', 'seq')), may hold values from -4 to 4
- decay_param: bfloat16 [2560], P(('dp', 'seq')), may hold values from 4.5 to 10.5
- out_proj: bfloat16 [2560, 2048], P(('dp', 'seq')), may hold values from -0.5 to 0.5
- norm_two: bfloat16 [2048], P(('dp', 'seq')), may hold values from 0.5 to 1.5
- mlp_gate: bfloat16 [2048, 6144], P(('dp', 'seq')), may hold values from -0.125 to 0.125
- mlp_up: bfloat16 [2048, 6144], P(('dp', 'seq')), may hold values from -0.125 to 0.125
- mlp_down: bfloat16 [6144, 2048], P(('dp', 'seq')), may hold values from -0.15625 to 0.15625
Outputs:
- block_out: bfloat16 [8, 1024, 2048], P('dp', 'seq')
- grad_tokens: float32 [8, 1024, 2048], P('dp', 'seq')
- grad_norm_one: float32 [2048], P(('dp', 'seq'))
- grad_branch_weight: float32 [2048, 2560], P(('dp', 'seq'))
- grad_input_proj: float32 [2048, 2560], P(('dp', 'seq'))
- grad_conv_weight: float32 [4, 2560], P(None, ('dp', 'seq'))
- grad_conv_bias: float32 [2560], P(('dp', 'seq'))
- grad_rate_weight: float32 [2560, 160], P(('dp', 'seq'))
- grad_igate_weight: float32 [2560, 160], P(('dp', 'seq'))
- grad_rate_bias: float32 [2560], P(('dp', 'seq'))
- grad_igate_bias: float32 [2560], P(('dp', 'seq'))
- grad_decay_param: float32 [2560], P(('dp', 'seq'))
- grad_out_proj: float32 [2560, 2048], P(('dp', 'seq'))
- grad_norm_two: float32 [2048], P(('dp', 'seq'))
- grad_mlp_gate: float32 [2048, 6144], P(('dp', 'seq'))
- grad_mlp_up: float32 [2048, 6144], P(('dp', 'seq'))
- grad_mlp_down: float32 [6144, 2048], P(('dp', 'seq'))
Inputs may be any that keep to these rules, and one draw needn't show every extreme that they name: `segment_ids`: along each row the ids start at 0 and rise by one where a new item begins. Among the 2 rows of each index of dp, one row is a single item of 1024 tokens; every other row holds exactly 5 items.
All inputs are finite; a program needn't handle non-finite values.
Results may differ from a plain program's by a relative error of at most 0.012.
The roundings to bfloat16 on the way count: a program that leaves them out, or rounds other values in their place, can miss the bound.
Values may be sent and summed in bfloat16 or wider, within the bound.
No kernel may reach another device: no remote copies, remote signals or barrier semaphores. Data moves between devices by JAX's collectives and lax.ppermute only.
A program may use at most 448 MiB of HBM per device.

v0:
```python
import jax
import jax.numpy as jnp
from jax import lax
from jax.sharding import PartitionSpec as P

HEADS = 16
BS = 160


eps_value = 1e-06
rate_scale = 8.0
floor_value = 0.001


def shifted(array, axis, by):
    count = lax.axis_size(axis)
    pairs = [(i, i + by) for i in range(count) if 0 <= i + by < count]
    return lax.ppermute(array, axis, pairs)


def prefix(part, axis, combine, identity):
    place = lax.axis_index(axis)
    gathered = jax.tree.map(lambda a: lax.all_gather(a, axis), part)
    state = jax.tree.map(lambda a, e: jnp.zeros_like(a) + jnp.asarray(e, a.dtype), part, identity)

    def prefix_one(hop, state):
        return combine(
            state, jax.tree.map(lambda a: lax.dynamic_index_in_dim(a, hop, 0, False), gathered)
        )

    return lax.fori_loop(0, place, prefix_one, state)


def carried_in(array, axis, join, neutral):
    count = lax.axis_size(axis)
    place = lax.axis_index(axis)
    ahead = count - 1 - place
    gathered = jax.tree.map(
        lambda a, kind: lax.all_gather(a.astype(kind), axis), array, (jnp.bfloat16, jnp.bfloat16)
    )
    state = jax.tree.map(lambda a, e: jnp.zeros_like(a) + jnp.asarray(e, a.dtype), array, neutral)

    def carried_one(hop, state):
        source = count - 1 - hop
        return join(
            state,
            jax.tree.map(
                lambda a, own: lax.dynamic_index_in_dim(a, source, 0, False).astype(own.dtype),
                gathered,
                array,
            ),
        )

    return lax.fori_loop(0, ahead, carried_one, state)


def gelu_tanh(value):
    return jax.nn.gelu(value, approximate=True)


def rms_scale(values, gain):
    return values * lax.rsqrt(jnp.mean(values * values, axis=-1, keepdims=True) + eps_value) * gain


def block_mix(inputs, weights):
    count = inputs.shape[0]
    blocks = weights.reshape(HEADS, BS, BS)
    mixed = jnp.einsum(
        "thi,hio->tho", inputs.reshape(count, HEADS, BS), blocks, preferred_element_type=jnp.float32
    )
    return mixed.reshape(count, HEADS * BS)


def block_mix_back(upstream, weights):
    count = upstream.shape[0]
    blocks = weights.reshape(HEADS, BS, BS)
    mixed = jnp.einsum(
        "tho,hio->thi",
        upstream.reshape(count, HEADS, BS),
        blocks,
        preferred_element_type=jnp.float32,
    )
    return mixed.reshape(count, HEADS * BS)


def block_grad(inputs, upstream):
    count = inputs.shape[0]
    summed = jnp.einsum(
        "thi,tho->hio",
        inputs.reshape(count, HEADS, BS),
        upstream.reshape(count, HEADS, BS),
        preferred_element_type=jnp.float32,
    )
    return summed.reshape(HEADS * BS, BS)


def gate_terms(rate_pre, igate_pre, conv_value, decay_value, start_flags):
    rate = jax.nn.sigmoid(rate_pre)
    igate = jax.nn.sigmoid(igate_pre)
    log_keep = -rate_scale * jax.nn.softplus(-decay_value) * rate
    keep = jnp.exp(log_keep)
    multiplier = jnp.where(
        start_flags, 1.0, jnp.sqrt(jnp.maximum(-jnp.expm1(2.0 * log_keep), floor_value))
    )
    return (jnp.where(start_flags, 0.0, keep), multiplier * igate * conv_value)


def combine(earlier, later):
    return (earlier[0] * later[0], later[1] + later[0] * earlier[1])


def per_device(
    tokens,
    segment_ids,
    cotangent,
    norm_one,
    branch_weight,
    input_proj,
    conv_weight,
    conv_bias,
    rate_weight,
    igate_weight,
    rate_bias,
    igate_bias,
    decay_param,
    out_proj,
    norm_two,
    mlp_gate,
    mlp_up,
    mlp_down,
):
    rec_full = (
        lax.all_gather(norm_one, ("dp", "seq"), axis=0, tiled=True),
        lax.all_gather(branch_weight, ("dp", "seq"), axis=0, tiled=True),
        lax.all_gather(input_proj, ("dp", "seq"), axis=0, tiled=True),
        lax.all_gather(conv_weight, ("dp", "seq"), axis=1, tiled=True),
        lax.all_gather(conv_bias, ("dp", "seq"), axis=0, tiled=True),
        lax.all_gather(rate_weight, ("dp", "seq"), axis=0, tiled=True),
        lax.all_gather(igate_weight, ("dp", "seq"), axis=0, tiled=True),
        lax.all_gather(rate_bias, ("dp", "seq"), axis=0, tiled=True),
        lax.all_gather(igate_bias, ("dp", "seq"), axis=0, tiled=True),
        lax.all_gather(decay_param, ("dp", "seq"), axis=0, tiled=True),
        lax.all_gather(out_proj, ("dp", "seq"), axis=0, tiled=True),
    )
    (
        gain_one,
        w_branch,
        w_input,
        w_conv,
        b_conv,
        w_rate,
        w_igate,
        b_rate,
        b_igate,
        decay_full,
        w_out,
    ) = rec_full
    row_count, span_len, width_d = tokens.shape
    tok_count = row_count * span_len
    kernel = w_conv.shape[0]
    reach = kernel - 1
    inputs = tokens.reshape(tok_count, width_d).astype(jnp.float32)
    normed_one_f, norm_one_back = jax.vjp(rms_scale, inputs, gain_one.astype(jnp.float32))
    normed_one = normed_one_f.astype(jnp.bfloat16)
    branch_pre = jnp.dot(normed_one, w_branch, preferred_element_type=jnp.float32)
    branch, branch_back = jax.vjp(gelu_tanh, branch_pre)
    conv_in = jnp.dot(normed_one, w_input, preferred_element_type=jnp.float32).astype(jnp.bfloat16)
    conv_in = conv_in.reshape(row_count, span_len, -1)
    seg_code = (segment_ids % 64).astype(jnp.bfloat16)
    tail_in, tail_code = shifted(
        (conv_in[:, span_len - reach :], seg_code[:, span_len - reach :]), "seq", 1
    )
    ext_in = jnp.concatenate([tail_in, conv_in], axis=1)
    ext_code = jnp.concatenate([tail_code, seg_code], axis=1)
    position = lax.broadcasted_iota(jnp.int32, (row_count, span_len), 1)
    row_begin = (lax.axis_index("seq") == 0) & (position == 0)
    start_flags = (ext_code[:, reach - 1 : reach - 1 + span_len] != seg_code) | row_begin
    conv_sum = b_conv.astype(jnp.float32) + w_conv[0].astype(jnp.float32) * conv_in.astype(
        jnp.float32
    )
    back_masks = [None]
    for shift_by in range(1, kernel):
        same_item = (
            ext_code[:, reach - shift_by : reach - shift_by + span_len] == seg_code
        ).astype(jnp.float32)
        back_masks.append(same_item[:, :, None])
        moved = ext_in[:, reach - shift_by : reach - shift_by + span_len].astype(jnp.float32)
        conv_sum = conv_sum + w_conv[shift_by].astype(jnp.float32) * moved * same_item[:, :, None]
    conv_low = conv_sum.astype(jnp.bfloat16).reshape(tok_count, -1)
    conv_value = conv_low.astype(jnp.float32)
    rate_pre = block_mix(conv_low, w_rate) + b_rate.astype(jnp.float32)
    igate_pre = block_mix(conv_low, w_igate) + b_igate.astype(jnp.float32)
    flags_flat = start_flags.reshape(tok_count, 1)

    def gate_local(rate_in, igate_in, conv_input, decay_input):
        return gate_terms(rate_in, igate_in, conv_input, decay_input, flags_flat)

    gate_out, gate_back = jax.vjp(
        gate_local, rate_pre, igate_pre, conv_value, decay_full.astype(jnp.float32)
    )
    keep_eff = gate_out[0].reshape(row_count, span_len, -1)
    drive = gate_out[1].reshape(row_count, span_len, -1)
    cum_keep, local_state = lax.associative_scan(combine, (keep_eff, drive), axis=1)
    width_r = keep_eff.shape[2]
    ones_row = jnp.ones((row_count, width_r), jnp.float32)
    zeros_row = jnp.zeros((row_count, width_r), jnp.float32)
    carried = prefix((cum_keep[:, -1], local_state[:, -1]), "seq", combine, (ones_row, zeros_row))
    state_in = carried[1]
    state = local_state + cum_keep * state_in[:, None, :]
    state_flat = state.reshape(tok_count, -1)
    mixed = (branch * state_flat).astype(jnp.bfloat16)
    resid = inputs + jnp.dot(mixed, w_out, preferred_element_type=jnp.float32)
    gain_two, w_gate, w_up, w_down = (
        lax.all_gather(norm_two, ("dp", "seq"), axis=0, tiled=True),
        lax.all_gather(mlp_gate, ("dp", "seq"), axis=0, tiled=True),
        lax.all_gather(mlp_up, ("dp", "seq"), axis=0, tiled=True),
        lax.all_gather(mlp_down, ("dp", "seq"), axis=0, tiled=True),
    )
    normed_two_f, norm_two_back = jax.vjp(rms_scale, resid, gain_two.astype(jnp.float32))
    normed_two = normed_two_f.astype(jnp.bfloat16)
    gate_pre = jnp.dot(normed_two, w_gate, preferred_element_type=jnp.float32)
    up_value = jnp.dot(normed_two, w_up, preferred_element_type=jnp.float32)
    gate_act, gate_act_back = jax.vjp(gelu_tanh, gate_pre)
    hidden = (gate_act * up_value).astype(jnp.bfloat16)
    block_out = (resid + jnp.dot(hidden, w_down, preferred_element_type=jnp.float32)).astype(
        jnp.bfloat16
    )
    block_out = block_out.reshape(row_count, span_len, width_d)
    w_gate_b, w_up_b, w_down_b = (
        lax.all_gather(mlp_gate, ("dp", "seq"), axis=0, tiled=True),
        lax.all_gather(mlp_up, ("dp", "seq"), axis=0, tiled=True),
        lax.all_gather(mlp_down, ("dp", "seq"), axis=0, tiled=True),
    )
    cot_low = cotangent.reshape(tok_count, width_d)
    grad_down = jnp.einsum("tf,td->fd", hidden, cot_low, preferred_element_type=jnp.float32)
    grad_hidden = jnp.einsum("td,fd->tf", cot_low, w_down_b, preferred_element_type=jnp.float32)
    grad_gate_pre = gate_act_back(grad_hidden * up_value)[0].astype(jnp.bfloat16)
    grad_up = (grad_hidden * gate_act).astype(jnp.bfloat16)
    grad_gate_w = jnp.einsum(
        "td,tf->df", normed_two, grad_gate_pre, preferred_element_type=jnp.float32
    )
    grad_up_w = jnp.einsum("td,tf->df", normed_two, grad_up, preferred_element_type=jnp.float32)
    grad_normed_two = jnp.einsum(
        "tf,df->td", grad_gate_pre, w_gate_b, preferred_element_type=jnp.float32
    )
    grad_normed_two = grad_normed_two + jnp.einsum(
        "tf,df->td", grad_up, w_up_b, preferred_element_type=jnp.float32
    )
    grad_resid_norm, grad_gain_two = norm_two_back(grad_normed_two)
    grad_resid = cot_low.astype(jnp.float32) + grad_resid_norm
    mlp_sums = (
        lax.psum_scatter(grad_gain_two, ("dp", "seq"), scatter_dimension=0, tiled=True),
        lax.psum_scatter(grad_gate_w, ("dp", "seq"), scatter_dimension=0, tiled=True),
        lax.psum_scatter(grad_up_w, ("dp", "seq"), scatter_dimension=0, tiled=True),
        lax.psum_scatter(grad_down, ("dp", "seq"), scatter_dimension=0, tiled=True),
    )
    w_branch_b, w_input_b, w_conv_b, w_rate_b, w_igate_b, w_out_b = (
        lax.all_gather(branch_weight, ("dp", "seq"), axis=0, tiled=True),
        lax.all_gather(input_proj, ("dp", "seq"), axis=0, tiled=True),
        lax.all_gather(conv_weight, ("dp", "seq"), axis=1, tiled=True),
        lax.all_gather(rate_weight, ("dp", "seq"), axis=0, tiled=True),
        lax.all_gather(igate_weight, ("dp", "seq"), axis=0, tiled=True),
        lax.all_gather(out_proj, ("dp", "seq"), axis=0, tiled=True),
    )
    grad_recur = grad_resid.astype(jnp.bfloat16)
    grad_out_w = jnp.einsum("tw,td->wd", mixed, grad_recur, preferred_element_type=jnp.float32)
    grad_mixed = jnp.einsum("td,wd->tw", grad_recur, w_out_b, preferred_element_type=jnp.float32)
    grad_branch = branch_back(grad_mixed * state_flat)[0].astype(jnp.bfloat16)
    grad_state = (grad_mixed * branch).reshape(row_count, span_len, -1)
    coef = jnp.concatenate([keep_eff[:, 1:], ones_row[:, None, :]], axis=1)
    cum_coef, local_adjoint = lax.associative_scan(
        combine, (coef, grad_state), reverse=True, axis=1
    )
    summary_keep = cum_coef[:, 0] * keep_eff[:, 0]
    summary_adjoint = keep_eff[:, 0] * local_adjoint[:, 0]
    incoming = carried_in((summary_keep, summary_adjoint), "seq", combine, (ones_row, zeros_row))
    adjoint = local_adjoint + cum_coef * incoming[1][:, None, :]
    state_prev = jnp.concatenate([state_in[:, None, :], state[:, :-1]], axis=1)
    grad_keep_eff = (adjoint * state_prev).reshape(tok_count, -1)
    grad_rate_f, grad_igate_f, grad_conv_direct, grad_decay = gate_back(
        (grad_keep_eff, adjoint.reshape(tok_count, -1))
    )
    grad_rate_pre = grad_rate_f.astype(jnp.bfloat16)
    grad_igate_pre = grad_igate_f.astype(jnp.bfloat16)
    grad_rate_bias = jnp.sum(grad_rate_pre.astype(jnp.float32), axis=0)
    grad_igate_bias = jnp.sum(grad_igate_pre.astype(jnp.float32), axis=0)
    grad_rate_w = block_grad(conv_low, grad_rate_pre)
    grad_igate_w = block_grad(conv_low, grad_igate_pre)
    grad_conv = (
        grad_conv_direct
        + block_mix_back(grad_rate_pre, w_rate_b)
        + block_mix_back(grad_igate_pre, w_igate_b)
    )
    grad_conv_low = grad_conv.astype(jnp.bfloat16).reshape(row_count, span_len, -1)
    grad_conv_f = grad_conv_low.astype(jnp.float32)
    grad_conv_bias = jnp.sum(grad_conv_f, axis=(0, 1))
    tap_grads = [jnp.sum(grad_conv_f * conv_in.astype(jnp.float32), axis=(0, 1))]
    for shift_by in range(1, kernel):
        moved = ext_in[:, reach - shift_by : reach - shift_by + span_len].astype(jnp.float32)
        tap_grads.append(jnp.sum(grad_conv_f * moved * back_masks[shift_by], axis=(0, 1)))
    grad_conv_w = jnp.stack(tap_grads, axis=0)
    head_grad, head_code = shifted((grad_conv_low[:, :reach], seg_code[:, :reach]), "seq", -1)
    ext_grad = jnp.concatenate([grad_conv_low, head_grad], axis=1)
    next_code = jnp.concatenate([seg_code, head_code], axis=1)
    grad_conv_in = w_conv_b[0].astype(jnp.float32) * grad_conv_f
    for shift_by in range(1, kernel):
        ahead_same = (next_code[:, shift_by : shift_by + span_len] == seg_code).astype(jnp.float32)[
            :, :, None
        ]
        ahead = ext_grad[:, shift_by : shift_by + span_len].astype(jnp.float32)
        grad_conv_in = grad_conv_in + w_conv_b[shift_by].astype(jnp.float32) * ahead * ahead_same
    grad_conv_in = grad_conv_in.astype(jnp.bfloat16).reshape(tok_count, -1)
    grad_branch_w = jnp.einsum(
        "td,tw->dw", normed_one, grad_branch, preferred_element_type=jnp.float32
    )
    grad_input_w = jnp.einsum(
        "td,tw->dw", normed_one, grad_conv_in, preferred_element_type=jnp.float32
    )
    grad_normed_one = jnp.einsum(
        "tw,dw->td", grad_branch, w_branch_b, preferred_element_type=jnp.float32
    )
    grad_normed_one = grad_normed_one + jnp.einsum(
        "tw,dw->td", grad_conv_in, w_input_b, preferred_element_type=jnp.float32
    )
    grad_inputs_norm, grad_gain_one = norm_one_back(grad_normed_one)
    grad_tokens = (grad_resid + grad_inputs_norm).reshape(row_count, span_len, width_d)
    rec_terms = (
        grad_gain_one,
        grad_branch_w,
        grad_input_w,
        grad_conv_w,
        grad_conv_bias,
        grad_rate_w,
        grad_igate_w,
        grad_rate_bias,
        grad_igate_bias,
        grad_decay,
        grad_out_w,
    )
    rec_sums = (
        lax.psum_scatter(rec_terms[0], ("dp", "seq"), scatter_dimension=0, tiled=True),
        lax.psum_scatter(rec_terms[1], ("dp", "seq"), scatter_dimension=0, tiled=True),
        lax.psum_scatter(rec_terms[2], ("dp", "seq"), scatter_dimension=0, tiled=True),
        lax.psum_scatter(rec_terms[3], ("dp", "seq"), scatter_dimension=1, tiled=True),
        lax.psum_scatter(rec_terms[4], ("dp", "seq"), scatter_dimension=0, tiled=True),
        lax.psum_scatter(rec_terms[5], ("dp", "seq"), scatter_dimension=0, tiled=True),
        lax.psum_scatter(rec_terms[6], ("dp", "seq"), scatter_dimension=0, tiled=True),
        lax.psum_scatter(rec_terms[7], ("dp", "seq"), scatter_dimension=0, tiled=True),
        lax.psum_scatter(rec_terms[8], ("dp", "seq"), scatter_dimension=0, tiled=True),
        lax.psum_scatter(rec_terms[9], ("dp", "seq"), scatter_dimension=0, tiled=True),
        lax.psum_scatter(rec_terms[10], ("dp", "seq"), scatter_dimension=0, tiled=True),
    )
    return (
        block_out,
        grad_tokens,
        rec_sums[0],
        rec_sums[1],
        rec_sums[2],
        rec_sums[3],
        rec_sums[4],
        rec_sums[5],
        rec_sums[6],
        rec_sums[7],
        rec_sums[8],
        rec_sums[9],
        rec_sums[10],
        mlp_sums[0],
        mlp_sums[1],
        mlp_sums[2],
        mlp_sums[3],
    )


def solution(mesh):
    return jax.shard_map(
        per_device,
        mesh=mesh,
        in_specs=(
            P("dp", "seq", None),
            P("dp", "seq"),
            P("dp", "seq", None),
            P(("dp", "seq")),
            P(("dp", "seq"), None),
            P(("dp", "seq"), None),
            P(None, ("dp", "seq")),
            P(("dp", "seq")),
            P(("dp", "seq"), None),
            P(("dp", "seq"), None),
            P(("dp", "seq")),
            P(("dp", "seq")),
            P(("dp", "seq")),
            P(("dp", "seq"), None),
            P(("dp", "seq")),
            P(("dp", "seq"), None),
            P(("dp", "seq"), None),
            P(("dp", "seq"), None),
        ),
        out_specs=(
            P("dp", "seq", None),
            P("dp", "seq", None),
            P(("dp", "seq")),
            P(("dp", "seq"), None),
            P(("dp", "seq"), None),
            P(None, ("dp", "seq")),
            P(("dp", "seq")),
            P(("dp", "seq"), None),
            P(("dp", "seq"), None),
            P(("dp", "seq")),
            P(("dp", "seq")),
            P(("dp", "seq")),
            P(("dp", "seq"), None),
            P(("dp", "seq")),
            P(("dp", "seq"), None),
            P(("dp", "seq"), None),
            P(("dp", "seq"), None),
        ),
        check_vma=False,
    )
```

profile of v0, /device:TPU:0, one launch (start us, length us, event | category | flops | bytes accessed | tf_op | source)
XLA Modules:
  0.0 3543.4 jit_solution(10863250849267413844)
XLA Ops:
  16.6 44.8 %all-reduce.71 = (bf16[2560]{0:T(1024)(128)(2,1)S(1)}, bf16[2048]{0:T(1024)(128)(2,1)S(1)}, bf16[2560]{0:T(1024)(128)(2,1)S(1)}, bf16[2560]{0:T(1024)(128)(2,1)S...) all-reduce(bf16[2560]{0:T(1024)(128)(2,1)S(1)} %dynamic-update-slic, ...), channel_id=1, replica_groups=mesh['dp'=4,'seq'=8] {'dp','seq'}, use_global_device_ids=true, to_apply=%add.59 | all-reduce | flops 14336 | bytes 57344
  62.8 41.3 %all-gather.4 = bf16[32,80,4]{1,2,0:T(4,128)(2,1)S(1)} all-gather(bf16[1,80,4]{1,2,0:T(4,128)(2,1)S(1)} %bitcast.197), channel_id=1, replica_groups=mesh['dp'=4,'seq'=8] {'dp','seq'}, dimensions={0}, use_global_device_ids=true | all-gather | bytes 21120 | tf_op jit(solution)/shard_map/all_gather | solution.py:136
  105.4 47.5 %all_gather.74 = bf16[2560,160]{1,0:T(8,128)(2,1)S(1)} all-gather(bf16[80,160]{1,0:T(8,128)(2,1)S(1)} %copy-done.93), channel_id=1, replica_groups=mesh['dp'=4,'seq'=8] {'dp','seq'}, dimensions={0}, use_global_device_ids=true | all-gather | bytes 844800 | tf_op jit(solution)/shard_map/all_gather | solution.py:138
  152.9 56.8 %all_gather.76 = bf16[2560,160]{1,0:T(8,128)(2,1)} all-gather(bf16[80,160]{1,0:T(8,128)(2,1)S(1)} %copy-done.94), channel_id=1, replica_groups=mesh['dp'=4,'seq'=8] {'dp','seq'}, dimensions={0}, use_global_device_ids=true | all-gather | bytes 844800 | tf_op jit(solution)/shard_map/all_gather | solution.py:139
  211.1 7.3 convolution_convert_fusion
  256.0 6.2 convert_multiply_fusion.7
  413.5 14.6 all-gather.1
  443.6 14.0 all-gather
  458.1 10.8 slice.595
  468.9 10.8 slice.601
  479.7 10.9 slice.591
  497.2 10.2 fusion.49
  507.3 6.6 multiply_reduce_fusion.3
  514.3 16.1 fusion.122
  530.4 71.8 %all-gather.20.cloned.1.call-done = bf16[2048,6144]{1,0:T(8,128)(2,1)} async-done(((bf16[64,6144]{1,0:T(8,128)(2,1)}), bf16[2048,6144]{1,0:T(8,128)(2,1)}) %all-gather.20.cloned.1.call-update) | async-done | bytes 25165840 | tf_op jit(solution)/shard_map/all_gather | solution.py:216
  602.2 14.2 fusion.123
  616.4 141.5 %all-gather.22.cloned.1.call-done = bf16[6144,2048]{1,0:T(8,128)(2,1)} async-done(((bf16[192,2048]{1,0:T(8,128)(2,1)}), bf16[6144,2048]{1,0:T(8,128)(2,1)}) %all-gather.22.cloned.1.call-update) | async-done | bytes 25165840 | tf_op jit(solution)/shard_map/all_gather | solution.py:217
  757.9 21.6 multiply_convert_fusion
  779.5 13.6 fusion.124
  793.1 14.9 multiply_reduce_fusion.1
  811.2 9.5 fusion.69
  827.0 10.8 slice.593
  837.8 10.7 slice.597
  913.4 6.7 slice.588
  977.0 14.0 all-gather.2
  991.5 14.0 all-gather.3
  1006.5 21.3 rev.9
  1027.8 20.9 rev.8
  1048.7 8.8 fusion.24
  1077.3 9.6 convert_reduce_fusion.1
  1112.4 10.4 convert_reduce_fusion
  1132.2 12.1 fusion.75
  1144.3 11.7 fusion.126
  1166.3 8.6 convolution_bitcast_fusion
  1175.1 21.2 fusion.129
  1196.3 21.2 fusion.130
  1217.6 21.4 fusion.131
  1248.7 13.1 fusion.52
  1261.8 8.7 fusion.58
  1270.5 41.4 %all-reduce.70 = (f32[2048]{0:T(1024)S(1)}, f32[2560]{0:T(1024)S(1)}, f32[2560]{0:T(1024)S(1)}, f32[2560]{0:T(1024)S(1)}, f32[2560]{0:T(1024)S(1)}, /*index=5*/f32[2048]{0:T(1024)S(1)}) all-reduce(f32[2048]{0:T(1024)S(1)} %get-tuple-element.151, f32[2560]{0:T(1024)S(1)} %copy-done.92, ...), channel_id=6, replica_groups=mesh['dp'=4,'seq'=8] {'dp','seq'}, use_global_device_ids=true, to_apply=%region_9.10.clone | all-reduce | flops 14336 | bytes 114688
  1320.3 75.3 %reduce-scatter.16.cloned.1.call-done = f32[80,160]{1,0:T(8,128)} async-done(((f32[2560,160]{1,0:T(8,128)}), f32[80,160]{1,0:T(8,128)}) %reduce-scatter.16.cloned.1.call-update) | async-done | bytes 51216 | tf_op jit(solution)/shard_map/reduce_scatter | solution.py:346
  1395.6 138.2 %reduce-scatter.18.cloned.1.call-done = f32[80,160]{1,0:T(8,128)} async-done(((f32[2560,160]{1,0:T(8,128)}), f32[80,160]{1,0:T(8,128)}) %reduce-scatter.18.cloned.1.call-update) | async-done | bytes 51216 | tf_op jit(solution)/shard_map/reduce_scatter | solution.py:347
  1533.8 229.7 %reduce-scatter.20.cloned.1.call-done = f32[80,2048]{1,0:T(8,128)} async-done(((f32[2560,2048]{1,0:T(8,128)}), f32[80,2048]{1,0:T(8,128)}) %reduce-scatter.20.cloned.1.call-update) | async-done | bytes 655376 | tf_op jit(solution)/shard_map/reduce_scatter | solution.py:351
  1763.6 229.8 %reduce-scatter.12.cloned.1.call-done = f32[64,2560]{1,0:T(8,128)} async-done(((f32[2048,2560]{1,0:T(8,128)}), f32[64,2560]{1,0:T(8,128)}) %reduce-scatter.12.cloned.1.call-update) | async-done | bytes 655376 | tf_op jit(solution)/shard_map/reduce_scatter | solution.py:342
  1993.4 229.7 %reduce-scatter.14.cloned.1.call-done = f32[64,2560]{1,0:T(8,128)} async-done(((f32[2048,2560]{1,0:T(8,128)}), f32[64,2560]{1,0:T(8,128)}) %reduce-scatter.14.cloned.1.call-update) | async-done | bytes 655376 | tf_op jit(solution)/shard_map/reduce_scatter | solution.py:343
  2223.1 436.3 %reduce-scatter.22.cloned.1.call-done = f32[64,6144]{1,0:T(8,128)} async-done(((f32[2048,6144]{1,0:T(8,128)}), f32[64,6144]{1,0:T(8,128)}) %reduce-scatter.22.cloned.1.call-update) | async-done | bytes 1572880 | tf_op jit(solution)/shard_map/reduce_scatter | solution.py:253
  2659.3 438.5 %reduce-scatter.24.cloned.1.call-done = f32[64,6144]{1,0:T(8,128)} async-done(((f32[2048,6144]{1,0:T(8,128)}), f32[64,6144]{1,0:T(8,128)}) %reduce-scatter.24.cloned.1.call-update) | async-done | bytes 1572880 | tf_op jit(solution)/shard_map/reduce_scatter | solution.py:254
  3097.9 438.6 %reduce-scatter.26.cloned.1.call-done = f32[192,2048]{1,0:T(8,128)} async-done(((f32[6144,2048]{1,0:T(8,128)}), f32[192,2048]{1,0:T(8,128)}) %reduce-scatter.26.cloned.1.call-update) | async-done | bytes 1572880 | tf_op jit(solution)/shard_map/reduce_scatter | solution.py:255
  (601 shorter events, 439.7 us)
Async XLA Ops:
  7.3 55.5 %copy-start.113 = (bf16[4,80]{1,0:T(4,128)(2,1)S(1)}, bf16[4,80]{1,0:T(4,128)(2,1)}, u32[]{:S(2)}) copy-start(bf16[4,80]{1,0:T(4,128)(2,1)} %param.28) | copy-start | bytes 1924
  7.3 97.8 %copy-start.5 = (bf16[2,128,2048]{2,1,0:T(8,128)(2,1)S(1)}, bf16[2,128,2048]{2,1,0:T(8,128)(2,1)}, u32[]{:S(2)}) copy-start(bf16[2,128,2048]{2,1,0:T(8,128)(2,1)} %param.22) | copy-start | bytes 3145732
  7.3 98.1 %copy-start.93 = (bf16[80,160]{1,0:T(8,128)(2,1)S(1)}, bf16[80,160]{1,0:T(8,128)(2,1)}, u32[]{:S(2)}) copy-start(bf16[80,160]{1,0:T(8,128)(2,1)} %param.30) | copy-start | bytes 76804
  7.3 203.8 %all-gather.14.cloned.1.call-start = ((), (), s32[]{:S(2)}) async-start(), calls=%async_computation.10 | async-start | bytes 10813440 | tf_op jit(solution)/shard_map/all_gather | solution.py:135
  8.0 489.1 %all-gather.12.cloned.1.call-start = ((), (), s32[]{:S(2)}) async-start(), calls=%async_computation.9 | async-start | bytes 10813440 | tf_op jit(solution)/shard_map/all_gather | solution.py:134
  8.8 498.6 %all-gather.16.cloned.1.call-start = ((), (), s32[]{:S(2)}) async-start(), calls=%async_computation.11 | async-start | bytes 10813440 | tf_op jit(solution)/shard_map/all_gather | solution.py:143
  9.5 143.4 %copy-start.94 = (bf16[80,160]{1,0:T(8,128)(2,1)S(1)}, bf16[80,160]{1,0:T(8,128)(2,1)}, u32[]{:S(2)}) copy-start(bf16[80,160]{1,0:T(8,128)(2,1)} %param.31) | copy-start | bytes 76804
  9.5 504.8 %all-gather.18.cloned.1.call-start = ((), (), s32[]{:S(2)}) async-start(), calls=%async_computation.12 | async-start | bytes 25952256 | tf_op jit(solution)/shard_map/all_gather | solution.py:215
  10.1 592.1 %all-gather.20.cloned.1.call-start = ((), (), s32[]{:S(2)}) async-start(), calls=%async_computation.13 | async-start | bytes 25952256 | tf_op jit(solution)/shard_map/all_gather | solution.py:216
  10.7 747.2 %all-gather.22.cloned.1.call-start = ((), (), s32[]{:S(2)}) async-start(), calls=%async_computation.14 | async-start | bytes 25952256 | tf_op jit(solution)/shard_map/all_gather | solution.py:217
  11.3 1307.6 %reduce-scatter.28.cloned.1.call-start = ((), (), s32[]{:S(2)}) async-start(), calls=%async_computation.23 | async-start | bytes 1351680
  11.4 209.3 %collective-permute-start = (bf16[2,3]{1,0:T(2,128)(2,1)S(1)}, bf16[2,3]{1,0:T(2,128)(2,1)S(1)}, u32[]{:S(2)}, u32[]{:S(2)}) collective-permute-start(bf16[2,3]{1,0:T(2,128)(2,1)S(1)} %get-tuple-element.285), channel_id=1, source_target_pairs={{0,1},{1,2},{2,3},{3,4},{4,5},{5,6},{6,7},{8,9},{9,10},{10,11},{11... | collective-permute-start | bytes 44 | tf_op jit(solution)/shard_map/ppermute | solution.py:18
  13.8 206.9 %collective-permute-start.3 = (bf16[2,3]{1,0:T(2,128)(2,1)S(1)}, bf16[2,3]{1,0:T(2,128)(2,1)S(1)}, u32[]{:S(2)}, u32[]{:S(2)}) collective-permute-start(bf16[2,3]{1,0:T(2,128)(2,1)S(1)} %get-tuple-element.284), channel_id=1, source_target_pairs={{1,0},{2,1},{3,2},{4,3},{5,4},{6,5},{7,6},{9,8},{10,9},{11,10},{12... | collective-permute-start | bytes 44 | tf_op jit(solution)/shard_map/ppermute | solution.py:18
  61.4 43.6 %copy-start.95 = (bf16[2560]{0:T(1024)(128)(2,1)}, bf16[2560]{0:T(1024)(128)(2,1)S(1)}, u32[]{:S(2)}) copy-start(bf16[2560]{0:T(1024)(128)(2,1)S(1)} %get-tuple-element.191) | copy-start | bytes 15364
  61.4 194.6 %copy-start.52 = (f32[2560]{0:T(1024)}, f32[2560]{0:T(1024)S(1)}, u32[]{:S(2)}) copy-start(f32[2560]{0:T(1024)S(1)} %convert_element_type.270) | copy-start | bytes 30724
  62.1 193.9 %copy-start.48 = (f32[2560]{0:T(1024)}, f32[2560]{0:T(1024)S(1)}, u32[]{:S(2)}) copy-start(f32[2560]{0:T(1024)S(1)} %convert_element_type.269) | copy-start | bytes 30724
  62.8 148.2 %copy-start.50 = (f32[2048]{0:T(1024)}, f32[2048]{0:T(1024)S(1)}, u32[]{:S(2)}) copy-start(f32[2048]{0:T(1024)S(1)} %convert_element_type.247) | copy-start | bytes 24580
  104.2 151.7 %copy-start.45 = (f32[2560]{0:T(1024)}, f32[2560]{0:T(1024)S(1)}, u32[]{:S(2)}) copy-start(f32[2560]{0:T(1024)S(1)} %fusion.99) | copy-start | bytes 30724
  105.1 116.5 %copy-start.58 = (f32[2560]{0:T(1024)}, f32[2560]{0:T(1024)S(1)}, u32[]{:S(2)}) copy-start(f32[2560]{0:T(1024)S(1)} %get-tuple-element.161) | copy-start | bytes 30724
  105.1 116.5 %copy-start.60 = (f32[2560]{0:T(1024)}, f32[2560]{0:T(1024)S(1)}, u32[]{:S(2)}) copy-start(f32[2560]{0:T(1024)S(1)} %get-tuple-element.162) | copy-start | bytes 30724
  105.1 116.5 %copy-start.62 = (f32[2560]{0:T(1024)}, f32[2560]{0:T(1024)S(1)}, u32[]{:S(2)}) copy-start(f32[2560]{0:T(1024)S(1)} %get-tuple-element.163) | copy-start | bytes 30724
  105.1 116.4 %copy-start.64 = (f32[2560]{0:T(1024)}, f32[2560]{0:T(1024)S(1)}, u32[]{:S(2)}) copy-start(f32[2560]{0:T(1024)S(1)} %get-tuple-element.164) | copy-start | bytes 30724
  105.4 113.0 %copy-start.97 = (f32[2,128]{1,0:T(2,128)}, f32[2,128]{1,0:T(2,128)S(1)}, u32[]{:S(2)}) copy-start(f32[2,128]{1,0:T(2,128)S(1)} %fusion.59) | copy-start | bytes 3076
  105.4 112.9 %copy-start.107 = (f32[256]{0:T(256)}, f32[256]{0:T(256)S(1)}, u32[]{:S(2)}) copy-start(f32[256]{0:T(256)S(1)} %bitcast_rsqrt_fusion) | copy-start | bytes 3076
  152.9 78.3 %copy-start.13 = (bf16[2560,160]{1,0:T(8,128)(2,1)}, bf16[2560,160]{1,0:T(8,128)(2,1)S(1)}, u32[]{:S(2)}) copy-start(bf16[2560,160]{1,0:T(8,128)(2,1)S(1)} %all_gather.74) | copy-start | bytes 2457604
  218.4 3.1 collective-permute-start.1
  221.4 34.6 copy-start.99
  241.6 14.4 copy-start
  514.0 294.0 %copy-start.23 = (f32[256,2048]{1,0:T(8,128)}, f32[256,2048]{1,0:T(8,128)S(1)}, u32[]{:S(2)}) copy-start(f32[256,2048]{1,0:T(8,128)S(1)} %get-tuple-element.289) | copy-start | bytes 6291460
  514.3 87.9 %copy-start.11 = (bf16[256,2048]{1,0:T(8,128)(2,1)}, bf16[256,2048]{1,0:T(8,128)(2,1)S(1)}, u32[]{:S(2)}) copy-start(bf16[256,2048]{1,0:T(8,128)(2,1)S(1)} %multiply_convert_fusion.2) | copy-start | bytes 3145732
  793.1 14.9 copy-start.32
  1027.7 21.0 copy-start.1
  1027.7 21.0 copy-start.46
  1027.7 21.0 copy-start.49
  1027.7 21.0 copy-start.53
  1027.7 21.0 copy-start.66
  1027.7 21.0 copy-start.100
  1124.6 271.1 %reduce-scatter.16.cloned.1.call-start = ((), (), s32[]{:S(2)}) async-start(), calls=%async_computation.17 | async-start | bytes 2703360 | tf_op jit(solution)/shard_map/reduce_scatter | solution.py:346
  1128.4 405.5 %reduce-scatter.18.cloned.1.call-start = ((), (), s32[]{:S(2)}) async-start(), calls=%async_computation.18 | async-start | bytes 2703360 | tf_op jit(solution)/shard_map/reduce_scatter | solution.py:347
  1132.1 631.4 %reduce-scatter.20.cloned.1.call-start = ((), (), s32[]{:S(2)}) async-start(), calls=%async_computation.19 | async-start | bytes 21626880 | tf_op jit(solution)/shard_map/reduce_scatter | solution.py:351
  1144.3 849.1 %reduce-scatter.12.cloned.1.call-start = ((), (), s32[]{:S(2)}) async-start(), calls=%async_computation.15 | async-start | bytes 21626880 | tf_op jit(solution)/shard_map/reduce_scatter | solution.py:342
  1156.1 1067.0 %reduce-scatter.14.cloned.1.call-start = ((), (), s32[]{:S(2)}) async-start(), calls=%async_computation.16 | async-start | bytes 21626880 | tf_op jit(solution)/shard_map/reduce_scatter | solution.py:343
  1157.1 3.1 collective-permute-start.2
  1175.0 1484.3 %reduce-scatter.22.cloned.1.call-start = ((), (), s32[]{:S(2)}) async-start(), calls=%async_computation.20 | async-start | bytes 51904512 | tf_op jit(solution)/shard_map/reduce_scatter | solution.py:253
  1196.3 1901.6 %reduce-scatter.24.cloned.1.call-start = ((), (), s32[]{:S(2)}) async-start(), calls=%async_computation.21 | async-start | bytes 51904512 | tf_op jit(solution)/shard_map/reduce_scatter | solution.py:254
  1217.5 2318.9 %reduce-scatter.26.cloned.1.call-start = ((), (), s32[]{:S(2)}) async-start(), calls=%async_computation.22 | async-start | bytes 51904512 | tf_op jit(solution)/shard_map/reduce_scatter | solution.py:255
  1248.6 13.1 copy-start.8
  1261.8 53.7 %copy-start.10 = (f32[256,2048]{1,0:T(8,128)S(1)}, f32[256,2048]{1,0:T(8,128)}, u32[]{:S(2)}) copy-start(f32[256,2048]{1,0:T(8,128)} %copy-done.9) | copy-start | bytes 6291460
  (93 other events, 481.6 us)
Sparse Core Ops, SparseCore 0:
  11.0 89.3 all-gather.13
  103.2 97.0 all-gather.11
  203.2 86.4 all-gather.15
  292.5 154.1 all-gather.17
  449.5 152.5 all-gather.19
  605.0 152.8 all-gather.21
  1124.7 132.9 reduce-scatter.27
  1260.6 134.9 reduce-scatter.15
  1398.6 135.2 reduce-scatter.17
  1536.7 226.8 reduce-scatter.19
  1766.5 226.7 reduce-scatter.11
  1996.2 226.8 reduce-scatter.13
  2231.2 428.0 reduce-scatter.21
  2667.3 430.5 reduce-scatter.23
  3105.9 430.5 reduce-scatter.25
where the time goes:
time: 3560 us; the launch traced here: 3540 us
  waiting for transfers between devices  2440 us (69%)
  local copies, waits for them, and re-layouts  401 us (11%)
  blocking collectives  288 us (8%)
  matrix products  258 us (7%)
  other arithmetic  137 us (4%)
    reduce_scatter x1, waiting for transfers between devices, per_device(): lax.psum_scatter(grad_down, ('dp', 'seq'), scatter_dimension=0, tiled=True)  439 us
    reduce_scatter x1, waiting for transfers between devices, per_device(): lax.psum_scatter(grad_up_w, ('dp', 'seq'), scatter_dimension=0, tiled=True)  439 us
    reduce_scatter x1, waiting for transfers between devices, per_device(): lax.psum_scatter(grad_gate_w, ('dp', 'seq'), scatter_dimension=0, tiled=T...  436 us
    reduce_scatter x1, waiting for transfers between devices, per_device(): lax.psum_scatter(rec_terms[1], ('dp', 'seq'), scatter_dimension=0, tiled=...  230 us
    reduce_scatter x1, waiting for transfers between devices, per_device(): lax.psum_scatter(rec_terms[10], ('dp', 'seq'), scatter_dimension=0, tiled...  230 us
    reduce_scatter x1, waiting for transfers between devices, per_device(): lax.psum_scatter(rec_terms[2], ('dp', 'seq'), scatter_dimension=0, tiled=...  230 us
    all_gather x1, waiting for transfers between devices, per_device(): lax.all_gather(mlp_down, ('dp', 'seq'), axis=0, tiled=True)  142 us
    reduce_scatter x1, waiting for transfers between devices, per_device(): lax.psum_scatter(rec_terms[6], ('dp', 'seq'), scatter_dimension=0, tiled=...  138 us
  transfers between devices with their start and end apart: 19, of which 12 were waited for; matrix products, arithmetic and copies ran while one was open for 13% of the time, Pallas kernels for 0%

commit v1 on v0

v1 whole, which is shorter than its diff:
```python
import functools

import jax
import jax.numpy as jnp
from jax import lax
from jax.experimental import pallas as pl
from jax.experimental.pallas import tpu as pltpu
from jax.sharding import PartitionSpec as P

HEADS = 16
BS = 160
AXES = ("dp", "seq")

eps_value = 1e-06
rate_scale = 8.0
floor_value = 0.001
low = jnp.bfloat16
wide = jnp.float32


def gelu_tanh(value):
    return jax.nn.gelu(value, approximate=True)


def dot_nn(left, right):
    return lax.dot_general(left, right, (((1,), (0,)), ((), ())), preferred_element_type=wide)


def dot_nt(left, right):
    return lax.dot_general(left, right, (((1,), (1,)), ((), ())), preferred_element_type=wide)


def dot_tn(left, right):
    return lax.dot_general(left, right, (((0,), (0,)), ((), ())), preferred_element_type=wide)


def lay_out_kernel(count, c_ref, *refs):
    parts, (out_ref, buffer, sem, out_sem) = refs[: 2 * count], refs[2 * count :]
    core = c_ref[0]
    copies = []
    for which in range(2):
        start = (core if which == 0 else 1 - core) * (out_ref.shape[0] // 2)
        for i, part in enumerate(parts[which * count : (which + 1) * count]):
            at = pl.ds(pl.multiple_of(start, 16), part.shape[0])
            j = which * count + i
            into = pltpu.make_async_copy(part, buffer.at[at], sem.at[j])
            into.start()
            copies.append((into, pltpu.make_async_copy(buffer.at[at], out_ref.at[at], out_sem.at[j])))
            start = start + part.shape[0]
    for into, out in copies:
        into.wait()
        out.start()
    for into, out in copies:
        out.wait()


def lay_out(core, own, other):
    rows = 2 * sum(part.shape[0] for part in own)
    shape = (rows,) + own[0].shape[1:]
    anywhere = pl.BlockSpec(memory_space=pl.ANY)
    return pl.pallas_call(
        functools.partial(lay_out_kernel, len(own)),
        out_shape=jax.ShapeDtypeStruct(shape, own[0].dtype),
        in_specs=[pl.BlockSpec(memory_space=pltpu.SMEM)] + [anywhere] * (2 * len(own)),
        out_specs=anywhere,
        scratch_shapes=[
            pltpu.VMEM(shape, own[0].dtype),
            pltpu.SemaphoreType.DMA((2 * len(own),)),
            pltpu.SemaphoreType.DMA((2 * len(own),)),
        ],
        compiler_params=pltpu.CompilerParams(vmem_limit_bytes=32 * 2**20),
    )(core.reshape(1).astype(jnp.int32), *own, *other)


def together(*arrays):
    return lax.optimization_barrier(arrays)


def cut_kernel(k_count, z_count, gate_ref, up_ref, out_ref):
    own = out_ref.shape[3] // (2 * z_count)
    for k in range(k_count):
        for c in range(2):
            for which, ref in enumerate((gate_ref, up_ref)):
                for z in range(z_count):
                    at = ((k * z_count + z) * 2 + c) * own
                    to = (which * z_count + z) * own
                    out_ref[k, c, :, to : to + own] = ref[:, at : at + own]


def join_kernel(k_count, z_count, in_ref, gate_ref, up_ref):
    own = in_ref.shape[3] // (2 * z_count)
    for k in range(k_count):
        for c in range(2):
            for which, ref in enumerate((gate_ref, up_ref)):
                for z in range(z_count):
                    to = ((k * z_count + z) * 2 + c) * own
                    at = (which * z_count + z) * own
                    ref[:, to : to + own] = in_ref[k, c, :, at : at + own].astype(ref.dtype)


def in_vmem(kernel, arrays, out_shape):
    vmem = pl.BlockSpec(memory_space=pltpu.VMEM)
    return pl.pallas_call(
        kernel,
        out_shape=out_shape,
        in_specs=[vmem] * len(arrays),
        out_specs=jax.tree.map(lambda _: vmem, out_shape),
        compiler_params=pltpu.CompilerParams(vmem_limit_bytes=48 * 2**20),
    )(*arrays)


class Place:
    def __init__(self):
        self.k_count = lax.axis_size("dp")
        self.s_count = lax.axis_size("seq")
        self.z_count = self.s_count // 2
        self.k = lax.axis_index("dp")
        self.s = lax.axis_index("seq")
        self.c = self.s % 2
        self.z = self.s // 2
        self.square = self.k_count == 4
        self.z_groups = [
            [k * self.s_count + 2 * z + c for z in range(self.z_count)]
            for k in range(self.k_count)
            for c in range(2)
        ]
        self.plane_groups = [
            [k * self.s_count + 2 * z + c for k in range(self.k_count) for c in range(2)]
            for z in range(self.z_count)
        ]

    def to_k(self, array, flip):
        return lax.ppermute(array, "dp", [(i, i ^ flip) for i in range(self.k_count)])

    def to_core(self, array):
        return lax.ppermute(array, "seq", [(i, i ^ 1) for i in range(self.s_count)])

    def to_z(self, array, by):
        pairs = [(i, i + 2 * by) for i in range(self.s_count) if 0 <= i + 2 * by < self.s_count]
        return lax.ppermute(array, "seq", pairs)

    def by_core(self, own, other):
        return jnp.where(self.c == 0, jnp.stack([own, other]), jnp.stack([other, own]))

    def gather_z(self, array):
        return lax.all_gather(array, AXES, axis_index_groups=self.z_groups, tiled=True)

    def z_pairs(self, pairs):
        return [(2 * a + c, 2 * b + c) for a, b in pairs for c in range(2)]

    def own_apart(self, split, axis):
        shape = [1] * split.ndim
        shape[axis] = self.z_count
        own = (jnp.arange(self.z_count) == self.z).reshape(shape)
        sent = jnp.moveaxis(jnp.where(own, 0.0, split).astype(low), axis, 0)
        kept = lax.dynamic_index_in_dim(split, self.z, axis, False)
        return sent.reshape((-1,) + sent.shape[-1:]), kept.reshape((-1,) + sent.shape[-1:])

    def scatter_z(self, parts):
        total = lax.psum_scatter(
            parts[0], AXES, scatter_dimension=0, axis_index_groups=self.z_groups, tiled=True
        )
        return total, parts[1]


    def sum_far(self, chunk):
        if self.z_count != 4:
            return ()
        pairs = self.z_pairs([(0, 1), (3, 2)])
        return (lax.ppermute(chunk(3 - self.z).astype(low), "seq", pairs),)

    def sum_near(self, chunk):
        if self.z_count != 4:
            return ()
        below = self.to_z(chunk(jnp.minimum(self.z + 1, 3)).astype(low), 1)
        above = self.to_z(chunk(jnp.maximum(self.z - 1, 0)).astype(low), -1)
        return below, above

    def sum_second(self, chunk, far):
        if self.z_count != 4:
            return ()
        second = (chunk(self.z ^ 2).astype(wide) + far[0].astype(wide)).astype(low)
        return (lax.ppermute(second, "seq", self.z_pairs([(0, 2), (1, 3), (2, 0), (3, 1)])),)

    def sum_all(self, chunk, near, second):
        if self.z_count != 4:
            whole = jnp.concatenate([chunk(i) for i in range(self.z_count)], axis=0).astype(low)
            whole = lax.psum_scatter(
                whole, AXES, scatter_dimension=0, axis_index_groups=self.z_groups, tiled=True
            )
            return whole.astype(wide)
        total = chunk(self.z).astype(wide)
        for part in near + second:
            total = total + part.astype(wide)
        return total

    def gather_line_small(self, array):
        if not (self.square and self.z_count == 4):
            whole = lax.all_gather(array, AXES)
            return whole.reshape((self.k_count, self.s_count) + array.shape)
        out = array[None]
        for bit in range(3):
            got = lax.ppermute(out, "seq", [(i, i ^ (1 << bit)) for i in range(8)])
            low_bit = (self.s >> bit) % 2 == 0
            out = jnp.where(low_bit, jnp.concatenate([out, got]), jnp.concatenate([got, out]))
        out = out[None]
        for bit in range(2):
            got = self.to_k(out, 1 << bit)
            low_bit = (self.k >> bit) % 2 == 0
            out = jnp.where(low_bit, jnp.concatenate([out, got]), jnp.concatenate([got, out]))
        return out

    def gather_plane(self, array):
        if not self.square:
            whole = lax.all_gather(array, AXES, axis_index_groups=self.plane_groups)
            whole = whole.reshape((self.k_count, 2) + array.shape)
            return jnp.swapaxes(whole, 0, 1).reshape((-1,) + array.shape[1:])
        half = array.shape[0] // 2
        from_x = self.to_k(array, 1)
        from_y = self.to_k(array, 2)
        far_a = self.to_k(from_x[:half], 2)
        far_b = self.to_k(from_y[half:], 1)
        mine = [array, from_x, from_y, far_a, far_b]
        return lay_out(self.c, mine, [self.to_core(part) for part in mine])

    def gather_plane_small(self, array):
        if not self.square:
            return self.gather_plane(array)
        near = jnp.stack([array, self.to_k(array, 1)])
        mine = jnp.concatenate([near, self.to_k(near, 2)])
        return self.by_core(mine, self.to_core(mine)).reshape((-1,) + array.shape[1:])

    def halves(self, array):
        count = array.shape[0] // 2
        own = lax.dynamic_slice_in_dim(array, self.c * count, count, 0)
        return own, lax.dynamic_slice_in_dim(array, (1 - self.c) * count, count, 0)

    def chip_product(self, left, right, dot, exact=False):
        own, other = self.halves(left)
        sent = dot(other, right)
        sent = self.to_core(sent if exact else sent.astype(low))
        chip = dot(own, right) + sent.astype(wide)
        return chip.reshape(self.k_count, own.shape[0] // self.k_count, -1)

    def sum_plane(self, chip, exact=False):
        if not self.square:
            return lax.psum_scatter(chip, "dp", scatter_dimension=0, tiled=False)
        half = chip.shape[2] // 2

        def send(parts, power, flip):
            if not exact:
                return self.to_k(parts.astype(low), flip).astype(wide), None
            scaled = (parts * jnp.exp2(-power)).astype(jnp.float16)
            power = jnp.broadcast_to(power, power.shape[:-1] + (128,)).astype(jnp.float16)
            got = self.to_k(jnp.concatenate([scaled, power], axis=-1), flip).astype(wide)
            got_power = got[..., half : half + 1]
            return got[..., :half] * jnp.exp2(got_power), got_power

        power = None
        if exact:
            largest = jnp.max(jnp.abs(chip), axis=2, keepdims=True)
            power = jnp.ceil(jnp.log2(jnp.clip(largest, 1e-30, 1e37)))

        def pick(a, i, j):
            return a if a is None else jnp.stack([a[i], a[j]])

        def above(a, i, b, j):
            return a if a is None else jnp.maximum(a[i], b[j]) + 1.0

        got_a, power_a = send(pick(chip[..., :half], 1, 3), pick(power, 1, 3), 1)
        got_b, power_b = send(pick(chip[..., half:], 2, 3), pick(power, 2, 3), 2)
        last_a, _ = send(chip[2, :, :half] + got_a[1], above(power_a, 1, power, 2), 2)
        last_b, _ = send(chip[1, :, half:] + got_b[1], above(power_b, 1, power, 1), 1)
        return jnp.concatenate(
            [chip[0, :, :half] + got_a[0] + last_a, chip[0, :, half:] + got_b[0] + last_b], axis=1
        )

    def exchange_plane(self, array):
        keep = lax.dynamic_index_in_dim(array, self.c, 1, False)
        got = self.to_core(lax.dynamic_index_in_dim(array, 1 - self.c, 1, False))
        pairs = jnp.moveaxis(self.by_core(keep, got), 0, 1)
        if not self.square:
            return lax.all_to_all(pairs, "dp", 0, 0, tiled=True)
        parts = [lax.dynamic_index_in_dim(pairs, self.k, 0, False)]
        for flip in range(1, 4):
            parts.append(self.to_k(lax.dynamic_index_in_dim(pairs, self.k ^ flip, 0, False), flip))
        odd = self.k % 2 == 1
        parts = [jnp.where(odd, parts[i ^ 1], parts[i]) for i in range(4)]
        upper = self.k >= 2
        return jnp.stack([jnp.where(upper, parts[i ^ 2], parts[i]) for i in range(4)])


def scan_loop(rows, span, step, state, reverse):
    for part in (1, 0) if reverse else (0, 1):
        base = part * rows * span

        def one(i, state, base=base):
            return step(base + (span - 1 - i if reverse else i), state)

        state = lax.fori_loop(0, span, one, state, unroll=8)
    return state


def summary_kernel(rows, span, keep_ref, drive_ref, out_ref):
    def step(at, state):
        keep = keep_ref[pl.ds(at, rows, stride=span), :]
        drive = drive_ref[pl.ds(at, rows, stride=span), :]
        return state[0] * keep, state[1] * keep + drive

    shape = (rows, keep_ref.shape[1])
    start = (jnp.ones(shape, wide), jnp.zeros(shape, wide))
    product, end = scan_loop(rows, span, step, start, False)
    out_ref[0] = product
    out_ref[1] = end


def state_kernel(rows, span, keep_ref, drive_ref, start_ref, state_ref, prev_ref):
    def step(at, state):
        prev_ref[pl.ds(at, rows, stride=span), :] = state
        keep = keep_ref[pl.ds(at, rows, stride=span), :]
        drive = drive_ref[pl.ds(at, rows, stride=span), :]
        state = state * keep + drive
        state_ref[pl.ds(at, rows, stride=span), :] = state
        return state

    scan_loop(rows, span, step, start_ref[...], False)


def back_summary_kernel(rows, span, keep_ref, grad_ref, out_ref):
    def step(at, state):
        keep = keep_ref[pl.ds(at, rows, stride=span), :]
        grad = grad_ref[pl.ds(at, rows, stride=span), :]
        return keep * (grad + state)

    out_ref[...] = scan_loop(rows, span, step, jnp.zeros(out_ref.shape, wide), True)


def adjoint_kernel(rows, span, keep_ref, grad_ref, start_ref, adjoint_ref):
    def step(at, state):
        keep = keep_ref[pl.ds(at, rows, stride=span), :]
        adjoint = grad_ref[pl.ds(at, rows, stride=span), :] + state
        adjoint_ref[pl.ds(at, rows, stride=span), :] = adjoint
        return keep * adjoint

    scan_loop(rows, span, step, start_ref[...], True)


def scan_call(kernel, rows, span, arrays, out_shape):
    def block(array):
        lead = array.ndim - 1
        return pl.BlockSpec(array.shape[:-1] + (128,), lambda i, lead=lead: (0,) * lead + (i,))

    return pl.pallas_call(
        functools.partial(kernel, rows, span),
        out_shape=out_shape,
        grid=(pl.cdiv(arrays[0].shape[-1], 128),),
        in_specs=[block(a) for a in arrays],
        out_specs=jax.tree.map(block, out_shape),
        compiler_params=pltpu.CompilerParams(vmem_limit_bytes=48 * 2**20),
    )(*arrays)


def per_device(
    tokens,
    segment_ids,
    cotangent,
    norm_one,
    branch_weight,
    input_proj,
    conv_weight,
    conv_bias,
    rate_weight,
    igate_weight,
    rate_bias,
    igate_bias,
    decay_param,
    out_proj,
    norm_two,
    mlp_gate,
    mlp_up,
    mlp_down,
):
    at = Place()
    k_count, z_count = at.k_count, at.z_count
    group = 2 * k_count
    row_dev, span, width_d = tokens.shape
    tok = row_dev * span
    rows = k_count * row_dev
    tok_all = 2 * rows * span
    d_own = norm_one.shape[0]
    w_own = conv_bias.shape[0]
    f_own = mlp_down.shape[0]
    width_r = branch_weight.shape[1]
    w_slot = width_r // group
    f_slot = f_own * z_count
    taps = conv_weight.shape[0]
    reach = taps - 1
    half_z = z_count // 2

    def by_feature(array):
        split = array.reshape(z_count, k_count, 2 * d_own, array.shape[1])
        return jnp.swapaxes(split, 0, 1).reshape(array.shape)

    small = jnp.concatenate(
        [
            norm_one,
            norm_two,
            conv_weight.reshape(-1),
            conv_bias,
            rate_bias,
            igate_bias,
            decay_param,
        ]
    )
    small_all = at.gather_line_small(small).reshape(k_count * at.s_count, -1)
    gain_one = small_all[:, :d_own].reshape(1, width_d).astype(wide)
    gain_two = small_all[:, d_own : 2 * d_own].reshape(1, width_d).astype(wide)
    mine = lax.dynamic_slice_in_dim(
        small_all[:, 2 * d_own :], at.k * at.s_count + at.c * z_count, z_count, 0
    )
    mine = mine.reshape(z_count, taps + 4, w_own).astype(wide)
    mine = jnp.swapaxes(mine, 0, 1).reshape(taps + 4, w_slot)
    w_conv = mine[:taps]
    b_conv, b_rate, b_igate, decay = (mine[taps + i][None, :] for i in range(4))

    out_cols = width_d + 2 * BS
    out_part = at.gather_z(jnp.concatenate([out_proj, rate_weight, igate_weight], axis=1))
    out_part = out_part.reshape(2, half_z * w_own, out_cols)
    out_keep = lax.dynamic_index_in_dim(out_part, at.c, 0, False)
    out_got = at.to_core(lax.dynamic_index_in_dim(out_part, 1 - at.c, 0, False))
    w3 = at.by_core(
        out_keep.reshape(half_z, w_own, out_cols), out_got.reshape(half_z, w_own, out_cols)
    )
    w3 = jnp.swapaxes(w3, 0, 1).reshape(w_slot, out_cols)
    w_out = w3[:, :width_d]
    heads = w_slot // BS

    def block_diagonal(columns):
        blocks = columns.reshape(heads, BS, 1, BS)
        same = jnp.eye(heads, dtype=low).reshape(heads, 1, heads, 1)
        return (blocks * same).reshape(w_slot, w_slot)

    w_gates = jnp.concatenate(
        [block_diagonal(w3[:, width_d : width_d + BS]), block_diagonal(w3[:, width_d + BS :])], axis=1
    )

    rec_cols = jnp.concatenate(
        [
            branch_weight.reshape(d_own, k_count, 2, w_slot),
            input_proj.reshape(d_own, k_count, 2, w_slot),
        ],
        axis=3,
    )
    rec_cols = at.exchange_plane(jnp.moveaxis(rec_cols, 0, 2))
    rec_cols, tokens, mlp_gate = together(rec_cols, tokens, mlp_gate)
    w1 = by_feature(at.gather_z(rec_cols.reshape(group * d_own, 2 * w_slot)))

    inputs = tokens.reshape(tok, width_d).astype(wide)
    s1 = lax.rsqrt(jnp.mean(inputs * inputs, axis=-1, keepdims=True) + eps_value)
    normed_one = (inputs * s1 * gain_one).astype(low)
    n1_all = at.gather_plane(normed_one)
    mlp_shape = jax.ShapeDtypeStruct((k_count, 2, d_own, 2 * f_slot), low)
    cut = functools.partial(cut_kernel, k_count, z_count)
    mlp_cols = at.exchange_plane(in_vmem(cut, (mlp_gate, mlp_up), mlp_shape))
    seg_code = at.gather_plane_small((segment_ids % 64).astype(low)).reshape(2, rows, span)
    n1_all, mlp_cols, seg_code, cot = together(n1_all, mlp_cols, seg_code, cotangent.reshape(tok, width_d))
    w2 = by_feature(at.gather_z(mlp_cols.reshape(group * d_own, 2 * f_slot)))

    def with_before(array):
        tail = array[:, :, span - reach :]
        return jnp.concatenate([jnp.stack([at.to_z(tail[1], 1), tail[0]]), array], axis=2)

    def with_after(array):
        head = array[:, :, :reach]
        return jnp.concatenate([array, jnp.stack([head[1], at.to_z(head[0], -1)])], axis=2)

    pre_one = dot_nn(n1_all, w1)
    w_down = at.gather_z(mlp_down)
    cot_all = at.gather_plane(cot)
    branch, branch_back = jax.vjp(gelu_tanh, pre_one[:, :w_slot])
    conv_in = pre_one[:, w_slot:].astype(low).reshape(2, rows, span, w_slot)
    ext_in = with_before(conv_in)
    ext_code = with_before(seg_code)
    position = lax.broadcasted_iota(jnp.int32, (2, rows, span), 2)
    position = position + span * lax.broadcasted_iota(jnp.int32, (2, rows, span), 0)
    row_begin = (at.z == 0) & (position == 0)
    starts = (ext_code[:, :, reach - 1 : reach - 1 + span] != seg_code) | row_begin
    conv_sum = b_conv + w_conv[0] * conv_in.astype(wide)
    same_items = [None]
    for shift_by in range(1, taps):
        same_item = ext_code[:, :, reach - shift_by : reach - shift_by + span] == seg_code
        same_item = same_item & ((at.z > 0) | (position >= shift_by))
        same_items.append(same_item.astype(wide)[..., None])
        moved = ext_in[:, :, reach - shift_by : reach - shift_by + span].astype(wide)
        conv_sum = conv_sum + w_conv[shift_by] * moved * same_items[shift_by]
    conv_low = conv_sum.astype(low).reshape(tok_all, w_slot)
    starts = starts.reshape(tok_all, 1)
    gates_pre = dot_nn(conv_low, w_gates)
    rate = jax.nn.sigmoid(gates_pre[:, :w_slot] + b_rate)
    igate = jax.nn.sigmoid(gates_pre[:, w_slot:] + b_igate)
    conv_value = conv_low.astype(wide)
    log_slope = -rate_scale * jax.nn.softplus(-decay)
    log_keep = log_slope * rate
    keep = jnp.exp(log_keep)
    room = -jnp.expm1(2.0 * log_keep)
    mult = jnp.where(starts, 1.0, jnp.sqrt(jnp.maximum(room, floor_value)))
    keep_eff = jnp.where(starts, 0.0, keep)
    drive = mult * igate * conv_value
    flat = jax.ShapeDtypeStruct((tok_all, w_slot), wide)
    ends = jax.ShapeDtypeStruct((rows, w_slot), wide)
    both = jax.ShapeDtypeStruct((2, rows, w_slot), wide)
    summary = scan_call(summary_kernel, rows, span, (keep_eff, drive), both)
    before = [at.to_z(summary, by) for by in range(1, z_count)]
    state_in = jnp.zeros((rows, w_slot), wide)
    for part in reversed(before):
        state_in = part[1] + part[0] * state_in
    state, state_prev = scan_call(
        state_kernel, rows, span, (keep_eff, drive, state_in), (flat, flat)
    )
    mixed = (branch * state).astype(low)
    mixed, cot_all = together(mixed, cot_all)

    chip_one = at.chip_product(mixed, w_out, dot_nn, exact=True)
    resid = inputs + at.sum_plane(chip_one, exact=True)
    resid, w2 = together(resid, w2)

    s2 = lax.rsqrt(jnp.mean(resid * resid, axis=-1, keepdims=True) + eps_value)
    normed_two = (resid * s2 * gain_two).astype(low)
    n2_all, w_down = together(at.gather_plane(normed_two), w_down)
    pre_two = dot_nn(n2_all, w2)
    gate_act, gate_back = jax.vjp(gelu_tanh, pre_two[:, :f_slot])
    up_value = pre_two[:, f_slot:]
    hidden = (gate_act * up_value).astype(low)

    grad_hidden = dot_nt(cot_all, w_down)
    grad_gate_pre = gate_back(grad_hidden * up_value)[0].astype(low)
    grad_up = (grad_hidden * gate_act).astype(low)
    grad_two = jnp.concatenate([grad_gate_pre, grad_up], axis=1)
    chip_two = at.chip_product(grad_two, w2, dot_nt)
    chip_two, hidden_then, grad_two = together(chip_two, hidden, grad_two)

    def rows_split(product):
        return product.reshape(k_count, z_count, 2 * d_own, -1)

    down_part = at.own_apart(dot_tn(hidden_then, cot_all).reshape(z_count, f_own, width_d), 0)
    w2_part = at.own_apart(rows_split(dot_tn(n2_all, grad_two)), 1)
    grad_n2, hidden, w2_part, down_part = together(at.sum_plane(chip_two), hidden, w2_part, down_part)
    down_sum = at.scatter_z(down_part)
    w2_sum = at.scatter_z(w2_part)
    chip_three = at.chip_product(hidden, w_down, dot_nn)
    scaled_two = gain_two * grad_n2
    cot_f = cot.astype(wide)
    mean_two = jnp.mean(scaled_two * resid, axis=-1, keepdims=True)
    grad_resid = cot_f + s2 * scaled_two - resid * (s2 * s2 * s2) * mean_two
    grad_recur = grad_resid.astype(low)
    gr_all = at.gather_plane(grad_recur)
    gr_all, chip_three, down_sum = together(gr_all, chip_three, down_sum)
    block_out = (resid + at.sum_plane(chip_three)).astype(low)

    def summed(pair):
        return pair[0].astype(wide) + pair[1].astype(wide)

    grad_down = summed(down_sum)

    grad_mixed = dot_nt(gr_all, w_out)
    grad_out = dot_tn(mixed, gr_all)
    grad_branch = branch_back(grad_mixed * state)[0].astype(low)
    grad_state = grad_mixed * branch
    back = scan_call(back_summary_kernel, rows, span, (keep_eff, grad_state), ends)
    own = jnp.stack([summary[0], back])
    after = [at.to_z(own, -by) for by in range(1, z_count)]
    carry_in = jnp.zeros((rows, w_slot), wide)
    for part in reversed(after):
        carry_in = part[1] + part[0] * carry_in
    adjoint = scan_call(
        adjoint_kernel, rows, span, (keep_eff, grad_state, carry_in), flat
    )
    not_start = jnp.where(starts, 0.0, 1.0)
    through_mult = jnp.where(
        room > floor_value, adjoint * igate * conv_value * keep * keep / mult, 0.0
    )
    grad_log_keep = not_start * (adjoint * state_prev * keep - through_mult)
    grad_rate_pre = (grad_log_keep * log_slope * rate * (1.0 - rate)).astype(low)
    grad_igate_pre = (adjoint * mult * conv_value * igate * (1.0 - igate)).astype(low)
    grad_decay = jnp.sum(grad_log_keep * rate, axis=0) * (rate_scale * jax.nn.sigmoid(-decay[0]))
    grad_rate_bias = jnp.sum(grad_rate_pre.astype(wide), axis=0)
    grad_igate_bias = jnp.sum(grad_igate_pre.astype(wide), axis=0)
    grad_gates = jnp.concatenate([grad_rate_pre, grad_igate_pre], axis=1)
    grad_gates_w = dot_tn(conv_low, grad_gates).reshape(heads, BS, 2, heads, BS)
    grad_gates_w = jnp.stack([grad_gates_w[h, :, :, h] for h in range(heads)])
    grad_gates_w = grad_gates_w.reshape(w_slot, 2 * BS)
    grad_conv = adjoint * mult * igate + dot_nt(grad_gates, w_gates)
    grad_conv, block_out = together(
        grad_conv.astype(low).reshape(2, rows, span, w_slot), block_out
    )
    grad_conv_f = grad_conv.astype(wide)
    grad_conv_bias = jnp.sum(grad_conv_f, axis=(0, 1, 2))
    tap_grads = [jnp.sum(grad_conv_f * conv_in.astype(wide), axis=(0, 1, 2))]
    for shift_by in range(1, taps):
        moved = ext_in[:, :, reach - shift_by : reach - shift_by + span].astype(wide)
        tap_grads.append(jnp.sum(grad_conv_f * moved * same_items[shift_by], axis=(0, 1, 2)))
    ext_grad = with_after(grad_conv)
    next_code = with_after(seg_code)
    grad_conv_in = w_conv[0] * grad_conv_f
    for shift_by in range(1, taps):
        ahead_same = next_code[:, :, shift_by : shift_by + span] == seg_code
        ahead_same = ahead_same & ((at.z < z_count - 1) | (position < 2 * span - shift_by))
        ahead = ext_grad[:, :, shift_by : shift_by + span].astype(wide)
        grad_conv_in = grad_conv_in + w_conv[shift_by] * ahead * ahead_same.astype(wide)[..., None]
    grad_conv_in = grad_conv_in.astype(low).reshape(tok_all, w_slot)
    grad_conv_in, w2_sum = together(grad_conv_in, w2_sum)
    grad_one = jnp.concatenate([grad_branch, grad_conv_in], axis=1)
    w1_split = rows_split(dot_tn(n1_all, grad_one))

    def w1_chunk(i):
        return lax.dynamic_index_in_dim(w1_split, i, 1, False)

    w1_far, w1_near = at.sum_far(w1_chunk), at.sum_near(w1_chunk)
    grad_w1 = at.sum_all(w1_chunk, w1_near, at.sum_second(w1_chunk, w1_far))
    grad_n1 = at.sum_plane(at.chip_product(grad_one, w1, dot_nt))
    scaled_one = gain_one * grad_n1
    mean_one = jnp.mean(scaled_one * inputs, axis=-1, keepdims=True)
    grad_tokens = grad_resid + s1 * scaled_one - inputs * (s1 * s1 * s1) * mean_one
    grad_tokens = grad_tokens.reshape(row_dev, span, width_d)
    block_out = block_out.reshape(row_dev, span, width_d)

    vectors = jnp.stack(tap_grads + [grad_conv_bias, grad_rate_bias, grad_igate_bias, grad_decay], axis=1)
    rec_rows = jnp.concatenate([grad_out, grad_gates_w, vectors], axis=1).astype(low)
    rec_rows = jnp.pad(rec_rows, ((0, 0), (0, -rec_rows.shape[1] % 128)))
    rec_rows = rec_rows.reshape(half_z, 2, w_own, -1)
    rows_keep = lax.dynamic_index_in_dim(rec_rows, at.c, 1, False)
    rows_got = at.to_core(lax.dynamic_index_in_dim(rec_rows, 1 - at.c, 1, False))
    rec_split = at.by_core(rows_keep, rows_got).reshape(z_count, w_own, -1)
    rec_part, w2_sum = together(at.own_apart(rec_split, 0), w2_sum)
    rec_rows = summed(at.scatter_z(rec_part))
    grad_out_w = rec_rows[:, :width_d]
    grad_rate_w = rec_rows[:, width_d : width_d + BS]
    grad_igate_w = rec_rows[:, width_d + BS : out_cols]
    grad_small = rec_rows[:, out_cols : out_cols + taps + 4].T

    def to_owner(array, columns):
        return at.exchange_plane(array.reshape(k_count, 2, d_own, columns))

    mlp_back = to_owner(summed(w2_sum).astype(low), 2 * f_slot)
    mlp_whole = jax.ShapeDtypeStruct(mlp_gate.shape, wide)
    join = functools.partial(join_kernel, k_count, z_count)
    grad_gate_w, grad_up_w = in_vmem(join, (mlp_back,), (mlp_whole, mlp_whole))
    rec_back = jnp.moveaxis(to_owner(grad_w1, 2 * w_slot), 2, 0).astype(wide)
    grad_branch_w = rec_back[..., :w_slot].reshape(d_own, width_r)
    grad_input_w = rec_back[..., w_slot:].reshape(d_own, width_r)

    def gain_grad(pairs, gain):
        total = sum(jnp.sum(weight.astype(wide) * grad, axis=1) for weight, grad in pairs)
        return total / gain.astype(wide)

    grad_norm_one = gain_grad(((branch_weight, grad_branch_w), (input_proj, grad_input_w)), norm_one)
    grad_norm_two = gain_grad(((mlp_gate, grad_gate_w), (mlp_up, grad_up_w)), norm_two)
    return (
        block_out,
        grad_tokens,
        grad_norm_one,
        grad_branch_w,
        grad_input_w,
        grad_small[:taps],
        grad_small[taps],
        grad_rate_w,
        grad_igate_w,
        grad_small[taps + 1],
        grad_small[taps + 2],
        grad_small[taps + 3],
        grad_out_w,
        grad_norm_two,
        grad_gate_w,
        grad_up_w,
        grad_down,
    )


def solution(mesh):
    rows, matrix = P(AXES), P(AXES, None)
    tokens = P("dp", "seq", None)
    return jax.shard_map(
        per_device,
        mesh=mesh,
        in_specs=(
            tokens,
            P("dp", "seq"),
            tokens,
            rows,
            matrix,
            matrix,
            P(None, AXES),
            rows,
            matrix,
            matrix,
            rows,
            rows,
            rows,
            matrix,
            rows,
            matrix,
            matrix,
            matrix,
        ),
        out_specs=(
            tokens,
            tokens,
            rows,
            matrix,
            matrix,
            P(None, AXES),
            rows,
            matrix,
            matrix,
            rows,
            rows,
            rows,
            matrix,
            rows,
            matrix,
            matrix,
            matrix,
        ),
        check_vma=False,
    )
```

time: 3560 us -> 936 us (0.26)
  waiting for transfers between devices: 2440 us -> 326 us
  blocking collectives: 288 us -> 0 us
  local copies, waits for them, and re-layouts: 401 us -> 117 us
  starting transfers between devices: 7.79 us -> 103 us
  matrix products: 258 us -> 178 us
  Pallas kernels: 0 us -> 48.1 us
    reduce_scatter x8 -> x3, waiting for transfers between devices: 2220 us -> 0.01 us  [scatter_z(): lax.psum_scatter(parts[0], AXES, scatter_dimension=0, axis_index_groups=s...]
    ppermute x4 -> x96, waiting for transfers between devices: 1.94 us -> 278 us  [the longest x48 202 us: to_k(): lax.ppermute(array, 'dp', [(i, i ^ flip) for i in range(self.k_count)])]
    all_gather x7 -> x0, blocking collectives: 202 us -> none  [the longest x1 56.8 us: per_device(): lax.all_gather(igate_weight, ('dp', 'seq'), axis=0, tiled=True)]
    slice x97 -> x31, local copies, waits for them, and re-layouts: 212 us -> 12.1 us  [the longest x1 3.51 us: per_device(): branch, branch_back = jax.vjp(gelu_tanh, pre_one[:, :w_slot])]
    all_gather x6 -> x4, waiting for transfers between devices: 213 us -> 48 us  [gather_z(): lax.all_gather(array, AXES, axis_index_groups=self.z_groups, tiled=True)]
    ppermute x4 -> x96, starting transfers between devices: 7.19 us -> 102 us  [the longest x48 57 us: to_k(): lax.ppermute(array, 'dp', [(i, i ^ flip) for i in range(self.k_count)])]
    unnamed x2 -> x0, blocking collectives: 86.2 us -> none
    dot_general x24 -> x19, matrix products: 258 us -> 178 us  [the longest x7 78.2 us: dot_nt(): lax.dot_general(left, right, (((1,), (1,)), ((), ())), preferred_element_...]
  transfers between devices with their start and end apart: 19 -> 103, of which waited for: 12 -> 39; matrix products, arithmetic and copies ran while one was open for 13% -> 31% of each run, Pallas kernels for 0% -> 5%
where the time goes in v1:
time: 936 us; the launch traced here: 927 us
  waiting for transfers between devices  326 us (35%)
  matrix products  178 us (19%)
  other arithmetic  137 us (15%)
  local copies, waits for them, and re-layouts  117 us (12%)
  starting transfers between devices  103 us (11%)
  Pallas kernels  48.1 us (5%)
  between operations  17.2 us (2%)
    ppermute x48, waiting for transfers between devices, to_k(): lax.ppermute(array, 'dp', [(i, i ^ flip) for i in range(self.k_count)])  202 us
    dot_general x7, matrix products, dot_nt(): lax.dot_general(left, right, (((1,), (1,)), ((), ())), preferred_element_...  78.2 us
    dot_general x7, matrix products, dot_nn(): lax.dot_general(left, right, (((1,), (0,)), ((), ())), preferred_element_...  57.8 us
    ppermute x48, starting transfers between devices, to_k(): lax.ppermute(array, 'dp', [(i, i ^ flip) for i in range(self.k_count)])  57 us
    all_gather x4, waiting for transfers between devices, gather_z(): lax.all_gather(array, AXES, axis_index_groups=self.z_groups, tiled=True)  48 us
    dot_general x5, matrix products, dot_tn(): lax.dot_general(left, right, (((0,), (0,)), ((), ())), preferred_element_...  42.2 us
    pallas_call x4, Pallas kernels, scan_call(): pl.pallas_call(functools.partial(kernel, rows, span), out_shape=out_shape...  34.3 us
    unnamed x269, local copies, waits for them, and re-layouts  34.2 us
  transfers between devices with their start and end apart: 103, of which 39 were waited for; matrix products, arithmetic and copies ran while one was open for 31% of the time, Pallas kernels for 5%

profile of v1, /device:TPU:0, one launch (start us, length us, event | category | flops | bytes accessed | tf_op | source)
XLA Modules:
  0.0 926.6 jit_solution(4592910668850105002)
XLA Ops:
  77.4 9.0 collective-permute-done.10.refs_2_
  88.6 6.3 collective-permute-done.20
  96.8 8.6 collective-permute-done.11.refs_3_
  136.7 9.0 fusion.218
  173.0 5.5 convert_multiply_fusion.7
  178.5 6.1 shard_map.307
  198.1 10.2 %shard_map.308 = (f32[2048,320]{1,0:T(8,128)S(1)}, f32[2048,320]{1,0:T(8,128)}) custom-call(f32[2048,320]{1,0:T(8,128)} %copy-done, f32[2048,320]{1,0:T(8,128)} %get-tuple-element.262.drive_ref, f32[8,320]{1,0:T(8,128)S(1)} %fusion.160.start_ref), custom_call_target="tpu_custom_call" | custom-call | tf_op jit(solution)/shard_map/pallas_call | solution.py:353
  213.5 5.9 fusion.114
  219.5 13.3 %collective-permute-done.40 = f32[1024,2048]{1,0:T(8,128)} collective-permute-done((f32[1024,2048]{1,0:T(8,128)}, f32[1024,2048]{1,0:T(8,128)}, u32[]{:S(2)}, u32[]{:S(2)}) %collective-permute-start.40) | collective-permute-done | bytes 8388640 | tf_op jit(solution)/shard_map/ppermute | solution.py:136
  232.8 6.5 abs_reduce_fusion
  250.6 22.2 %collective-permute-done.41 = f16[2,256,1152]{2,1,0:T(8,128)(2,1)S(1)} collective-permute-done((f16[2,256,1152]{2,1,0:T(8,128)(2,1)}, f16[2,256,1152]{2,1,0:T(8,128)(2,1)S(1)}, u32[]{:S(2)}, u32[]{:S(2)}) %collective-permute-start.41) | collective-permute-done | bytes 1179680 | tf_op jit(solution)/shard_map/ppermute | solution.py:133
  280.0 10.3 %collective-permute-done.42 = f16[256,1152]{1,0:T(8,128)(2,1)S(1)} collective-permute-done((f16[256,1152]{1,0:T(8,128)(2,1)S(1)}, f16[256,1152]{1,0:T(8,128)(2,1)S(1)}, u32[]{:S(2)}, u32[]{:S(2)}) %collective-permute-start.42) | collective-permute-done | bytes 589856 | tf_op jit(solution)/shard_map/ppermute | solution.py:133
  294.1 42.0 %all-gather.9.cloned.1.call-done = bf16[2048,1536]{1,0:T(8,128)(2,1)} async-done(((bf16[512,1536]{1,0:T(8,128)(2,1)}), bf16[2048,1536]{1,0:T(8,128)(2,1)}) %all-gather.9.cloned.1.call-update) | async-done | bytes 6291472 | tf_op jit(solution)/shard_map/all_gather | solution.py:146
  336.2 6.2 copy.292
  348.1 22.2 %collective-permute-done.45.refs_1_ = bf16[256,2048]{1,0:T(8,128)(2,1)S(1)} collective-permute-done((bf16[256,2048]{1,0:T(8,128)(2,1)S(1)}, bf16[256,2048]{1,0:T(8,128)(2,1)S(1)}, u32[]{:S(2)}, u32[]{:S(2)}) %collective-permute-start.45) | collective-permute-done | bytes 1048608 | tf_op jit(solution)/shard_map/ppermute | solution.py:133
  374.0 9.6 %collective-permute-done.47.refs_3_ = bf16[128,2048]{1,0:T(8,128)(2,1)S(1)} collective-permute-done((bf16[128,2048]{1,0:T(8,128)(2,1)S(1)}, bf16[128,2048]{1,0:T(8,128)(2,1)S(1)}, u32[]{:S(2)}, u32[]{:S(2)}) %collective-permute-start.47) | collective-permute-done | bytes 524320 | tf_op jit(solution)/shard_map/ppermute | solution.py:133
  393.4 6.0 all-gather.11.cloned.1.call-done
  399.3 19.2 %fusion.219 = f32[2048,1536]{0,1:T(8,128)} fusion(bf16[2048,2048]{1,0:T(8,128)(2,1)} %copy-done.4, bf16[2048,1536]{1,0:T(8,128)(2,1)} %bitcast.420), kind=kOutput, calls=%fused_computation.462 | convolution fusion | flops 12884901888 | bytes 27262976 | tf_op jit(solution)/shard_map/dot_general | solution.py:26
  418.5 17.3 %multiply_convert_fusion.1 = (bf16[2048,768]{0,1:T(8,128)(2,1)S(1)}, bf16[2048,768]{0,1:T(8,128)(2,1)S(1)}, bf16[2048,768]{0,1:T(8,128)(2,1)}) fusion(f32[2048,1536]{0,1:T(8,128)} %fusion.219, bf16[2048,2048]{1,0:T(8,128)(2,1)} %copy-done.3, bf16[768,2048]{1,0:T(8,128)(2,1)S(1)} %copy-done.120), kind=kOutput, calls=%fused_computation.27 | convolution fusion | flops 6483345408 | bytes 33554432 | tf_op jit(solution)/shard_map/dot_general | solution.py:30
  435.9 13.4 %convolution_convert_fusion = bf16[1024,2048]{1,0:T(8,128)(2,1)} fusion(bf16[2048,1536]{1,0:T(8,128)(2,1)} %bitcast.421, s32[]{:T(128)S(6)} %select_n.493, bf16[2048,768]{0,1:T(8,128)(2,1)S(1)} %get-tuple-element.242, bf16[2048,768]{0,1:T(8,128)(2,1)S(1)} %get-tuple-element.241), kind=kOutput, calls=%fused_computation.40 | convolution fusion | flops 6450839552 | bytes 16777220 | tf_op jit(solution)/shard_map/dot_general | solution.py:30
  456.8 12.5 %convert_add_fusion.2 = f32[1024,2048]{1,0:T(8,128)} fusion(bf16[1024,2048]{1,0:T(8,128)(2,1)} %collective-permute-done.54, bf16[2048,1536]{1,0:T(8,128)(2,1)} %bitcast.422, s32[]{:T(128)S(6)} %select_n.492, bf16[2048,768]{0,1:T(8,128)(2,1)} %copy-done.55, bf16[2048,768]{0,1:T(8,128)(2,1)} %copy-done.54), kind=kOutput, calls=%fused_computation.6 | convolution fusion | flops 6452936704 | bytes 25165828 | tf_op jit(solution)/shard_map/dot_general | solution.py:30
  478.5 15.9 %fusion.220 = f32[2048,1536]{1,0:T(8,128)} fusion(bf16[2048,2048]{1,0:T(8,128)(2,1)S(1)} %bitcast.374, bf16[2048,1536]{0,1:T(8,128)(2,1)S(1)} %pad_maximum_fusion), kind=kOutput, calls=%fused_computation.463 | convolution fusion | flops 12884901888 | bytes 27262976 | tf_op jit(solution)/shard_map/dot_general | solution.py:34
  494.4 10.7 %select_convert_fusion = (bf16[768,2048]{1,0:T(8,128)(2,1)}, f32[768,2048]{1,0:T(8,128)}) fusion(pred[768]{0:T(1024)(128)(4,1)S(1)} %broadcast_in_dim.118, bf16[2048,768]{0,1:T(8,128)(2,1)} %get-tuple-element.74, bf16[2048,2048]{1,0:T(8,128)(2,1)S(1)} %bitcast.372), kind=kOutput, calls=%fused_computation.25 | convolution fusion | flops 6444023808 | bytes 20972288 | tf_op jit(solution)/shard_map/dot_general | solution.py:34
  505.1 9.1 fusion
  525.5 5.8 collective-permute-done.56
  535.3 8.0 convolution_convert_fusion.2
  547.8 23.5 %collective-permute-done.59.refs_1_ = bf16[256,2048]{1,0:T(8,128)(2,1)S(1)} collective-permute-done((bf16[256,2048]{1,0:T(8,128)(2,1)S(1)}, bf16[256,2048]{1,0:T(8,128)(2,1)S(1)}, u32[]{:S(2)}, u32[]{:S(2)}) %collective-permute-start.59) | collective-permute-done | bytes 1048608 | tf_op jit(solution)/shard_map/ppermute | solution.py:133
  575.0 10.1 %collective-permute-done.61.refs_3_ = bf16[128,2048]{1,0:T(8,128)(2,1)} collective-permute-done((bf16[128,2048]{1,0:T(8,128)(2,1)S(1)}, bf16[128,2048]{1,0:T(8,128)(2,1)}, u32[]{:S(2)}, u32[]{:S(2)}) %collective-permute-start.61) | collective-permute-done | bytes 524320 | tf_op jit(solution)/shard_map/ppermute | solution.py:133
  599.2 7.6 convert_add_fusion.1
  606.8 13.5 %fusion.22 = (bf16[2048,320]{1,0:T(8,128)(2,1)}, f32[2048,320]{1,0:T(8,128)}) fusion(f32[2048,320]{1,0:T(8,128)} %copy.324, f32[2048,320]{1,0:T(8,128)S(1)} %copy-done.12, bf16[2048,2048]{1,0:T(8,128)(2,1)} %copy-done.5, bf16[320,2368]{1,0:T(8,128)(2,1)} %bitcast.413), kind=kOutput, calls=%fused_computation.57 | convolution fusion | flops 2699427840 | bytes 19398656 | tf_op jit(solution)/shard_map/dot_general | solution.py:30
  620.3 8.6 shard_map.312
  645.3 9.4 %shard_map.313 = f32[2048,320]{1,0:T(8,128)S(1)} custom-call(f32[2048,320]{1,0:T(8,128)} %copy-done, f32[2048,320]{1,0:T(8,128)} %get-tuple-element.261.grad_ref, f32[8,320]{1,0:T(8,128)S(1)} %fusion.154.start_ref), custom_call_target="tpu_custom_call" | custom-call | tf_op jit(solution)/shard_map/pallas_call | solution.py:353
  654.9 6.4 multiply_reduce_fusion
  661.3 6.2 fusion.205
  676.2 7.7 add_convert_fusion.1
  694.2 9.1 collective-permute-done.73
  721.7 5.8 fusion.40
  738.0 6.6 convolution_convert_fusion.1
  744.7 9.9 %fusion.56 = f32[2048,640]{1,0:T(8,128)S(1)} fusion(bf16[2048,2048]{1,0:T(8,128)(2,1)} %copy-done.2, bf16[2048,320]{1,0:T(8,128)(2,1)S(1)} %bitcast.440, bf16[2048,320]{1,0:T(8,128)(2,1)S(1)} %copy-done.123), kind=kOutput, calls=%fused_computation.104 | convolution fusion | flops 5373952000 | bytes 16252928 | tf_op jit(solution)/shard_map/dot_general | solution.py:34
  762.7 5.7 collective-permute-start.83
  769.1 7.3 collective-permute-done.85
  786.2 8.5 collective-permute-done.83
  795.8 32.6 %collective-permute-done.86 = bf16[4,128,640]{2,1,0:T(8,128)(2,1)} collective-permute-done((bf16[4,128,640]{2,1,0:T(8,128)(2,1)}, bf16[4,128,640]{2,1,0:T(8,128)(2,1)}, u32[]{:S(2)}, u32[]{:S(2)}) %collective-permute-start.86) | collective-permute-done | bytes 655392 | tf_op jit(solution)/shard_map/ppermute | solution.py:183
  837.8 6.9 collective-permute-done.88
  844.7 6.5 collective-permute-done.89
  854.5 7.1 convert_add_fusion
  872.1 20.5 %collective-permute-done.79 = bf16[2,256,1024]{2,1,0:T(8,128)(2,1)} collective-permute-done((bf16[2,256,1024]{2,1,0:T(8,128)(2,1)}, bf16[2,256,1024]{2,1,0:T(8,128)(2,1)}, u32[]{:S(2)}, u32[]{:S(2)}) %collective-permute-start.79) | collective-permute-done | bytes 1048608 | tf_op jit(solution)/shard_map/ppermute | solution.py:133
  903.7 9.1 collective-permute-done.80
  (696 shorter events, 369.8 us)
Async XLA Ops:
  7.2 100.1 %all-gather.7.cloned.1.call-start = ((), (), s32[]{:S(2)}) async-start(), calls=%async_computation.4 | async-start | bytes 1945600 | tf_op jit(solution)/shard_map/all_gather | solution.py:146
  18.7 20.0 %collective-permute-start = (bf16[4,64,640]{2,1,0:T(8,128)(2,1)S(1)}, bf16[4,64,640]{2,1,0:T(8,128)(2,1)S(1)}, u32[]{:S(2)}, u32[]{:S(2)}) collective-permute-start(bf16[4,64,640]{2,1,0:T(8,128)(2,1)S(1)} %bitcast.452), channel_id=1, source_target_pairs={{0,1},{1,0},{2,3},{3,2},{4,5},{5,4},{6,7},{7,6},{8,9},{9,8},{10,11... | collective-permute-start | bytes 983048 | tf_op jit(solution)/shard_map/ppermute | solution.py:136
  22.7 111.9 %all-gather.5.cloned.1.call-start = ((), (), s32[]{:S(2)}) async-start(), calls=%async_computation.3 | async-start | bytes 3276800 | tf_op jit(solution)/shard_map/all_gather | solution.py:146
  50.8 285.4 %all-gather.9.cloned.1.call-start = ((), (), s32[]{:S(2)}) async-start(), calls=%async_computation.5 | async-start | bytes 7864320 | tf_op jit(solution)/shard_map/all_gather | solution.py:146
  51.4 26.0 %collective-permute-start.9 = (bf16[256,2048]{1,0:T(8,128)(2,1)S(1)}, bf16[256,2048]{1,0:T(8,128)(2,1)S(1)}, u32[]{:S(2)}, u32[]{:S(2)}) collective-permute-start(bf16[256,2048]{1,0:T(8,128)(2,1)S(1)} %fusion.68.refs_0_), channel_id=1, source_target_pairs={{0,8},{8,0},{16,24},{24,16},{1,9},{9,1},{17,25},{25,17},{2,10},{10... | collective-permute-start | bytes 3145736 | tf_op jit(solution)/shard_map/ppermute | solution.py:133
  52.0 34.4 %collective-permute-start.10 = (bf16[256,2048]{1,0:T(8,128)(2,1)S(1)}, bf16[256,2048]{1,0:T(8,128)(2,1)S(1)}, u32[]{:S(2)}, u32[]{:S(2)}) collective-permute-start(bf16[256,2048]{1,0:T(8,128)(2,1)S(1)} %fusion.68.refs_0_), channel_id=1, source_target_pairs={{0,16},{8,24},{16,0},{24,8},{1,17},{9,25},{17,1},{25,9},{2,18},{10... | collective-permute-start | bytes 3145736 | tf_op jit(solution)/shard_map/ppermute | solution.py:133
  57.8 30.1 %collective-permute-start.19 = (bf16[2,64,1536]{2,1,0:T(8,128)(2,1)}, bf16[2,64,1536]{2,1,0:T(8,128)(2,1)S(1)}, u32[]{:S(2)}, u32[]{:S(2)}) collective-permute-start(bf16[2,64,1536]{2,1,0:T(8,128)(2,1)} %get-tuple-element.299), channel_id=1, source_target_pairs={{0,24},{8,16},{16,8},{24,0},{1,25},{9,17},{17,9},{25,1},{2,26},{10... | collective-permute-start | bytes 1179656 | tf_op jit(solution)/shard_map/ppermute | solution.py:133
  59.3 35.6 %collective-permute-start.20 = (bf16[2,64,1536]{2,1,0:T(8,128)(2,1)}, bf16[2,64,1536]{2,1,0:T(8,128)(2,1)}, u32[]{:S(2)}, u32[]{:S(2)}) collective-permute-start(bf16[2,64,1536]{2,1,0:T(8,128)(2,1)} %get-tuple-element.298), channel_id=1, source_target_pairs={{0,16},{8,24},{16,0},{24,8},{1,17},{9,25},{17,1},{25,9},{2,18},{10... | collective-permute-start | bytes 1179656 | tf_op jit(solution)/shard_map/ppermute | solution.py:133
  59.9 35.0 %collective-permute-start.21 = (bf16[2,64,1536]{2,1,0:T(8,128)(2,1)}, bf16[2,64,1536]{2,1,0:T(8,128)(2,1)}, u32[]{:S(2)}, u32[]{:S(2)}) collective-permute-start(bf16[2,64,1536]{2,1,0:T(8,128)(2,1)} %get-tuple-element.297), channel_id=1, source_target_pairs={{0,8},{8,0},{16,24},{24,16},{1,9},{9,1},{17,25},{25,17},{2,10},{10... | collective-permute-start | bytes 1179656 | tf_op jit(solution)/shard_map/ppermute | solution.py:133
  77.4 32.6 %collective-permute-start.13 = (bf16[256,2048]{1,0:T(8,128)(2,1)S(1)}, bf16[256,2048]{1,0:T(8,128)(2,1)}, u32[]{:S(2)}, u32[]{:S(2)}) collective-permute-start(bf16[256,2048]{1,0:T(8,128)(2,1)S(1)} %fusion.68.refs_0_), channel_id=1, source_target_pairs={{0,1},{1,0},{2,3},{3,2},{4,5},{5,4},{6,7},{7,6},{8,9},{9,8},{10,11... | collective-permute-start | bytes 3145736 | tf_op jit(solution)/shard_map/ppermute | solution.py:136
  86.4 19.1 %collective-permute-start.11 = (bf16[128,2048]{1,0:T(8,128)(2,1)S(1)}, bf16[128,2048]{1,0:T(8,128)(2,1)}, u32[]{:S(2)}, u32[]{:S(2)}) collective-permute-start(bf16[128,2048]{1,0:T(8,128)(2,1)S(1)} %slice.610), channel_id=1, source_target_pairs={{0,16},{8,24},{16,0},{24,8},{1,17},{9,25},{17,1},{25,9},{2,18},{10... | collective-permute-start | bytes 1572872 | tf_op jit(solution)/shard_map/ppermute | solution.py:133
  110.0 20.4 %collective-permute-start.27 = (bf16[160,2368]{1,0:T(8,128)(2,1)}, bf16[160,2368]{1,0:T(8,128)(2,1)}, u32[]{:S(2)}, u32[]{:S(2)}) collective-permute-start(bf16[160,2368]{1,0:T(8,128)(2,1)} %get-tuple-element.307), channel_id=1, source_target_pairs={{0,1},{1,0},{2,3},{3,2},{4,5},{5,4},{6,7},{7,6},{8,9},{9,8},{10,11... | collective-permute-start | bytes 2273288 | tf_op jit(solution)/shard_map/ppermute | solution.py:136
  116.4 46.8 %collective-permute-start.31 = (bf16[256,2048]{1,0:T(8,128)(2,1)S(1)}, bf16[256,2048]{1,0:T(8,128)(2,1)S(1)}, u32[]{:S(2)}, u32[]{:S(2)}) collective-permute-start(bf16[256,2048]{1,0:T(8,128)(2,1)S(1)} %bitcast.377), channel_id=1, source_target_pairs={{0,8},{8,0},{16,24},{24,16},{1,9},{9,1},{17,25},{25,17},{2,10},{10... | collective-permute-start | bytes 3145736 | tf_op jit(solution)/shard_map/ppermute | solution.py:133
  117.9 46.9 %collective-permute-start.32 = (bf16[256,2048]{1,0:T(8,128)(2,1)S(1)}, bf16[256,2048]{1,0:T(8,128)(2,1)S(1)}, u32[]{:S(2)}, u32[]{:S(2)}) collective-permute-start(bf16[256,2048]{1,0:T(8,128)(2,1)S(1)} %bitcast.378), channel_id=1, source_target_pairs={{0,16},{8,24},{16,0},{24,8},{1,17},{9,25},{17,1},{25,9},{2,18},{10... | collective-permute-start | bytes 3145736 | tf_op jit(solution)/shard_map/ppermute | solution.py:133
  118.5 91.6 %collective-permute-start.35 = (bf16[256,2048]{1,0:T(8,128)(2,1)S(1)}, bf16[256,2048]{1,0:T(8,128)(2,1)}, u32[]{:S(2)}, u32[]{:S(2)}) collective-permute-start(bf16[256,2048]{1,0:T(8,128)(2,1)S(1)} %bitcast.379), channel_id=1, source_target_pairs={{0,1},{1,0},{2,3},{3,2},{4,5},{5,4},{6,7},{7,6},{8,9},{9,8},{10,11... | collective-permute-start | bytes 3145736 | tf_op jit(solution)/shard_map/ppermute | solution.py:136
  163.3 21.4 %collective-permute-start.33 = (bf16[128,2048]{1,0:T(8,128)(2,1)S(1)}, bf16[128,2048]{1,0:T(8,128)(2,1)S(1)}, u32[]{:S(2)}, u32[]{:S(2)}) collective-permute-start(bf16[128,2048]{1,0:T(8,128)(2,1)S(1)} %slice.641), channel_id=1, source_target_pairs={{0,16},{8,24},{16,0},{24,8},{1,17},{9,25},{17,1},{25,9},{2,18},{10... | collective-permute-start | bytes 1572872 | tf_op jit(solution)/shard_map/ppermute | solution.py:133
  165.6 21.2 %collective-permute-start.34 = (bf16[128,2048]{1,0:T(8,128)(2,1)}, bf16[128,2048]{1,0:T(8,128)(2,1)}, u32[]{:S(2)}, u32[]{:S(2)}) collective-permute-start(bf16[128,2048]{1,0:T(8,128)(2,1)} %slice.642), channel_id=1, source_target_pairs={{0,8},{8,0},{16,24},{24,16},{1,9},{9,1},{17,25},{25,17},{2,10},{10... | collective-permute-start | bytes 1572872 | tf_op jit(solution)/shard_map/ppermute | solution.py:133
  166.1 43.9 %collective-permute-start.36 = (bf16[256,2048]{1,0:T(8,128)(2,1)S(1)}, bf16[256,2048]{1,0:T(8,128)(2,1)}, u32[]{:S(2)}, u32[]{:S(2)}) collective-permute-start(bf16[256,2048]{1,0:T(8,128)(2,1)S(1)} %collective-permute-done.31.refs_1_), channel_id=1, source_target_pairs={{0,1},{1,0},{2,3},{3,2},{4,5},{5,4},{6,7},{7,6},{8,9},{9,8},{10,11... | collective-permute-start | bytes 3145736 | tf_op jit(solution)/shard_map/ppermute | solution.py:136
  166.1 43.9 %collective-permute-start.37 = (bf16[256,2048]{1,0:T(8,128)(2,1)S(1)}, bf16[256,2048]{1,0:T(8,128)(2,1)}, u32[]{:S(2)}, u32[]{:S(2)}) collective-permute-start(bf16[256,2048]{1,0:T(8,128)(2,1)S(1)} %collective-permute-done.32.refs_2_), channel_id=1, source_target_pairs={{0,1},{1,0},{2,3},{3,2},{4,5},{5,4},{6,7},{7,6},{8,9},{9,8},{10,11... | collective-permute-start | bytes 3145736 | tf_op jit(solution)/shard_map/ppermute | solution.py:136
  219.4 179.9 %all-gather.11.cloned.1.call-start = ((), (), s32[]{:S(2)}) async-start(), calls=%async_computation.6 | async-start | bytes 3932160 | tf_op jit(solution)/shard_map/all_gather | solution.py:146
  244.6 28.2 %collective-permute-start.41 = (f16[2,256,1152]{2,1,0:T(8,128)(2,1)}, f16[2,256,1152]{2,1,0:T(8,128)(2,1)S(1)}, u32[]{:S(2)}, u32[]{:S(2)}) collective-permute-start(f16[2,256,1152]{2,1,0:T(8,128)(2,1)} %pad_maximum_fusion.9), channel_id=1, source_target_pairs={{0,8},{8,0},{16,24},{24,16},{1,9},{9,1},{17,25},{25,17},{2,10},{10... | collective-permute-start | bytes 3538952 | tf_op jit(solution)/shard_map/ppermute | solution.py:133
  246.1 360.7 %reduce-scatter.4.cloned.1.call-start = ((), (), s32[]{:S(2)}) async-start(), calls=%async_computation.7 | async-start | bytes 3932160 | tf_op jit(solution)/shard_map/reduce_scatter | solution.py:160
  249.7 28.2 %collective-permute-start.43 = (f16[2,256,1152]{2,1,0:T(8,128)(2,1)}, f16[2,256,1152]{2,1,0:T(8,128)(2,1)}, u32[]{:S(2)}, u32[]{:S(2)}) collective-permute-start(f16[2,256,1152]{2,1,0:T(8,128)(2,1)} %pad_maximum_fusion.10), channel_id=1, source_target_pairs={{0,16},{8,24},{16,0},{24,8},{1,17},{9,25},{17,1},{25,9},{2,18},{10... | collective-permute-start | bytes 3538952 | tf_op jit(solution)/shard_map/ppermute | solution.py:133
  292.7 49.6 %collective-permute-start.44 = (f16[256,1152]{1,0:T(8,128)(2,1)S(1)}, f16[256,1152]{1,0:T(8,128)(2,1)S(1)}, u32[]{:S(2)}, u32[]{:S(2)}) collective-permute-start(f16[256,1152]{1,0:T(8,128)(2,1)S(1)} %pad_maximum_fusion.16), channel_id=1, source_target_pairs={{0,8},{8,0},{16,24},{24,16},{1,9},{9,1},{17,25},{25,17},{2,10},{10... | collective-permute-start | bytes 1769480 | tf_op jit(solution)/shard_map/ppermute | solution.py:133
  345.1 25.2 %collective-permute-start.45 = (bf16[256,2048]{1,0:T(8,128)(2,1)S(1)}, bf16[256,2048]{1,0:T(8,128)(2,1)S(1)}, u32[]{:S(2)}, u32[]{:S(2)}) collective-permute-start(bf16[256,2048]{1,0:T(8,128)(2,1)S(1)} %multiply_convert_fusion.4.refs_0_), channel_id=1, source_target_pairs={{0,8},{8,0},{16,24},{24,16},{1,9},{9,1},{17,25},{25,17},{2,10},{10... | collective-permute-start | bytes 3145736 | tf_op jit(solution)/shard_map/ppermute | solution.py:133
  346.6 25.3 %collective-permute-start.46 = (bf16[256,2048]{1,0:T(8,128)(2,1)S(1)}, bf16[256,2048]{1,0:T(8,128)(2,1)S(1)}, u32[]{:S(2)}, u32[]{:S(2)}) collective-permute-start(bf16[256,2048]{1,0:T(8,128)(2,1)S(1)} %multiply_convert_fusion.4.refs_0_), channel_id=1, source_target_pairs={{0,16},{8,24},{16,0},{24,8},{1,17},{9,25},{17,1},{25,9},{2,18},{10... | collective-permute-start | bytes 3145736 | tf_op jit(solution)/shard_map/ppermute | solution.py:133
  348.1 38.3 %collective-permute-start.49 = (bf16[256,2048]{1,0:T(8,128)(2,1)S(1)}, bf16[256,2048]{1,0:T(8,128)(2,1)S(1)}, u32[]{:S(2)}, u32[]{:S(2)}) collective-permute-start(bf16[256,2048]{1,0:T(8,128)(2,1)S(1)} %multiply_convert_fusion.4.refs_0_), channel_id=1, source_target_pairs={{0,1},{1,0},{2,3},{3,2},{4,5},{5,4},{6,7},{7,6},{8,9},{9,8},{10,11... | collective-permute-start | bytes 3145736 | tf_op jit(solution)/shard_map/ppermute | solution.py:136
  475.5 38.6 %collective-permute-start.55 = (bf16[2,256,1024]{2,1,0:T(8,128)(2,1)}, bf16[2,256,1024]{2,1,0:T(8,128)(2,1)}, u32[]{:S(2)}, u32[]{:S(2)}) collective-permute-start(bf16[2,256,1024]{2,1,0:T(8,128)(2,1)} %pad_maximum_fusion.11), channel_id=1, source_target_pairs={{0,8},{8,0},{16,24},{24,16},{1,9},{9,1},{17,25},{25,17},{2,10},{10... | collective-permute-start | bytes 3145736 | tf_op jit(solution)/shard_map/ppermute | solution.py:133
  477.0 38.6 %collective-permute-start.57 = (bf16[2,256,1024]{2,1,0:T(8,128)(2,1)}, bf16[2,256,1024]{2,1,0:T(8,128)(2,1)S(1)}, u32[]{:S(2)}, u32[]{:S(2)}) collective-permute-start(bf16[2,256,1024]{2,1,0:T(8,128)(2,1)} %stack.352), channel_id=1, source_target_pairs={{0,16},{8,24},{16,0},{24,8},{1,17},{9,25},{17,1},{25,9},{2,18},{10... | collective-permute-start | bytes 3145736 | tf_op jit(solution)/shard_map/ppermute | solution.py:133
  535.3 202.8 %reduce-scatter.6.cloned.1.call-start = ((), (), s32[]{:S(2)}) async-start(), calls=%async_computation.8 | async-start | bytes 7864320 | tf_op jit(solution)/shard_map/reduce_scatter | solution.py:160
  543.3 55.8 %collective-permute-start.68 = (bf16[1024,2048]{1,0:T(8,128)(2,1)}, bf16[1024,2048]{1,0:T(8,128)(2,1)}, u32[]{:S(2)}, u32[]{:S(2)}) collective-permute-start(bf16[1024,2048]{1,0:T(8,128)(2,1)} %convolution_convert_fusion.2), channel_id=1, source_target_pairs={{0,1},{1,0},{2,3},{3,2},{4,5},{5,4},{6,7},{7,6},{8,9},{9,8},{10,11... | collective-permute-start | bytes 12582920 | tf_op jit(solution)/shard_map/ppermute | solution.py:136
  545.7 25.6 %collective-permute-start.59 = (bf16[256,2048]{1,0:T(8,128)(2,1)S(1)}, bf16[256,2048]{1,0:T(8,128)(2,1)S(1)}, u32[]{:S(2)}, u32[]{:S(2)}) collective-permute-start(bf16[256,2048]{1,0:T(8,128)(2,1)S(1)} %get-tuple-element.239.refs_0_), channel_id=1, source_target_pairs={{0,8},{8,0},{16,24},{24,16},{1,9},{9,1},{17,25},{25,17},{2,10},{10... | collective-permute-start | bytes 3145736 | tf_op jit(solution)/shard_map/ppermute | solution.py:133
  546.3 26.6 %collective-permute-start.60 = (bf16[256,2048]{1,0:T(8,128)(2,1)S(1)}, bf16[256,2048]{1,0:T(8,128)(2,1)S(1)}, u32[]{:S(2)}, u32[]{:S(2)}) collective-permute-start(bf16[256,2048]{1,0:T(8,128)(2,1)S(1)} %get-tuple-element.239.refs_0_), channel_id=1, source_target_pairs={{0,16},{8,24},{16,0},{24,8},{1,17},{9,25},{17,1},{25,9},{2,18},{10... | collective-permute-start | bytes 3145736 | tf_op jit(solution)/shard_map/ppermute | solution.py:133
  547.8 25.8 %collective-permute-start.63 = (bf16[256,2048]{1,0:T(8,128)(2,1)S(1)}, bf16[256,2048]{1,0:T(8,128)(2,1)S(1)}, u32[]{:S(2)}, u32[]{:S(2)}) collective-permute-start(bf16[256,2048]{1,0:T(8,128)(2,1)S(1)} %get-tuple-element.239.refs_0_), channel_id=1, source_target_pairs={{0,1},{1,0},{2,3},{3,2},{4,5},{5,4},{6,7},{7,6},{8,9},{9,8},{10,11... | collective-permute-start | bytes 3145736 | tf_op jit(solution)/shard_map/ppermute | solution.py:136
  572.9 18.3 %collective-permute-start.64 = (bf16[256,2048]{1,0:T(8,128)(2,1)S(1)}, bf16[256,2048]{1,0:T(8,128)(2,1)}, u32[]{:S(2)}, u32[]{:S(2)}) collective-permute-start(bf16[256,2048]{1,0:T(8,128)(2,1)S(1)} %collective-permute-done.59.refs_1_), channel_id=1, source_target_pairs={{0,1},{1,0},{2,3},{3,2},{4,5},{5,4},{6,7},{7,6},{8,9},{9,8},{10,11... | collective-permute-start | bytes 3145736 | tf_op jit(solution)/shard_map/ppermute | solution.py:136
  591.2 279.0 %reduce-scatter.8.cloned.1.call-start = ((), (), s32[]{:S(2)}) async-start(), calls=%async_computation.9 | async-start | bytes 1945600 | tf_op jit(solution)/shard_map/reduce_scatter | solution.py:160
  643.7 40.2 %collective-permute-start.72 = (bf16[2,256,1024]{2,1,0:T(8,128)(2,1)}, bf16[2,256,1024]{2,1,0:T(8,128)(2,1)}, u32[]{:S(2)}, u32[]{:S(2)}) collective-permute-start(bf16[2,256,1024]{2,1,0:T(8,128)(2,1)} %pad_maximum_fusion.12), channel_id=1, source_target_pairs={{0,8},{8,0},{16,24},{24,16},{1,9},{9,1},{17,25},{25,17},{2,10},{10... | collective-permute-start | bytes 3145736 | tf_op jit(solution)/shard_map/ppermute | solution.py:133
  644.2 41.7 %collective-permute-start.74 = (bf16[2,256,1024]{2,1,0:T(8,128)(2,1)}, bf16[2,256,1024]{2,1,0:T(8,128)(2,1)}, u32[]{:S(2)}, u32[]{:S(2)}) collective-permute-start(bf16[2,256,1024]{2,1,0:T(8,128)(2,1)} %stack.353), channel_id=1, source_target_pairs={{0,16},{8,24},{16,0},{24,8},{1,17},{9,25},{17,1},{25,9},{2,18},{10... | collective-permute-start | bytes 3145736 | tf_op jit(solution)/shard_map/ppermute | solution.py:133
  754.7 99.8 %collective-permute-start.78 = (bf16[1024,2048]{1,0:T(8,128)(2,1)}, bf16[1024,2048]{1,0:T(8,128)(2,1)}, u32[]{:S(2)}, u32[]{:S(2)}) collective-permute-start(bf16[1024,2048]{1,0:T(8,128)(2,1)} %convolution_convert_fusion.1), channel_id=1, source_target_pairs={{0,1},{1,0},{2,3},{3,2},{4,5},{5,4},{6,7},{7,6},{8,9},{9,8},{10,11... | collective-permute-start | bytes 12582920 | tf_op jit(solution)/shard_map/ppermute | solution.py:136
  756.1 20.3 %collective-permute-start.85 = (bf16[4,128,640]{2,1,0:T(8,128)(2,1)S(1)}, bf16[4,128,640]{2,1,0:T(8,128)(2,1)S(1)}, u32[]{:S(2)}, u32[]{:S(2)}) collective-permute-start(bf16[4,128,640]{2,1,0:T(8,128)(2,1)S(1)} %get-tuple-element.267), channel_id=1, source_target_pairs={{0,2},{1,3},{6,4},{7,5},{8,10},{9,11},{14,12},{15,13},{16,18},{17,... | collective-permute-start | bytes 1966088 | tf_op jit(solution)/shard_map/ppermute | solution.py:170
  761.4 23.3 %collective-permute-start.84 = (bf16[4,128,640]{2,1,0:T(8,128)(2,1)}, bf16[4,128,640]{2,1,0:T(8,128)(2,1)S(1)}, u32[]{:S(2)}, u32[]{:S(2)}) collective-permute-start(bf16[4,128,640]{2,1,0:T(8,128)(2,1)} %get-tuple-element.268), channel_id=1, source_target_pairs={{2,0},{3,1},{4,2},{5,3},{6,4},{7,5},{10,8},{11,9},{12,10},{13,11},... | collective-permute-start | bytes 1966088 | tf_op jit(solution)/shard_map/ppermute | solution.py:140
  762.7 31.9 %collective-permute-start.83 = (bf16[4,128,640]{2,1,0:T(8,128)(2,1)}, bf16[4,128,640]{2,1,0:T(8,128)(2,1)}, u32[]{:S(2)}, u32[]{:S(2)}) collective-permute-start(bf16[4,128,640]{2,1,0:T(8,128)(2,1)} %get-tuple-element.266), channel_id=1, source_target_pairs={{0,2},{1,3},{2,4},{3,5},{4,6},{5,7},{8,10},{9,11},{10,12},{11,13},... | collective-permute-start | bytes 1966088 | tf_op jit(solution)/shard_map/ppermute | solution.py:140
  777.4 51.0 %collective-permute-start.86 = (bf16[4,128,640]{2,1,0:T(8,128)(2,1)}, bf16[4,128,640]{2,1,0:T(8,128)(2,1)}, u32[]{:S(2)}, u32[]{:S(2)}) collective-permute-start(bf16[4,128,640]{2,1,0:T(8,128)(2,1)} %fusion.81), channel_id=1, source_target_pairs={{0,4},{1,5},{2,6},{3,7},{4,0},{5,1},{6,2},{7,3},{8,12},{9,13},{10,... | collective-permute-start | bytes 1966088 | tf_op jit(solution)/shard_map/ppermute | solution.py:183
  783.2 47.4 %collective-permute-start.93 = (bf16[2,64,1536]{2,1,0:T(8,128)(2,1)S(1)}, bf16[2,64,1536]{2,1,0:T(8,128)(2,1)S(1)}, u32[]{:S(2)}, u32[]{:S(2)}) collective-permute-start(bf16[2,64,1536]{2,1,0:T(8,128)(2,1)S(1)} %get-tuple-element.289), channel_id=1, source_target_pairs={{0,24},{8,16},{16,8},{24,0},{1,25},{9,17},{17,9},{25,1},{2,26},{10... | collective-permute-start | bytes 1179656 | tf_op jit(solution)/shard_map/ppermute | solution.py:133
  784.7 45.9 %collective-permute-start.94 = (bf16[2,64,1536]{2,1,0:T(8,128)(2,1)S(1)}, bf16[2,64,1536]{2,1,0:T(8,128)(2,1)S(1)}, u32[]{:S(2)}, u32[]{:S(2)}) collective-permute-start(bf16[2,64,1536]{2,1,0:T(8,128)(2,1)S(1)} %get-tuple-element.288), channel_id=1, source_target_pairs={{0,16},{8,24},{16,0},{24,8},{1,17},{9,25},{17,1},{25,9},{2,18},{10... | collective-permute-start | bytes 1179656 | tf_op jit(solution)/shard_map/ppermute | solution.py:133
  794.6 36.0 %collective-permute-start.95 = (bf16[2,64,1536]{2,1,0:T(8,128)(2,1)S(1)}, bf16[2,64,1536]{2,1,0:T(8,128)(2,1)S(1)}, u32[]{:S(2)}, u32[]{:S(2)}) collective-permute-start(bf16[2,64,1536]{2,1,0:T(8,128)(2,1)S(1)} %get-tuple-element.287), channel_id=1, source_target_pairs={{0,8},{8,0},{16,24},{24,16},{1,9},{9,1},{17,25},{25,17},{2,10},{10... | collective-permute-start | bytes 1179656 | tf_op jit(solution)/shard_map/ppermute | solution.py:133
  867.3 25.3 %collective-permute-start.79 = (bf16[2,256,1024]{2,1,0:T(8,128)(2,1)}, bf16[2,256,1024]{2,1,0:T(8,128)(2,1)}, u32[]{:S(2)}, u32[]{:S(2)}) collective-permute-start(bf16[2,256,1024]{2,1,0:T(8,128)(2,1)} %pad_maximum_fusion.13), channel_id=1, source_target_pairs={{0,8},{8,0},{16,24},{24,16},{1,9},{9,1},{17,25},{25,17},{2,10},{10... | collective-permute-start | bytes 3145736 | tf_op jit(solution)/shard_map/ppermute | solution.py:133
  868.1 26.0 %collective-permute-start.81 = (bf16[2,256,1024]{2,1,0:T(8,128)(2,1)}, bf16[2,256,1024]{2,1,0:T(8,128)(2,1)}, u32[]{:S(2)}, u32[]{:S(2)}) collective-permute-start(bf16[2,256,1024]{2,1,0:T(8,128)(2,1)} %stack.354), channel_id=1, source_target_pairs={{0,16},{8,24},{16,0},{24,8},{1,17},{9,25},{17,1},{25,9},{2,18},{10... | collective-permute-start | bytes 3145736 | tf_op jit(solution)/shard_map/ppermute | solution.py:133
  (189 other events, 2226.2 us)
Sparse Core Ops, SparseCore 0:
  22.9 37.2 all-gather.6
  62.2 53.6 all-gather.4
  219.6 116.5 all-gather.8
  337.6 61.7 all-gather.10
  535.4 58.0 reduce-scatter.3
  595.6 112.3 reduce-scatter.5
  783.0 50.9 reduce-scatter.7

commit v2 on v1

v2 whole, which is shorter than its diff:
```python
import functools

import jax
import jax.numpy as jnp
from jax import lax
from jax.experimental import pallas as pl
from jax.experimental.pallas import tpu as pltpu
from jax.sharding import PartitionSpec as P

HEADS = 16
BS = 160
AXES = ("dp", "seq")

eps_value = 1e-06
rate_scale = 8.0
floor_value = 0.001
low = jnp.bfloat16
wide = jnp.float32


def gelu_tanh(value):
    return jax.nn.gelu(value, approximate=True)


def dot_nn(left, right):
    return lax.dot_general(left, right, (((1,), (0,)), ((), ())), preferred_element_type=wide)


def dot_nt(left, right):
    return lax.dot_general(left, right, (((1,), (1,)), ((), ())), preferred_element_type=wide)


def dot_tn(left, right):
    return lax.dot_general(left, right, (((0,), (0,)), ((), ())), preferred_element_type=wide)


def lay_out_kernel(count, c_ref, *refs):
    parts, (out_ref, buffer, sem, out_sem) = refs[: 2 * count], refs[2 * count :]
    core = c_ref[0]
    copies = []
    for which in range(2):
        start = (core if which == 0 else 1 - core) * (out_ref.shape[0] // 2)
        for i, part in enumerate(parts[which * count : (which + 1) * count]):
            at = pl.ds(pl.multiple_of(start, 16), part.shape[0])
            j = which * count + i
            into = pltpu.make_async_copy(part, buffer.at[at], sem.at[j])
            into.start()
            copies.append((into, pltpu.make_async_copy(buffer.at[at], out_ref.at[at], out_sem.at[j])))
            start = start + part.shape[0]
    for into, out in copies:
        into.wait()
        out.start()
    for into, out in copies:
        out.wait()


def lay_out(core, own, other):
    rows = 2 * sum(part.shape[0] for part in own)
    shape = (rows,) + own[0].shape[1:]
    anywhere = pl.BlockSpec(memory_space=pl.ANY)
    return pl.pallas_call(
        functools.partial(lay_out_kernel, len(own)),
        out_shape=jax.ShapeDtypeStruct(shape, own[0].dtype),
        in_specs=[pl.BlockSpec(memory_space=pltpu.SMEM)] + [anywhere] * (2 * len(own)),
        out_specs=anywhere,
        scratch_shapes=[
            pltpu.VMEM(shape, own[0].dtype),
            pltpu.SemaphoreType.DMA((2 * len(own),)),
            pltpu.SemaphoreType.DMA((2 * len(own),)),
        ],
        compiler_params=pltpu.CompilerParams(vmem_limit_bytes=32 * 2**20),
    )(core.reshape(1).astype(jnp.int32), *own, *other)


def together(*arrays):
    return lax.optimization_barrier(arrays)


def cut_kernel(k_count, z_count, gate_ref, up_ref, out_ref):
    own = out_ref.shape[3] // (2 * z_count)
    for k in range(k_count):
        for c in range(2):
            for which, ref in enumerate((gate_ref, up_ref)):
                for z in range(z_count):
                    at = ((k * z_count + z) * 2 + c) * own
                    to = (which * z_count + z) * own
                    out_ref[k, c, :, to : to + own] = ref[:, at : at + own]


def join_kernel(k_count, z_count, in_ref, gate_ref, up_ref):
    own = in_ref.shape[3] // (2 * z_count)
    for k in range(k_count):
        for c in range(2):
            for which, ref in enumerate((gate_ref, up_ref)):
                for z in range(z_count):
                    to = ((k * z_count + z) * 2 + c) * own
                    at = (which * z_count + z) * own
                    ref[:, to : to + own] = in_ref[k, c, :, at : at + own].astype(ref.dtype)


def in_vmem(kernel, arrays, out_shape):
    vmem = pl.BlockSpec(memory_space=pltpu.VMEM)
    return pl.pallas_call(
        kernel,
        out_shape=out_shape,
        in_specs=[vmem] * len(arrays),
        out_specs=jax.tree.map(lambda _: vmem, out_shape),
        compiler_params=pltpu.CompilerParams(vmem_limit_bytes=48 * 2**20),
    )(*arrays)


class Place:
    def __init__(self):
        self.k_count = lax.axis_size("dp")
        self.s_count = lax.axis_size("seq")
        self.z_count = self.s_count // 2
        self.k = lax.axis_index("dp")
        self.s = lax.axis_index("seq")
        self.c = self.s % 2
        self.z = self.s // 2
        self.square = self.k_count == 4
        self.z_groups = [
            [k * self.s_count + 2 * z + c for z in range(self.z_count)]
            for k in range(self.k_count)
            for c in range(2)
        ]
        self.plane_groups = [
            [k * self.s_count + 2 * z + c for k in range(self.k_count) for c in range(2)]
            for z in range(self.z_count)
        ]

    def to_k(self, array, flip):
        return lax.ppermute(array, "dp", [(i, i ^ flip) for i in range(self.k_count)])

    def to_core(self, array):
        return lax.ppermute(array, "seq", [(i, i ^ 1) for i in range(self.s_count)])

    def to_z(self, array, by):
        pairs = [(i, i + 2 * by) for i in range(self.s_count) if 0 <= i + 2 * by < self.s_count]
        return lax.ppermute(array, "seq", pairs)

    def by_core(self, own, other):
        return jnp.where(self.c == 0, jnp.stack([own, other]), jnp.stack([other, own]))

    def gather_z(self, array):
        return lax.all_gather(array, AXES, axis_index_groups=self.z_groups, tiled=True)

    def z_pairs(self, pairs):
        return [(2 * a + c, 2 * b + c) for a, b in pairs for c in range(2)]

    def own_apart(self, split, axis):
        shape = [1] * split.ndim
        shape[axis] = self.z_count
        own = (jnp.arange(self.z_count) == self.z).reshape(shape)
        sent = jnp.moveaxis(jnp.where(own, 0.0, split).astype(low), axis, 0)
        kept = lax.dynamic_index_in_dim(split, self.z, axis, False)
        return sent.reshape((-1,) + sent.shape[-1:]), kept.reshape((-1,) + sent.shape[-1:])

    def scatter_z(self, parts):
        total = lax.psum_scatter(
            parts[0], AXES, scatter_dimension=0, axis_index_groups=self.z_groups, tiled=True
        )
        return total, parts[1]


    def sum_far(self, chunk):
        if self.z_count != 4:
            return ()
        pairs = self.z_pairs([(0, 1), (3, 2)])
        return (lax.ppermute(chunk(3 - self.z).astype(low), "seq", pairs),)

    def sum_near(self, chunk):
        if self.z_count != 4:
            return ()
        below = self.to_z(chunk(jnp.minimum(self.z + 1, 3)).astype(low), 1)
        above = self.to_z(chunk(jnp.maximum(self.z - 1, 0)).astype(low), -1)
        return below, above

    def sum_second(self, chunk, far):
        if self.z_count != 4:
            return ()
        second = (chunk(self.z ^ 2).astype(wide) + far[0].astype(wide)).astype(low)
        return (lax.ppermute(second, "seq", self.z_pairs([(0, 2), (1, 3), (2, 0), (3, 1)])),)

    def sum_all(self, sent, kept, near, second):
        total = kept.astype(wide)
        if self.z_count != 4:
            whole = lax.psum_scatter(
                sent.reshape(-1, sent.shape[-1]),
                AXES,
                scatter_dimension=0,
                axis_index_groups=self.z_groups,
                tiled=True,
            )
            return total + whole.astype(wide)
        for part in near + second:
            total = total + part.astype(wide)
        return total

    def gather_seq_small(self, array):
        if self.s_count != 8:
            return lax.all_gather(array, "seq")
        out = array[None]
        for bit in range(3):
            got = lax.ppermute(out, "seq", [(i, i ^ (1 << bit)) for i in range(8)])
            low_bit = (self.s >> bit) % 2 == 0
            out = jnp.where(low_bit, jnp.concatenate([out, got]), jnp.concatenate([got, out]))
        return out

    def gather_dp_small(self, array):
        if not self.square:
            return lax.all_gather(array, "dp")
        out = array[None]
        for bit in range(2):
            got = self.to_k(out, 1 << bit)
            low_bit = (self.k >> bit) % 2 == 0
            out = jnp.where(low_bit, jnp.concatenate([out, got]), jnp.concatenate([got, out]))
        return out

    def gather_plane(self, array):
        if not self.square:
            whole = lax.all_gather(array, AXES, axis_index_groups=self.plane_groups)
            whole = whole.reshape((self.k_count, 2) + array.shape)
            return jnp.swapaxes(whole, 0, 1).reshape((-1,) + array.shape[1:])
        return self.gather_end(self.gather_far(self.gather_near(array)))

    def gather_near(self, array):
        if not self.square:
            return (array,)
        return array, self.to_k(array, 1), self.to_k(array, 2)

    def gather_far(self, near):
        if not self.square:
            return near
        array, from_x, from_y = near
        half = array.shape[0] // 2
        return array, from_x, from_y, self.to_k(from_x[:half], 2), self.to_k(from_y[half:], 1)

    def gather_end(self, mine):
        if not self.square:
            return self.gather_plane(mine[0])
        return lay_out(self.c, mine, [self.to_core(part) for part in mine])

    def gather_tail(self, tail):
        if not self.square:
            tail = jnp.swapaxes(self.gather_plane(tail[None]).reshape((2, -1) + tail.shape), 0, 1)
            return self.to_z(tail[:, 1].reshape((-1,) + tail.shape[3:]), 1)
        tail = self.to_z(tail, 1)
        tail = jnp.where(self.c == 1, tail, self.to_core(tail))
        tail = jnp.concatenate([tail, self.to_k(tail, 1)])
        return jnp.concatenate([tail, self.to_k(tail, 2)])

    def gather_plane_small(self, array):
        if not self.square:
            return self.gather_plane(array)
        near = jnp.stack([array, self.to_k(array, 1)])
        mine = jnp.concatenate([near, self.to_k(near, 2)])
        return self.by_core(mine, self.to_core(mine)).reshape((-1,) + array.shape[1:])

    def halves(self, array):
        count = array.shape[0] // 2
        own = lax.dynamic_slice_in_dim(array, self.c * count, count, 0)
        return own, lax.dynamic_slice_in_dim(array, (1 - self.c) * count, count, 0)

    def chip_product(self, left, right, dot, exact=False):
        own, other = self.halves(left)
        count = own.shape[0] // 2
        got = []
        for i in range(2):
            part = dot(other[i * count : (i + 1) * count], right)
            if exact:
                part = self.pack(part, self.power_of(part))
                got.append(self.unpack(self.to_core(part))[0])
            else:
                got.append(self.to_core(part.astype(low)).astype(wide))
        chip = []
        for i in range(2):
            part = dot(own[i * count : (i + 1) * count], right) + got[i]
            chip += list(part.reshape(self.k_count // 2, -1, part.shape[-1]))
        return chip

    def power_of(self, values):
        largest = jnp.max(jnp.abs(values), axis=-1, keepdims=True)
        return jnp.ceil(jnp.log2(jnp.clip(largest, 1e-30, 1e37)))

    def pack(self, parts, power):
        scaled = (parts * jnp.exp2(-power)).astype(jnp.float16)
        power = jnp.broadcast_to(power, power.shape[:-1] + (128,)).astype(jnp.float16)
        return jnp.concatenate([scaled, power], axis=-1)

    def unpack(self, got):
        got = got.astype(wide)
        width = got.shape[-1] - 128
        power = got[..., width : width + 1]
        return got[..., :width] * jnp.exp2(power), power

    def chip_parts(self, left, right, side, between=None):
        if not self.square:
            return self.chip_product(left, right, dot_nt if side else dot_nn), None
        count = left.shape[0] // 8
        other = other_call(self.c, left, right, count, side)
        got = self.to_core(other)
        extra = None
        if between is not None:
            left, extra = between(other, left)
        return own_call(self.c, left, right, got, count, side), extra

    def near_parts(self, parts):
        if not self.square:
            return self.near_plane(parts)
        chip, next_a, next_b, a, b = parts
        return (chip, next_a, next_b, *together(self.to_k(a, 1), self.to_k(b, 2)))

    def near_product(self, left, right, between=None):
        parts, extra = self.chip_parts(left, right, 1, between)
        return self.near_parts(parts), extra

    def far_product(self, near):
        if not self.square:
            return self.far_plane(near)
        chip, next_a, next_b, got_a, got_b = near
        half = next_a.shape[1]
        got_a, got_b = got_a.astype(wide), got_b.astype(wide)
        own_a, own_b = chip[:, :half] + got_a[0], chip[:, half:] + got_b[0]
        return self.last_plane(next_a + got_a[1], next_b + got_b[1], None, None, own_a, own_b)

    def near_plane(self, chip, exact=False):
        if not self.square:
            return (lax.psum_scatter(jnp.stack(chip), "dp", scatter_dimension=0, tiled=False),)
        half = chip[0].shape[1] // 2
        power = [self.power_of(part) for part in chip] if exact else None

        def pick(a, i, j):
            return a if a is None else jnp.stack([a[i], a[j]])

        got_a = self.send_plane(jnp.stack([chip[1][:, :half], chip[3][:, :half]]), pick(power, 1, 3), 1)
        got_b = self.send_plane(jnp.stack([chip[2][:, half:], chip[3][:, half:]]), pick(power, 2, 3), 2)
        got_a, got_b = together(got_a, got_b)
        return chip, power, got_a, got_b

    def send_plane(self, parts, power, flip):
        if power is None:
            return self.to_k(parts.astype(low), flip), None
        return self.unpack(self.to_k(self.pack(parts, power), flip))

    def far_plane(self, near):
        if not self.square:
            return near[0]
        chip, power, (got_a, power_a), (got_b, power_b) = near
        half = chip[0].shape[1] // 2
        got_a, got_b = got_a.astype(wide), got_b.astype(wide)

        def above(a, i, b, j):
            return a if a is None else jnp.maximum(a[i], b[j]) + 1.0

        next_a, next_b = chip[2][:, :half] + got_a[1], chip[1][:, half:] + got_b[1]
        return self.last_plane(
            next_a,
            next_b,
            above(power_a, 1, power, 2),
            above(power_b, 1, power, 1),
            chip[0][:, :half] + got_a[0],
            chip[0][:, half:] + got_b[0],
        )

    def last_plane(self, next_a, next_b, power_a, power_b, own_a, own_b):
        if power_a is None:
            next_a, next_b = together(next_a.astype(low), next_b.astype(low))
            last_a, last_b = self.to_k(next_a, 2).astype(wide), self.to_k(next_b, 1).astype(wide)
        else:
            next_a, next_b = together(self.pack(next_a, power_a), self.pack(next_b, power_b))
            last_a, last_b = self.unpack(self.to_k(next_a, 2))[0], self.unpack(self.to_k(next_b, 1))[0]
        return jnp.concatenate([own_a + last_a, own_b + last_b], axis=1)

    def sum_plane(self, chip, exact=False):
        return self.far_plane(self.near_plane(chip, exact))

    def exchange_plane(self, array):
        return self.exchange_dp(self.exchange_core(array))

    def exchange_core(self, array):
        keep = lax.dynamic_index_in_dim(array, self.c, 1, False)
        got = self.to_core(lax.dynamic_index_in_dim(array, 1 - self.c, 1, False))
        return jnp.moveaxis(self.by_core(keep, got), 0, 1)

    def exchange_dp(self, pairs):
        if not self.square:
            return lax.all_to_all(pairs, "dp", 0, 0, tiled=True)
        parts = [lax.dynamic_index_in_dim(pairs, self.k, 0, False)]
        for flip in range(1, 4):
            parts.append(self.to_k(lax.dynamic_index_in_dim(pairs, self.k ^ flip, 0, False), flip))
        odd = self.k % 2 == 1
        parts = [jnp.where(odd, parts[i ^ 1], parts[i]) for i in range(4)]
        upper = self.k >= 2
        return jnp.stack([jnp.where(upper, parts[i ^ 2], parts[i]) for i in range(4)])


def gelu_pair(x):
    slope = 0.7978845608028654
    inner = jnp.tanh(slope * (x + 0.044715 * x * x * x))
    half = 0.5 * (1.0 + inner)
    return x * half, half + 0.5 * x * (1.0 - inner * inner) * slope * (1.0 + 0.134145 * x * x)


def rms_normed(values, gain):
    values = values.astype(wide)
    scale = lax.rsqrt(jnp.mean(values * values, axis=1, keepdims=True) + eps_value)
    return (values * scale * gain).astype(low)


def ordered(values, order):
    if order is None:
        return values
    size = values.shape[1] // len(order)
    return jnp.concatenate([values[:, i * size : (i + 1) * size] for i in order], axis=1)


def minus_expm1(x):
    near = 1.0
    for i in range(8, 1, -1):
        near = 1.0 + near * x * (1.0 / i)
    return jnp.where(x > -0.5, -x * near, 1.0 - jnp.exp(x))


def gates_of(conv_low, w_gates, params, not_start):
    width = conv_low.shape[1]
    pre = jnp.dot(conv_low, w_gates, preferred_element_type=wide)
    rate = jax.nn.sigmoid(pre[:, :width] + params[5:6])
    igate = jax.nn.sigmoid(pre[:, width:] + params[6:7])
    log_keep = params[7:8] * rate
    room = minus_expm1(2.0 * log_keep)
    mult = jnp.where(not_start > 0.5, jnp.sqrt(jnp.maximum(room, floor_value)), 1.0)
    return rate, igate, jnp.exp(log_keep), room, mult


def put_lanes(ref, at, value):
    for j in range(ref.shape[0]):
        part = value[:, 128 * j : 128 * (j + 1)]
        ref[j, at, : part.shape[1]] = part


def get_lanes(ref, at, width):
    parts = [ref[j, at, : min(128, width - 128 * j)] for j in range(ref.shape[0])]
    return jnp.concatenate(parts, axis=1)


def lane_shape(tokens, width, kind=wide):
    return jax.ShapeDtypeStruct((pl.cdiv(width, 128), tokens, 128), kind)


def conv_kernel(
    rows, span, order, x_ref, w_ref, halo_ref, gain_ref, params_ref, gates_ref,
    normed_ref, masks_ref, branch_ref, in_ref, low_ref, keep_ref, drive_ref, sums_ref, before_ref, tail, line,
):
    step = pl.program_id(0)
    width = in_ref.shape[1]
    count = x_ref.shape[0]
    row_dev = count // span

    @pl.when(step == 0)
    def _():
        normed = rms_normed(halo_ref[...], gain_ref[...])
        before = jnp.dot(ordered(normed, order), w_ref[:, width:], preferred_element_type=wide)
        tail[...] = before.astype(low).astype(wide)
        before_ref[...] = tail[...]

    features = gain_ref.shape[1]
    normed = rms_normed(x_ref[:, :features], gain_ref[...])
    normed_ref[...] = normed
    masks_ref[...] = x_ref[:, features : features + 8].astype(wide)
    pre = jnp.dot(ordered(normed, order), w_ref[...], preferred_element_type=wide)
    branch_ref[...] = pre[:, :width]
    conv_in = pre[:, width:].astype(low)
    in_ref[...] = conv_in
    conv_in = conv_in.astype(wide)
    params = params_ref[...]
    for row in range(row_dev):
        at = slice(row * span, (row + 1) * span)
        own = conv_in[at]
        place = pl.ds(pl.multiple_of((lax.rem(step * row_dev + row, rows)) * 8, 8), 8)
        line[:8] = tail[place]
        line[8:] = own
        tail[place] = own[span - 8 :]
        masks = masks_ref[at]
        total = params[4:5] + params[0:1] * own
        for by in range(1, 4):
            total = total + params[by : by + 1] * line[8 - by : 8 - by + span] * masks[:, by - 1 : by]
        conv_low = total.astype(low)
        low_ref[at] = conv_low
        not_start = masks[:, 3:4]
        rate, igate, keep, room, mult = gates_of(conv_low, gates_ref[...], params, not_start)
        to = pl.ds(pl.multiple_of((step * row_dev + row) * span, 8), span)
        put_lanes(keep_ref, to, keep * not_start)
        put_lanes(drive_ref, to, mult * igate * conv_low.astype(wide))

    @pl.when(step == pl.num_programs(0) - 1)
    def _():
        lanes = keep_ref.shape[0]

        def one(i, state):
            out = []
            for j in range(lanes):
                keep = keep_ref.at[j][pl.ds(i, rows, stride=span), :]
                drive = drive_ref.at[j][pl.ds(i, rows, stride=span), :]
                out.append((state[j][0] * keep, state[j][1] * keep + drive))
            return tuple(out)

        shape = (rows, 128)
        state = tuple((jnp.ones(shape, wide), jnp.zeros(shape, wide)) for _ in range(lanes))
        for half in range(2):
            base = half * rows * span
            state = lax.fori_loop(0, span, lambda i, s, base=base: one(base + i, s), state, unroll=8)
        for j in range(lanes):
            sums_ref[0, j] = state[j][0]
            sums_ref[1, j] = state[j][1]


def state_kernel(rows, span, keep_ref, drive_ref, start_ref, branch_ref, state_ref, mixed_ref):
    lanes = keep_ref.shape[0]
    width = mixed_ref.shape[1]

    def one(i, state):
        out = []
        for j in range(lanes):
            at = pl.ds(i, rows, stride=span)
            value = state[j] * keep_ref.at[j][at, :] + drive_ref.at[j][at, :]
            state_ref.at[j][at, :] = value
            out.append(value)
        return tuple(out)

    state = tuple(start_ref[j] for j in range(lanes))
    for half in range(2):
        base = half * rows * span
        state = lax.fori_loop(0, span, lambda i, s, base=base: one(base + i, s), state, unroll=8)

    @pl.loop(0, 2 * rows)
    def _(block):
        at = pl.ds(pl.multiple_of(block * span, 16), span)
        value, _ = gelu_pair(branch_ref[at])
        mixed_ref[at] = (value * get_lanes(state_ref, at, width)).astype(low)


def mlp_kernel(x_ref, cot_ref, w_ref, down_ref, hidden_ref, grad_ref):
    width = hidden_ref.shape[1]
    pre = jnp.dot(x_ref[...], w_ref[...], preferred_element_type=wide)
    grad = lax.dot_general(
        cot_ref[...], down_ref[...], (((1,), (1,)), ((), ())), preferred_element_type=wide
    )
    up = pre[:, width:]
    value, slope = gelu_pair(pre[:, :width])
    hidden_ref[...] = (value * up).astype(low)
    grad_ref[:, :width] = (grad * up * slope).astype(low)
    grad_ref[:, width:] = (grad * value).astype(low)


def other_kernel(side, core_ref, x_ref, w_ref, out_ref):
    product = lax.dot_general(
        x_ref[...], w_ref[...], (((1,), (side,)), ((), ())), preferred_element_type=wide
    )
    out_ref[...] = product.astype(low)


def own_kernel(side, core_ref, x_ref, w_ref, got_ref, chip_ref, next_a_ref, next_b_ref, a_ref, b_ref):
    step = pl.program_id(0)
    product = lax.dot_general(
        x_ref[...], w_ref[...], (((1,), (side,)), ((), ())), preferred_element_type=wide
    )
    product = product + got_ref[...].astype(wide)
    half = product.shape[1] // 2

    @pl.when(step == 0)
    def _():
        chip_ref[...] = product

    @pl.when(step == 1)
    def _():
        next_b_ref[...] = product[:, half:]

    @pl.when(step == 2)
    def _():
        next_a_ref[...] = product[:, :half]

    @pl.when((step == 1) | (step == 3))
    def _():
        a_ref[0] = product[:, :half].astype(low)

    @pl.when(step >= 2)
    def _():
        b_ref[0] = product[:, half:].astype(low)


def back_kernel(
    rows, span, x_ref, w_ref, branch_ref, state_ref, keep_ref, grad_branch_ref, grad_state_ref, sum_ref
):
    step = pl.program_id(0)
    lanes, _, _ = keep_ref.shape
    width = w_ref.shape[0]
    count = x_ref.shape[0]
    mixed = lax.dot_general(
        x_ref[...], w_ref[...], (((1,), (1,)), ((), ())), preferred_element_type=wide
    )
    for row in range(count // span):
        at = slice(row * span, (row + 1) * span)
        to = pl.ds(pl.multiple_of(step * count + row * span, 8), span)
        value, slope = gelu_pair(branch_ref[at])
        state = get_lanes(state_ref, to, width)
        grad_branch_ref[at] = (mixed[at] * state * slope).astype(low)
        put_lanes(grad_state_ref, to, mixed[at] * value)

    @pl.when(step == pl.num_programs(0) - 1)
    def _():
        def one(i, state):
            out = []
            for j in range(lanes):
                at = pl.ds(i, rows, stride=span)
                out.append(keep_ref.at[j][at, :] * (grad_state_ref.at[j][at, :] + state[j]))
            return tuple(out)

        state = tuple(jnp.zeros((rows, 128), wide) for _ in range(lanes))
        for half in (1, 0):
            last = half * rows * span + span - 1
            state = lax.fori_loop(0, span, lambda i, s, last=last: one(last - i, s), state, unroll=8)
        for j in range(lanes):
            sum_ref[j] = state[j]


def adjoint_kernel(
    rows, span, keep_ref, grad_ref, carry_ref, state_ref, start_ref, low_ref, gates_ref, params_ref,
    masks_ref, in_ref, before_ref, grad_conv_ref, small_ref, adjoint, through, gates_grad_ref, sums_ref, line,
):
    lanes = keep_ref.shape[0]
    width = low_ref.shape[1]

    def one(i, state, before):
        out = []
        for j in range(lanes):
            at = pl.ds(i, rows, stride=span)
            value = grad_ref.at[j][at, :] + state[j]
            adjoint.at[j][at, :] = value
            through.at[j][at, :] = value * before(j)
            out.append(keep_ref.at[j][at, :] * value)
        return tuple(out)

    state = tuple(carry_ref[j] for j in range(lanes))
    for half in (1, 0):
        first = half * rows * span

        def inner(i, s, first=first):
            at = first + span - 1 - i
            return one(at, s, lambda j: state_ref.at[j][pl.ds(at - 1, rows, stride=span), :])

        state = lax.fori_loop(0, span - 1, inner, state, unroll=8)
        if half:
            state = one(first, state, lambda j: state_ref.at[j][pl.ds(span - 1, rows, stride=span), :])
        else:
            state = one(first, state, lambda j: start_ref[j])

    params = params_ref[...]
    gates_grad_ref[...] = jnp.zeros(gates_grad_ref.shape, wide)
    sums_ref[...] = jnp.zeros(sums_ref.shape, wide)

    @pl.loop(0, 2 * rows)
    def _(block):
        at = pl.ds(pl.multiple_of(block * span, 16), span)
        conv_low = low_ref[at]
        conv_value = conv_low.astype(wide)
        not_start = masks_ref[at][:, 3:4]
        rate, igate, keep, room, mult = gates_of(conv_low, gates_ref[...], params, not_start)
        adj = get_lanes(adjoint, at, width)
        thr = get_lanes(through, at, width)
        spread = jnp.where(room > floor_value, adj * igate * conv_value * keep * keep / mult, 0.0)
        grad_log = not_start * (thr * keep - spread)
        grad_rate = (grad_log * params[7:8] * rate * (1.0 - rate)).astype(low)
        scaled = adj * mult
        grad_igate = (scaled * conv_value * igate * (1.0 - igate)).astype(low)
        both = jnp.concatenate([grad_rate, grad_igate], axis=1)
        grad_conv = scaled * igate + lax.dot_general(
            both, gates_ref[...], (((1,), (1,)), ((), ())), preferred_element_type=wide
        )
        grad_conv = grad_conv.astype(low)
        grad_conv_ref[at] = grad_conv
        gates_grad_ref[...] += lax.dot_general(
            conv_low, both, (((0,), (0,)), ((), ())), preferred_element_type=wide
        )
        masks = masks_ref[at]
        grad_conv = grad_conv.astype(wide)
        conv_in = in_ref[at].astype(wide)
        within = lax.rem(block, rows)
        line[:8] = before_ref[pl.ds(pl.multiple_of(within * 8, 8), 8)]

        @pl.when(block >= rows)
        def _():
            last = pl.ds(pl.multiple_of(within * span + span - 16, 16), 16)
            line[:8] = in_ref[last].astype(wide)[8:]

        line[8:] = conv_in
        values = [grad_conv * conv_in]
        for by in range(1, 4):
            values.append(grad_conv * line[8 - by : 8 - by + span] * masks[:, by - 1 : by])
        values += [grad_conv, grad_rate.astype(wide), grad_igate.astype(wide), grad_log * rate * params[8:9]]
        for i, value in enumerate(values):
            sums_ref[i : i + 1] += jnp.sum(value, axis=0, keepdims=True)

    block = small_ref.shape[1] // 2 - 64
    for head in range(width // block):
        at = slice(head * block, (head + 1) * block)
        small_ref[at, :block] = gates_grad_ref[at, at].astype(low)
        then = slice(width + head * block, width + (head + 1) * block)
        small_ref[at, block : 2 * block] = gates_grad_ref[at, then].astype(low)
    small_ref[:, 2 * block :] = sums_ref[...].T[:width].astype(low)


def conv_back_kernel(rows, span, grad_ref, halo_ref, masks_ref, halo_masks_ref, params_ref, one_ref, line):
    params = params_ref[...]

    def work(block, grad_next, masks_next):
        at = pl.ds(pl.multiple_of(block * span, 16), span)
        own = grad_ref[at].astype(wide)
        total = params[0:1] * own
        masks = masks_ref[at]
        for by in range(1, 4):
            line[:span] = own * masks[:, by - 1 : by]
            line[span:] = grad_next * masks_next[:, by - 1 : by]
            total = total + params[by : by + 1] * line[by : by + span]
        one_ref[at] = total.astype(low)

    @pl.loop(0, rows)
    def _(block):
        then = pl.ds(pl.multiple_of((block + rows) * span, 16), 16)
        work(block, grad_ref[then].astype(wide)[:8], masks_ref[then][:8])

    @pl.loop(0, rows)
    def _(block):
        then = pl.ds(pl.multiple_of(block * 16, 16), 16)
        work(block + rows, halo_ref[then].astype(wide)[:8], halo_masks_ref[then][:8])


def whole_block(array):
    return pl.BlockSpec(array.shape, lambda *i, n=len(array.shape): (0,) * n)


def token_block(array, count):
    return pl.BlockSpec((count,) + array.shape[1:], lambda i, n=len(array.shape): (i,) + (0,) * (n - 1))


def half_of(core, x, count, width):
    return pl.BlockSpec((count, width), lambda k, core_ref: (core_ref[0] * (x.shape[0] // (2 * count)) + k, 0))


def half_call(kernel, core, x, w, count, extra, outputs):
    def spec(array, block, index):
        return pl.BlockSpec(block, lambda k, core_ref: index(k))

    return pl.pallas_call(
        kernel,
        out_shape=[array for array, _, _ in outputs],
        grid_spec=pltpu.PrefetchScalarGridSpec(
            num_scalar_prefetch=1,
            grid=(x.shape[0] // (2 * count),),
            in_specs=[
                half_of(core, x, count, x.shape[1]),
                pl.BlockSpec(w.shape, lambda k, core_ref: (0, 0)),
            ]
            + [spec(*one) for one in extra],
            out_specs=[spec(*one) for one in outputs],
        ),
        cost_estimate=pl.CostEstimate(flops=0, bytes_accessed=0, transcendentals=0),
        compiler_params=pltpu.CompilerParams(vmem_limit_bytes=56 * 2**20),
    )(core.reshape(1).astype(jnp.int32), x, w, *[array for array, _, _ in extra])


def other_call(core, x, w, count, side):
    width = w.shape[1 - side]
    out = jax.ShapeDtypeStruct((x.shape[0] // 2, width), low)
    kernel = functools.partial(other_kernel, side)
    return half_call(kernel, 1 - core, x, w, count, [], [(out, (count, width), lambda k: (k, 0))])[0]


def own_call(core, x, w, got, count, side):
    width = w.shape[1 - side]
    a = jax.ShapeDtypeStruct((2, count, width // 2), low)
    chip = jax.ShapeDtypeStruct((count, width), wide)
    after = jax.ShapeDtypeStruct((count, width // 2), wide)
    return half_call(
        functools.partial(own_kernel, side),
        core,
        x,
        w,
        count,
        [(got, (count, width), lambda k: (k, 0))],
        [
            (chip, chip.shape, lambda k: (0, 0)),
            (after, after.shape, lambda k: (0, 0)),
            (after, after.shape, lambda k: (0, 0)),
            (a, (1, count, width // 2), lambda k: (k // 2, 0, 0)),
            (a, (1, count, width // 2), lambda k: (k // 3, 0, 0)),
        ],
    )


def rows_kernel(turned, core_ref, x_ref, grad_ref, sent_ref, kept_ref):
    count = kept_ref.shape[1]
    total = lax.dot_general(
        x_ref[...], grad_ref[...], (((int(turned),), (0,)), ((), ())), preferred_element_type=wide
    )
    planes = sent_ref.shape[0]
    first = lax.rem(pl.program_id(0), core_ref[1]) * planes
    for i in range(planes):
        part = total[i * count : (i + 1) * count]
        mine = first + i == core_ref[0]
        sent_ref[i, 0] = jnp.where(mine, jnp.zeros_like(part), part).astype(low)

        @pl.when(mine)
        def _(part=part):
            kept_ref[0] = part


def rows_call(z, z_count, k_count, x, grad, turned):
    tokens, features = x.shape[::-1] if turned else x.shape
    count = features // (z_count * k_count)
    planes = max(2, 128 // count)
    width = grad.shape[1]
    per = z_count // planes
    sent = jax.ShapeDtypeStruct((z_count, k_count, count, width), low)
    kept = jax.ShapeDtypeStruct((k_count, count, width), wide)
    block = (planes * count, tokens) if turned else (tokens, planes * count)
    return pl.pallas_call(
        functools.partial(rows_kernel, turned),
        out_shape=[sent, kept],
        grid_spec=pltpu.PrefetchScalarGridSpec(
            num_scalar_prefetch=1,
            grid=(k_count * per,),
            in_specs=[
                pl.BlockSpec(block, lambda i, ref: (i, 0) if turned else (0, i)),
                pl.BlockSpec(grad.shape, lambda i, ref: (0, 0)),
            ],
            out_specs=[
                pl.BlockSpec((planes, 1, count, width), lambda i, ref: (i % per, i // per, 0, 0)),
                pl.BlockSpec((1, count, width), lambda i, ref: (i // per, 0, 0)),
            ],
        ),
        cost_estimate=pl.CostEstimate(flops=0, bytes_accessed=0, transcendentals=0),
        compiler_params=pltpu.CompilerParams(vmem_limit_bytes=56 * 2**20),
    )(jnp.stack([z, jnp.int32(per)]).astype(jnp.int32), x, grad)


def turn_kernel(x_ref, out_ref):
    out_ref[...] = x_ref[...].T


def turn(x):
    block = 256
    return pl.pallas_call(
        turn_kernel,
        out_shape=jax.ShapeDtypeStruct(x.shape[::-1], x.dtype),
        grid=(x.shape[1] // block,),
        in_specs=[pl.BlockSpec((x.shape[0], block), lambda i: (0, i))],
        out_specs=pl.BlockSpec((block, x.shape[0]), lambda i: (i, 0)),
        cost_estimate=pl.CostEstimate(flops=0, bytes_accessed=0, transcendentals=0),
        compiler_params=pltpu.CompilerParams(vmem_limit_bytes=48 * 2**20),
    )(x)


def down_kernel(core_ref, hidden_ref, cot_ref, sent_ref, kept_ref):
    total = lax.dot_general(
        cot_ref[...], hidden_ref[...], (((0,), (0,)), ((), ())), preferred_element_type=wide
    )
    total = total.T
    count = kept_ref.shape[0]
    for i in range(sent_ref.shape[0]):
        part = total[i * count : (i + 1) * count]
        mine = core_ref[0] == i
        sent_ref[i] = jnp.where(mine, jnp.zeros_like(part), part).astype(low)

        @pl.when(mine)
        def _(part=part):
            kept_ref[...] = part


def down_call(z, z_count, hidden, cot):
    tokens, features = cot.shape
    count = hidden.shape[1] // z_count
    columns = 256
    sent = jax.ShapeDtypeStruct((z_count, count, features), low)
    kept = jax.ShapeDtypeStruct((count, features), wide)
    return pl.pallas_call(
        down_kernel,
        out_shape=[sent, kept],
        grid_spec=pltpu.PrefetchScalarGridSpec(
            num_scalar_prefetch=1,
            grid=(features // columns,),
            in_specs=[
                pl.BlockSpec(hidden.shape, lambda i, ref: (0, 0)),
                pl.BlockSpec((tokens, columns), lambda i, ref: (0, i)),
            ],
            out_specs=[
                pl.BlockSpec((z_count, count, columns), lambda i, ref: (0, 0, i)),
                pl.BlockSpec((count, columns), lambda i, ref: (0, i)),
            ],
        ),
        cost_estimate=pl.CostEstimate(flops=0, bytes_accessed=0, transcendentals=0),
        compiler_params=pltpu.CompilerParams(vmem_limit_bytes=56 * 2**20),
    )(z.reshape(1).astype(jnp.int32), hidden, cot)


def kernel_call(kernel, steps, inputs, outputs, scratch=()):
    def spec(array, count):
        return whole_block(array) if count is None else token_block(array, count)

    return pl.pallas_call(
        kernel,
        out_shape=[array for array, _ in outputs],
        grid=(steps,),
        in_specs=[spec(array, count) for array, count in inputs],
        out_specs=[spec(array, count) for array, count in outputs],
        scratch_shapes=scratch,
        cost_estimate=pl.CostEstimate(flops=0, bytes_accessed=0, transcendentals=0),
        compiler_params=pltpu.CompilerParams(vmem_limit_bytes=56 * 2**20),
    )(*[array for array, _ in inputs])


def per_device(
    tokens,
    segment_ids,
    cotangent,
    norm_one,
    branch_weight,
    input_proj,
    conv_weight,
    conv_bias,
    rate_weight,
    igate_weight,
    rate_bias,
    igate_bias,
    decay_param,
    out_proj,
    norm_two,
    mlp_gate,
    mlp_up,
    mlp_down,
):
    at = Place()
    k_count, z_count = at.k_count, at.z_count
    group = 2 * k_count
    row_dev, span, width_d = tokens.shape
    tok = row_dev * span
    rows = k_count * row_dev
    tok_all = 2 * rows * span
    d_own = norm_one.shape[0]
    w_own = conv_bias.shape[0]
    f_own = mlp_down.shape[0]
    width_r = branch_weight.shape[1]
    w_slot = width_r // group
    f_slot = f_own * z_count
    taps = conv_weight.shape[0]
    reach = taps - 1
    half_z = z_count // 2

    def by_feature(array):
        split = array.reshape(z_count, -1, 2 * d_own, array.shape[1])
        return jnp.swapaxes(split, 0, 1).reshape(array.shape)

    small = jnp.concatenate(
        [
            norm_one,
            norm_two,
            conv_weight.reshape(-1),
            conv_bias,
            rate_bias,
            igate_bias,
            decay_param,
        ]
    )
    rec_cols = jnp.concatenate(
        [
            branch_weight.reshape(d_own, k_count, 2, w_slot),
            input_proj.reshape(d_own, k_count, 2, w_slot),
        ],
        axis=3,
    )
    rec_cols = at.exchange_plane(jnp.moveaxis(rec_cols, 0, 2))
    out_part = at.gather_z(out_proj)
    rec_cols, out_part = together(rec_cols, out_part)
    w1 = at.gather_z(rec_cols.reshape(group * d_own, 2 * w_slot))

    gate_rows = jnp.concatenate([rate_weight, igate_weight], axis=1)
    small = jnp.pad(small, (0, -small.shape[0] % (2 * BS))).reshape(-1, 2 * BS)
    gate_rows = at.gather_seq_small(jnp.concatenate([gate_rows, small]))
    small = gate_rows[:, w_own:].reshape(at.s_count, -1)
    gains = at.gather_dp_small(small[:, : 2 * d_own]).reshape(k_count * at.s_count, -1)
    gain_one = gains[:, :d_own].reshape(1, width_d).astype(wide)
    gain_two = gains[:, d_own:].reshape(1, width_d).astype(wide)
    mine = lax.dynamic_slice_in_dim(small[:, 2 * d_own :], at.c * z_count, z_count, 0)
    mine = mine[:, : (taps + 4) * w_own].reshape(z_count, taps + 4, w_own).astype(wide)
    mine = jnp.swapaxes(mine, 0, 1).reshape(taps + 4, w_slot)
    w_conv = mine[:taps]
    b_conv, b_rate, b_igate, decay = (mine[taps + i][None, :] for i in range(4))
    log_slope = -rate_scale * jax.nn.softplus(-decay)
    decay_slope = rate_scale * jax.nn.sigmoid(-decay)
    params = jnp.concatenate([w_conv, b_conv, b_rate, b_igate, log_slope] + [decay_slope] * 8)
    gate_rows = lax.dynamic_slice_in_dim(gate_rows[:, :w_own], at.c * z_count, z_count, 0)
    gate_rows = gate_rows.reshape(w_slot, 2 * BS)
    heads = w_slot // BS

    def block_diagonal(columns):
        blocks = columns.reshape(heads, BS, 1, BS)
        same = jnp.eye(heads, dtype=low).reshape(heads, 1, heads, 1)
        return (blocks * same).reshape(w_slot, w_slot)

    w_gates = jnp.concatenate([block_diagonal(gate_rows[:, :BS]), block_diagonal(gate_rows[:, BS:])], axis=1)

    seg_code = (segment_ids % 64).astype(low)
    pairs = [(i, i + 1) for i in range(at.s_count - 1)]
    ext_code = jnp.concatenate([lax.ppermute(seg_code[:, span - reach :], "seq", pairs), seg_code], axis=1)
    position = lax.broadcasted_iota(jnp.int32, (row_dev, span), 1)
    masks = [
        (ext_code[:, reach - by : reach - by + span] == seg_code) & ((at.s > 0) | (position >= by))
        for by in range(1, taps)
    ]
    masks = jnp.stack(masks + [masks[0]] * (9 - taps), axis=-1).astype(low).reshape(tok, 8)
    tokens = tokens.reshape(tok, width_d)
    beside = jnp.concatenate([tokens, jnp.pad(masks, ((0, 0), (0, 120)))], axis=1)
    tail = tokens.reshape(row_dev, span, width_d)[:, span - 8 :].reshape(row_dev * 8, width_d)
    tail = at.gather_tail(tail)
    beside, tail, params, gate_rows, gain_one, gain_two, mlp_gate = together(
        beside, tail, params, gate_rows, gain_one, gain_two, mlp_gate
    )
    order = None
    if 2 * d_own % 128 == 0:
        order = [k * z_count + z for z in range(z_count) for k in range(k_count)]
    beside_near = at.gather_near(beside)
    inputs = tokens.astype(wide)
    s1 = lax.rsqrt(jnp.mean(inputs * inputs, axis=-1, keepdims=True) + eps_value)
    mlp_shape = jax.ShapeDtypeStruct((k_count, 2, d_own, 2 * f_slot), low)
    cut = functools.partial(cut_kernel, k_count, z_count)
    mlp_pairs = at.exchange_core(in_vmem(cut, (mlp_gate, mlp_up), mlp_shape))
    beside_near, mlp_pairs, w_gates = together(beside_near, mlp_pairs, w_gates)
    beside_far = at.gather_far(beside_near)
    mlp_cols = at.exchange_dp(mlp_pairs)
    cot = cotangent.reshape(tok, width_d)
    tokens_all, mlp_cols, cot = together(at.gather_end(beside_far), mlp_cols, cot)
    shape = jax.ShapeDtypeStruct

    half_rows = group * d_own // 2
    w2_parts = [
        at.gather_z(part.reshape(half_rows, 2 * f_slot))
        for part in (mlp_cols[: k_count // 2], mlp_cols[k_count // 2 :])
    ]

    steps = tok_all // tok
    cot_near = at.gather_near(cot)
    flat32, flat16 = shape((tok_all, w_slot), wide), shape((tok_all, w_slot), low)
    lanes = lane_shape(tok_all, w_slot)
    ends = shape((lanes.shape[0], rows, 128), wide)
    n1_all, masks, branch_pre, conv_in, conv_low, keep_eff, drive, summary, conv_before = kernel_call(
        functools.partial(conv_kernel, rows, span, order),
        steps,
        [(tokens_all, tok), (w1 if order else by_feature(w1), None), (tail, None), (gain_one, None), (params, None), (w_gates, None)],
        [(shape((tok_all, width_d), low), tok), (shape((tok_all, 8), wide), tok), (flat32, tok), (flat16, tok), (flat16, tok), (lanes, None), (lanes, None), (shape((2,) + ends.shape, wide), None), (shape((rows * 8, w_slot), wide), None)],
        [pltpu.VMEM((rows * 8, w_slot), wide), pltpu.VMEM((span + 8, w_slot), wide)],
    )
    w_down = at.gather_z(mlp_down)
    summary, cot_near, out_part, w1 = together(summary, cot_near, out_part, w1)
    w1 = by_feature(w1)
    out_part = out_part.reshape(2, half_z * w_own, width_d)
    out_keep = lax.dynamic_index_in_dim(out_part, at.c, 0, False)
    out_got = at.to_core(lax.dynamic_index_in_dim(out_part, 1 - at.c, 0, False))
    w_out = at.by_core(
        out_keep.reshape(half_z, w_own, width_d), out_got.reshape(half_z, w_own, width_d)
    )
    w_out = jnp.swapaxes(w_out, 0, 1).reshape(w_slot, width_d)
    cot_far = at.gather_far(cot_near)
    before = [at.to_z(summary, by) for by in range(1, z_count)]
    state_in = jnp.zeros(ends.shape, wide)
    for part in reversed(before):
        state_in = part[1] + part[0] * state_in
    state, mixed = kernel_call(
        functools.partial(state_kernel, rows, span),
        1,
        [(keep_eff, None), (drive, None), (state_in, None), (branch_pre, None)],
        [(lanes, None), (flat16, None)],
    )
    masks_after = at.to_z(masks.reshape(2, rows, span, 8)[0, :, :16], -1).reshape(rows * 16, 8)
    mixed, cot_far, w2_parts[0], masks_after = together(mixed, cot_far, w2_parts[0], masks_after)

    chip_one = at.chip_product(mixed, w_out, dot_nn, exact=True)
    near_sum, cot_far = together(at.near_plane(chip_one, exact=True), cot_far)
    n1_turned = turn(n1_all)
    cot_all = at.gather_end(cot_far)
    resid, cot_all, n1_turned = together(inputs + at.far_plane(near_sum), cot_all, n1_turned)
    resid, w2_parts[1] = together(resid, w2_parts[1])
    w2 = jnp.concatenate([by_feature(part) for part in w2_parts])

    s2 = lax.rsqrt(jnp.mean(resid * resid, axis=-1, keepdims=True) + eps_value)
    normed_two = (resid * s2 * gain_two).astype(low)
    n2_near, w2 = together(at.gather_near(normed_two), w2)
    n2_all, w_down = together(at.gather_end(at.gather_far(n2_near)), w_down)
    hidden, grad_two = kernel_call(
        mlp_kernel,
        steps,
        [(n2_all, tok), (cot_all, tok), (w2, None), (w_down, None)],
        [(shape((tok_all, f_slot), low), tok), (shape((tok_all, 2 * f_slot), low), tok)],
    )
    def rows_apart(x, grad, turned=False):
        sent, kept = rows_call(at.z, z_count, k_count, x, grad, turned)
        return sent.reshape(-1, sent.shape[-1]), kept.reshape(-1, kept.shape[-1])

    near_two, _ = at.near_product(grad_two, w2)
    chip_two, grad_two = together(near_two[0], grad_two)
    w2_part = rows_apart(n2_all, grad_two)
    near_two, w2_part, hidden = together(near_two, w2_part, hidden)
    w2_sum = at.scatter_z(w2_part)
    grad_n2 = at.far_product(near_two)
    down_sent, down_kept = down_call(at.z, z_count, hidden, cot_all)
    down_part = down_sent.reshape(-1, width_d), down_kept
    grad_n2, down_part = together(grad_n2, down_part)
    down_sum = at.scatter_z(down_part)
    scaled_two = gain_two * grad_n2
    cot_f = cot.astype(wide)
    mean_two = jnp.mean(scaled_two * resid, axis=-1, keepdims=True)
    grad_resid = cot_f + s2 * scaled_two - resid * (s2 * s2 * s2) * mean_two
    grad_recur = grad_resid.astype(low)
    grad_recur, hidden = together(grad_recur, hidden)
    chip_three, _ = at.chip_parts(hidden, w_down, 0)
    gr_near, chip_three = together(at.gather_near(grad_recur), chip_three)
    gr_all = at.gather_end(at.gather_far(gr_near))

    def summed(pair):
        return pair[0].astype(wide) + pair[1].astype(wide)

    def to_owner(array, columns):
        return at.exchange_plane(array.reshape(k_count, 2, d_own, columns))


    grad_branch, grad_state, back = kernel_call(
        functools.partial(back_kernel, rows, span),
        steps,
        [(gr_all, tok), (w_out, None), (branch_pre, tok), (state, None), (keep_eff, None)],
        [(flat16, tok), (lanes, None), (ends, None)],
    )
    back, mixed, chip_three, w2_sum = together(back, mixed, chip_three, w2_sum)

    def by_owner(array):
        split = array.reshape(half_z, 2, w_own, -1)
        keep = lax.dynamic_index_in_dim(split, at.c, 1, False)
        got = at.to_core(lax.dynamic_index_in_dim(split, 1 - at.c, 1, False))
        return at.by_core(keep, got).reshape(z_count, w_own, -1)

    own = jnp.stack([summary[0], back])
    after = [at.to_z(own, -by) for by in range(1, z_count)]
    grad_out = dot_tn(mixed, gr_all)
    after, grad_out = together(after, grad_out)
    carry_in = jnp.zeros(ends.shape, wide)
    for part in reversed(after):
        carry_in = part[1] + part[0] * carry_in
    near_three = at.near_parts(chip_three)
    mlp_pairs = at.exchange_core(summed(w2_sum).reshape(k_count, 2, d_own, 2 * f_slot))
    carry_in, mlp_pairs, near_three = together(carry_in, mlp_pairs, near_three)
    mlp_back = at.exchange_dp(mlp_pairs)
    grad_conv, rec_small = kernel_call(
        functools.partial(adjoint_kernel, rows, span),
        1,
        [
            (array, None)
            for array in (keep_eff, grad_state, carry_in, state, state_in, conv_low, w_gates, params, masks, conv_in, conv_before)
        ],
        [(flat16, None), (shape((w_slot, 2 * BS + 128), low), None)],
        [
            pltpu.VMEM(lanes.shape, wide),
            pltpu.VMEM(lanes.shape, wide),
            pltpu.VMEM((w_slot, 2 * w_slot), wide),
            pltpu.VMEM((128, w_slot), wide),
            pltpu.VMEM((span + 8, w_slot), wide),
        ],
    )
    grad_conv, near_three, mlp_back, down_sum = together(grad_conv, near_three, mlp_back, down_sum)
    block_out = (resid + at.far_product(near_three)).astype(low)
    head = at.to_z(grad_conv.reshape(2, rows, span, w_slot)[0, :, :16], -1).reshape(rows * 16, w_slot)
    rec_part = at.own_apart(by_owner(jnp.concatenate([grad_out.astype(low), rec_small], axis=1)), 0)
    head, rec_part = together(head, rec_part)
    rec_sum = at.scatter_z(rec_part)
    (grad_conv_in,) = kernel_call(
        functools.partial(conv_back_kernel, rows, span),
        1,
        [(array, None) for array in (grad_conv, head, masks, masks_after, params)],
        [(flat16, None)],
        [pltpu.VMEM((span + 8, w_slot), wide)],
    )
    grad_one = jnp.concatenate([grad_branch, grad_conv_in], axis=1)

    def product_between(other, left):
        other, then = together(other, left)
        parts = rows_apart(n1_turned, then, True)
        return together(left, parts)

    near_one, w1_part = at.near_product(grad_one, w1, product_between)
    if w1_part is None:
        w1_part = rows_apart(n1_turned, grad_one, True)
    w1_sum = at.scatter_z(w1_part)
    grad_n1 = at.far_product(near_one)
    w1_sum, grad_n1, block_out, rec_sum = together(w1_sum, grad_n1, block_out, rec_sum)
    rec_back = at.exchange_plane(summed(w1_sum).reshape(k_count, 2, d_own, 2 * w_slot))
    scaled_one = gain_one * grad_n1
    mean_one = jnp.mean(scaled_one * inputs, axis=-1, keepdims=True)
    grad_tokens = grad_resid + s1 * scaled_one - inputs * (s1 * s1 * s1) * mean_one
    grad_tokens = grad_tokens.reshape(row_dev, span, width_d)
    block_out = block_out.reshape(row_dev, span, width_d)

    rec_rows = summed(rec_sum)
    grad_out_w = rec_rows[:, :width_d]
    grad_rate_w = rec_rows[:, width_d : width_d + BS]
    grad_igate_w = rec_rows[:, width_d + BS : width_d + 2 * BS]
    grad_small = rec_rows[:, width_d + 2 * BS : width_d + 2 * BS + taps + 4].T
    grad_down = summed(down_sum)
    mlp_whole = jax.ShapeDtypeStruct(mlp_gate.shape, wide)
    join = functools.partial(join_kernel, k_count, z_count)
    grad_gate_w, grad_up_w = in_vmem(join, (mlp_back,), (mlp_whole, mlp_whole))
    rec_back = jnp.moveaxis(rec_back, 2, 0)
    grad_branch_w = rec_back[..., :w_slot].reshape(d_own, width_r)
    grad_input_w = rec_back[..., w_slot:].reshape(d_own, width_r)

    def gain_grad(pairs, gain):
        total = sum(jnp.sum(weight.astype(wide) * grad, axis=1) for weight, grad in pairs)
        return total / gain.astype(wide)

    grad_norm_one = gain_grad(((branch_weight, grad_branch_w), (input_proj, grad_input_w)), norm_one)
    grad_norm_two = gain_grad(((mlp_gate, grad_gate_w), (mlp_up, grad_up_w)), norm_two)
    return (
        block_out,
        grad_tokens,
        grad_norm_one,
        grad_branch_w,
        grad_input_w,
        grad_small[:taps],
        grad_small[taps],
        grad_rate_w,
        grad_igate_w,
        grad_small[taps + 1],
        grad_small[taps + 2],
        grad_small[taps + 3],
        grad_out_w,
        grad_norm_two,
        grad_gate_w,
        grad_up_w,
        grad_down,
    )


def solution(mesh):
    rows, matrix = P(AXES), P(AXES, None)
    tokens = P("dp", "seq", None)
    return jax.shard_map(
        per_device,
        mesh=mesh,
        in_specs=(
            tokens,
            P("dp", "seq"),
            tokens,
            rows,
            matrix,
            matrix,
            P(None, AXES),
            rows,
            matrix,
            matrix,
            rows,
            rows,
            rows,
            matrix,
            rows,
            matrix,
            matrix,
            matrix,
        ),
        out_specs=(
            tokens,
            tokens,
            rows,
            matrix,
            matrix,
            P(None, AXES),
            rows,
            matrix,
            matrix,
            rows,
            rows,
            rows,
            matrix,
            rows,
            matrix,
            matrix,
            matrix,
        ),
        check_vma=False,
    )
```

time: 936 us -> 787 us (0.84)
  Pallas kernels: 48.1 us -> 266 us
  matrix products: 178 us -> 11.7 us
  waiting for transfers between devices: 326 us -> 224 us
  local copies, waits for them, and re-layouts: 117 us -> 71.3 us
  other arithmetic: 137 us -> 102 us
  starting transfers between devices: 103 us -> 86.5 us
    pallas_call x4 -> x16, Pallas kernels: 34.3 us -> 256 us  [the longest x6 139 us: kernel_call(): pl.pallas_call(kernel, out_shape=[array for array, _ in outputs], grid=(s...]
    dot_general x7 -> x0, matrix products: 78.2 us -> none  [dot_nt(): lax.dot_general(left, right, (((1,), (1,)), ((), ())), preferred_element_...]
    dot_general x7 -> x4, matrix products: 57.8 us -> 7.64 us  [dot_nn(): lax.dot_general(left, right, (((1,), (0,)), ((), ())), preferred_element_...]
    all_gather x4 -> x5, waiting for transfers between devices: 48 us -> 1.41 us  [gather_z(): lax.all_gather(array, AXES, axis_index_groups=self.z_groups, tiled=True)]
    dot_general x5 -> x1, matrix products: 42.2 us -> 4.01 us  [dot_tn(): lax.dot_general(left, right, (((0,), (0,)), ((), ())), preferred_element_...]
    ppermute x5 -> x4, waiting for transfers between devices: 42.8 us -> 16.7 us  [the longest x3 16.7 us: gather_seq_small(): got = lax.ppermute(out, 'seq', [(i, i ^ 1 << bit) for i in range(8)])]
    reduce_sum x4 -> x0, other arithmetic: 20.7 us -> none  [the longest x1 6.37 us: per_device(): jnp.sum(grad_log_keep * rate, axis=0)]
    ppermute x48, waiting for transfers between devices: 202 us -> 181 us  [to_k(): lax.ppermute(array, 'dp', [(i, i ^ flip) for i in range(self.k_count)])]
  transfers between devices with their start and end apart: 103 -> 102, of which waited for: 39 -> 43; matrix products, arithmetic and copies ran while one was open for 31% -> 18% of each run, Pallas kernels for 5% -> 28%
where the time goes in v2:
time: 787 us; the launch traced here: 777 us
  Pallas kernels  266 us (34%)
  waiting for transfers between devices  224 us (28%)
  other arithmetic  102 us (13%)
  starting transfers between devices  86.5 us (11%)
  local copies, waits for them, and re-layouts  71.3 us (9%)
  between operations  15.8 us (2%)
  matrix products  11.7 us (1%)
    ppermute x48, waiting for transfers between devices, to_k(): lax.ppermute(array, 'dp', [(i, i ^ flip) for i in range(self.k_count)])  181 us
    pallas_call x6, Pallas kernels, kernel_call(): pl.pallas_call(kernel, out_shape=[array for array, _ in outputs], grid=(s...  139 us
    pallas_call x6, Pallas kernels, half_call(): pl.pallas_call(kernel, out_shape=[array for array, _, _ in outputs], grid...  59.4 us
    ppermute x48, starting transfers between devices, to_k(): lax.ppermute(array, 'dp', [(i, i ^ flip) for i in range(self.k_count)])  56 us
    pallas_call x2, Pallas kernels, rows_call(): pl.pallas_call(functools.partial(rows_kernel, turned), out_shape=[sent, k...  33.8 us
    unnamed x142, local copies, waits for them, and re-layouts  27.4 us
    ppermute x9, starting transfers between devices, to_z(): return lax.ppermute(array, 'seq', pairs)  18.8 us
    ppermute x32, waiting for transfers between devices, to_core(): return lax.ppermute(array, 'seq', [(i, i ^ 1) for i in range(self.s_count)])  18.7 us
  transfers between devices with their start and end apart: 102, of which 43 were waited for; matrix products, arithmetic and copies ran while one was open for 18% of the time, Pallas kernels for 28%

profile of v2, /device:TPU:0, one launch (start us, length us, event | category | flops | bytes accessed | tf_op | source)
XLA Modules:
  0.0 776.9 jit_solution(9884588677429614050)
XLA Ops:
  11.9 4.5 collective-permute-start.1
  17.2 4.1 concatenate.116
  26.6 3.2 maximum_bitcast_fusion.1
  34.3 10.8 %collective-permute-done.6 = bf16[2,83,320]{2,1,0:T(8,128)(2,1)S(1)} collective-permute-done((bf16[2,83,320]{2,1,0:T(8,128)(2,1)S(1)}, bf16[2,83,320]{2,1,0:T(8,128)(2,1)S(1)}, u32[]{:S(2)}, u32[]{:S(2)}) %collective-permute-start.6) | collective-permute-done | bytes 106272 | tf_op jit(solution)/shard_map/ppermute | solution.py:205
  53.9 5.8 collective-permute-done.7
  82.7 18.5 %collective-permute-done.11.refs_2_ = bf16[256,2176]{1,0:T(8,128)(2,1)} collective-permute-done((bf16[256,2176]{1,0:T(8,128)(2,1)S(1)}, bf16[256,2176]{1,0:T(8,128)(2,1)}, u32[]{:S(2)}, u32[]{:S(2)}) %collective-permute-start.11) | collective-permute-done | bytes 1114144 | tf_op jit(solution)/shard_map/ppermute | solution.py:133
  109.5 4.2 collective-permute-done.22
  113.7 8.5 %collective-permute-done.21 = bf16[2,64,1536]{2,1,0:T(8,128)(2,1)S(1)} collective-permute-done((bf16[2,64,1536]{2,1,0:T(8,128)(2,1)S(1)}, bf16[2,64,1536]{2,1,0:T(8,128)(2,1)S(1)}, u32[]{:S(2)}, u32[]{:S(2)}) %collective-permute-start.21) | collective-permute-done | bytes 393248 | tf_op jit(solution)/shard_map/ppermute | solution.py:133
  123.1 8.2 %collective-permute-done.14.refs_4_ = bf16[128,2176]{1,0:T(8,128)(2,1)S(1)} collective-permute-done((bf16[128,2176]{1,0:T(8,128)(2,1)S(1)}, bf16[128,2176]{1,0:T(8,128)(2,1)S(1)}, u32[]{:S(2)}, u32[]{:S(2)}) %collective-permute-start.14) | collective-permute-done | bytes 557088 | tf_op jit(solution)/shard_map/ppermute | solution.py:133
  137.0 3.5 copy-done.2
  144.6 31.0 %shard_map.307 = (bf16[2048,2048]{1,0:T(8,128)(2,1)}, f32[2048,8]{1,0:T(8,128)}, f32[2048,320]{1,0:T(8,128)}, bf16[2048,320]{1,0:T(8,128)(2,1)}, bf16[2048,320]{...) custom-call(bf16[2048,2176]{1,0:T(8,128)(2,1)} %copy-done.2, ...), custom_call_target="tpu_custom_call" | custom-call | tf_op jit(solution)/shard_map/pallas_call | solution.py:910
  176.9 3.7 collective-permute-start.31
  189.0 12.6 %shard_map.308 = (f32[3,2048,128]{2,1,0:T(8,128)}, bf16[2048,320]{1,0:T(8,128)(2,1)}) custom-call(f32[3,2048,128]{2,1,0:T(8,128)} %get-tuple-element.208.keep_ref, f32[3,2048,128]{2,1,0:T(8,128)} %get-tuple-element.209.drive_ref, f32[3,8,128]{2,1,0:T(8,128)} %fusion.62.start_ref, f32[2048,320]{1,0:T(8,128)} %get-tuple-element.213.branch_ref), custom_call_target="tpu_custom_call" | custom-call | tf_op jit(solution)/shard_map/pallas_call | solution.py:910
  233.3 24.2 %collective-permute-done.38 = f16[2,256,1152]{2,1,0:T(8,128)(2,1)S(1)} collective-permute-done((f16[2,256,1152]{2,1,0:T(8,128)(2,1)S(1)}, f16[2,256,1152]{2,1,0:T(8,128)(2,1)S(1)}, u32[]{:S(2)}, u32[]{:S(2)}) %collective-permute-start.38) | collective-permute-done | bytes 1179680 | tf_op jit(solution)/shard_map/ppermute | solution.py:133
  270.7 10.3 %shard_map.310.x_ref = bf16[2048,2048]{1,0:T(8,128)(2,1)} custom-call(bf16[2048,2048]{1,0:T(8,128)(2,1)} %get-tuple-element.247.x_ref), custom_call_target="tpu_custom_call" | custom-call | tf_op jit(solution)/shard_map/pallas_call | solution.py:853
  291.0 3.3 copy-done
  301.1 3.0 pad_maximum_fusion.w_ref
  304.1 17.8 %collective-permute-done.48.refs_2_ = bf16[256,2048]{1,0:T(8,128)(2,1)S(1)} collective-permute-done((bf16[256,2048]{1,0:T(8,128)(2,1)S(1)}, bf16[256,2048]{1,0:T(8,128)(2,1)S(1)}, u32[]{:S(2)}, u32[]{:S(2)}) %collective-permute-start.48) | collective-permute-done | bytes 1048608 | tf_op jit(solution)/shard_map/ppermute | solution.py:133
  325.1 10.9 %collective-permute-done.50.refs_4_ = bf16[128,2048]{1,0:T(8,128)(2,1)S(1)} collective-permute-done((bf16[128,2048]{1,0:T(8,128)(2,1)S(1)}, bf16[128,2048]{1,0:T(8,128)(2,1)S(1)}, u32[]{:S(2)}, u32[]{:S(2)}) %collective-permute-start.50) | collective-permute-done | bytes 524320 | tf_op jit(solution)/shard_map/ppermute | solution.py:133
  340.1 3.3 copy-done.1
  343.4 26.7 %shard_map.312 = (bf16[2048,768]{1,0:T(8,128)(2,1)}, bf16[2048,1536]{1,0:T(8,128)(2,1)}) custom-call(bf16[2048,2048]{1,0:T(8,128)(2,1)} %copy-done.1, bf16[2048,2048]{1,0:T(8,128)(2,1)} %copy-done, bf16[2048,1536]{1,0:T(8,128)(2,1)} %pad_maximum_fusion.w_ref, bf16[768,2048]{1,0:T(8,128)(2,1)} %all-gather.14.cloned.1.call-done.down_ref.w_ref), custom_call_target="tpu_custom_call" | custom-call | tf_op jit(solution)/shard_map/pallas_call | solution.py:910
  370.2 11.4 %shard_map.313 = bf16[1024,2048]{1,0:T(8,128)(2,1)} custom-call(s32[1]{0:T(128)} %bitcast.72.core_ref, bf16[2048,1536]{1,0:T(8,128)(2,1)} %get-tuple-element.268.x_ref.grad_ref, bf16[2048,1536]{1,0:T(8,128)(2,1)} %pad_maximum_fusion.w_ref), custom_call_target="tpu_custom_call" | custom-call | tf_op jit(solution)/shard_map/pallas_call | solution.py:754
  381.7 7.2 collective-permute-done.56.got_ref
  390.9 13.7 %shard_map.314 = (f32[256,2048]{1,0:T(8,128)}, f32[256,1024]{1,0:T(8,128)}, f32[256,1024]{1,0:T(8,128)}, bf16[2,256,1024]{2,1,0:T(8,128)(2,1)}, bf16[2,256,1024]{2,1,0:T(8,128)(2,1)}) custom-call(s32[1]{0:T(128)} %bitcast.c_ref.core_ref, bf16[2048,1536]{1,0:T(8,128)(2,1)} %get-tuple-element.268.x_ref.grad_ref, bf16[2048,1536]{1,0:T(8,128)(2,1)} %pad_maximum_fusion.w_ref, ...), custom_call_target="tpu_custom_call" | custom-call | tf_op jit(solution)/shard_map/pallas_call | solution.py:754
  407.7 20.4 %shard_map.315 = (bf16[4,4,128,1536]{3,2,1,0:T(8,128)(2,1)}, f32[4,128,1536]{2,1,0:T(8,128)}) custom-call(s32[2]{0:T(128)} %pad_add_fusion.core_ref, bf16[2048,2048]{1,0:T(8,128)(2,1)} %copy-done.1, bf16[2048,1536]{1,0:T(8,128)(2,1)} %get-tuple-element.268.x_ref.grad_ref), custom_call_target="tpu_custom_call" | custom-call | tf_op jit(solution)/shard_map/pallas_call | solution.py:827
  438.5 13.7 %shard_map.316 = (bf16[4,192,2048]{2,1,0:T(8,128)(2,1)}, f32[192,2048]{1,0:T(8,128)}) custom-call(s32[1]{0:T(128)} %bitcast.73.core_ref, bf16[2048,768]{1,0:T(8,128)(2,1)} %get-tuple-element.284.hidden_ref.x_ref, bf16[2048,2048]{1,0:T(8,128)(2,1)} %copy-done), custom_call_target="tpu_custom_call" | custom-call | tf_op jit(solution)/shard_map/pallas_call | solution.py:886
  460.9 7.3 shard_map.317
  470.8 4.9 collective-permute-done.63.got_ref
  475.8 9.8 %shard_map.318 = (f32[256,2048]{1,0:T(8,128)}, f32[256,1024]{1,0:T(8,128)}, f32[256,1024]{1,0:T(8,128)}, bf16[2,256,1024]{2,1,0:T(8,128)(2,1)}, bf16[2,256,1024]{2,1,0:T(8,128)(2,1)}) custom-call(s32[1]{0:T(128)} %bitcast.c_ref.core_ref, bf16[2048,768]{1,0:T(8,128)(2,1)} %get-tuple-element.284.hidden_ref.x_ref, ...), custom_call_target="tpu_custom_call" | custom-call | tf_op jit(solution)/shard_map/pallas_call | solution.py:754
  485.5 8.3 %collective-permute-done.62.refs_2_ = bf16[256,2048]{1,0:T(8,128)(2,1)S(1)} collective-permute-done((bf16[256,2048]{1,0:T(8,128)(2,1)S(1)}, bf16[256,2048]{1,0:T(8,128)(2,1)S(1)}, u32[]{:S(2)}, u32[]{:S(2)}) %collective-permute-start.62) | collective-permute-done | bytes 1048608 | tf_op jit(solution)/shard_map/ppermute | solution.py:133
  497.9 10.2 %collective-permute-done.65.refs_4_ = bf16[128,2048]{1,0:T(8,128)(2,1)S(1)} collective-permute-done((bf16[128,2048]{1,0:T(8,128)(2,1)S(1)}, bf16[128,2048]{1,0:T(8,128)(2,1)S(1)}, u32[]{:S(2)}, u32[]{:S(2)}) %collective-permute-start.65) | collective-permute-done | bytes 524320 | tf_op jit(solution)/shard_map/ppermute | solution.py:133
  512.6 3.3 copy-done.3
  515.9 20.8 %shard_map.320 = (bf16[2048,320]{1,0:T(8,128)(2,1)}, f32[3,2048,128]{2,1,0:T(8,128)}, f32[3,8,128]{2,1,0:T(8,128)}) custom-call(bf16[2048,2048]{1,0:T(8,128)(2,1)} %copy-done.3, bf16[320,2048]{1,0:T(8,128)(2,1)} %bitcast.369, f32[2048,320]{1,0:T(8,128)} %get-tuple-element.213.branch_ref, f32[3,2048,128]{2,1,0:T(8,128)} %get-tuple-element.293.state_ref, ...), custom_call_target="tpu_custom_call" | custom-call | tf_op jit(solution)/shard_map/pallas_call | solution.py:910
  536.7 3.1 reduce-scatter.5.cloned.1.call-done
  552.2 4.0 fusion.92
  556.8 15.5 %collective-permute-done.75 = bf16[2,256,1024]{2,1,0:T(8,128)(2,1)S(1)} collective-permute-done((bf16[2,256,1024]{2,1,0:T(8,128)(2,1)S(1)}, bf16[2,256,1024]{2,1,0:T(8,128)(2,1)S(1)}, u32[]{:S(2)}, u32[]{:S(2)}) %collective-permute-start.75) | collective-permute-done | bytes 1048608 | tf_op jit(solution)/shard_map/ppermute | solution.py:133
  580.6 41.2 %shard_map.321 = (bf16[2048,320]{1,0:T(8,128)(2,1)}, bf16[320,448]{1,0:T(8,128)(2,1)}) custom-call(f32[3,2048,128]{2,1,0:T(8,128)} %get-tuple-element.208.keep_ref, f32[3,2048,128]{2,1,0:T(8,128)} %get-tuple-element.295.grad_ref, f32[3,8,128]{2,1,0:T(8,128)} %add_bitcast_fusion.carry_ref, f32[3,2048,128]{2,1,0:T(8,128)} %get-tuple-element.293.state_ref, ...), custom_call_target="tpu_custom_call" | custom-call | tf_op jit(solution)/shard_map/pallas_call | solution.py:910
  636.0 3.6 copy.153
  639.6 6.3 shard_map.322
  645.9 3.9 pad_maximum_fusion.2.x_ref.grad_ref
  649.8 7.2 shard_map.323
  657.4 13.3 %shard_map.324 = (bf16[4,4,128,640]{3,2,1,0:T(8,128)(2,1)}, f32[4,128,640]{2,1,0:T(8,128)}) custom-call(s32[2]{0:T(128)} %pad_add_fusion.core_ref, bf16[2048,2048]{1,0:T(8,128)(2,1)} %shard_map.310.x_ref, bf16[2048,640]{1,0:T(8,128)(2,1)} %pad_maximum_fusion.2.x_ref.grad_ref), custom_call_target="tpu_custom_call" | custom-call | tf_op jit(solution)/shard_map/pallas_call | solution.py:827
  685.4 9.9 %shard_map.325 = (f32[256,2048]{1,0:T(8,128)}, f32[256,1024]{1,0:T(8,128)}, f32[256,1024]{1,0:T(8,128)}, bf16[2,256,1024]{2,1,0:T(8,128)(2,1)}, bf16[2,256,1024]{2,1,0:T(8,128)(2,1)}) custom-call(s32[1]{0:T(128)} %bitcast.c_ref.core_ref, bf16[2048,640]{1,0:T(8,128)(2,1)} %pad_maximum_fusion.2.x_ref.grad_ref, bf16[2048,640]{1,0:T(8,128)(2,1)} %bitcast.375, ...), custom_call_target="tpu_custom_call" | custom-call | tf_op jit(solution)/shard_map/pallas_call | solution.py:754
  700.6 19.7 %collective-permute-done.83 = bf16[2,256,1024]{2,1,0:T(8,128)(2,1)S(1)} collective-permute-done((bf16[2,256,1024]{2,1,0:T(8,128)(2,1)}, bf16[2,256,1024]{2,1,0:T(8,128)(2,1)S(1)}, u32[]{:S(2)}, u32[]{:S(2)}) %collective-permute-start.83) | collective-permute-done | bytes 1048608 | tf_op jit(solution)/shard_map/ppermute | solution.py:133
  726.1 9.2 %collective-permute-done.85 = bf16[256,1024]{1,0:T(8,128)(2,1)S(1)} collective-permute-done((bf16[256,1024]{1,0:T(8,128)(2,1)S(1)}, bf16[256,1024]{1,0:T(8,128)(2,1)S(1)}, u32[]{:S(2)}, u32[]{:S(2)}) %collective-permute-start.85) | collective-permute-done | bytes 524320 | tf_op jit(solution)/shard_map/ppermute | solution.py:133
  743.2 3.6 fusion.4
  754.3 4.6 collective-permute-done.92
  758.9 7.0 collective-permute-done.91
  (547 shorter events, 259.4 us)
Async XLA Ops:
  7.2 67.1 %all-gather.6.cloned.1.call-start = ((), (), s32[]{:S(2)}) async-start(), calls=%async_computation.4 | async-start | bytes 1638400 | tf_op jit(solution)/shard_map/all_gather | solution.py:146
  7.9 136.7 %all-gather.8.cloned.1.call-start = ((), (), s32[]{:S(2)}) async-start(), calls=%async_computation.5 | async-start | bytes 3276800 | tf_op jit(solution)/shard_map/all_gather | solution.py:146
  8.7 21.3 %collective-permute-start = (bf16[2,3]{1,0:T(2,128)(2,1)S(1)}, bf16[2,3]{1,0:T(2,128)(2,1)S(1)}, u32[]{:S(2)}, u32[]{:S(2)}) collective-permute-start(bf16[2,3]{1,0:T(2,128)(2,1)S(1)} %slice.330), channel_id=1, source_target_pairs={{0,1},{1,2},{2,3},{3,4},{4,5},{5,6},{6,7},{8,9},{9,10},{10,11},{11... | collective-permute-start | bytes 44 | tf_op jit(solution)/shard_map/ppermute | solution.py:1014
  11.9 18.6 %collective-permute-start.1 = (bf16[16,2048]{1,0:T(8,128)(2,1)S(1)}, bf16[16,2048]{1,0:T(8,128)(2,1)S(1)}, u32[]{:S(2)}, u32[]{:S(2)}) collective-permute-start(bf16[16,2048]{1,0:T(8,128)(2,1)S(1)} %slice_bitcast_fusion.18), channel_id=1, source_target_pairs={{0,2},{1,3},{2,4},{3,5},{4,6},{5,7},{8,10},{9,11},{10,12},{11,13},... | collective-permute-start | bytes 196616 | tf_op jit(solution)/shard_map/ppermute | solution.py:140
  29.8 17.2 %collective-permute-start.23 = (bf16[4,64,640]{2,1,0:T(8,128)(2,1)S(1)}, bf16[4,64,640]{2,1,0:T(8,128)(2,1)S(1)}, u32[]{:S(2)}, u32[]{:S(2)}) collective-permute-start(bf16[4,64,640]{2,1,0:T(8,128)(2,1)S(1)} %bitcast.405), channel_id=1, source_target_pairs={{0,1},{1,0},{2,3},{3,2},{4,5},{5,4},{6,7},{7,6},{8,9},{9,8},{10,11... | collective-permute-start | bytes 983048 | tf_op jit(solution)/shard_map/ppermute | solution.py:136
  49.6 22.5 %collective-permute-start.26 = (bf16[2,64,640]{2,1,0:T(8,128)(2,1)}, bf16[2,64,640]{2,1,0:T(8,128)(2,1)}, u32[]{:S(2)}, u32[]{:S(2)}) collective-permute-start(bf16[2,64,640]{2,1,0:T(8,128)(2,1)} %get-tuple-element.567), channel_id=1, source_target_pairs={{0,8},{8,0},{16,24},{24,16},{1,9},{9,1},{17,25},{25,17},{2,10},{10... | collective-permute-start | bytes 491528 | tf_op jit(solution)/shard_map/ppermute | solution.py:133
  51.1 21.0 %collective-permute-start.25 = (bf16[2,64,640]{2,1,0:T(8,128)(2,1)}, bf16[2,64,640]{2,1,0:T(8,128)(2,1)}, u32[]{:S(2)}, u32[]{:S(2)}) collective-permute-start(bf16[2,64,640]{2,1,0:T(8,128)(2,1)} %get-tuple-element.568), channel_id=1, source_target_pairs={{0,16},{8,24},{16,0},{24,8},{1,17},{9,25},{17,1},{25,9},{2,18},{10... | collective-permute-start | bytes 491528 | tf_op jit(solution)/shard_map/ppermute | solution.py:133
  51.7 20.5 %collective-permute-start.24 = (bf16[2,64,640]{2,1,0:T(8,128)(2,1)S(1)}, bf16[2,64,640]{2,1,0:T(8,128)(2,1)}, u32[]{:S(2)}, u32[]{:S(2)}) collective-permute-start(bf16[2,64,640]{2,1,0:T(8,128)(2,1)S(1)} %get-tuple-element.569), channel_id=1, source_target_pairs={{0,24},{8,16},{16,8},{24,0},{1,25},{9,17},{17,9},{25,1},{2,26},{10... | collective-permute-start | bytes 491528 | tf_op jit(solution)/shard_map/ppermute | solution.py:133
  74.3 131.3 %all-gather.10.cloned.1.call-start = ((), (), s32[]{:S(2)}) async-start(), calls=%async_computation.6 | async-start | bytes 3932160 | tf_op jit(solution)/shard_map/all_gather | solution.py:146
  75.2 26.0 %collective-permute-start.11 = (bf16[256,2176]{1,0:T(8,128)(2,1)S(1)}, bf16[256,2176]{1,0:T(8,128)(2,1)}, u32[]{:S(2)}, u32[]{:S(2)}) collective-permute-start(bf16[256,2176]{1,0:T(8,128)(2,1)S(1)} %pad_maximum_fusion.11.refs_0_), channel_id=1, source_target_pairs={{0,16},{8,24},{16,0},{24,8},{1,17},{9,25},{17,1},{25,9},{2,18},{10... | collective-permute-start | bytes 3342344 | tf_op jit(solution)/shard_map/ppermute | solution.py:133
  76.6 24.9 %collective-permute-start.10 = (bf16[256,2176]{1,0:T(8,128)(2,1)S(1)}, bf16[256,2176]{1,0:T(8,128)(2,1)}, u32[]{:S(2)}, u32[]{:S(2)}) collective-permute-start(bf16[256,2176]{1,0:T(8,128)(2,1)S(1)} %pad_maximum_fusion.11.refs_0_), channel_id=1, source_target_pairs={{0,8},{8,0},{16,24},{24,16},{1,9},{9,1},{17,25},{25,17},{2,10},{10... | collective-permute-start | bytes 3342344 | tf_op jit(solution)/shard_map/ppermute | solution.py:133
  102.1 20.0 %collective-permute-start.21 = (bf16[2,64,1536]{2,1,0:T(8,128)(2,1)S(1)}, bf16[2,64,1536]{2,1,0:T(8,128)(2,1)S(1)}, u32[]{:S(2)}, u32[]{:S(2)}) collective-permute-start(bf16[2,64,1536]{2,1,0:T(8,128)(2,1)S(1)} %get-tuple-element.546), channel_id=1, source_target_pairs={{0,16},{8,24},{16,0},{24,8},{1,17},{9,25},{17,1},{25,9},{2,18},{10... | collective-permute-start | bytes 1179656 | tf_op jit(solution)/shard_map/ppermute | solution.py:133
  103.6 19.4 %collective-permute-start.20 = (bf16[2,64,1536]{2,1,0:T(8,128)(2,1)S(1)}, bf16[2,64,1536]{2,1,0:T(8,128)(2,1)S(1)}, u32[]{:S(2)}, u32[]{:S(2)}) collective-permute-start(bf16[2,64,1536]{2,1,0:T(8,128)(2,1)S(1)} %get-tuple-element.547), channel_id=1, source_target_pairs={{0,24},{8,16},{16,8},{24,0},{1,25},{9,17},{17,9},{25,1},{2,26},{10... | collective-permute-start | bytes 1179656 | tf_op jit(solution)/shard_map/ppermute | solution.py:133
  106.2 25.1 %collective-permute-start.14 = (bf16[128,2176]{1,0:T(8,128)(2,1)S(1)}, bf16[128,2176]{1,0:T(8,128)(2,1)S(1)}, u32[]{:S(2)}, u32[]{:S(2)}) collective-permute-start(bf16[128,2176]{1,0:T(8,128)(2,1)S(1)} %slice.354), channel_id=1, source_target_pairs={{0,8},{8,0},{16,24},{24,16},{1,9},{9,1},{17,25},{25,17},{2,10},{10... | collective-permute-start | bytes 1671176 | tf_op jit(solution)/shard_map/ppermute | solution.py:133
  107.9 23.6 %collective-permute-start.13 = (bf16[128,2176]{1,0:T(8,128)(2,1)S(1)}, bf16[128,2176]{1,0:T(8,128)(2,1)S(1)}, u32[]{:S(2)}, u32[]{:S(2)}) collective-permute-start(bf16[128,2176]{1,0:T(8,128)(2,1)S(1)} %slice.353), channel_id=1, source_target_pairs={{0,16},{8,24},{16,0},{24,8},{1,17},{9,25},{17,1},{25,9},{2,18},{10... | collective-permute-start | bytes 1671176 | tf_op jit(solution)/shard_map/ppermute | solution.py:133
  113.7 20.4 %collective-permute-start.16 = (bf16[256,2176]{1,0:T(8,128)(2,1)}, bf16[256,2176]{1,0:T(8,128)(2,1)S(1)}, u32[]{:S(2)}, u32[]{:S(2)}) collective-permute-start(bf16[256,2176]{1,0:T(8,128)(2,1)} %collective-permute-done.10.refs_1_), channel_id=1, source_target_pairs={{0,1},{1,0},{2,3},{3,2},{4,5},{5,4},{6,7},{7,6},{8,9},{9,8},{10,11... | collective-permute-start | bytes 3342344 | tf_op jit(solution)/shard_map/ppermute | solution.py:136
  141.8 152.5 %all-gather.12.cloned.1.call-start = ((), (), s32[]{:S(2)}) async-start(), calls=%async_computation.7 | async-start | bytes 3932160 | tf_op jit(solution)/shard_map/all_gather | solution.py:146
  142.2 33.4 %collective-permute-start.28 = (bf16[256,2048]{1,0:T(8,128)(2,1)S(1)}, bf16[256,2048]{1,0:T(8,128)(2,1)S(1)}, u32[]{:S(2)}, u32[]{:S(2)}) collective-permute-start(bf16[256,2048]{1,0:T(8,128)(2,1)S(1)} %bitcast.363), channel_id=1, source_target_pairs={{0,16},{8,24},{16,0},{24,8},{1,17},{9,25},{17,1},{25,9},{2,18},{10... | collective-permute-start | bytes 3145736 | tf_op jit(solution)/shard_map/ppermute | solution.py:133
  143.7 32.0 %collective-permute-start.27 = (bf16[256,2048]{1,0:T(8,128)(2,1)S(1)}, bf16[256,2048]{1,0:T(8,128)(2,1)S(1)}, u32[]{:S(2)}, u32[]{:S(2)}) collective-permute-start(bf16[256,2048]{1,0:T(8,128)(2,1)S(1)} %bitcast.364), channel_id=1, source_target_pairs={{0,8},{8,0},{16,24},{24,16},{1,9},{9,1},{17,25},{25,17},{2,10},{10... | collective-permute-start | bytes 3145736 | tf_op jit(solution)/shard_map/ppermute | solution.py:133
  176.9 24.7 %collective-permute-start.35 = (bf16[160,2048]{1,0:T(8,128)(2,1)}, bf16[160,2048]{1,0:T(8,128)(2,1)}, u32[]{:S(2)}, u32[]{:S(2)}) collective-permute-start(bf16[160,2048]{1,0:T(8,128)(2,1)} %get-tuple-element.558), channel_id=1, source_target_pairs={{0,1},{1,0},{2,3},{3,2},{4,5},{5,4},{6,7},{7,6},{8,9},{9,8},{10,11... | collective-permute-start | bytes 1966088 | tf_op jit(solution)/shard_map/ppermute | solution.py:136
  184.5 19.7 %collective-permute-start.33 = (bf16[128,2048]{1,0:T(8,128)(2,1)S(1)}, bf16[128,2048]{1,0:T(8,128)(2,1)}, u32[]{:S(2)}, u32[]{:S(2)}) collective-permute-start(bf16[128,2048]{1,0:T(8,128)(2,1)S(1)} %slice.362), channel_id=1, source_target_pairs={{0,8},{8,0},{16,24},{24,16},{1,9},{9,1},{17,25},{25,17},{2,10},{10... | collective-permute-start | bytes 1572872 | tf_op jit(solution)/shard_map/ppermute | solution.py:133
  185.7 18.5 %collective-permute-start.32 = (bf16[128,2048]{1,0:T(8,128)(2,1)S(1)}, bf16[128,2048]{1,0:T(8,128)(2,1)}, u32[]{:S(2)}, u32[]{:S(2)}) collective-permute-start(bf16[128,2048]{1,0:T(8,128)(2,1)S(1)} %slice.361), channel_id=1, source_target_pairs={{0,16},{8,24},{16,0},{24,8},{1,17},{9,25},{17,1},{25,9},{2,18},{10... | collective-permute-start | bytes 1572872 | tf_op jit(solution)/shard_map/ppermute | solution.py:133
  187.1 17.1 %collective-permute-start.34 = (f32[8,16,8]{2,1,0:T(8,128)S(1)}, f32[8,16,8]{2,1,0:T(8,128)S(1)}, u32[]{:S(2)}, u32[]{:S(2)}) collective-permute-start(f32[8,16,8]{2,1,0:T(8,128)S(1)} %slice_bitcast_fusion.17), channel_id=1, source_target_pairs={{2,0},{3,1},{4,2},{5,3},{6,4},{7,5},{10,8},{11,9},{12,10},{13,11},... | collective-permute-start | bytes 12296 | tf_op jit(solution)/shard_map/ppermute | solution.py:140
  216.4 127.1 %all-gather.14.cloned.1.call-start = ((), (), s32[]{:S(2)}) async-start(), calls=%async_computation.8 | async-start | bytes 3932160 | tf_op jit(solution)/shard_map/all_gather | solution.py:146
  229.5 28.0 %collective-permute-start.38 = (f16[2,256,1152]{2,1,0:T(8,128)(2,1)S(1)}, f16[2,256,1152]{2,1,0:T(8,128)(2,1)S(1)}, u32[]{:S(2)}, u32[]{:S(2)}) collective-permute-start(f16[2,256,1152]{2,1,0:T(8,128)(2,1)S(1)} %pad_maximum_fusion.9), channel_id=1, source_target_pairs={{0,8},{8,0},{16,24},{24,16},{1,9},{9,1},{17,25},{25,17},{2,10},{10... | collective-permute-start | bytes 3538952 | tf_op jit(solution)/shard_map/ppermute | solution.py:133
  231.8 27.7 %collective-permute-start.39 = (f16[2,256,1152]{2,1,0:T(8,128)(2,1)S(1)}, f16[2,256,1152]{2,1,0:T(8,128)(2,1)S(1)}, u32[]{:S(2)}, u32[]{:S(2)}) collective-permute-start(f16[2,256,1152]{2,1,0:T(8,128)(2,1)S(1)} %pad_maximum_fusion.10), channel_id=1, source_target_pairs={{0,16},{8,24},{16,0},{24,8},{1,17},{9,25},{17,1},{25,9},{2,18},{10... | collective-permute-start | bytes 3538952 | tf_op jit(solution)/shard_map/ppermute | solution.py:133
  270.4 269.4 %reduce-scatter.5.cloned.1.call-start = ((), (), s32[]{:S(2)}) async-start(), calls=%async_computation.9 | async-start | bytes 7864320 | tf_op jit(solution)/shard_map/reduce_scatter | solution.py:160
  296.8 25.1 %collective-permute-start.48 = (bf16[256,2048]{1,0:T(8,128)(2,1)S(1)}, bf16[256,2048]{1,0:T(8,128)(2,1)S(1)}, u32[]{:S(2)}, u32[]{:S(2)}) collective-permute-start(bf16[256,2048]{1,0:T(8,128)(2,1)S(1)} %multiply_convert_fusion.2.refs_0_), channel_id=1, source_target_pairs={{0,16},{8,24},{16,0},{24,8},{1,17},{9,25},{17,1},{25,9},{2,18},{10... | collective-permute-start | bytes 3145736 | tf_op jit(solution)/shard_map/ppermute | solution.py:133
  298.3 24.8 %collective-permute-start.47 = (bf16[256,2048]{1,0:T(8,128)(2,1)S(1)}, bf16[256,2048]{1,0:T(8,128)(2,1)S(1)}, u32[]{:S(2)}, u32[]{:S(2)}) collective-permute-start(bf16[256,2048]{1,0:T(8,128)(2,1)S(1)} %multiply_convert_fusion.2.refs_0_), channel_id=1, source_target_pairs={{0,8},{8,0},{16,24},{24,16},{1,9},{9,1},{17,25},{25,17},{2,10},{10... | collective-permute-start | bytes 3145736 | tf_op jit(solution)/shard_map/ppermute | solution.py:133
  404.7 25.5 %collective-permute-start.57 = (bf16[2,256,1024]{2,1,0:T(8,128)(2,1)}, bf16[2,256,1024]{2,1,0:T(8,128)(2,1)}, u32[]{:S(2)}, u32[]{:S(2)}) collective-permute-start(bf16[2,256,1024]{2,1,0:T(8,128)(2,1)} %get-tuple-element.264), channel_id=1, source_target_pairs={{0,8},{8,0},{16,24},{24,16},{1,9},{9,1},{17,25},{25,17},{2,10},{10... | collective-permute-start | bytes 3145736 | tf_op jit(solution)/shard_map/ppermute | solution.py:133
  405.8 25.2 %collective-permute-start.58 = (bf16[2,256,1024]{2,1,0:T(8,128)(2,1)}, bf16[2,256,1024]{2,1,0:T(8,128)(2,1)}, u32[]{:S(2)}, u32[]{:S(2)}) collective-permute-start(bf16[2,256,1024]{2,1,0:T(8,128)(2,1)} %get-tuple-element.265), channel_id=1, source_target_pairs={{0,16},{8,24},{16,0},{24,8},{1,17},{9,25},{17,1},{25,9},{2,18},{10... | collective-permute-start | bytes 3145736 | tf_op jit(solution)/shard_map/ppermute | solution.py:133
  431.1 195.4 %reduce-scatter.7.cloned.1.call-start = ((), (), s32[]{:S(2)}) async-start(), calls=%async_computation.10 | async-start | bytes 3932160 | tf_op jit(solution)/shard_map/reduce_scatter | solution.py:160
  468.3 25.6 %collective-permute-start.62 = (bf16[256,2048]{1,0:T(8,128)(2,1)S(1)}, bf16[256,2048]{1,0:T(8,128)(2,1)S(1)}, u32[]{:S(2)}, u32[]{:S(2)}) collective-permute-start(bf16[256,2048]{1,0:T(8,128)(2,1)S(1)} %get-tuple-element.290.refs_0_), channel_id=1, source_target_pairs={{0,16},{8,24},{16,0},{24,8},{1,17},{9,25},{17,1},{25,9},{2,18},{10... | collective-permute-start | bytes 3145736 | tf_op jit(solution)/shard_map/ppermute | solution.py:133
  469.4 25.3 %collective-permute-start.61 = (bf16[256,2048]{1,0:T(8,128)(2,1)S(1)}, bf16[256,2048]{1,0:T(8,128)(2,1)S(1)}, u32[]{:S(2)}, u32[]{:S(2)}) collective-permute-start(bf16[256,2048]{1,0:T(8,128)(2,1)S(1)} %get-tuple-element.290.refs_0_), channel_id=1, source_target_pairs={{0,8},{8,0},{16,24},{24,16},{1,9},{9,1},{17,25},{25,17},{2,10},{10... | collective-permute-start | bytes 3145736 | tf_op jit(solution)/shard_map/ppermute | solution.py:133
  470.8 266.0 %reduce-scatter.11.cloned.1.call-start = ((), (), s32[]{:S(2)}) async-start(), calls=%async_computation.12 | async-start | bytes 2048000 | tf_op jit(solution)/shard_map/reduce_scatter | solution.py:160
  542.1 32.4 %collective-permute-start.74 = (f32[4,64,1536]{2,1,0:T(8,128)S(1)}, f32[4,64,1536]{2,1,0:T(8,128)S(1)}, u32[]{:S(2)}, u32[]{:S(2)}) collective-permute-start(f32[4,64,1536]{2,1,0:T(8,128)S(1)} %get-tuple-element.520), channel_id=1, source_target_pairs={{0,1},{1,0},{2,3},{3,2},{4,5},{5,4},{6,7},{7,6},{8,9},{9,8},{10,11... | collective-permute-start | bytes 4718600 | tf_op jit(solution)/shard_map/ppermute | solution.py:136
  547.3 25.0 %collective-permute-start.75 = (bf16[2,256,1024]{2,1,0:T(8,128)(2,1)S(1)}, bf16[2,256,1024]{2,1,0:T(8,128)(2,1)S(1)}, u32[]{:S(2)}, u32[]{:S(2)}) collective-permute-start(bf16[2,256,1024]{2,1,0:T(8,128)(2,1)S(1)} %copy-done.68), channel_id=1, source_target_pairs={{0,8},{8,0},{16,24},{24,16},{1,9},{9,1},{17,25},{25,17},{2,10},{10... | collective-permute-start | bytes 3145736 | tf_op jit(solution)/shard_map/ppermute | solution.py:133
  550.7 23.8 %collective-permute-start.76 = (bf16[2,256,1024]{2,1,0:T(8,128)(2,1)S(1)}, bf16[2,256,1024]{2,1,0:T(8,128)(2,1)S(1)}, u32[]{:S(2)}, u32[]{:S(2)}) collective-permute-start(bf16[2,256,1024]{2,1,0:T(8,128)(2,1)S(1)} %copy-done.67), channel_id=1, source_target_pairs={{0,16},{8,24},{16,0},{24,8},{1,17},{9,25},{17,1},{25,9},{2,18},{10... | collective-permute-start | bytes 3145736 | tf_op jit(solution)/shard_map/ppermute | solution.py:133
  576.9 47.3 %collective-permute-start.79 = (f32[2,64,1536]{2,1,0:T(8,128)}, f32[2,64,1536]{2,1,0:T(8,128)}, u32[]{:S(2)}, u32[]{:S(2)}) collective-permute-start(f32[2,64,1536]{2,1,0:T(8,128)} %get-tuple-element.516), channel_id=1, source_target_pairs={{0,8},{8,0},{16,24},{24,16},{1,9},{9,1},{17,25},{25,17},{2,10},{10... | collective-permute-start | bytes 2359304 | tf_op jit(solution)/shard_map/ppermute | solution.py:133
  578.4 45.9 %collective-permute-start.78 = (f32[2,64,1536]{2,1,0:T(8,128)}, f32[2,64,1536]{2,1,0:T(8,128)}, u32[]{:S(2)}, u32[]{:S(2)}) collective-permute-start(f32[2,64,1536]{2,1,0:T(8,128)} %get-tuple-element.517), channel_id=1, source_target_pairs={{0,16},{8,24},{16,0},{24,8},{1,17},{9,25},{17,1},{25,9},{2,18},{10... | collective-permute-start | bytes 2359304 | tf_op jit(solution)/shard_map/ppermute | solution.py:133
  579.9 44.4 %collective-permute-start.77 = (f32[2,64,1536]{2,1,0:T(8,128)}, f32[2,64,1536]{2,1,0:T(8,128)}, u32[]{:S(2)}, u32[]{:S(2)}) collective-permute-start(f32[2,64,1536]{2,1,0:T(8,128)} %get-tuple-element.518), channel_id=1, source_target_pairs={{0,24},{8,16},{16,8},{24,0},{1,25},{9,17},{17,9},{25,1},{2,26},{10... | collective-permute-start | bytes 2359304 | tf_op jit(solution)/shard_map/ppermute | solution.py:133
  635.5 101.3 %reduce-scatter.9.cloned.1.call-start = ((), (), s32[]{:S(2)}) async-start(), calls=%async_computation.11 | async-start | bytes 3276800 | tf_op jit(solution)/shard_map/reduce_scatter | solution.py:160
  657.0 28.4 %collective-permute-start.82 = (bf16[1024,2048]{1,0:T(8,128)(2,1)}, bf16[1024,2048]{1,0:T(8,128)(2,1)}, u32[]{:S(2)}, u32[]{:S(2)}) collective-permute-start(bf16[1024,2048]{1,0:T(8,128)(2,1)} %shard_map.323), channel_id=1, source_target_pairs={{0,1},{1,0},{2,3},{3,2},{4,5},{5,4},{6,7},{7,6},{8,9},{9,8},{10,11... | collective-permute-start | bytes 12582920 | tf_op jit(solution)/shard_map/ppermute | solution.py:136
  678.1 20.7 %collective-permute-start.87 = (bf16[256,1024]{1,0:T(8,128)(2,1)}, bf16[256,1024]{1,0:T(8,128)(2,1)}, u32[]{:S(2)}, u32[]{:S(2)}) collective-permute-start(bf16[256,1024]{1,0:T(8,128)(2,1)} %fusion.15), channel_id=1, source_target_pairs={{0,16},{8,24},{16,0},{24,8},{1,17},{9,25},{17,1},{25,9},{2,18},{10... | collective-permute-start | bytes 1572872 | tf_op jit(solution)/shard_map/ppermute | solution.py:133
  679.6 19.2 %collective-permute-start.88 = (bf16[256,1024]{1,0:T(8,128)(2,1)}, bf16[256,1024]{1,0:T(8,128)(2,1)}, u32[]{:S(2)}, u32[]{:S(2)}) collective-permute-start(bf16[256,1024]{1,0:T(8,128)(2,1)} %fusion.13), channel_id=1, source_target_pairs={{0,8},{8,0},{16,24},{24,16},{1,9},{9,1},{17,25},{25,17},{2,10},{10... | collective-permute-start | bytes 1572872 | tf_op jit(solution)/shard_map/ppermute | solution.py:133
  695.3 24.9 %collective-permute-start.83 = (bf16[2,256,1024]{2,1,0:T(8,128)(2,1)}, bf16[2,256,1024]{2,1,0:T(8,128)(2,1)S(1)}, u32[]{:S(2)}, u32[]{:S(2)}) collective-permute-start(bf16[2,256,1024]{2,1,0:T(8,128)(2,1)} %get-tuple-element.345), channel_id=1, source_target_pairs={{0,8},{8,0},{16,24},{24,16},{1,9},{9,1},{17,25},{25,17},{2,10},{10... | collective-permute-start | bytes 3145736 | tf_op jit(solution)/shard_map/ppermute | solution.py:133
  696.0 24.7 %collective-permute-start.84 = (bf16[2,256,1024]{2,1,0:T(8,128)(2,1)}, bf16[2,256,1024]{2,1,0:T(8,128)(2,1)S(1)}, u32[]{:S(2)}, u32[]{:S(2)}) collective-permute-start(bf16[2,256,1024]{2,1,0:T(8,128)(2,1)} %get-tuple-element.346), channel_id=1, source_target_pairs={{0,16},{8,24},{16,0},{24,8},{1,17},{9,25},{17,1},{25,9},{2,18},{10... | collective-permute-start | bytes 3145736 | tf_op jit(solution)/shard_map/ppermute | solution.py:133
  749.6 16.4 %collective-permute-start.91 = (f32[2,64,640]{2,1,0:T(8,128)S(1)}, f32[2,64,640]{2,1,0:T(8,128)S(1)}, u32[]{:S(2)}, u32[]{:S(2)}) collective-permute-start(f32[2,64,640]{2,1,0:T(8,128)S(1)} %get-tuple-element.553), channel_id=1, source_target_pairs={{0,16},{8,24},{16,0},{24,8},{1,17},{9,25},{17,1},{25,9},{2,18},{10... | collective-permute-start | bytes 983048 | tf_op jit(solution)/shard_map/ppermute | solution.py:133
  (123 other events, 882.0 us)
Sparse Core Ops, SparseCore 0:
  9.6 37.2 all-gather.5
  74.4 52.3 all-gather.7
  141.9 63.6 all-gather.9
  216.5 62.7 all-gather.11
  280.7 62.1 all-gather.13
  431.2 108.6 reduce-scatter.4
  542.1 61.1 reduce-scatter.6
  635.6 38.5 reduce-scatter.10
  676.6 51.1 reduce-scatter.8

commit v3 on v2

--- a/solution.py
+++ b/solution.py
@@ -241,14 +241,11 @@
             return self.gather_plane(mine[0])
         return lay_out(self.c, mine, [self.to_core(part) for part in mine])
 
-    def gather_tail(self, tail):
-        if not self.square:
-            tail = jnp.swapaxes(self.gather_plane(tail[None]).reshape((2, -1) + tail.shape), 0, 1)
-            return self.to_z(tail[:, 1].reshape((-1,) + tail.shape[3:]), 1)
-        tail = self.to_z(tail, 1)
-        tail = jnp.where(self.c == 1, tail, self.to_core(tail))
-        tail = jnp.concatenate([tail, self.to_k(tail, 1)])
-        return jnp.concatenate([tail, self.to_k(tail, 2)])
+    def gather_rows(self, array):
+        if not self.square:
+            return lax.all_gather(array, "dp", tiled=True)
+        array = jnp.concatenate([array, self.to_k(array, 1)])
+        return jnp.concatenate([array, self.to_k(array, 2)])
 
     def gather_plane_small(self, array):
         if not self.square:
@@ -294,26 +291,22 @@
         power = got[..., width : width + 1]
         return got[..., :width] * jnp.exp2(power), power
 
-    def chip_parts(self, left, right, side, between=None):
-        if not self.square:
-            return self.chip_product(left, right, dot_nt if side else dot_nn), None
-        count = left.shape[0] // 8
-        other = other_call(self.c, left, right, count, side)
-        got = self.to_core(other)
-        extra = None
-        if between is not None:
-            left, extra = between(other, left)
-        return own_call(self.c, left, right, got, count, side), extra
+    def chip_send(self, left, right, side):
+        if not self.square:
+            return None, None
+        other = other_call(self.c, left, right, left.shape[0] // 8, side)
+        return other, self.to_core(other)
+
+    def chip_own(self, left, right, got, side):
+        if not self.square:
+            return self.chip_product(left, right, dot_nt if side else dot_nn)
+        return own_call(self.c, left, right, got, left.shape[0] // 8, side)
 
     def near_parts(self, parts):
         if not self.square:
             return self.near_plane(parts)
         chip, next_a, next_b, a, b = parts
         return (chip, next_a, next_b, *together(self.to_k(a, 1), self.to_k(b, 2)))
-
-    def near_product(self, left, right, between=None):
-        parts, extra = self.chip_parts(left, right, 1, between)
-        return self.near_parts(parts), extra
 
     def far_product(self, near):
         if not self.square:
@@ -433,24 +426,31 @@
     return rate, igate, jnp.exp(log_keep), room, mult
 
 
-def put_lanes(ref, at, value):
-    for j in range(ref.shape[0]):
-        part = value[:, 128 * j : 128 * (j + 1)]
-        ref[j, at, : part.shape[1]] = part
-
-
-def get_lanes(ref, at, width):
-    parts = [ref[j, at, : min(128, width - 128 * j)] for j in range(ref.shape[0])]
-    return jnp.concatenate(parts, axis=1)
-
-
-def lane_shape(tokens, width, kind=wide):
-    return jax.ShapeDtypeStruct((pl.cdiv(width, 128), tokens, 128), kind)
+def shifted(values, by, fill):
+    count = values.shape[0]
+    size = abs(by)
+    if size % 8 == 0:
+        free = jnp.full((size, values.shape[1]), fill, values.dtype)
+        if by > 0:
+            return jnp.concatenate([free, values[: count - size]])
+        return jnp.concatenate([values[size:], free])
+    place = lax.broadcasted_iota(jnp.int32, values.shape, 0)
+    moved = pltpu.roll(values, by % count, 0)
+    return jnp.where(place >= by if by > 0 else place < count - size, moved, fill)
+
+
+def scan_rows(keep, drive, sign):
+    by = 1
+    while by < keep.shape[0]:
+        drive = drive + keep * shifted(drive, sign * by, 0.0)
+        keep = keep * shifted(keep, sign * by, 1.0)
+        by *= 2
+    return keep, drive
 
 
 def conv_kernel(
     rows, span, order, x_ref, w_ref, halo_ref, gain_ref, params_ref, gates_ref,
-    normed_ref, masks_ref, branch_ref, in_ref, low_ref, keep_ref, drive_ref, sums_ref, before_ref, tail, line,
+    normed_ref, masks_ref, branch_ref, in_ref, low_ref, keep_ref, part_ref, run_ref, sums_ref, before_ref, tail, line, ends,
 ):
     step = pl.program_id(0)
     width = in_ref.shape[1]
@@ -489,55 +489,37 @@
         low_ref[at] = conv_low
         not_start = masks[:, 3:4]
         rate, igate, keep, room, mult = gates_of(conv_low, gates_ref[...], params, not_start)
-        to = pl.ds(pl.multiple_of((step * row_dev + row) * span, 8), span)
-        put_lanes(keep_ref, to, keep * not_start)
-        put_lanes(drive_ref, to, mult * igate * conv_low.astype(wide))
-
-    @pl.when(step == pl.num_programs(0) - 1)
-    def _():
-        lanes = keep_ref.shape[0]
-
-        def one(i, state):
-            out = []
-            for j in range(lanes):
-                keep = keep_ref.at[j][pl.ds(i, rows, stride=span), :]
-                drive = drive_ref.at[j][pl.ds(i, rows, stride=span), :]
-                out.append((state[j][0] * keep, state[j][1] * keep + drive))
-            return tuple(out)
-
-        shape = (rows, 128)
-        state = tuple((jnp.ones(shape, wide), jnp.zeros(shape, wide)) for _ in range(lanes))
-        for half in range(2):
-            base = half * rows * span
-            state = lax.fori_loop(0, span, lambda i, s, base=base: one(base + i, s), state, unroll=8)
-        for j in range(lanes):
-            sums_ref[0, j] = state[j][0]
-            sums_ref[1, j] = state[j][1]
-
-
-def state_kernel(rows, span, keep_ref, drive_ref, start_ref, branch_ref, state_ref, mixed_ref):
-    lanes = keep_ref.shape[0]
-    width = mixed_ref.shape[1]
-
-    def one(i, state):
-        out = []
-        for j in range(lanes):
-            at = pl.ds(i, rows, stride=span)
-            value = state[j] * keep_ref.at[j][at, :] + drive_ref.at[j][at, :]
-            state_ref.at[j][at, :] = value
-            out.append(value)
-        return tuple(out)
-
-    state = tuple(start_ref[j] for j in range(lanes))
-    for half in range(2):
-        base = half * rows * span
-        state = lax.fori_loop(0, span, lambda i, s, base=base: one(base + i, s), state, unroll=8)
-
-    @pl.loop(0, 2 * rows)
-    def _(block):
-        at = pl.ds(pl.multiple_of(block * span, 16), span)
+        keep = keep * not_start
+        keep_ref[at] = keep
+        run, part = scan_rows(keep, mult * igate * conv_low.astype(wide), 1)
+
+        @pl.when(step * row_dev < rows)
+        def _(run=run, part=part, place=place, at=at):
+            run_ref[at] = run
+            part_ref[at] = part
+            ends[0, place] = run[span - 8 :]
+            ends[1, place] = part[span - 8 :]
+
+        @pl.when(step * row_dev >= rows)
+        def _(run=run, part=part, place=place, at=at):
+            part = part + run * ends[1, place][7:8]
+            run = run * ends[0, place][7:8]
+            run_ref[at] = run
+            part_ref[at] = part
+            sums_ref[0, place] = run[span - 8 :]
+            sums_ref[1, place] = part[span - 8 :]
+
+
+def state_kernel(rows, span, part_ref, run_ref, start_ref, branch_ref, state_ref, mixed_ref):
+    step = pl.program_id(0)
+    row_dev = part_ref.shape[0] // span
+    for row in range(row_dev):
+        at = slice(row * span, (row + 1) * span)
+        place = pl.ds(pl.multiple_of((lax.rem(step * row_dev + row, rows)) * 8, 8), 8)
+        state = part_ref[at] + run_ref[at] * start_ref[place][7:8]
+        state_ref[at] = state
         value, _ = gelu_pair(branch_ref[at])
-        mixed_ref[at] = (value * get_lanes(state_ref, at, width)).astype(low)
+        mixed_ref[at] = (value * state).astype(low)
 
 
 def mlp_kernel(x_ref, cot_ref, w_ref, down_ref, hidden_ref, grad_ref):
@@ -590,86 +572,75 @@
 
 
 def back_kernel(
-    rows, span, x_ref, w_ref, branch_ref, state_ref, keep_ref, grad_branch_ref, grad_state_ref, sum_ref
+    rows, span, x_ref, w_ref, branch_ref, state_ref, keep_ref, grad_branch_ref, part_ref, run_ref, sum_ref, ends
 ):
     step = pl.program_id(0)
-    lanes, _, _ = keep_ref.shape
-    width = w_ref.shape[0]
     count = x_ref.shape[0]
+    row_dev = count // span
     mixed = lax.dot_general(
         x_ref[...], w_ref[...], (((1,), (1,)), ((), ())), preferred_element_type=wide
     )
-    for row in range(count // span):
+    late = step * row_dev < rows
+    for row in range(row_dev):
         at = slice(row * span, (row + 1) * span)
-        to = pl.ds(pl.multiple_of(step * count + row * span, 8), span)
+        block = (pl.num_programs(0) - 1 - step) * row_dev + row
+        place = pl.ds(pl.multiple_of(lax.rem(block, rows) * 8, 8), 8)
         value, slope = gelu_pair(branch_ref[at])
-        state = get_lanes(state_ref, to, width)
-        grad_branch_ref[at] = (mixed[at] * state * slope).astype(low)
-        put_lanes(grad_state_ref, to, mixed[at] * value)
-
-    @pl.when(step == pl.num_programs(0) - 1)
+        grad_branch_ref[at] = (mixed[at] * state_ref[at] * slope).astype(low)
+        grad = mixed[at] * value
+        keep = keep_ref[at]
+        run, part = scan_rows(keep, keep * grad, -1)
+
+        @pl.when(late)
+        def _(run=run, part=part, grad=grad, place=place, at=at):
+            ends[0, place] = run[:8]
+            ends[1, place] = part[:8]
+            run_ref[at] = shifted(run, -1, 1.0)
+            part_ref[at] = grad + shifted(part, -1, 0.0)
+
+        @pl.when(jnp.logical_not(late))
+        def _(run=run, part=part, grad=grad, place=place, at=at):
+            next_run, next_part = ends[0, place][:1], ends[1, place][:1]
+            part = part + run * next_part
+            run = run * next_run
+            last = lax.broadcasted_iota(jnp.int32, run.shape, 0) == span - 1
+            run_ref[at] = jnp.where(last, next_run, shifted(run, -1, 1.0))
+            part_ref[at] = grad + jnp.where(last, next_part, shifted(part, -1, 0.0))
+            sum_ref[place] = part[:8]
+
+
+def adjoint_kernel(
+    rows, span, part_ref, run_ref, carry_ref, state_ref, start_ref, low_ref, gates_ref, params_ref,
+    masks_ref, in_ref, before_ref, grad_conv_ref, small_ref, gates_grad_ref, sums_ref, line, ends, tail,
+):
+    step = pl.program_id(0)
+    width = low_ref.shape[1]
+    row_dev = low_ref.shape[0] // span
+    params = params_ref[...]
+
+    @pl.when(step == 0)
     def _():
-        def one(i, state):
-            out = []
-            for j in range(lanes):
-                at = pl.ds(i, rows, stride=span)
-                out.append(keep_ref.at[j][at, :] * (grad_state_ref.at[j][at, :] + state[j]))
-            return tuple(out)
-
-        state = tuple(jnp.zeros((rows, 128), wide) for _ in range(lanes))
-        for half in (1, 0):
-            last = half * rows * span + span - 1
-            state = lax.fori_loop(0, span, lambda i, s, last=last: one(last - i, s), state, unroll=8)
-        for j in range(lanes):
-            sum_ref[j] = state[j]
-
-
-def adjoint_kernel(
-    rows, span, keep_ref, grad_ref, carry_ref, state_ref, start_ref, low_ref, gates_ref, params_ref,
-    masks_ref, in_ref, before_ref, grad_conv_ref, small_ref, adjoint, through, gates_grad_ref, sums_ref, line,
-):
-    lanes = keep_ref.shape[0]
-    width = low_ref.shape[1]
-
-    def one(i, state, before):
-        out = []
-        for j in range(lanes):
-            at = pl.ds(i, rows, stride=span)
-            value = grad_ref.at[j][at, :] + state[j]
-            adjoint.at[j][at, :] = value
-            through.at[j][at, :] = value * before(j)
-            out.append(keep_ref.at[j][at, :] * value)
-        return tuple(out)
-
-    state = tuple(carry_ref[j] for j in range(lanes))
-    for half in (1, 0):
-        first = half * rows * span
-
-        def inner(i, s, first=first):
-            at = first + span - 1 - i
-            return one(at, s, lambda j: state_ref.at[j][pl.ds(at - 1, rows, stride=span), :])
-
-        state = lax.fori_loop(0, span - 1, inner, state, unroll=8)
-        if half:
-            state = one(first, state, lambda j: state_ref.at[j][pl.ds(span - 1, rows, stride=span), :])
-        else:
-            state = one(first, state, lambda j: start_ref[j])
-
-    params = params_ref[...]
-    gates_grad_ref[...] = jnp.zeros(gates_grad_ref.shape, wide)
-    sums_ref[...] = jnp.zeros(sums_ref.shape, wide)
-
-    @pl.loop(0, 2 * rows)
-    def _(block):
-        at = pl.ds(pl.multiple_of(block * span, 16), span)
+        gates_grad_ref[...] = jnp.zeros(gates_grad_ref.shape, wide)
+        sums_ref[...] = jnp.zeros(sums_ref.shape, wide)
+        ends[...] = start_ref[...]
+        tail[...] = before_ref[...]
+
+    for row in range(row_dev):
+        at = slice(row * span, (row + 1) * span)
+        place = pl.ds(pl.multiple_of((lax.rem(step * row_dev + row, rows)) * 8, 8), 8)
         conv_low = low_ref[at]
         conv_value = conv_low.astype(wide)
-        not_start = masks_ref[at][:, 3:4]
+        masks = masks_ref[at]
+        not_start = masks[:, 3:4]
         rate, igate, keep, room, mult = gates_of(conv_low, gates_ref[...], params, not_start)
-        adj = get_lanes(adjoint, at, width)
-        thr = get_lanes(through, at, width)
+        adj = part_ref[at] + run_ref[at] * carry_ref[place][:1]
+        state = state_ref[at]
+        line[:8] = ends[place]
+        line[8:] = state
+        ends[place] = state[span - 8 :]
+        through = adj * line[7 : 7 + span]
         spread = jnp.where(room > floor_value, adj * igate * conv_value * keep * keep / mult, 0.0)
-        grad_log = not_start * (thr * keep - spread)
+        grad_log = not_start * (through * keep - spread)
         grad_rate = (grad_log * params[7:8] * rate * (1.0 - rate)).astype(low)
         scaled = adj * mult
         grad_igate = (scaled * conv_value * igate * (1.0 - igate)).astype(low)
@@ -682,18 +653,11 @@
         gates_grad_ref[...] += lax.dot_general(
             conv_low, both, (((0,), (0,)), ((), ())), preferred_element_type=wide
         )
-        masks = masks_ref[at]
         grad_conv = grad_conv.astype(wide)
         conv_in = in_ref[at].astype(wide)
-        within = lax.rem(block, rows)
-        line[:8] = before_ref[pl.ds(pl.multiple_of(within * 8, 8), 8)]
-
-        @pl.when(block >= rows)
-        def _():
-            last = pl.ds(pl.multiple_of(within * span + span - 16, 16), 16)
-            line[:8] = in_ref[last].astype(wide)[8:]
-
+        line[:8] = tail[place]
         line[8:] = conv_in
+        tail[place] = conv_in[span - 8 :]
         values = [grad_conv * conv_in]
         for by in range(1, 4):
             values.append(grad_conv * line[8 - by : 8 - by + span] * masks[:, by - 1 : by])
@@ -701,16 +665,18 @@
         for i, value in enumerate(values):
             sums_ref[i : i + 1] += jnp.sum(value, axis=0, keepdims=True)
 
-    block = small_ref.shape[1] // 2 - 64
-    for head in range(width // block):
-        at = slice(head * block, (head + 1) * block)
-        small_ref[at, :block] = gates_grad_ref[at, at].astype(low)
-        then = slice(width + head * block, width + (head + 1) * block)
-        small_ref[at, block : 2 * block] = gates_grad_ref[at, then].astype(low)
-    small_ref[:, 2 * block :] = sums_ref[...].T[:width].astype(low)
-
-
-def conv_back_kernel(rows, span, grad_ref, halo_ref, masks_ref, halo_masks_ref, params_ref, one_ref, line):
+    @pl.when(step == pl.num_programs(0) - 1)
+    def _():
+        block = small_ref.shape[1] // 2 - 64
+        for head in range(width // block):
+            at = slice(head * block, (head + 1) * block)
+            small_ref[at, :block] = gates_grad_ref[at, at].astype(low)
+            then = slice(width + head * block, width + (head + 1) * block)
+            small_ref[at, block : 2 * block] = gates_grad_ref[at, then].astype(low)
+        small_ref[:, 2 * block :] = sums_ref[...].T[:width].astype(low)
+
+
+def conv_back_kernel(rows, span, grad_ref, halo_ref, masks_ref, halo_masks_ref, branch_ref, params_ref, one_ref, line):
     params = params_ref[...]
 
     def work(block, grad_next, masks_next):
@@ -722,7 +688,9 @@
             line[:span] = own * masks[:, by - 1 : by]
             line[span:] = grad_next * masks_next[:, by - 1 : by]
             total = total + params[by : by + 1] * line[by : by + span]
-        one_ref[at] = total.astype(low)
+        width = branch_ref.shape[1]
+        one_ref[at, :width] = branch_ref[at]
+        one_ref[at, width:] = total.astype(low)
 
     @pl.loop(0, rows)
     def _(block):
@@ -739,8 +707,11 @@
     return pl.BlockSpec(array.shape, lambda *i, n=len(array.shape): (0,) * n)
 
 
-def token_block(array, count):
-    return pl.BlockSpec((count,) + array.shape[1:], lambda i, n=len(array.shape): (i,) + (0,) * (n - 1))
+def token_block(array, count, steps, backwards):
+    def index(i):
+        return (steps - 1 - i if backwards else i,) + (0,) * (len(array.shape) - 1)
+
+    return pl.BlockSpec((count,) + array.shape[1:], index)
 
 
 def half_of(core, x, count, width):
@@ -798,10 +769,10 @@
     )
 
 
-def rows_kernel(turned, core_ref, x_ref, grad_ref, sent_ref, kept_ref):
+def rows_kernel(core_ref, x_ref, grad_ref, sent_ref, kept_ref):
     count = kept_ref.shape[1]
     total = lax.dot_general(
-        x_ref[...], grad_ref[...], (((int(turned),), (0,)), ((), ())), preferred_element_type=wide
+        x_ref[...], grad_ref[...], (((0,), (0,)), ((), ())), preferred_element_type=wide
     )
     planes = sent_ref.shape[0]
     first = lax.rem(pl.program_id(0), core_ref[1]) * planes
@@ -815,23 +786,22 @@
             kept_ref[0] = part
 
 
-def rows_call(z, z_count, k_count, x, grad, turned):
-    tokens, features = x.shape[::-1] if turned else x.shape
+def rows_call(z, z_count, k_count, x, grad):
+    tokens, features = x.shape
     count = features // (z_count * k_count)
     planes = max(2, 128 // count)
     width = grad.shape[1]
     per = z_count // planes
     sent = jax.ShapeDtypeStruct((z_count, k_count, count, width), low)
     kept = jax.ShapeDtypeStruct((k_count, count, width), wide)
-    block = (planes * count, tokens) if turned else (tokens, planes * count)
     return pl.pallas_call(
-        functools.partial(rows_kernel, turned),
+        rows_kernel,
         out_shape=[sent, kept],
         grid_spec=pltpu.PrefetchScalarGridSpec(
             num_scalar_prefetch=1,
             grid=(k_count * per,),
             in_specs=[
-                pl.BlockSpec(block, lambda i, ref: (i, 0) if turned else (0, i)),
+                pl.BlockSpec((tokens, planes * count), lambda i, ref: (0, i)),
                 pl.BlockSpec(grad.shape, lambda i, ref: (0, 0)),
             ],
             out_specs=[
@@ -842,23 +812,6 @@
         cost_estimate=pl.CostEstimate(flops=0, bytes_accessed=0, transcendentals=0),
         compiler_params=pltpu.CompilerParams(vmem_limit_bytes=56 * 2**20),
     )(jnp.stack([z, jnp.int32(per)]).astype(jnp.int32), x, grad)
-
-
-def turn_kernel(x_ref, out_ref):
-    out_ref[...] = x_ref[...].T
-
-
-def turn(x):
-    block = 256
-    return pl.pallas_call(
-        turn_kernel,
-        out_shape=jax.ShapeDtypeStruct(x.shape[::-1], x.dtype),
-        grid=(x.shape[1] // block,),
-        in_specs=[pl.BlockSpec((x.shape[0], block), lambda i: (0, i))],
-        out_specs=pl.BlockSpec((block, x.shape[0]), lambda i: (i, 0)),
-        cost_estimate=pl.CostEstimate(flops=0, bytes_accessed=0, transcendentals=0),
-        compiler_params=pltpu.CompilerParams(vmem_limit_bytes=48 * 2**20),
-    )(x)
 
 
 def down_kernel(core_ref, hidden_ref, cot_ref, sent_ref, kept_ref):
@@ -903,9 +856,9 @@
     )(z.reshape(1).astype(jnp.int32), hidden, cot)
 
 
-def kernel_call(kernel, steps, inputs, outputs, scratch=()):
+def kernel_call(kernel, steps, inputs, outputs, scratch=(), backwards=False):
     def spec(array, count):
-        return whole_block(array) if count is None else token_block(array, count)
+        return whole_block(array) if count is None else token_block(array, count, steps, backwards)
 
     return pl.pallas_call(
         kernel,
@@ -978,18 +931,58 @@
         ],
         axis=3,
     )
-    rec_cols = at.exchange_plane(jnp.moveaxis(rec_cols, 0, 2))
-    out_part = at.gather_z(out_proj)
-    rec_cols, out_part = together(rec_cols, out_part)
+    rec_pairs = at.exchange_core(jnp.moveaxis(rec_cols, 0, 2))
+
+    seg_code = (segment_ids % 64).astype(low)
+    pairs = [(i, i + 1) for i in range(at.s_count - 1)]
+    before = lax.ppermute(seg_code[:, span - reach :], "seq", pairs)
+    tokens = tokens.reshape(tok, width_d)
+    tail = tokens.reshape(row_dev, span, width_d)[:, span - 8 :].reshape(row_dev * 8, width_d)
+    tail = at.to_z(tail, 1)
+
+    small = jnp.pad(small, (0, -small.shape[0] % 128)).reshape(-1, 128)
+    small_rows = small.shape[0]
+    small = jnp.pad(small, ((0, w_own - small_rows), (0, 0)))
+    out_rows = jnp.concatenate([out_proj, rate_weight, igate_weight, small], axis=1)
+    out_rows, before, tail = together(out_rows, before, tail)
+    out_part = at.gather_z(out_rows)
+
+    rec_cols = at.exchange_dp(rec_pairs)
+    order = None
+    if 2 * d_own % 128 == 0:
+        order = [k * z_count + z for z in range(z_count) for k in range(k_count)]
+    ext_code = jnp.concatenate([before, seg_code], axis=1)
+    position = lax.broadcasted_iota(jnp.int32, (row_dev, span), 1)
+    masks = [
+        (ext_code[:, reach - by : reach - by + span] == seg_code) & ((at.s > 0) | (position >= by))
+        for by in range(1, taps)
+    ]
+    masks = jnp.stack(masks + [masks[0]] * (9 - taps), axis=-1).astype(low).reshape(tok, 8)
+    beside = jnp.concatenate([tokens, jnp.pad(masks, ((0, 0), (0, 120)))], axis=1)
+    beside, rec_cols = together(beside, rec_cols)
     w1 = at.gather_z(rec_cols.reshape(group * d_own, 2 * w_slot))
-
-    gate_rows = jnp.concatenate([rate_weight, igate_weight], axis=1)
-    small = jnp.pad(small, (0, -small.shape[0] % (2 * BS))).reshape(-1, 2 * BS)
-    gate_rows = at.gather_seq_small(jnp.concatenate([gate_rows, small]))
-    small = gate_rows[:, w_own:].reshape(at.s_count, -1)
+    beside_near = at.gather_near(beside)
+    tail = jnp.where(at.c == 1, tail, at.to_core(tail))
+    inputs = tokens.astype(wide)
+    s1 = lax.rsqrt(jnp.mean(inputs * inputs, axis=-1, keepdims=True) + eps_value)
+    mlp_shape = jax.ShapeDtypeStruct((k_count, 2, d_own, 2 * f_slot), low)
+    cut = functools.partial(cut_kernel, k_count, z_count)
+    mlp_pairs = at.exchange_core(in_vmem(cut, (mlp_gate, mlp_up), mlp_shape))
+    beside_near, tail, mlp_pairs, out_part = together(beside_near, tail, mlp_pairs, out_part)
+    tail = at.gather_rows(tail)
+
+    out_split = out_part.reshape(2, half_z, w_own, -1)
+
+    def of_slot(columns):
+        part = out_split[..., columns]
+        keep = lax.dynamic_index_in_dim(part, at.c, 0, False)
+        got = at.to_core(lax.dynamic_index_in_dim(part, 1 - at.c, 0, False))
+        return jnp.swapaxes(at.by_core(keep, got), 0, 1).reshape(w_slot, -1)
+
+    gate_rows = of_slot(slice(width_d, width_d + 2 * BS))
+    small = out_part.reshape(z_count, w_own, -1)[:, :small_rows, width_d + 2 * BS :].reshape(z_count, -1)
+    small = jnp.swapaxes(at.by_core(small, at.to_core(small)), 0, 1).reshape(at.s_count, -1)
     gains = at.gather_dp_small(small[:, : 2 * d_own]).reshape(k_count * at.s_count, -1)
-    gain_one = gains[:, :d_own].reshape(1, width_d).astype(wide)
-    gain_two = gains[:, d_own:].reshape(1, width_d).astype(wide)
     mine = lax.dynamic_slice_in_dim(small[:, 2 * d_own :], at.c * z_count, z_count, 0)
     mine = mine[:, : (taps + 4) * w_own].reshape(z_count, taps + 4, w_own).astype(wide)
     mine = jnp.swapaxes(mine, 0, 1).reshape(taps + 4, w_slot)
@@ -998,8 +991,7 @@
     log_slope = -rate_scale * jax.nn.softplus(-decay)
     decay_slope = rate_scale * jax.nn.sigmoid(-decay)
     params = jnp.concatenate([w_conv, b_conv, b_rate, b_igate, log_slope] + [decay_slope] * 8)
-    gate_rows = lax.dynamic_slice_in_dim(gate_rows[:, :w_own], at.c * z_count, z_count, 0)
-    gate_rows = gate_rows.reshape(w_slot, 2 * BS)
+    beside_near, tail, gains, gate_rows = together(beside_near, tail, gains, gate_rows)
     heads = w_slot // BS
 
     def block_diagonal(columns):
@@ -1009,33 +1001,11 @@
 
     w_gates = jnp.concatenate([block_diagonal(gate_rows[:, :BS]), block_diagonal(gate_rows[:, BS:])], axis=1)
 
-    seg_code = (segment_ids % 64).astype(low)
-    pairs = [(i, i + 1) for i in range(at.s_count - 1)]
-    ext_code = jnp.concatenate([lax.ppermute(seg_code[:, span - reach :], "seq", pairs), seg_code], axis=1)
-    position = lax.broadcasted_iota(jnp.int32, (row_dev, span), 1)
-    masks = [
-        (ext_code[:, reach - by : reach - by + span] == seg_code) & ((at.s > 0) | (position >= by))
-        for by in range(1, taps)
-    ]
-    masks = jnp.stack(masks + [masks[0]] * (9 - taps), axis=-1).astype(low).reshape(tok, 8)
-    tokens = tokens.reshape(tok, width_d)
-    beside = jnp.concatenate([tokens, jnp.pad(masks, ((0, 0), (0, 120)))], axis=1)
-    tail = tokens.reshape(row_dev, span, width_d)[:, span - 8 :].reshape(row_dev * 8, width_d)
-    tail = at.gather_tail(tail)
-    beside, tail, params, gate_rows, gain_one, gain_two, mlp_gate = together(
-        beside, tail, params, gate_rows, gain_one, gain_two, mlp_gate
-    )
-    order = None
-    if 2 * d_own % 128 == 0:
-        order = [k * z_count + z for z in range(z_count) for k in range(k_count)]
-    beside_near = at.gather_near(beside)
-    inputs = tokens.astype(wide)
-    s1 = lax.rsqrt(jnp.mean(inputs * inputs, axis=-1, keepdims=True) + eps_value)
-    mlp_shape = jax.ShapeDtypeStruct((k_count, 2, d_own, 2 * f_slot), low)
-    cut = functools.partial(cut_kernel, k_count, z_count)
-    mlp_pairs = at.exchange_core(in_vmem(cut, (mlp_gate, mlp_up), mlp_shape))
-    beside_near, mlp_pairs, w_gates = together(beside_near, mlp_pairs, w_gates)
-    beside_far = at.gather_far(beside_near)
+    beside_far, mlp_pairs, w_gates, params = together(
+        at.gather_far(beside_near), mlp_pairs, w_gates, params
+    )
+    gain_one = gains[:, :d_own].reshape(1, width_d).astype(wide)
+    gain_two = gains[:, d_own:].reshape(1, width_d).astype(wide)
     mlp_cols = at.exchange_dp(mlp_pairs)
     cot = cotangent.reshape(tok, width_d)
     tokens_all, mlp_cols, cot = together(at.gather_end(beside_far), mlp_cols, cot)
@@ -1050,44 +1020,48 @@
     steps = tok_all // tok
     cot_near = at.gather_near(cot)
     flat32, flat16 = shape((tok_all, w_slot), wide), shape((tok_all, w_slot), low)
-    lanes = lane_shape(tok_all, w_slot)
-    ends = shape((lanes.shape[0], rows, 128), wide)
-    n1_all, masks, branch_pre, conv_in, conv_low, keep_eff, drive, summary, conv_before = kernel_call(
+    ends = shape((rows * 8, w_slot), wide)
+
+    def by_row(array):
+        return jnp.repeat(array, 8, axis=0)
+
+    n1_all, masks, branch_pre, conv_in, conv_low, keep_eff, part, run, summary, conv_before = kernel_call(
         functools.partial(conv_kernel, rows, span, order),
         steps,
         [(tokens_all, tok), (w1 if order else by_feature(w1), None), (tail, None), (gain_one, None), (params, None), (w_gates, None)],
-        [(shape((tok_all, width_d), low), tok), (shape((tok_all, 8), wide), tok), (flat32, tok), (flat16, tok), (flat16, tok), (lanes, None), (lanes, None), (shape((2,) + ends.shape, wide), None), (shape((rows * 8, w_slot), wide), None)],
-        [pltpu.VMEM((rows * 8, w_slot), wide), pltpu.VMEM((span + 8, w_slot), wide)],
-    )
+        [(shape((tok_all, width_d), low), tok), (shape((tok_all, 8), wide), tok), (flat32, tok), (flat16, tok), (flat16, tok)]
+        + [(flat32, tok)] * 3
+        + [(shape((2,) + ends.shape, wide), None), (ends, None)],
+        [
+            pltpu.VMEM(ends.shape, wide),
+            pltpu.VMEM((span + 8, w_slot), wide),
+            pltpu.VMEM((2,) + ends.shape, wide),
+        ],
+    )
+    summary = summary.reshape(2, rows, 8, w_slot)[:, :, 7]
     w_down = at.gather_z(mlp_down)
-    summary, cot_near, out_part, w1 = together(summary, cot_near, out_part, w1)
+    summary, cot_near, out_split, w1 = together(summary, cot_near, out_split, w1)
     w1 = by_feature(w1)
-    out_part = out_part.reshape(2, half_z * w_own, width_d)
-    out_keep = lax.dynamic_index_in_dim(out_part, at.c, 0, False)
-    out_got = at.to_core(lax.dynamic_index_in_dim(out_part, 1 - at.c, 0, False))
-    w_out = at.by_core(
-        out_keep.reshape(half_z, w_own, width_d), out_got.reshape(half_z, w_own, width_d)
-    )
-    w_out = jnp.swapaxes(w_out, 0, 1).reshape(w_slot, width_d)
+    w_out = of_slot(slice(0, width_d))
     cot_far = at.gather_far(cot_near)
     before = [at.to_z(summary, by) for by in range(1, z_count)]
-    state_in = jnp.zeros(ends.shape, wide)
-    for part in reversed(before):
-        state_in = part[1] + part[0] * state_in
+    state_in = jnp.zeros((rows, w_slot), wide)
+    for one in reversed(before):
+        state_in = one[1] + one[0] * state_in
+    state_in = by_row(state_in)
     state, mixed = kernel_call(
         functools.partial(state_kernel, rows, span),
-        1,
-        [(keep_eff, None), (drive, None), (state_in, None), (branch_pre, None)],
-        [(lanes, None), (flat16, None)],
+        steps,
+        [(part, tok), (run, tok), (state_in, None), (branch_pre, tok)],
+        [(flat32, tok), (flat16, tok)],
     )
     masks_after = at.to_z(masks.reshape(2, rows, span, 8)[0, :, :16], -1).reshape(rows * 16, 8)
-    mixed, cot_far, w2_parts[0], masks_after = together(mixed, cot_far, w2_parts[0], masks_after)
+    mixed, cot_far, w2_parts[0], masks_after, w1 = together(mixed, cot_far, w2_parts[0], masks_after, w1)
 
     chip_one = at.chip_product(mixed, w_out, dot_nn, exact=True)
     near_sum, cot_far = together(at.near_plane(chip_one, exact=True), cot_far)
-    n1_turned = turn(n1_all)
     cot_all = at.gather_end(cot_far)
-    resid, cot_all, n1_turned = together(inputs + at.far_plane(near_sum), cot_all, n1_turned)
+    resid, cot_all = together(inputs + at.far_plane(near_sum), cot_all)
     resid, w2_parts[1] = together(resid, w2_parts[1])
     w2 = jnp.concatenate([by_feature(part) for part in w2_parts])
 
@@ -1101,29 +1075,31 @@
         [(n2_all, tok), (cot_all, tok), (w2, None), (w_down, None)],
         [(shape((tok_all, f_slot), low), tok), (shape((tok_all, 2 * f_slot), low), tok)],
     )
-    def rows_apart(x, grad, turned=False):
-        sent, kept = rows_call(at.z, z_count, k_count, x, grad, turned)
+    def rows_apart(x, grad):
+        sent, kept = rows_call(at.z, z_count, k_count, x, grad)
         return sent.reshape(-1, sent.shape[-1]), kept.reshape(-1, kept.shape[-1])
 
-    near_two, _ = at.near_product(grad_two, w2)
+    _, got_two = at.chip_send(grad_two, w2, 1)
+    near_two = at.near_parts(at.chip_own(grad_two, w2, got_two, 1))
     chip_two, grad_two = together(near_two[0], grad_two)
     w2_part = rows_apart(n2_all, grad_two)
     near_two, w2_part, hidden = together(near_two, w2_part, hidden)
     w2_sum = at.scatter_z(w2_part)
     grad_n2 = at.far_product(near_two)
-    down_sent, down_kept = down_call(at.z, z_count, hidden, cot_all)
-    down_part = down_sent.reshape(-1, width_d), down_kept
-    grad_n2, down_part = together(grad_n2, down_part)
-    down_sum = at.scatter_z(down_part)
+    other_three, got_three = at.chip_send(hidden, w_down, 0)
+    grad_n2, other_three, hidden = together(grad_n2, other_three, hidden)
     scaled_two = gain_two * grad_n2
     cot_f = cot.astype(wide)
     mean_two = jnp.mean(scaled_two * resid, axis=-1, keepdims=True)
     grad_resid = cot_f + s2 * scaled_two - resid * (s2 * s2 * s2) * mean_two
     grad_recur = grad_resid.astype(low)
     grad_recur, hidden = together(grad_recur, hidden)
-    chip_three, _ = at.chip_parts(hidden, w_down, 0)
-    gr_near, chip_three = together(at.gather_near(grad_recur), chip_three)
-    gr_all = at.gather_end(at.gather_far(gr_near))
+    chip_three = at.chip_own(hidden, w_down, got_three, 0)
+    down_sent, down_kept = down_call(at.z, z_count, hidden, cot_all)
+    down_part = down_sent.reshape(-1, width_d), down_kept
+    gr_near, chip_three, down_part = together(at.gather_near(grad_recur), chip_three, down_part)
+    down_sum = at.scatter_z(down_part)
+    gr_all, chip_three = together(at.gather_end(at.gather_far(gr_near)), chip_three)
 
     def summed(pair):
         return pair[0].astype(wide) + pair[1].astype(wide)
@@ -1132,13 +1108,16 @@
         return at.exchange_plane(array.reshape(k_count, 2, d_own, columns))
 
 
-    grad_branch, grad_state, back = kernel_call(
+    grad_branch, back_part, back_run, back = kernel_call(
         functools.partial(back_kernel, rows, span),
         steps,
-        [(gr_all, tok), (w_out, None), (branch_pre, tok), (state, None), (keep_eff, None)],
-        [(flat16, tok), (lanes, None), (ends, None)],
-    )
-    back, mixed, chip_three, w2_sum = together(back, mixed, chip_three, w2_sum)
+        [(gr_all, tok), (w_out, None), (branch_pre, tok), (state, tok), (keep_eff, tok)],
+        [(flat16, tok), (flat32, tok), (flat32, tok), (ends, None)],
+        [pltpu.VMEM((2,) + ends.shape, wide)],
+        backwards=True,
+    )
+    back = back.reshape(rows, 8, w_slot)[:, 0]
+    back, mixed, near_three = together(back, mixed, at.near_parts(chip_three))
 
     def by_owner(array):
         split = array.reshape(half_z, 2, w_own, -1)
@@ -1149,57 +1128,68 @@
     own = jnp.stack([summary[0], back])
     after = [at.to_z(own, -by) for by in range(1, z_count)]
     grad_out = dot_tn(mixed, gr_all)
-    after, grad_out = together(after, grad_out)
-    carry_in = jnp.zeros(ends.shape, wide)
+    after, grad_out, w2_sum = together(after, grad_out, w2_sum)
+    carry_in = jnp.zeros((rows, w_slot), wide)
     for part in reversed(after):
         carry_in = part[1] + part[0] * carry_in
-    near_three = at.near_parts(chip_three)
     mlp_pairs = at.exchange_core(summed(w2_sum).reshape(k_count, 2, d_own, 2 * f_slot))
-    carry_in, mlp_pairs, near_three = together(carry_in, mlp_pairs, near_three)
+    carry_in, mlp_pairs = together(carry_in, mlp_pairs)
     mlp_back = at.exchange_dp(mlp_pairs)
     grad_conv, rec_small = kernel_call(
         functools.partial(adjoint_kernel, rows, span),
-        1,
+        steps,
         [
-            (array, None)
-            for array in (keep_eff, grad_state, carry_in, state, state_in, conv_low, w_gates, params, masks, conv_in, conv_before)
+            (back_part, tok),
+            (back_run, tok),
+            (by_row(carry_in), None),
+            (state, tok),
+            (state_in, None),
+            (conv_low, tok),
+            (w_gates, None),
+            (params, None),
+            (masks, tok),
+            (conv_in, tok),
+            (conv_before, None),
         ],
-        [(flat16, None), (shape((w_slot, 2 * BS + 128), low), None)],
+        [(flat16, tok), (shape((w_slot, 2 * BS + 128), low), None)],
         [
-            pltpu.VMEM(lanes.shape, wide),
-            pltpu.VMEM(lanes.shape, wide),
             pltpu.VMEM((w_slot, 2 * w_slot), wide),
             pltpu.VMEM((128, w_slot), wide),
             pltpu.VMEM((span + 8, w_slot), wide),
+            pltpu.VMEM(ends.shape, wide),
+            pltpu.VMEM(ends.shape, wide),
         ],
     )
-    grad_conv, near_three, mlp_back, down_sum = together(grad_conv, near_three, mlp_back, down_sum)
+    grad_conv, near_three, mlp_back = together(grad_conv, near_three, mlp_back)
     block_out = (resid + at.far_product(near_three)).astype(low)
     head = at.to_z(grad_conv.reshape(2, rows, span, w_slot)[0, :, :16], -1).reshape(rows * 16, w_slot)
     rec_part = at.own_apart(by_owner(jnp.concatenate([grad_out.astype(low), rec_small], axis=1)), 0)
     head, rec_part = together(head, rec_part)
     rec_sum = at.scatter_z(rec_part)
-    (grad_conv_in,) = kernel_call(
+    (grad_one,) = kernel_call(
         functools.partial(conv_back_kernel, rows, span),
         1,
-        [(array, None) for array in (grad_conv, head, masks, masks_after, params)],
-        [(flat16, None)],
+        [(array, None) for array in (grad_conv, head, masks, masks_after, grad_branch, params)],
+        [(shape((tok_all, 2 * w_slot), low), None)],
         [pltpu.VMEM((span + 8, w_slot), wide)],
     )
-    grad_one = jnp.concatenate([grad_branch, grad_conv_in], axis=1)
-
-    def product_between(other, left):
-        other, then = together(other, left)
-        parts = rows_apart(n1_turned, then, True)
-        return together(left, parts)
-
-    near_one, w1_part = at.near_product(grad_one, w1, product_between)
-    if w1_part is None:
-        w1_part = rows_apart(n1_turned, grad_one, True)
+
+    grad_one, block_out = together(grad_one, block_out)
+    other_one, got_one = at.chip_send(grad_one, w1, 1)
+    other_one, then = together(other_one, grad_one)
+    w1_part = rows_apart(n1_all, then)
+    then, w1_part = together(then, w1_part)
+    near_one = at.near_parts(at.chip_own(then, w1, got_one, 1))
     w1_sum = at.scatter_z(w1_part)
+    mlp_whole = jax.ShapeDtypeStruct(mlp_gate.shape, wide)
+    join = functools.partial(join_kernel, k_count, z_count)
+    grad_gate_w, grad_up_w = in_vmem(join, (mlp_back,), (mlp_whole, mlp_whole))
+    near_one, grad_gate_w, grad_up_w, down_sum = together(near_one, grad_gate_w, grad_up_w, down_sum)
     grad_n1 = at.far_product(near_one)
-    w1_sum, grad_n1, block_out, rec_sum = together(w1_sum, grad_n1, block_out, rec_sum)
-    rec_back = at.exchange_plane(summed(w1_sum).reshape(k_count, 2, d_own, 2 * w_slot))
+    w1_sum, grad_n1, rec_sum = together(w1_sum, grad_n1, rec_sum)
+    rec_pairs = at.exchange_core(summed(w1_sum).reshape(k_count, 2, d_own, 2 * w_slot))
+    rec_pairs, grad_n1, rec_sum = together(rec_pairs, grad_n1, rec_sum)
+    rec_back = at.exchange_dp(rec_pairs)
     scaled_one = gain_one * grad_n1
     mean_one = jnp.mean(scaled_one * inputs, axis=-1, keepdims=True)
     grad_tokens = grad_resid + s1 * scaled_one - inputs * (s1 * s1 * s1) * mean_one
@@ -1212,9 +1202,6 @@
     grad_igate_w = rec_rows[:, width_d + BS : width_d + 2 * BS]
     grad_small = rec_rows[:, width_d + 2 * BS : width_d + 2 * BS + taps + 4].T
     grad_down = summed(down_sum)
-    mlp_whole = jax.ShapeDtypeStruct(mlp_gate.shape, wide)
-    join = functools.partial(join_kernel, k_count, z_count)
-    grad_gate_w, grad_up_w = in_vmem(join, (mlp_back,), (mlp_whole, mlp_whole))
     rec_back = jnp.moveaxis(rec_back, 2, 0)
     grad_branch_w = rec_back[..., :w_slot].reshape(d_own, width_r)
     grad_input_w = rec_back[..., w_slot:].reshape(d_own, width_r)

time: 787 us -> 745 us (0.947)
  Pallas kernels: 266 us -> 232 us
  starting transfers between devices: 86.5 us -> 76.9 us
  other arithmetic: 102 us -> 93.1 us
    pallas_call x6, Pallas kernels: 139 us -> 115 us  [kernel_call(): pl.pallas_call(kernel, out_shape=[array for array, _ in outputs], grid=(s...]
    ppermute x48, waiting for transfers between devices: 181 us -> 205 us  [to_k(): lax.ppermute(array, 'dp', [(i, i ^ flip) for i in range(self.k_count)])]
    ppermute x4 -> x1, waiting for transfers between devices: 16.7 us -> 0.01 us  [per_device(): before = lax.ppermute(seg_code[:, span - reach:], 'seq', pairs)]
    pallas_call x3 -> x2, Pallas kernels: 44 us -> 33.9 us  [rows_call(): pl.pallas_call(rows_kernel, out_shape=[sent, kept], grid_spec=pltpu.Prefe...]
    ppermute x32 -> x34, waiting for transfers between devices: 18.7 us -> 17.4 us  [to_core(): return lax.ppermute(array, 'seq', [(i, i ^ 1) for i in range(self.s_count)])]
    unnamed x142 -> x175, local copies, waits for them, and re-layouts: 27.4 us -> 27.1 us
  transfers between devices with their start and end apart: 102 -> 101, of which waited for: 43 -> 47; matrix products, arithmetic and copies ran while one was open for 18% -> 18% of each run, Pallas kernels for 28% -> 25%
where the time goes in v3:
time: 745 us; the launch traced here: 735 us
  Pallas kernels  232 us (31%)
  waiting for transfers between devices  231 us (31%)
  other arithmetic  93.1 us (12%)
  starting transfers between devices  76.9 us (10%)
  local copies, waits for them, and re-layouts  70.7 us (9%)
  between operations  16.3 us (2%)
  matrix products  15.3 us (2%)
    ppermute x48, waiting for transfers between devices, to_k(): lax.ppermute(array, 'dp', [(i, i ^ flip) for i in range(self.k_count)])  205 us
    pallas_call x6, Pallas kernels, kernel_call(): pl.pallas_call(kernel, out_shape=[array for array, _ in outputs], grid=(s...  115 us
    pallas_call x6, Pallas kernels, half_call(): pl.pallas_call(kernel, out_shape=[array for array, _, _ in outputs], grid...  59.4 us
    ppermute x48, starting transfers between devices, to_k(): lax.ppermute(array, 'dp', [(i, i ^ flip) for i in range(self.k_count)])  49 us
    pallas_call x2, Pallas kernels, rows_call(): pl.pallas_call(rows_kernel, out_shape=[sent, kept], grid_spec=pltpu.Prefe...  33.9 us
    unnamed x175, local copies, waits for them, and re-layouts  27.1 us
    ppermute x9, starting transfers between devices, to_z(): return lax.ppermute(array, 'seq', pairs)  17.7 us
    ppermute x34, waiting for transfers between devices, to_core(): return lax.ppermute(array, 'seq', [(i, i ^ 1) for i in range(self.s_count)])  17.4 us
  transfers between devices with their start and end apart: 101, of which 47 were waited for; matrix products, arithmetic and copies ran while one was open for 18% of the time, Pallas kernels for 25%

profile of v3, /device:TPU:0, one launch (start us, length us, event | category | flops | bytes accessed | tf_op | source)
XLA Modules:
  0.0 735.4 jit_solution(13423283244038157159)
XLA Ops:
  11.2 4.5 collective-permute-start.1
  18.7 3.2 maximum_bitcast_fusion.1
  35.6 3.8 collective-permute-done.4
  49.2 16.9 %collective-permute-done.7.refs_2_ = bf16[256,2176]{1,0:T(8,128)(2,1)} collective-permute-done((bf16[256,2176]{1,0:T(8,128)(2,1)S(1)}, bf16[256,2176]{1,0:T(8,128)(2,1)}, u32[]{:S(2)}, u32[]{:S(2)}) %collective-permute-start.7) | collective-permute-done | bytes 1114144 | tf_op jit(solution)/shard_map/ppermute | solution.py:133
  77.6 2.8 collective-permute-done.11
  88.1 9.7 %collective-permute-done.17.refs_4_ = bf16[128,2176]{1,0:T(8,128)(2,1)S(1)} collective-permute-done((bf16[128,2176]{1,0:T(8,128)(2,1)}, bf16[128,2176]{1,0:T(8,128)(2,1)S(1)}, u32[]{:S(2)}, u32[]{:S(2)}) %collective-permute-start.17) | collective-permute-done | bytes 557088 | tf_op jit(solution)/shard_map/ppermute | solution.py:133
  104.0 8.1 %collective-permute-done.25 = bf16[2,64,1536]{2,1,0:T(8,128)(2,1)S(1)} collective-permute-done((bf16[2,64,1536]{2,1,0:T(8,128)(2,1)S(1)}, bf16[2,64,1536]{2,1,0:T(8,128)(2,1)S(1)}, u32[]{:S(2)}, u32[]{:S(2)}) %collective-permute-start.25) | collective-permute-done | bytes 393248 | tf_op jit(solution)/shard_map/ppermute | solution.py:133
  112.1 5.2 collective-permute-done.24
  120.1 2.9 shard_map.306.x_ref
  123.0 3.5 copy-done.2
  131.2 32.9 %shard_map.307 = (bf16[2048,2048]{1,0:T(8,128)(2,1)}, f32[2048,8]{1,0:T(8,128)}, f32[2048,320]{1,0:T(8,128)}, bf16[2048,320]{1,0:T(8,128)(2,1)}, bf16[2048,320]{...) custom-call(bf16[2048,2176]{1,0:T(8,128)(2,1)} %copy-done.2, ...), custom_call_target="tpu_custom_call" | custom-call | tf_op jit(solution)/shard_map/pallas_call | solution.py:863
  165.1 3.0 collective-permute-start.30
  179.1 8.3 %shard_map.308 = (f32[2048,320]{1,0:T(8,128)}, bf16[2048,320]{1,0:T(8,128)(2,1)}) custom-call(f32[2048,320]{1,0:T(8,128)} %get-tuple-element.250.part_ref, f32[2048,320]{1,0:T(8,128)} %get-tuple-element.251.run_ref, f32[64,320]{1,0:T(8,128)} %broadcast_bitcast_fusion.1.start_ref, f32[2048,320]{1,0:T(8,128)} %get-tuple-element.254.branch_ref), custom_call_target="tpu_custom_call" | custom-call | tf_op jit(solution)/shard_map/pallas_call | solution.py:863
  191.9 2.8 abs_reduce_fusion
  218.9 24.5 %collective-permute-done.37 = f16[2,256,1152]{2,1,0:T(8,128)(2,1)S(1)} collective-permute-done((f16[2,256,1152]{2,1,0:T(8,128)(2,1)S(1)}, f16[2,256,1152]{2,1,0:T(8,128)(2,1)S(1)}, u32[]{:S(2)}, u32[]{:S(2)}) %collective-permute-start.37) | collective-permute-done | bytes 1179680 | tf_op jit(solution)/shard_map/ppermute | solution.py:133
  259.0 11.3 %collective-permute-done.39 = f16[256,1152]{1,0:T(8,128)(2,1)} collective-permute-done((f16[256,1152]{1,0:T(8,128)(2,1)}, f16[256,1152]{1,0:T(8,128)(2,1)}, u32[]{:S(2)}, u32[]{:S(2)}) %collective-permute-start.39) | collective-permute-done | bytes 589856 | tf_op jit(solution)/shard_map/ppermute | solution.py:133
  279.3 3.4 copy-done
  289.4 3.0 pad_maximum_fusion.w_ref
  292.4 17.8 %collective-permute-done.47.refs_2_ = bf16[256,2048]{1,0:T(8,128)(2,1)S(1)} collective-permute-done((bf16[256,2048]{1,0:T(8,128)(2,1)S(1)}, bf16[256,2048]{1,0:T(8,128)(2,1)S(1)}, u32[]{:S(2)}, u32[]{:S(2)}) %collective-permute-start.47) | collective-permute-done | bytes 1048608 | tf_op jit(solution)/shard_map/ppermute | solution.py:133
  313.7 10.5 %collective-permute-done.49.refs_4_ = bf16[128,2048]{1,0:T(8,128)(2,1)S(1)} collective-permute-done((bf16[128,2048]{1,0:T(8,128)(2,1)S(1)}, bf16[128,2048]{1,0:T(8,128)(2,1)S(1)}, u32[]{:S(2)}, u32[]{:S(2)}) %collective-permute-start.49) | collective-permute-done | bytes 524320 | tf_op jit(solution)/shard_map/ppermute | solution.py:133
  328.3 3.4 copy-done.1
  331.7 26.8 %shard_map.311 = (bf16[2048,768]{1,0:T(8,128)(2,1)}, bf16[2048,1536]{1,0:T(8,128)(2,1)}) custom-call(bf16[2048,2048]{1,0:T(8,128)(2,1)} %copy-done.1, bf16[2048,2048]{1,0:T(8,128)(2,1)} %copy-done, bf16[2048,1536]{1,0:T(8,128)(2,1)} %pad_maximum_fusion.w_ref, bf16[768,2048]{1,0:T(8,128)(2,1)} %all-gather.14.cloned.1.call-done.down_ref.w_ref), custom_call_target="tpu_custom_call" | custom-call | tf_op jit(solution)/shard_map/pallas_call | solution.py:863
  358.5 11.4 %shard_map.312 = bf16[1024,2048]{1,0:T(8,128)(2,1)} custom-call(s32[1]{0:T(128)} %bitcast.81.core_ref, bf16[2048,1536]{1,0:T(8,128)(2,1)} %get-tuple-element.308.x_ref.grad_ref, bf16[2048,1536]{1,0:T(8,128)(2,1)} %pad_maximum_fusion.w_ref), custom_call_target="tpu_custom_call" | custom-call | tf_op jit(solution)/shard_map/pallas_call | solution.py:725
  370.0 7.2 collective-permute-done.55.got_ref
  379.3 13.8 %shard_map.313 = (f32[256,2048]{1,0:T(8,128)}, f32[256,1024]{1,0:T(8,128)}, f32[256,1024]{1,0:T(8,128)}, bf16[2,256,1024]{2,1,0:T(8,128)(2,1)}, bf16[2,256,1024]{2,1,0:T(8,128)(2,1)}) custom-call(s32[1]{0:T(128)} %bitcast.c_ref.core_ref, bf16[2048,1536]{1,0:T(8,128)(2,1)} %get-tuple-element.308.x_ref.grad_ref, bf16[2048,1536]{1,0:T(8,128)(2,1)} %pad_maximum_fusion.w_ref, ...), custom_call_target="tpu_custom_call" | custom-call | tf_op jit(solution)/shard_map/pallas_call | solution.py:725
  395.3 20.4 %shard_map.314 = (bf16[4,4,128,1536]{3,2,1,0:T(8,128)(2,1)}, f32[4,128,1536]{2,1,0:T(8,128)}) custom-call(s32[2]{0:T(128)} %pad_add_fusion.core_ref, bf16[2048,2048]{1,0:T(8,128)(2,1)} %copy-done.1, bf16[2048,1536]{1,0:T(8,128)(2,1)} %get-tuple-element.308.x_ref.grad_ref), custom_call_target="tpu_custom_call" | custom-call | tf_op jit(solution)/shard_map/pallas_call | solution.py:797
  415.8 2.8 collective-permute-done.56
  419.6 7.4 %shard_map.315 = bf16[1024,2048]{1,0:T(8,128)(2,1)} custom-call(s32[1]{0:T(128)} %bitcast.81.core_ref, bf16[2048,768]{1,0:T(8,128)(2,1)} %get-tuple-element.323.x_ref.hidden_ref, bf16[768,2048]{1,0:T(8,128)(2,1)} %all-gather.14.cloned.1.call-done.down_ref.w_ref), custom_call_target="tpu_custom_call" | custom-call | tf_op jit(solution)/shard_map/pallas_call | solution.py:725
  432.2 12.7 %collective-permute-done.58 = bf16[256,1024]{1,0:T(8,128)(2,1)S(1)} collective-permute-done((bf16[256,1024]{1,0:T(8,128)(2,1)S(1)}, bf16[256,1024]{1,0:T(8,128)(2,1)S(1)}, u32[]{:S(2)}, u32[]{:S(2)}) %collective-permute-start.58) | collective-permute-done | bytes 524320 | tf_op jit(solution)/shard_map/ppermute | solution.py:133
  451.9 13.9 %shard_map.317 = (bf16[4,192,2048]{2,1,0:T(8,128)(2,1)}, f32[192,2048]{1,0:T(8,128)}) custom-call(s32[1]{0:T(128)} %bitcast.82.core_ref, bf16[2048,768]{1,0:T(8,128)(2,1)} %get-tuple-element.323.x_ref.hidden_ref, bf16[2048,2048]{1,0:T(8,128)(2,1)} %copy-done), custom_call_target="tpu_custom_call" | custom-call | tf_op jit(solution)/shard_map/pallas_call | solution.py:839
  467.8 9.8 %shard_map.316 = (f32[256,2048]{1,0:T(8,128)}, f32[256,1024]{1,0:T(8,128)}, f32[256,1024]{1,0:T(8,128)}, bf16[2,256,1024]{2,1,0:T(8,128)(2,1)}, bf16[2,256,1024]{2,1,0:T(8,128)(2,1)}) custom-call(s32[1]{0:T(128)} %bitcast.c_ref.core_ref, bf16[2048,768]{1,0:T(8,128)(2,1)} %get-tuple-element.323.x_ref.hidden_ref, ...), custom_call_target="tpu_custom_call" | custom-call | tf_op jit(solution)/shard_map/pallas_call | solution.py:725
  480.1 10.4 %collective-permute-done.64.refs_4_ = bf16[128,2048]{1,0:T(8,128)(2,1)S(1)} collective-permute-done((bf16[128,2048]{1,0:T(8,128)(2,1)S(1)}, bf16[128,2048]{1,0:T(8,128)(2,1)S(1)}, u32[]{:S(2)}, u32[]{:S(2)}) %collective-permute-start.64) | collective-permute-done | bytes 524320 | tf_op jit(solution)/shard_map/ppermute | solution.py:133
  494.8 3.4 copy-done.3
  499.8 16.4 %shard_map.319 = (bf16[2048,320]{1,0:T(8,128)(2,1)}, f32[2048,320]{1,0:T(8,128)}, f32[2048,320]{1,0:T(8,128)}, f32[64,320]{1,0:T(8,128)}) custom-call(bf16[2048,2048]{1,0:T(8,128)(2,1)} %copy-done.3, bf16[320,2048]{1,0:T(8,128)(2,1)} %bitcast.393, f32[2048,320]{1,0:T(8,128)} %get-tuple-element.254.branch_ref, f32[2048,320]{1,0:T(8,128)} %get-tuple-element.340.state_ref, ...), custom_call_target="tpu_custom_call" | custom-call | tf_op jit(solution)/shard_map/pallas_call | solution.py:863
  517.1 6.5 collective-permute-done.70
  527.9 7.6 %fusion.97 = bf16[320,2048]{1,0:T(8,128)(2,1)} fusion(bf16[2048,320]{1,0:T(8,128)(2,1)S(1)} %copy-done.40, bf16[2048,2048]{1,0:T(8,128)(2,1)} %copy-done.3), kind=kOutput, calls=%fused_computation.321 | convolution fusion | flops 2684354560 | bytes 11010048 | tf_op jit(solution)/shard_map/dot_general | solution.py:34
  539.4 3.1 collective-permute-done.75
  548.5 22.5 %shard_map.320 = (bf16[2048,320]{1,0:T(8,128)(2,1)}, bf16[320,448]{1,0:T(8,128)(2,1)}) custom-call(f32[2048,320]{1,0:T(8,128)} %get-tuple-element.342.part_ref, f32[2048,320]{1,0:T(8,128)} %get-tuple-element.343.run_ref, f32[64,320]{1,0:T(8,128)} %broadcast_bitcast_fusion.carry_ref, f32[2048,320]{1,0:T(8,128)} %get-tuple-element.340.state_ref, ...), custom_call_target="tpu_custom_call" | custom-call | tf_op jit(solution)/shard_map/pallas_call | solution.py:863
  572.3 9.6 %collective-permute-done.77 = f32[2,64,1536]{2,1,0:T(8,128)S(1)} collective-permute-done((f32[2,64,1536]{2,1,0:T(8,128)}, f32[2,64,1536]{2,1,0:T(8,128)S(1)}, u32[]{:S(2)}, u32[]{:S(2)}) %collective-permute-start.77) | collective-permute-done | bytes 786464 | tf_op jit(solution)/shard_map/ppermute | solution.py:133
  596.4 8.2 %shard_map.321.x_ref.grad_ref = bf16[2048,640]{1,0:T(8,128)(2,1)} custom-call(bf16[2048,320]{1,0:T(8,128)(2,1)} %get-tuple-element.372.grad_ref, bf16[128,320]{1,0:T(8,128)(2,1)} %bitcast.109.halo_ref, f32[2048,8]{1,0:T(8,128)} %get-tuple-element.260.masks_ref, f32[128,8]{1,0:T(8,128)} %bitcast.435, bf16[2048,320]{1,0:T(8,128)(2,1)} %get-tuple-element.377.branch_ref, ...), custom_call_target="tpu_custom_call" | custom-call | tf_op jit(solution)/shard_map/pallas_call | solution.py:863
  608.4 7.2 shard_map.322
  615.6 13.5 %shard_map.323 = (bf16[4,4,128,640]{3,2,1,0:T(8,128)(2,1)}, f32[4,128,640]{2,1,0:T(8,128)}) custom-call(s32[2]{0:T(128)} %pad_add_fusion.core_ref, bf16[2048,2048]{1,0:T(8,128)(2,1)} %get-tuple-element.389.x_ref, bf16[2048,640]{1,0:T(8,128)(2,1)} %shard_map.321.x_ref.grad_ref), custom_call_target="tpu_custom_call" | custom-call | tf_op jit(solution)/shard_map/pallas_call | solution.py:797
  629.1 9.9 %shard_map.324 = (f32[256,2048]{1,0:T(8,128)}, f32[256,1024]{1,0:T(8,128)}, f32[256,1024]{1,0:T(8,128)}, bf16[2,256,1024]{2,1,0:T(8,128)(2,1)}, bf16[2,256,1024]{2,1,0:T(8,128)(2,1)}) custom-call(s32[1]{0:T(128)} %bitcast.c_ref.core_ref, bf16[2048,640]{1,0:T(8,128)(2,1)} %shard_map.321.x_ref.grad_ref, bf16[2048,640]{1,0:T(8,128)(2,1)} %bitcast.399, ...), custom_call_target="tpu_custom_call" | custom-call | tf_op jit(solution)/shard_map/pallas_call | solution.py:725
  644.1 21.0 %collective-permute-done.84 = bf16[2,256,1024]{2,1,0:T(8,128)(2,1)} collective-permute-done((bf16[2,256,1024]{2,1,0:T(8,128)(2,1)}, bf16[2,256,1024]{2,1,0:T(8,128)(2,1)}, u32[]{:S(2)}, u32[]{:S(2)}) %collective-permute-start.84) | collective-permute-done | bytes 1048608 | tf_op jit(solution)/shard_map/ppermute | solution.py:133
  677.9 7.0 collective-permute-done.86
  688.1 7.6 %reduce-scatter.7.cloned.1.call-done = bf16[512,640]{1,0:T(8,128)(2,1)} async-done(((bf16[2048,640]{1,0:T(8,128)(2,1)}), bf16[512,640]{1,0:T(8,128)(2,1)}) %reduce-scatter.7.cloned.1.call-update) | async-done | bytes 655376 | tf_op jit(solution)/shard_map/reduce_scatter | solution.py:160
  709.2 3.5 fusion.4
  716.3 6.9 collective-permute-done.90
  (584 shorter events, 247.2 us)
Async XLA Ops:
  7.2 59.1 %all-gather.6.cloned.1.call-start = ((), (), s32[]{:S(2)}) async-start(), calls=%async_computation.4 | async-start | bytes 2048000 | tf_op jit(solution)/shard_map/all_gather | solution.py:146
  8.0 17.2 %collective-permute-start = (bf16[2,3]{1,0:T(2,128)(2,1)S(1)}, bf16[2,3]{1,0:T(2,128)(2,1)S(1)}, u32[]{:S(2)}, u32[]{:S(2)}) collective-permute-start(bf16[2,3]{1,0:T(2,128)(2,1)S(1)} %slice.336), channel_id=1, source_target_pairs={{0,1},{1,2},{2,3},{3,4},{4,5},{5,6},{6,7},{8,9},{9,10},{10,11},{11... | collective-permute-start | bytes 44 | tf_op jit(solution)/shard_map/ppermute | solution.py:938
  25.2 106.0 %all-gather.8.cloned.1.call-start = ((), (), s32[]{:S(2)}) async-start(), calls=%async_computation.5 | async-start | bytes 3276800 | tf_op jit(solution)/shard_map/all_gather | solution.py:146
  40.4 25.6 %collective-permute-start.7 = (bf16[256,2176]{1,0:T(8,128)(2,1)S(1)}, bf16[256,2176]{1,0:T(8,128)(2,1)}, u32[]{:S(2)}, u32[]{:S(2)}) collective-permute-start(bf16[256,2176]{1,0:T(8,128)(2,1)S(1)} %pad_maximum_fusion.10.refs_0_), channel_id=1, source_target_pairs={{0,16},{8,24},{16,0},{24,8},{1,17},{9,25},{17,1},{25,9},{2,18},{10... | collective-permute-start | bytes 3342344 | tf_op jit(solution)/shard_map/ppermute | solution.py:133
  42.0 24.3 %collective-permute-start.6 = (bf16[256,2176]{1,0:T(8,128)(2,1)S(1)}, bf16[256,2176]{1,0:T(8,128)(2,1)}, u32[]{:S(2)}, u32[]{:S(2)}) collective-permute-start(bf16[256,2176]{1,0:T(8,128)(2,1)S(1)} %pad_maximum_fusion.10.refs_0_), channel_id=1, source_target_pairs={{0,8},{8,0},{16,24},{24,16},{1,9},{9,1},{17,25},{25,17},{2,10},{10... | collective-permute-start | bytes 3342344 | tf_op jit(solution)/shard_map/ppermute | solution.py:133
  45.8 146.1 %all-gather.10.cloned.1.call-start = ((), (), s32[]{:S(2)}) async-start(), calls=%async_computation.6 | async-start | bytes 3932160 | tf_op jit(solution)/shard_map/all_gather | solution.py:146
  101.0 16.3 %collective-permute-start.24 = (bf16[2,64,1536]{2,1,0:T(8,128)(2,1)S(1)}, bf16[2,64,1536]{2,1,0:T(8,128)(2,1)S(1)}, u32[]{:S(2)}, u32[]{:S(2)}) collective-permute-start(bf16[2,64,1536]{2,1,0:T(8,128)(2,1)S(1)} %get-tuple-element.604), channel_id=1, source_target_pairs={{0,16},{8,24},{16,0},{24,8},{1,17},{9,25},{17,1},{25,9},{2,18},{10... | collective-permute-start | bytes 1179656 | tf_op jit(solution)/shard_map/ppermute | solution.py:133
  101.5 15.8 %collective-permute-start.23 = (bf16[2,64,1536]{2,1,0:T(8,128)(2,1)S(1)}, bf16[2,64,1536]{2,1,0:T(8,128)(2,1)S(1)}, u32[]{:S(2)}, u32[]{:S(2)}) collective-permute-start(bf16[2,64,1536]{2,1,0:T(8,128)(2,1)S(1)} %get-tuple-element.605), channel_id=1, source_target_pairs={{0,24},{8,16},{16,8},{24,0},{1,25},{9,17},{17,9},{25,1},{2,26},{10... | collective-permute-start | bytes 1179656 | tf_op jit(solution)/shard_map/ppermute | solution.py:133
  103.5 16.6 %collective-permute-start.18 = (bf16[256,2176]{1,0:T(8,128)(2,1)S(1)}, bf16[256,2176]{1,0:T(8,128)(2,1)S(1)}, u32[]{:S(2)}, u32[]{:S(2)}) collective-permute-start(bf16[256,2176]{1,0:T(8,128)(2,1)S(1)} %pad_maximum_fusion.10.refs_0_), channel_id=1, source_target_pairs={{0,1},{1,0},{2,3},{3,2},{4,5},{5,4},{6,7},{7,6},{8,9},{9,8},{10,11... | collective-permute-start | bytes 3342344 | tf_op jit(solution)/shard_map/ppermute | solution.py:136
  103.5 16.6 %collective-permute-start.19 = (bf16[256,2176]{1,0:T(8,128)(2,1)}, bf16[256,2176]{1,0:T(8,128)(2,1)S(1)}, u32[]{:S(2)}, u32[]{:S(2)}) collective-permute-start(bf16[256,2176]{1,0:T(8,128)(2,1)} %collective-permute-done.6.refs_1_), channel_id=1, source_target_pairs={{0,1},{1,0},{2,3},{3,2},{4,5},{5,4},{6,7},{7,6},{8,9},{9,8},{10,11... | collective-permute-start | bytes 3342344 | tf_op jit(solution)/shard_map/ppermute | solution.py:136
  127.8 154.8 %all-gather.12.cloned.1.call-start = ((), (), s32[]{:S(2)}) async-start(), calls=%async_computation.7 | async-start | bytes 3932160 | tf_op jit(solution)/shard_map/all_gather | solution.py:146
  128.3 36.8 %collective-permute-start.27 = (bf16[256,2048]{1,0:T(8,128)(2,1)S(1)}, bf16[256,2048]{1,0:T(8,128)(2,1)S(1)}, u32[]{:S(2)}, u32[]{:S(2)}) collective-permute-start(bf16[256,2048]{1,0:T(8,128)(2,1)S(1)} %bitcast.387), channel_id=1, source_target_pairs={{0,16},{8,24},{16,0},{24,8},{1,17},{9,25},{17,1},{25,9},{2,18},{10... | collective-permute-start | bytes 3145736 | tf_op jit(solution)/shard_map/ppermute | solution.py:133
  128.7 36.4 %collective-permute-start.26 = (bf16[256,2048]{1,0:T(8,128)(2,1)S(1)}, bf16[256,2048]{1,0:T(8,128)(2,1)S(1)}, u32[]{:S(2)}, u32[]{:S(2)}) collective-permute-start(bf16[256,2048]{1,0:T(8,128)(2,1)S(1)} %bitcast.388), channel_id=1, source_target_pairs={{0,8},{8,0},{16,24},{24,16},{1,9},{9,1},{17,25},{25,17},{2,10},{10... | collective-permute-start | bytes 3145736 | tf_op jit(solution)/shard_map/ppermute | solution.py:133
  172.2 15.1 %collective-permute-start.34 = (bf16[2,80,2048]{2,1,0:T(8,128)(2,1)S(1)}, bf16[2,80,2048]{2,1,0:T(8,128)(2,1)S(1)}, u32[]{:S(2)}, u32[]{:S(2)}) collective-permute-start(bf16[2,80,2048]{2,1,0:T(8,128)(2,1)S(1)} %get-tuple-element.616), channel_id=1, source_target_pairs={{0,1},{1,0},{2,3},{3,2},{4,5},{5,4},{6,7},{7,6},{8,9},{9,8},{10,11... | collective-permute-start | bytes 1966088 | tf_op jit(solution)/shard_map/ppermute | solution.py:136
  173.2 15.6 %collective-permute-start.33 = (f32[8,16,8]{2,1,0:T(8,128)S(1)}, f32[8,16,8]{2,1,0:T(8,128)S(1)}, u32[]{:S(2)}, u32[]{:S(2)}) collective-permute-start(f32[8,16,8]{2,1,0:T(8,128)S(1)} %slice_bitcast_fusion.17), channel_id=1, source_target_pairs={{2,0},{3,1},{4,2},{5,3},{6,4},{7,5},{10,8},{11,9},{12,10},{13,11},... | collective-permute-start | bytes 12296 | tf_op jit(solution)/shard_map/ppermute | solution.py:140
  176.3 14.5 %collective-permute-start.32 = (bf16[128,2048]{1,0:T(8,128)(2,1)S(1)}, bf16[128,2048]{1,0:T(8,128)(2,1)}, u32[]{:S(2)}, u32[]{:S(2)}) collective-permute-start(bf16[128,2048]{1,0:T(8,128)(2,1)S(1)} %slice.367), channel_id=1, source_target_pairs={{0,8},{8,0},{16,24},{24,16},{1,9},{9,1},{17,25},{25,17},{2,10},{10... | collective-permute-start | bytes 1572872 | tf_op jit(solution)/shard_map/ppermute | solution.py:133
  202.6 129.1 %all-gather.14.cloned.1.call-start = ((), (), s32[]{:S(2)}) async-start(), calls=%async_computation.8 | async-start | bytes 3932160 | tf_op jit(solution)/shard_map/all_gather | solution.py:146
  215.5 28.0 %collective-permute-start.37 = (f16[2,256,1152]{2,1,0:T(8,128)(2,1)S(1)}, f16[2,256,1152]{2,1,0:T(8,128)(2,1)S(1)}, u32[]{:S(2)}, u32[]{:S(2)}) collective-permute-start(f16[2,256,1152]{2,1,0:T(8,128)(2,1)S(1)} %pad_maximum_fusion.8), channel_id=1, source_target_pairs={{0,8},{8,0},{16,24},{24,16},{1,9},{9,1},{17,25},{25,17},{2,10},{10... | collective-permute-start | bytes 3538952 | tf_op jit(solution)/shard_map/ppermute | solution.py:133
  217.4 27.7 %collective-permute-start.38 = (f16[2,256,1152]{2,1,0:T(8,128)(2,1)S(1)}, f16[2,256,1152]{2,1,0:T(8,128)(2,1)S(1)}, u32[]{:S(2)}, u32[]{:S(2)}) collective-permute-start(f16[2,256,1152]{2,1,0:T(8,128)(2,1)S(1)} %pad_maximum_fusion.9), channel_id=1, source_target_pairs={{0,16},{8,24},{16,0},{24,8},{1,17},{9,25},{17,1},{25,9},{2,18},{10... | collective-permute-start | bytes 3538952 | tf_op jit(solution)/shard_map/ppermute | solution.py:133
  255.8 14.5 %collective-permute-start.39 = (f16[256,1152]{1,0:T(8,128)(2,1)}, f16[256,1152]{1,0:T(8,128)(2,1)}, u32[]{:S(2)}, u32[]{:S(2)}) collective-permute-start(f16[256,1152]{1,0:T(8,128)(2,1)} %pad_maximum_fusion.12), channel_id=1, source_target_pairs={{0,16},{8,24},{16,0},{24,8},{1,17},{9,25},{17,1},{25,9},{2,18},{10... | collective-permute-start | bytes 1769480 | tf_op jit(solution)/shard_map/ppermute | solution.py:133
  257.3 14.2 %collective-permute-start.40 = (f16[256,1152]{1,0:T(8,128)(2,1)}, f16[256,1152]{1,0:T(8,128)(2,1)}, u32[]{:S(2)}, u32[]{:S(2)}) collective-permute-start(f16[256,1152]{1,0:T(8,128)(2,1)} %pad_maximum_fusion.13), channel_id=1, source_target_pairs={{0,8},{8,0},{16,24},{24,16},{1,9},{9,1},{17,25},{25,17},{2,10},{10... | collective-permute-start | bytes 1769480 | tf_op jit(solution)/shard_map/ppermute | solution.py:133
  257.9 277.7 %reduce-scatter.5.cloned.1.call-start = ((), (), s32[]{:S(2)}) async-start(), calls=%async_computation.9 | async-start | bytes 7864320 | tf_op jit(solution)/shard_map/reduce_scatter | solution.py:160
  258.4 18.9 %collective-permute-start.44 = (bf16[128,2048]{1,0:T(8,128)(2,1)}, bf16[128,2048]{1,0:T(8,128)(2,1)S(1)}, u32[]{:S(2)}, u32[]{:S(2)}) collective-permute-start(bf16[128,2048]{1,0:T(8,128)(2,1)} %collective-permute-done.31.refs_3_), channel_id=1, source_target_pairs={{0,1},{1,0},{2,3},{3,2},{4,5},{5,4},{6,7},{7,6},{8,9},{9,8},{10,11... | collective-permute-start | bytes 1572872 | tf_op jit(solution)/shard_map/ppermute | solution.py:136
  258.4 18.9 %collective-permute-start.45 = (bf16[128,2048]{1,0:T(8,128)(2,1)}, bf16[128,2048]{1,0:T(8,128)(2,1)S(1)}, u32[]{:S(2)}, u32[]{:S(2)}) collective-permute-start(bf16[128,2048]{1,0:T(8,128)(2,1)} %collective-permute-done.32.refs_4_), channel_id=1, source_target_pairs={{0,1},{1,0},{2,3},{3,2},{4,5},{5,4},{6,7},{7,6},{8,9},{9,8},{10,11... | collective-permute-start | bytes 1572872 | tf_op jit(solution)/shard_map/ppermute | solution.py:136
  258.9 18.4 %collective-permute-start.41 = (bf16[256,2048]{1,0:T(8,128)(2,1)S(1)}, bf16[256,2048]{1,0:T(8,128)(2,1)S(1)}, u32[]{:S(2)}, u32[]{:S(2)}) collective-permute-start(bf16[256,2048]{1,0:T(8,128)(2,1)S(1)} %bitcast.389), channel_id=1, source_target_pairs={{0,1},{1,0},{2,3},{3,2},{4,5},{5,4},{6,7},{7,6},{8,9},{9,8},{10,11... | collective-permute-start | bytes 3145736 | tf_op jit(solution)/shard_map/ppermute | solution.py:136
  285.1 25.1 %collective-permute-start.47 = (bf16[256,2048]{1,0:T(8,128)(2,1)S(1)}, bf16[256,2048]{1,0:T(8,128)(2,1)S(1)}, u32[]{:S(2)}, u32[]{:S(2)}) collective-permute-start(bf16[256,2048]{1,0:T(8,128)(2,1)S(1)} %multiply_convert_fusion.2.refs_0_), channel_id=1, source_target_pairs={{0,16},{8,24},{16,0},{24,8},{1,17},{9,25},{17,1},{25,9},{2,18},{10... | collective-permute-start | bytes 3145736 | tf_op jit(solution)/shard_map/ppermute | solution.py:133
  286.6 24.8 %collective-permute-start.46 = (bf16[256,2048]{1,0:T(8,128)(2,1)S(1)}, bf16[256,2048]{1,0:T(8,128)(2,1)S(1)}, u32[]{:S(2)}, u32[]{:S(2)}) collective-permute-start(bf16[256,2048]{1,0:T(8,128)(2,1)S(1)} %multiply_convert_fusion.2.refs_0_), channel_id=1, source_target_pairs={{0,8},{8,0},{16,24},{24,16},{1,9},{9,1},{17,25},{25,17},{2,10},{10... | collective-permute-start | bytes 3145736 | tf_op jit(solution)/shard_map/ppermute | solution.py:133
  393.0 25.5 %collective-permute-start.56 = (bf16[2,256,1024]{2,1,0:T(8,128)(2,1)}, bf16[2,256,1024]{2,1,0:T(8,128)(2,1)}, u32[]{:S(2)}, u32[]{:S(2)}) collective-permute-start(bf16[2,256,1024]{2,1,0:T(8,128)(2,1)} %get-tuple-element.304), channel_id=1, source_target_pairs={{0,8},{8,0},{16,24},{24,16},{1,9},{9,1},{17,25},{25,17},{2,10},{10... | collective-permute-start | bytes 3145736 | tf_op jit(solution)/shard_map/ppermute | solution.py:133
  394.1 25.2 %collective-permute-start.57 = (bf16[2,256,1024]{2,1,0:T(8,128)(2,1)}, bf16[2,256,1024]{2,1,0:T(8,128)(2,1)}, u32[]{:S(2)}, u32[]{:S(2)}) collective-permute-start(bf16[2,256,1024]{2,1,0:T(8,128)(2,1)} %get-tuple-element.305), channel_id=1, source_target_pairs={{0,16},{8,24},{16,0},{24,8},{1,17},{9,25},{17,1},{25,9},{2,18},{10... | collective-permute-start | bytes 3145736 | tf_op jit(solution)/shard_map/ppermute | solution.py:133
  419.4 246.2 %reduce-scatter.9.cloned.1.call-start = ((), (), s32[]{:S(2)}) async-start(), calls=%async_computation.11 | async-start | bytes 3932160 | tf_op jit(solution)/shard_map/reduce_scatter | solution.py:160
  427.0 38.7 %collective-permute-start.62 = (bf16[1024,2048]{1,0:T(8,128)(2,1)}, bf16[1024,2048]{1,0:T(8,128)(2,1)S(1)}, u32[]{:S(2)}, u32[]{:S(2)}) collective-permute-start(bf16[1024,2048]{1,0:T(8,128)(2,1)} %shard_map.315), channel_id=1, source_target_pairs={{0,1},{1,0},{2,3},{3,2},{4,5},{5,4},{6,7},{7,6},{8,9},{9,8},{10,11... | collective-permute-start | bytes 12582920 | tf_op jit(solution)/shard_map/ppermute | solution.py:136
  430.5 14.4 %collective-permute-start.58 = (bf16[256,1024]{1,0:T(8,128)(2,1)S(1)}, bf16[256,1024]{1,0:T(8,128)(2,1)S(1)}, u32[]{:S(2)}, u32[]{:S(2)}) collective-permute-start(bf16[256,1024]{1,0:T(8,128)(2,1)S(1)} %fusion.33), channel_id=1, source_target_pairs={{0,16},{8,24},{16,0},{24,8},{1,17},{9,25},{17,1},{25,9},{2,18},{10... | collective-permute-start | bytes 1572872 | tf_op jit(solution)/shard_map/ppermute | solution.py:133
  449.5 28.0 %collective-permute-start.61 = (bf16[256,2048]{1,0:T(8,128)(2,1)S(1)}, bf16[256,2048]{1,0:T(8,128)(2,1)S(1)}, u32[]{:S(2)}, u32[]{:S(2)}) collective-permute-start(bf16[256,2048]{1,0:T(8,128)(2,1)S(1)} %get-tuple-element.331.refs_0_), channel_id=1, source_target_pairs={{0,16},{8,24},{16,0},{24,8},{1,17},{9,25},{17,1},{25,9},{2,18},{10... | collective-permute-start | bytes 3145736 | tf_op jit(solution)/shard_map/ppermute | solution.py:133
  451.0 26.6 %collective-permute-start.60 = (bf16[256,2048]{1,0:T(8,128)(2,1)S(1)}, bf16[256,2048]{1,0:T(8,128)(2,1)S(1)}, u32[]{:S(2)}, u32[]{:S(2)}) collective-permute-start(bf16[256,2048]{1,0:T(8,128)(2,1)S(1)} %get-tuple-element.331.refs_0_), channel_id=1, source_target_pairs={{0,8},{8,0},{16,24},{24,16},{1,9},{9,1},{17,25},{25,17},{2,10},{10... | collective-permute-start | bytes 3145736 | tf_op jit(solution)/shard_map/ppermute | solution.py:133
  498.2 25.4 %collective-permute-start.70 = (bf16[2,256,1024]{2,1,0:T(8,128)(2,1)}, bf16[2,256,1024]{2,1,0:T(8,128)(2,1)S(1)}, u32[]{:S(2)}, u32[]{:S(2)}) collective-permute-start(bf16[2,256,1024]{2,1,0:T(8,128)(2,1)} %get-tuple-element.348), channel_id=1, source_target_pairs={{0,8},{8,0},{16,24},{24,16},{1,9},{9,1},{17,25},{25,17},{2,10},{10... | collective-permute-start | bytes 3145736 | tf_op jit(solution)/shard_map/ppermute | solution.py:133
  499.1 24.9 %collective-permute-start.71 = (bf16[2,256,1024]{2,1,0:T(8,128)(2,1)S(1)}, bf16[2,256,1024]{2,1,0:T(8,128)(2,1)S(1)}, u32[]{:S(2)}, u32[]{:S(2)}) collective-permute-start(bf16[2,256,1024]{2,1,0:T(8,128)(2,1)S(1)} %copy-done.83), channel_id=1, source_target_pairs={{0,16},{8,24},{16,0},{24,8},{1,17},{9,25},{17,1},{25,9},{2,18},{10... | collective-permute-start | bytes 3145736 | tf_op jit(solution)/shard_map/ppermute | solution.py:133
  538.9 149.1 %reduce-scatter.11.cloned.1.call-start = ((), (), s32[]{:S(2)}) async-start(), calls=%async_computation.12 | async-start | bytes 2048000 | tf_op jit(solution)/shard_map/reduce_scatter | solution.py:160
  544.3 27.9 %collective-permute-start.78 = (f32[2,64,1536]{2,1,0:T(8,128)}, f32[2,64,1536]{2,1,0:T(8,128)S(1)}, u32[]{:S(2)}, u32[]{:S(2)}) collective-permute-start(f32[2,64,1536]{2,1,0:T(8,128)} %get-tuple-element.572), channel_id=1, source_target_pairs={{0,8},{8,0},{16,24},{24,16},{1,9},{9,1},{17,25},{25,17},{2,10},{10... | collective-permute-start | bytes 2359304 | tf_op jit(solution)/shard_map/ppermute | solution.py:133
  545.5 36.4 %collective-permute-start.77 = (f32[2,64,1536]{2,1,0:T(8,128)}, f32[2,64,1536]{2,1,0:T(8,128)S(1)}, u32[]{:S(2)}, u32[]{:S(2)}) collective-permute-start(f32[2,64,1536]{2,1,0:T(8,128)} %get-tuple-element.573), channel_id=1, source_target_pairs={{0,16},{8,24},{16,0},{24,8},{1,17},{9,25},{17,1},{25,9},{2,18},{10... | collective-permute-start | bytes 2359304 | tf_op jit(solution)/shard_map/ppermute | solution.py:133
  546.1 35.8 %collective-permute-start.76 = (f32[2,64,1536]{2,1,0:T(8,128)S(1)}, f32[2,64,1536]{2,1,0:T(8,128)S(1)}, u32[]{:S(2)}, u32[]{:S(2)}) collective-permute-start(f32[2,64,1536]{2,1,0:T(8,128)S(1)} %get-tuple-element.574), channel_id=1, source_target_pairs={{0,24},{8,16},{16,8},{24,0},{1,25},{9,17},{17,9},{25,1},{2,26},{10... | collective-permute-start | bytes 2359304 | tf_op jit(solution)/shard_map/ppermute | solution.py:133
  572.2 19.2 %collective-permute-start.80 = (bf16[2,80,2496]{2,1,0:T(8,128)(2,1)S(1)}, bf16[2,80,2496]{2,1,0:T(8,128)(2,1)S(1)}, u32[]{:S(2)}, u32[]{:S(2)}) collective-permute-start(bf16[2,80,2496]{2,1,0:T(8,128)(2,1)S(1)} %get-tuple-element.598), channel_id=1, source_target_pairs={{0,1},{1,0},{2,3},{3,2},{4,5},{5,4},{6,7},{7,6},{8,9},{9,8},{10,11... | collective-permute-start | bytes 2396168 | tf_op jit(solution)/shard_map/ppermute | solution.py:136
  589.6 15.0 %collective-permute-start.81 = (bf16[256,1024]{1,0:T(8,128)(2,1)}, bf16[256,1024]{1,0:T(8,128)(2,1)}, u32[]{:S(2)}, u32[]{:S(2)}) collective-permute-start(bf16[256,1024]{1,0:T(8,128)(2,1)} %fusion.25), channel_id=1, source_target_pairs={{0,16},{8,24},{16,0},{24,8},{1,17},{9,25},{17,1},{25,9},{2,18},{10... | collective-permute-start | bytes 1572872 | tf_op jit(solution)/shard_map/ppermute | solution.py:133
  590.2 14.4 %collective-permute-start.82 = (bf16[256,1024]{1,0:T(8,128)(2,1)}, bf16[256,1024]{1,0:T(8,128)(2,1)}, u32[]{:S(2)}, u32[]{:S(2)}) collective-permute-start(bf16[256,1024]{1,0:T(8,128)(2,1)} %fusion.23), channel_id=1, source_target_pairs={{0,8},{8,0},{16,24},{24,16},{1,9},{9,1},{17,25},{25,17},{2,10},{10... | collective-permute-start | bytes 1572872 | tf_op jit(solution)/shard_map/ppermute | solution.py:133
  596.3 99.4 %reduce-scatter.7.cloned.1.call-start = ((), (), s32[]{:S(2)}) async-start(), calls=%async_computation.10 | async-start | bytes 3276800 | tf_op jit(solution)/shard_map/reduce_scatter | solution.py:160
  639.1 26.0 %collective-permute-start.84 = (bf16[2,256,1024]{2,1,0:T(8,128)(2,1)}, bf16[2,256,1024]{2,1,0:T(8,128)(2,1)}, u32[]{:S(2)}, u32[]{:S(2)}) collective-permute-start(bf16[2,256,1024]{2,1,0:T(8,128)(2,1)} %get-tuple-element.398), channel_id=1, source_target_pairs={{0,8},{8,0},{16,24},{24,16},{1,9},{9,1},{17,25},{25,17},{2,10},{10... | collective-permute-start | bytes 3145736 | tf_op jit(solution)/shard_map/ppermute | solution.py:133
  640.0 25.6 %collective-permute-start.85 = (bf16[2,256,1024]{2,1,0:T(8,128)(2,1)}, bf16[2,256,1024]{2,1,0:T(8,128)(2,1)}, u32[]{:S(2)}, u32[]{:S(2)}) collective-permute-start(bf16[2,256,1024]{2,1,0:T(8,128)(2,1)} %get-tuple-element.399), channel_id=1, source_target_pairs={{0,16},{8,24},{16,0},{24,8},{1,17},{9,25},{17,1},{25,9},{2,18},{10... | collective-permute-start | bytes 3145736 | tf_op jit(solution)/shard_map/ppermute | solution.py:133
  707.2 16.0 %collective-permute-start.90 = (f32[2,64,640]{2,1,0:T(8,128)S(1)}, f32[2,64,640]{2,1,0:T(8,128)S(1)}, u32[]{:S(2)}, u32[]{:S(2)}) collective-permute-start(f32[2,64,640]{2,1,0:T(8,128)S(1)} %get-tuple-element.611), channel_id=1, source_target_pairs={{0,16},{8,24},{16,0},{24,8},{1,17},{9,25},{17,1},{25,9},{2,18},{10... | collective-permute-start | bytes 983048 | tf_op jit(solution)/shard_map/ppermute | solution.py:133
  708.7 14.6 %collective-permute-start.89 = (f32[2,64,640]{2,1,0:T(8,128)S(1)}, f32[2,64,640]{2,1,0:T(8,128)S(1)}, u32[]{:S(2)}, u32[]{:S(2)}) collective-permute-start(f32[2,64,640]{2,1,0:T(8,128)S(1)} %get-tuple-element.612), channel_id=1, source_target_pairs={{0,24},{8,16},{16,8},{24,0},{1,25},{9,17},{17,9},{25,1},{2,26},{10... | collective-permute-start | bytes 983048 | tf_op jit(solution)/shard_map/ppermute | solution.py:133
  (137 other events, 984.0 us)
Sparse Core Ops, SparseCore 0:
  25.3 37.3 all-gather.5
  64.9 53.6 all-gather.7
  128.0 63.6 all-gather.9
  202.7 62.5 all-gather.11
  266.7 62.1 all-gather.13
  419.5 109.2 reduce-scatter.4
  539.0 64.3 reduce-scatter.8
  605.7 36.3 reduce-scatter.10
  644.5 51.1 reduce-scatter.6

commit v4 on v3

--- a/solution.py
+++ b/solution.py
@@ -235,6 +235,11 @@
         array, from_x, from_y = near
         half = array.shape[0] // 2
         return array, from_x, from_y, self.to_k(from_x[:half], 2), self.to_k(from_y[half:], 1)
+
+    def gather_core(self, mine):
+        if not self.square:
+            return [self.gather_plane(mine[0])], None
+        return list(mine), [self.to_core(part) for part in mine]
 
     def gather_end(self, mine):
         if not self.square:
@@ -736,7 +741,7 @@
             out_specs=[spec(*one) for one in outputs],
         ),
         cost_estimate=pl.CostEstimate(flops=0, bytes_accessed=0, transcendentals=0),
-        compiler_params=pltpu.CompilerParams(vmem_limit_bytes=56 * 2**20),
+        compiler_params=pltpu.CompilerParams(vmem_limit_bytes=60 * 2**20),
     )(core.reshape(1).astype(jnp.int32), x, w, *[array for array, _, _ in extra])
 
 
@@ -810,7 +815,7 @@
             ],
         ),
         cost_estimate=pl.CostEstimate(flops=0, bytes_accessed=0, transcendentals=0),
-        compiler_params=pltpu.CompilerParams(vmem_limit_bytes=56 * 2**20),
+        compiler_params=pltpu.CompilerParams(vmem_limit_bytes=60 * 2**20),
     )(jnp.stack([z, jnp.int32(per)]).astype(jnp.int32), x, grad)
 
 
@@ -852,7 +857,7 @@
             ],
         ),
         cost_estimate=pl.CostEstimate(flops=0, bytes_accessed=0, transcendentals=0),
-        compiler_params=pltpu.CompilerParams(vmem_limit_bytes=56 * 2**20),
+        compiler_params=pltpu.CompilerParams(vmem_limit_bytes=60 * 2**20),
     )(z.reshape(1).astype(jnp.int32), hidden, cot)
 
 
@@ -868,8 +873,87 @@
         out_specs=[spec(array, count) for array, count in outputs],
         scratch_shapes=scratch,
         cost_estimate=pl.CostEstimate(flops=0, bytes_accessed=0, transcendentals=0),
-        compiler_params=pltpu.CompilerParams(vmem_limit_bytes=56 * 2**20),
+        compiler_params=pltpu.CompilerParams(vmem_limit_bytes=60 * 2**20),
     )(*[array for array, _ in inputs])
+
+
+def gathered_kernel(kernel, parts, steps, backwards, keep, given, core_ref, *refs):
+    own, other = refs[:parts], refs[parts : 2 * parts]
+    refs = refs[2 * parts :]
+    inputs, refs = refs[:given], refs[given:]
+    out_ref, refs = (refs[0], refs[1:]) if keep else (None, refs)
+    buffer, sem, out_sem = refs[-3:]
+    half = buffer.shape[0] // 2
+    count = buffer.shape[0] // steps
+    step = pl.program_id(0)
+    block = steps - 1 - step if backwards else step
+
+    @pl.when(step == 0)
+    def _():
+        for which, group in enumerate((own, other)):
+            side = core_ref[0] if which == 0 else 1 - core_ref[0]
+            start = 0
+            for i, part in enumerate(group):
+                to = pl.ds(pl.multiple_of(side * half + start, 16), part.shape[0])
+                pltpu.make_async_copy(part, buffer.at[to], sem.at[side * parts + i]).start()
+                start = start + part.shape[0]
+
+    at = pl.ds(pl.multiple_of(block * count, 16), count)
+    side = block // (steps // 2)
+    place = lax.rem(block, steps // 2)
+    whole = steps // 2 - 1
+
+    @pl.when(place < whole)
+    def _():
+        pltpu.make_async_copy(buffer.at[at], buffer.at[at], sem.at[side * parts + place]).wait()
+
+    @pl.when(place == whole)
+    def _():
+        for i in range(whole, parts):
+            to = pl.ds(pl.multiple_of(block * count, 16), own[i].shape[0])
+            pltpu.make_async_copy(buffer.at[to], buffer.at[to], sem.at[side * parts + i]).wait()
+
+    if keep:
+        pltpu.make_async_copy(buffer.at[at], out_ref.at[at], out_sem.at[block]).start()
+    kernel(buffer.at[at], *inputs, *refs[:-3])
+    if keep:
+
+        @pl.when(step == steps - 1)
+        def _():
+            for i in range(steps):
+                to = pl.ds(i * count, count)
+                pltpu.make_async_copy(buffer.at[to], out_ref.at[to], out_sem.at[i]).wait()
+
+
+def gathered_call(kernel, core, gathered, steps, inputs, outputs, scratch=(), backwards=False, keep=True, cost=0):
+    own, other = gathered
+    if other is None:
+        count = own[0].shape[0] // steps
+        results = kernel_call(kernel, steps, [(own[0], count)] + inputs, outputs, scratch, backwards)
+        return ([own[0]] if keep else []) + list(results)
+
+    def spec(array, count):
+        return whole_block(array) if count is None else token_block(array, count, steps, backwards)
+
+    anywhere = pl.BlockSpec(memory_space=pl.ANY)
+    tokens = jax.ShapeDtypeStruct((2 * sum(p.shape[0] for p in own),) + own[0].shape[1:], own[0].dtype)
+    return pl.pallas_call(
+        functools.partial(gathered_kernel, kernel, len(own), steps, backwards, keep, len(inputs)),
+        out_shape=([tokens] if keep else []) + [array for array, _ in outputs],
+        grid=(steps,),
+        in_specs=[pl.BlockSpec(memory_space=pltpu.SMEM)]
+        + [anywhere] * (2 * len(own))
+        + [spec(array, count) for array, count in inputs],
+        out_specs=([anywhere] if keep else []) + [spec(array, count) for array, count in outputs],
+        scratch_shapes=list(scratch)
+        + [
+            pltpu.VMEM(tokens.shape, tokens.dtype),
+            pltpu.SemaphoreType.DMA((2 * len(own),)),
+            pltpu.SemaphoreType.DMA((steps,)),
+        ],
+        cost_estimate=pl.CostEstimate(flops=0, bytes_accessed=cost << 20, transcendentals=0),
+        compiler_params=pltpu.CompilerParams(vmem_limit_bytes=60 * 2**20),
+    )(core.reshape(1).astype(jnp.int32), *own, *other, *[array for array, _ in inputs])
 
 
 def per_device(
@@ -1008,7 +1092,7 @@
     gain_two = gains[:, d_own:].reshape(1, width_d).astype(wide)
     mlp_cols = at.exchange_dp(mlp_pairs)
     cot = cotangent.reshape(tok, width_d)
-    tokens_all, mlp_cols, cot = together(at.gather_end(beside_far), mlp_cols, cot)
+    tokens_parts, mlp_cols, cot = together(at.gather_core(beside_far), mlp_cols, cot)
     shape = jax.ShapeDtypeStruct
 
     half_rows = group * d_own // 2
@@ -1025,10 +1109,12 @@
     def by_row(array):
         return jnp.repeat(array, 8, axis=0)
 
-    n1_all, masks, branch_pre, conv_in, conv_low, keep_eff, part, run, summary, conv_before = kernel_call(
+    n1_all, masks, branch_pre, conv_in, conv_low, keep_eff, part, run, summary, conv_before = gathered_call(
         functools.partial(conv_kernel, rows, span, order),
+        at.c,
+        tokens_parts,
         steps,
-        [(tokens_all, tok), (w1 if order else by_feature(w1), None), (tail, None), (gain_one, None), (params, None), (w_gates, None)],
+        [(w1 if order else by_feature(w1), None), (tail, None), (gain_one, None), (params, None), (w_gates, None)],
         [(shape((tok_all, width_d), low), tok), (shape((tok_all, 8), wide), tok), (flat32, tok), (flat16, tok), (flat16, tok)]
         + [(flat32, tok)] * 3
         + [(shape((2,) + ends.shape, wide), None), (ends, None)],
@@ -1037,6 +1123,7 @@
             pltpu.VMEM((span + 8, w_slot), wide),
             pltpu.VMEM((2,) + ends.shape, wide),
         ],
+        keep=False,
     )
     summary = summary.reshape(2, rows, 8, w_slot)[:, :, 7]
     w_down = at.gather_z(mlp_down)
@@ -1061,18 +1148,20 @@
     chip_one = at.chip_product(mixed, w_out, dot_nn, exact=True)
     near_sum, cot_far = together(at.near_plane(chip_one, exact=True), cot_far)
     cot_all = at.gather_end(cot_far)
-    resid, cot_all = together(inputs + at.far_plane(near_sum), cot_all)
+    resid = inputs + at.far_plane(near_sum)
     resid, w2_parts[1] = together(resid, w2_parts[1])
     w2 = jnp.concatenate([by_feature(part) for part in w2_parts])
 
     s2 = lax.rsqrt(jnp.mean(resid * resid, axis=-1, keepdims=True) + eps_value)
     normed_two = (resid * s2 * gain_two).astype(low)
-    n2_near, w2 = together(at.gather_near(normed_two), w2)
-    n2_all, w_down = together(at.gather_end(at.gather_far(n2_near)), w_down)
-    hidden, grad_two = kernel_call(
+    n2_near, w2, cot_all = together(at.gather_near(normed_two), w2, cot_all)
+    n2_parts, w_down = together(at.gather_core(at.gather_far(n2_near)), w_down)
+    n2_all, hidden, grad_two = gathered_call(
         mlp_kernel,
+        at.c,
+        n2_parts,
         steps,
-        [(n2_all, tok), (cot_all, tok), (w2, None), (w_down, None)],
+        [(cot_all, tok), (w2, None), (w_down, None)],
         [(shape((tok_all, f_slot), low), tok), (shape((tok_all, 2 * f_slot), low), tok)],
     )
     def rows_apart(x, grad):
@@ -1099,7 +1188,7 @@
     down_part = down_sent.reshape(-1, width_d), down_kept
     gr_near, chip_three, down_part = together(at.gather_near(grad_recur), chip_three, down_part)
     down_sum = at.scatter_z(down_part)
-    gr_all, chip_three = together(at.gather_end(at.gather_far(gr_near)), chip_three)
+    gr_parts, chip_three = together(at.gather_core(at.gather_far(gr_near)), chip_three)
 
     def summed(pair):
         return pair[0].astype(wide) + pair[1].astype(wide)
@@ -1108,13 +1197,16 @@
         return at.exchange_plane(array.reshape(k_count, 2, d_own, columns))
 
 
-    grad_branch, back_part, back_run, back = kernel_call(
+    gr_all, grad_branch, back_part, back_run, back = gathered_call(
         functools.partial(back_kernel, rows, span),
+        at.c,
+        gr_parts,
         steps,
-        [(gr_all, tok), (w_out, None), (branch_pre, tok), (state, tok), (keep_eff, tok)],
+        [(w_out, None), (branch_pre, tok), (state, tok), (keep_eff, tok)],
         [(flat16, tok), (flat32, tok), (flat32, tok), (ends, None)],
         [pltpu.VMEM((2,) + ends.shape, wide)],
         backwards=True,
+        cost=70,
     )
     back = back.reshape(rows, 8, w_slot)[:, 0]
     back, mixed, near_three = together(back, mixed, at.near_parts(chip_three))

time: 745 us -> 738 us (level)
  waiting for transfers between devices: 231 us -> 217 us
    pallas_call x0 -> x3, Pallas kernels: none -> 82.8 us  [gathered_call(): pl.pallas_call(functools.partial(gathered_kernel, kernel, len(own), steps...]
    pallas_call x6 -> x3, Pallas kernels: 115 us -> 38.8 us  [kernel_call(): pl.pallas_call(kernel, out_shape=[array for array, _ in outputs], grid=(s...]
    ppermute x48, waiting for transfers between devices: 205 us -> 192 us  [to_k(): lax.ppermute(array, 'dp', [(i, i ^ flip) for i in range(self.k_count)])]
    unnamed x175 -> x187, local copies, waits for them, and re-layouts: 27.1 us -> 17.1 us
  transfers between devices with their start and end apart: 101 -> 101, of which waited for: 47 -> 45; matrix products, arithmetic and copies ran while one was open for 18% -> 20% of each run, Pallas kernels for 25% -> 25%
where the time goes in v4:
time: 738 us; the launch traced here: 728 us
  Pallas kernels  234 us (32%)
  waiting for transfers between devices  217 us (29%)
  other arithmetic  100 us (14%)
  starting transfers between devices  80.3 us (11%)
  local copies, waits for them, and re-layouts  64.6 us (9%)
  between operations  16.2 us (2%)
  matrix products  15.6 us (2%)
    ppermute x48, waiting for transfers between devices, to_k(): lax.ppermute(array, 'dp', [(i, i ^ flip) for i in range(self.k_count)])  192 us
    pallas_call x3, Pallas kernels, gathered_call(): pl.pallas_call(functools.partial(gathered_kernel, kernel, len(own), steps...  82.8 us
    pallas_call x6, Pallas kernels, half_call(): pl.pallas_call(kernel, out_shape=[array for array, _, _ in outputs], grid...  59.4 us
    ppermute x48, starting transfers between devices, to_k(): lax.ppermute(array, 'dp', [(i, i ^ flip) for i in range(self.k_count)])  51.2 us
    pallas_call x3, Pallas kernels, kernel_call(): pl.pallas_call(kernel, out_shape=[array for array, _ in outputs], grid=(s...  38.8 us
    pallas_call x2, Pallas kernels, rows_call(): pl.pallas_call(rows_kernel, out_shape=[sent, kept], grid_spec=pltpu.Prefe...  33.9 us
    ppermute x9, starting transfers between devices, to_z(): return lax.ppermute(array, 'seq', pairs)  17.7 us
    unnamed x187, local copies, waits for them, and re-layouts  17.1 us
  transfers between devices with their start and end apart: 101, of which 45 were waited for; matrix products, arithmetic and copies ran while one was open for 20% of the time, Pallas kernels for 25%

profile of v4, /device:TPU:0, one launch (start us, length us, event | category | flops | bytes accessed | tf_op | source)
XLA Modules:
  0.0 727.9 jit_solution(13997385964304306408)
XLA Ops:
  8.0 2.3 collective-permute-start
  11.2 4.5 collective-permute-start.1
  18.7 3.2 maximum_bitcast_fusion.1
  33.2 2.5 collective-permute-done.5
  35.7 3.8 collective-permute-done.4
  47.8 18.6 %collective-permute-done.7.refs_2_ = bf16[256,2176]{1,0:T(8,128)(2,1)} collective-permute-done((bf16[256,2176]{1,0:T(8,128)(2,1)}, bf16[256,2176]{1,0:T(8,128)(2,1)}, u32[]{:S(2)}, u32[]{:S(2)}) %collective-permute-start.7) | collective-permute-done | bytes 1114144 | tf_op jit(solution)/shard_map/ppermute | solution.py:133
  77.9 2.8 collective-permute-done.11
  88.4 9.7 %collective-permute-done.17.refs_4_ = bf16[128,2176]{1,0:T(8,128)(2,1)S(1)} collective-permute-done((bf16[128,2176]{1,0:T(8,128)(2,1)}, bf16[128,2176]{1,0:T(8,128)(2,1)S(1)}, u32[]{:S(2)}, u32[]{:S(2)}) %collective-permute-start.17) | collective-permute-done | bytes 557088 | tf_op jit(solution)/shard_map/ppermute | solution.py:133
  103.2 8.1 %collective-permute-done.25 = bf16[2,64,1536]{2,1,0:T(8,128)(2,1)S(1)} collective-permute-done((bf16[2,64,1536]{2,1,0:T(8,128)(2,1)S(1)}, bf16[2,64,1536]{2,1,0:T(8,128)(2,1)S(1)}, u32[]{:S(2)}, u32[]{:S(2)}) %collective-permute-start.25) | collective-permute-done | bytes 393248 | tf_op jit(solution)/shard_map/ppermute | solution.py:133
  111.3 5.1 collective-permute-done.24
  125.0 34.1 %shard_map.306 = (bf16[2048,2048]{1,0:T(8,128)(2,1)}, f32[2048,8]{1,0:T(8,128)}, f32[2048,320]{1,0:T(8,128)}, bf16[2048,320]{1,0:T(8,128)(2,1)}, bf16[2048,320]{...) custom-call(s32[1]{0:T(128)} %bitcast.core_ref.c_ref, ...), custom_call_target="tpu_custom_call" | custom-call | tf_op jit(solution)/shard_map/pallas_call | solution.py:940
  160.2 3.1 collective-permute-start.30
  177.5 8.3 %shard_map.307 = (f32[2048,320]{1,0:T(8,128)}, bf16[2048,320]{1,0:T(8,128)(2,1)}) custom-call(f32[2048,320]{1,0:T(8,128)} %get-tuple-element.287.part_ref, f32[2048,320]{1,0:T(8,128)} %get-tuple-element.288.run_ref, f32[64,320]{1,0:T(8,128)} %broadcast_bitcast_fusion.1.start_ref, f32[2048,320]{1,0:T(8,128)} %get-tuple-element.291.branch_ref.refs_11_), custom_call_target="tpu_custom_call" | custom-call | tf_op jit(solution)/shard_map/pallas_call | solution.py:868
  190.1 2.8 abs_reduce_fusion
  216.5 25.1 %collective-permute-done.37 = f16[2,256,1152]{2,1,0:T(8,128)(2,1)S(1)} collective-permute-done((f16[2,256,1152]{2,1,0:T(8,128)(2,1)S(1)}, f16[2,256,1152]{2,1,0:T(8,128)(2,1)S(1)}, u32[]{:S(2)}, u32[]{:S(2)}) %collective-permute-start.37) | collective-permute-done | bytes 1179680 | tf_op jit(solution)/shard_map/ppermute | solution.py:133
  256.6 11.3 %collective-permute-done.39 = f16[256,1152]{1,0:T(8,128)(2,1)} collective-permute-done((f16[256,1152]{1,0:T(8,128)(2,1)}, f16[256,1152]{1,0:T(8,128)(2,1)}, u32[]{:S(2)}, u32[]{:S(2)}) %collective-permute-start.39) | collective-permute-done | bytes 589856 | tf_op jit(solution)/shard_map/ppermute | solution.py:133
  282.4 3.0 pad_maximum_fusion.refs_11_.w_ref
  285.4 3.0 shard_map.308.refs_10_.cot_ref
  288.4 3.3 copy-done
  291.7 11.9 %collective-permute-done.42.refs_2_ = bf16[256,2048]{1,0:T(8,128)(2,1)} collective-permute-done((bf16[256,2048]{1,0:T(8,128)(2,1)}, bf16[256,2048]{1,0:T(8,128)(2,1)}, u32[]{:S(2)}, u32[]{:S(2)}) %collective-permute-start.42) | collective-permute-done | bytes 1048608 | tf_op jit(solution)/shard_map/ppermute | solution.py:133
  309.7 9.1 %collective-permute-done.49.refs_4_ = bf16[128,2048]{1,0:T(8,128)(2,1)} collective-permute-done((bf16[128,2048]{1,0:T(8,128)(2,1)S(1)}, bf16[128,2048]{1,0:T(8,128)(2,1)}, u32[]{:S(2)}, u32[]{:S(2)}) %collective-permute-start.49) | collective-permute-done | bytes 524320 | tf_op jit(solution)/shard_map/ppermute | solution.py:133
  320.3 6.8 all-gather.14.cloned.1.call-done.refs_12_.w_ref
  328.5 28.7 %shard_map.309 = (bf16[2048,2048]{1,0:T(8,128)(2,1)}, bf16[2048,768]{1,0:T(8,128)(2,1)}, bf16[2048,1536]{1,0:T(8,128)(2,1)}) custom-call(s32[1]{0:T(128)} %bitcast.core_ref.c_ref, bf16[256,2048]{1,0:T(8,128)(2,1)} %multiply_convert_fusion.2.refs_0_, bf16[256,2048]{1,0:T(8,128)(2,1)} %collective-permute-done.41.refs_1_, ...), custom_call_target="tpu_custom_call" | custom-call | tf_op jit(solution)/shard_map/pallas_call | solution.py:940
  357.2 11.4 %shard_map.310 = bf16[1024,2048]{1,0:T(8,128)(2,1)} custom-call(s32[1]{0:T(128)} %bitcast.81.core_ref, bf16[2048,1536]{1,0:T(8,128)(2,1)} %get-tuple-element.354.x_ref.grad_ref, bf16[2048,1536]{1,0:T(8,128)(2,1)} %pad_maximum_fusion.refs_11_.w_ref), custom_call_target="tpu_custom_call" | custom-call | tf_op jit(solution)/shard_map/pallas_call | solution.py:730
  369.7 7.1 collective-permute-done.55.got_ref
  376.8 13.8 %shard_map.311 = (f32[256,2048]{1,0:T(8,128)}, f32[256,1024]{1,0:T(8,128)}, f32[256,1024]{1,0:T(8,128)}, bf16[2,256,1024]{2,1,0:T(8,128)(2,1)}, bf16[2,256,1024]{2,1,0:T(8,128)(2,1)}) custom-call(s32[1]{0:T(128)} %bitcast.core_ref.c_ref, bf16[2048,1536]{1,0:T(8,128)(2,1)} %get-tuple-element.354.x_ref.grad_ref, ...), custom_call_target="tpu_custom_call" | custom-call | tf_op jit(solution)/shard_map/pallas_call | solution.py:730
  394.1 20.4 %shard_map.312 = (bf16[4,4,128,1536]{3,2,1,0:T(8,128)(2,1)}, f32[4,128,1536]{2,1,0:T(8,128)}) custom-call(s32[2]{0:T(128)} %pad_add_fusion.core_ref, bf16[2048,2048]{1,0:T(8,128)(2,1)} %get-tuple-element.353.x_ref, bf16[2048,1536]{1,0:T(8,128)(2,1)} %get-tuple-element.354.x_ref.grad_ref), custom_call_target="tpu_custom_call" | custom-call | tf_op jit(solution)/shard_map/pallas_call | solution.py:802
  417.7 7.4 %shard_map.313 = bf16[1024,2048]{1,0:T(8,128)(2,1)} custom-call(s32[1]{0:T(128)} %bitcast.81.core_ref, bf16[2048,768]{1,0:T(8,128)(2,1)} %get-tuple-element.369.x_ref.hidden_ref, bf16[768,2048]{1,0:T(8,128)(2,1)} %all-gather.14.cloned.1.call-done.refs_12_.w_ref), custom_call_target="tpu_custom_call" | custom-call | tf_op jit(solution)/shard_map/pallas_call | solution.py:730
  429.1 12.3 %collective-permute-done.58 = bf16[256,1024]{1,0:T(8,128)(2,1)S(1)} collective-permute-done((bf16[256,1024]{1,0:T(8,128)(2,1)S(1)}, bf16[256,1024]{1,0:T(8,128)(2,1)S(1)}, u32[]{:S(2)}, u32[]{:S(2)}) %collective-permute-start.58) | collective-permute-done | bytes 524320 | tf_op jit(solution)/shard_map/ppermute | solution.py:133
  448.3 13.7 %shard_map.315 = (bf16[4,192,2048]{2,1,0:T(8,128)(2,1)}, f32[192,2048]{1,0:T(8,128)}) custom-call(s32[1]{0:T(128)} %bitcast.82.core_ref, bf16[2048,768]{1,0:T(8,128)(2,1)} %get-tuple-element.369.x_ref.hidden_ref, bf16[2048,2048]{1,0:T(8,128)(2,1)} %copy-done), custom_call_target="tpu_custom_call" | custom-call | tf_op jit(solution)/shard_map/pallas_call | solution.py:844
  462.0 9.8 %shard_map.314 = (f32[256,2048]{1,0:T(8,128)}, f32[256,1024]{1,0:T(8,128)}, f32[256,1024]{1,0:T(8,128)}, bf16[2,256,1024]{2,1,0:T(8,128)(2,1)}, bf16[2,256,1024]{2,1,0:T(8,128)(2,1)}) custom-call(s32[1]{0:T(128)} %bitcast.core_ref.c_ref, bf16[2048,768]{1,0:T(8,128)(2,1)} %get-tuple-element.369.x_ref.hidden_ref, ...), custom_call_target="tpu_custom_call" | custom-call | tf_op jit(solution)/shard_map/pallas_call | solution.py:730
  475.5 9.3 %collective-permute-done.64.refs_4_ = bf16[128,2048]{1,0:T(8,128)(2,1)S(1)} collective-permute-done((bf16[128,2048]{1,0:T(8,128)(2,1)S(1)}, bf16[128,2048]{1,0:T(8,128)(2,1)S(1)}, u32[]{:S(2)}, u32[]{:S(2)}) %collective-permute-start.64) | collective-permute-done | bytes 524320 | tf_op jit(solution)/shard_map/ppermute | solution.py:133
  491.4 19.9 %shard_map.316 = (bf16[2048,2048]{1,0:T(8,128)(2,1)}, bf16[2048,320]{1,0:T(8,128)(2,1)}, f32[2048,320]{1,0:T(8,128)}, f32[2048,320]{1,0:T(8,128)}, f32[64,320]{1,0:T(8,128)}) custom-call(s32[1]{0:T(128)} %bitcast.core_ref.c_ref, bf16[256,2048]{1,0:T(8,128)(2,1)} %copy-done.25, bf16[256,2048]{1,0:T(8,128)(2,1)} %copy-done.33, bf16[256,2048]{1,0:T(8,128)(2,1)} %copy-done.32, ...), custom_call_target="tpu_custom_call" | custom-call | bytes 73400320 | tf_op jit(solution)/shard_map/pallas_call | solution.py:940
  519.4 8.0 %fusion.97 = bf16[320,2048]{1,0:T(8,128)(2,1)} fusion(bf16[2048,320]{1,0:T(8,128)(2,1)} %get-tuple-element.408, bf16[2048,2048]{1,0:T(8,128)(2,1)} %get-tuple-element.409), kind=kOutput, calls=%fused_computation.321 | convolution fusion | flops 2684354560 | bytes 11010048 | tf_op jit(solution)/shard_map/dot_general | solution.py:34
  531.7 2.9 collective-permute-done.75
  535.7 3.6 fusion.2
  545.0 22.4 %shard_map.317 = (bf16[2048,320]{1,0:T(8,128)(2,1)}, bf16[320,448]{1,0:T(8,128)(2,1)}) custom-call(f32[2048,320]{1,0:T(8,128)} %get-tuple-element.397.part_ref, f32[2048,320]{1,0:T(8,128)} %get-tuple-element.398.run_ref, f32[64,320]{1,0:T(8,128)} %broadcast_bitcast_fusion.carry_ref, f32[2048,320]{1,0:T(8,128)} %get-tuple-element.395.refs_12_.state_ref, ...), custom_call_target="tpu_custom_call" | custom-call | tf_op jit(solution)/shard_map/pallas_call | solution.py:868
  569.1 9.6 %collective-permute-done.77 = f32[2,64,1536]{2,1,0:T(8,128)} collective-permute-done((f32[2,64,1536]{2,1,0:T(8,128)}, f32[2,64,1536]{2,1,0:T(8,128)}, u32[]{:S(2)}, u32[]{:S(2)}) %collective-permute-start.77) | collective-permute-done | bytes 786464 | tf_op jit(solution)/shard_map/ppermute | solution.py:133
  594.3 8.2 %shard_map.318.x_ref.grad_ref = bf16[2048,640]{1,0:T(8,128)(2,1)} custom-call(bf16[2048,320]{1,0:T(8,128)(2,1)} %get-tuple-element.428.grad_ref, bf16[128,320]{1,0:T(8,128)(2,1)} %bitcast.109.halo_ref, f32[2048,8]{1,0:T(8,128)} %get-tuple-element.297.masks_ref, f32[128,8]{1,0:T(8,128)} %bitcast.434, bf16[2048,320]{1,0:T(8,128)(2,1)} %get-tuple-element.433.branch_ref, ...), custom_call_target="tpu_custom_call" | custom-call | tf_op jit(solution)/shard_map/pallas_call | solution.py:868
  602.5 3.5 fusion.27
  607.3 7.2 shard_map.319
  614.4 13.4 %shard_map.320 = (bf16[4,4,128,640]{3,2,1,0:T(8,128)(2,1)}, f32[4,128,640]{2,1,0:T(8,128)}) custom-call(s32[2]{0:T(128)} %pad_add_fusion.core_ref, bf16[2048,2048]{1,0:T(8,128)(2,1)} %get-tuple-element.445.x_ref, bf16[2048,640]{1,0:T(8,128)(2,1)} %shard_map.318.x_ref.grad_ref), custom_call_target="tpu_custom_call" | custom-call | tf_op jit(solution)/shard_map/pallas_call | solution.py:802
  627.9 9.9 %shard_map.321 = (f32[256,2048]{1,0:T(8,128)}, f32[256,1024]{1,0:T(8,128)}, f32[256,1024]{1,0:T(8,128)}, bf16[2,256,1024]{2,1,0:T(8,128)(2,1)}, bf16[2,256,1024]{2,1,0:T(8,128)(2,1)}) custom-call(s32[1]{0:T(128)} %bitcast.core_ref.c_ref, bf16[2048,640]{1,0:T(8,128)(2,1)} %shard_map.318.x_ref.grad_ref, bf16[2048,640]{1,0:T(8,128)(2,1)} %bitcast.399, ...), custom_call_target="tpu_custom_call" | custom-call | tf_op jit(solution)/shard_map/pallas_call | solution.py:730
  644.7 19.1 %collective-permute-done.84 = bf16[2,256,1024]{2,1,0:T(8,128)(2,1)} collective-permute-done((bf16[2,256,1024]{2,1,0:T(8,128)(2,1)}, bf16[2,256,1024]{2,1,0:T(8,128)(2,1)}, u32[]{:S(2)}, u32[]{:S(2)}) %collective-permute-start.84) | collective-permute-done | bytes 1048608 | tf_op jit(solution)/shard_map/ppermute | solution.py:133
  677.2 7.2 collective-permute-done.86
  684.4 2.4 fusion.19
  701.7 3.5 fusion.4
  708.8 6.9 collective-permute-done.90
  (593 shorter events, 247.6 us)
Async XLA Ops:
  7.2 59.4 %all-gather.6.cloned.1.call-start = ((), (), s32[]{:S(2)}) async-start(), calls=%async_computation.4 | async-start | bytes 2048000 | tf_op jit(solution)/shard_map/all_gather | solution.py:146
  8.0 17.2 %collective-permute-start = (bf16[2,3]{1,0:T(2,128)(2,1)S(1)}, bf16[2,3]{1,0:T(2,128)(2,1)S(1)}, u32[]{:S(2)}, u32[]{:S(2)}) collective-permute-start(bf16[2,3]{1,0:T(2,128)(2,1)S(1)} %slice.336), channel_id=1, source_target_pairs={{0,1},{1,2},{2,3},{3,4},{4,5},{5,6},{6,7},{8,9},{9,10},{10,11},{11... | collective-permute-start | bytes 44 | tf_op jit(solution)/shard_map/ppermute | solution.py:1022
  25.2 99.8 %all-gather.8.cloned.1.call-start = ((), (), s32[]{:S(2)}) async-start(), calls=%async_computation.5 | async-start | bytes 3276800 | tf_op jit(solution)/shard_map/all_gather | solution.py:146
  40.5 25.8 %collective-permute-start.7 = (bf16[256,2176]{1,0:T(8,128)(2,1)}, bf16[256,2176]{1,0:T(8,128)(2,1)}, u32[]{:S(2)}, u32[]{:S(2)}) collective-permute-start(bf16[256,2176]{1,0:T(8,128)(2,1)} %pad_maximum_fusion.10.refs_0_), channel_id=1, source_target_pairs={{0,16},{8,24},{16,0},{24,8},{1,17},{9,25},{17,1},{25,9},{2,18},{10... | collective-permute-start | bytes 3342344 | tf_op jit(solution)/shard_map/ppermute | solution.py:133
  42.1 24.5 %collective-permute-start.6 = (bf16[256,2176]{1,0:T(8,128)(2,1)}, bf16[256,2176]{1,0:T(8,128)(2,1)}, u32[]{:S(2)}, u32[]{:S(2)}) collective-permute-start(bf16[256,2176]{1,0:T(8,128)(2,1)} %pad_maximum_fusion.10.refs_0_), channel_id=1, source_target_pairs={{0,8},{8,0},{16,24},{24,16},{1,9},{9,1},{17,25},{25,17},{2,10},{10... | collective-permute-start | bytes 3342344 | tf_op jit(solution)/shard_map/ppermute | solution.py:133
  46.0 144.0 %all-gather.10.cloned.1.call-start = ((), (), s32[]{:S(2)}) async-start(), calls=%async_computation.6 | async-start | bytes 3932160 | tf_op jit(solution)/shard_map/all_gather | solution.py:146
  100.2 16.2 %collective-permute-start.24 = (bf16[2,64,1536]{2,1,0:T(8,128)(2,1)S(1)}, bf16[2,64,1536]{2,1,0:T(8,128)(2,1)S(1)}, u32[]{:S(2)}, u32[]{:S(2)}) collective-permute-start(bf16[2,64,1536]{2,1,0:T(8,128)(2,1)S(1)} %get-tuple-element.660), channel_id=1, source_target_pairs={{0,16},{8,24},{16,0},{24,8},{1,17},{9,25},{17,1},{25,9},{2,18},{10... | collective-permute-start | bytes 1179656 | tf_op jit(solution)/shard_map/ppermute | solution.py:133
  100.7 15.7 %collective-permute-start.23 = (bf16[2,64,1536]{2,1,0:T(8,128)(2,1)S(1)}, bf16[2,64,1536]{2,1,0:T(8,128)(2,1)S(1)}, u32[]{:S(2)}, u32[]{:S(2)}) collective-permute-start(bf16[2,64,1536]{2,1,0:T(8,128)(2,1)S(1)} %get-tuple-element.661), channel_id=1, source_target_pairs={{0,24},{8,16},{16,8},{24,0},{1,25},{9,17},{17,9},{25,1},{2,26},{10... | collective-permute-start | bytes 1179656 | tf_op jit(solution)/shard_map/ppermute | solution.py:133
  102.7 16.6 %collective-permute-start.18 = (bf16[256,2176]{1,0:T(8,128)(2,1)}, bf16[256,2176]{1,0:T(8,128)(2,1)S(1)}, u32[]{:S(2)}, u32[]{:S(2)}) collective-permute-start(bf16[256,2176]{1,0:T(8,128)(2,1)} %pad_maximum_fusion.10.refs_0_), channel_id=1, source_target_pairs={{0,1},{1,0},{2,3},{3,2},{4,5},{5,4},{6,7},{7,6},{8,9},{9,8},{10,11... | collective-permute-start | bytes 3342344 | tf_op jit(solution)/shard_map/ppermute | solution.py:136
  102.7 16.6 %collective-permute-start.19 = (bf16[256,2176]{1,0:T(8,128)(2,1)}, bf16[256,2176]{1,0:T(8,128)(2,1)S(1)}, u32[]{:S(2)}, u32[]{:S(2)}) collective-permute-start(bf16[256,2176]{1,0:T(8,128)(2,1)} %collective-permute-done.6.refs_1_), channel_id=1, source_target_pairs={{0,1},{1,0},{2,3},{3,2},{4,5},{5,4},{6,7},{7,6},{8,9},{9,8},{10,11... | collective-permute-start | bytes 3342344 | tf_op jit(solution)/shard_map/ppermute | solution.py:136
  121.9 152.8 %all-gather.12.cloned.1.call-start = ((), (), s32[]{:S(2)}) async-start(), calls=%async_computation.7 | async-start | bytes 3932160 | tf_op jit(solution)/shard_map/all_gather | solution.py:146
  122.1 38.1 %collective-permute-start.27 = (bf16[256,2048]{1,0:T(8,128)(2,1)S(1)}, bf16[256,2048]{1,0:T(8,128)(2,1)S(1)}, u32[]{:S(2)}, u32[]{:S(2)}) collective-permute-start(bf16[256,2048]{1,0:T(8,128)(2,1)S(1)} %bitcast.387), channel_id=1, source_target_pairs={{0,16},{8,24},{16,0},{24,8},{1,17},{9,25},{17,1},{25,9},{2,18},{10... | collective-permute-start | bytes 3145736 | tf_op jit(solution)/shard_map/ppermute | solution.py:133
  122.3 37.9 %collective-permute-start.26 = (bf16[256,2048]{1,0:T(8,128)(2,1)S(1)}, bf16[256,2048]{1,0:T(8,128)(2,1)S(1)}, u32[]{:S(2)}, u32[]{:S(2)}) collective-permute-start(bf16[256,2048]{1,0:T(8,128)(2,1)S(1)} %bitcast.388), channel_id=1, source_target_pairs={{0,8},{8,0},{16,24},{24,16},{1,9},{9,1},{17,25},{25,17},{2,10},{10... | collective-permute-start | bytes 3145736 | tf_op jit(solution)/shard_map/ppermute | solution.py:133
  160.2 14.6 %collective-permute-start.30 = (f32[2,8,320]{2,1,0:T(8,128)S(1)}, f32[2,8,320]{2,1,0:T(8,128)S(1)}, u32[]{:S(2)}, u32[]{:S(2)}) collective-permute-start(f32[2,8,320]{2,1,0:T(8,128)S(1)} %bitcast.437), channel_id=1, source_target_pairs={{0,6},{1,7},{8,14},{9,15},{16,22},{17,23},{24,30},{25,31}} | collective-permute-start | bytes 61448 | tf_op jit(solution)/shard_map/ppermute | solution.py:140
  169.7 16.1 %collective-permute-start.34 = (bf16[2,80,2048]{2,1,0:T(8,128)(2,1)}, bf16[2,80,2048]{2,1,0:T(8,128)(2,1)}, u32[]{:S(2)}, u32[]{:S(2)}) collective-permute-start(bf16[2,80,2048]{2,1,0:T(8,128)(2,1)} %get-tuple-element.672), channel_id=1, source_target_pairs={{0,1},{1,0},{2,3},{3,2},{4,5},{5,4},{6,7},{7,6},{8,9},{9,8},{10,11... | collective-permute-start | bytes 1966088 | tf_op jit(solution)/shard_map/ppermute | solution.py:136
  170.9 17.9 %collective-permute-start.33 = (f32[8,16,8]{2,1,0:T(8,128)S(1)}, f32[8,16,8]{2,1,0:T(8,128)S(1)}, u32[]{:S(2)}, u32[]{:S(2)}) collective-permute-start(f32[8,16,8]{2,1,0:T(8,128)S(1)} %slice_bitcast_fusion.17), channel_id=1, source_target_pairs={{2,0},{3,1},{4,2},{5,3},{6,4},{7,5},{10,8},{11,9},{12,10},{13,11},... | collective-permute-start | bytes 12296 | tf_op jit(solution)/shard_map/ppermute | solution.py:140
  200.8 126.3 %all-gather.14.cloned.1.call-start = ((), (), s32[]{:S(2)}) async-start(), calls=%async_computation.8 | async-start | bytes 3932160 | tf_op jit(solution)/shard_map/all_gather | solution.py:146
  213.7 28.0 %collective-permute-start.37 = (f16[2,256,1152]{2,1,0:T(8,128)(2,1)S(1)}, f16[2,256,1152]{2,1,0:T(8,128)(2,1)S(1)}, u32[]{:S(2)}, u32[]{:S(2)}) collective-permute-start(f16[2,256,1152]{2,1,0:T(8,128)(2,1)S(1)} %pad_maximum_fusion.8), channel_id=1, source_target_pairs={{0,8},{8,0},{16,24},{24,16},{1,9},{9,1},{17,25},{25,17},{2,10},{10... | collective-permute-start | bytes 3538952 | tf_op jit(solution)/shard_map/ppermute | solution.py:133
  214.9 27.7 %collective-permute-start.38 = (f16[2,256,1152]{2,1,0:T(8,128)(2,1)S(1)}, f16[2,256,1152]{2,1,0:T(8,128)(2,1)S(1)}, u32[]{:S(2)}, u32[]{:S(2)}) collective-permute-start(f16[2,256,1152]{2,1,0:T(8,128)(2,1)S(1)} %pad_maximum_fusion.9), channel_id=1, source_target_pairs={{0,16},{8,24},{16,0},{24,8},{1,17},{9,25},{17,1},{25,9},{2,18},{10... | collective-permute-start | bytes 3538952 | tf_op jit(solution)/shard_map/ppermute | solution.py:133
  255.4 272.5 %reduce-scatter.5.cloned.1.call-start = ((), (), s32[]{:S(2)}) async-start(), calls=%async_computation.9 | async-start | bytes 7864320 | tf_op jit(solution)/shard_map/reduce_scatter | solution.py:160
  256.0 22.2 %collective-permute-start.46 = (bf16[128,2048]{1,0:T(8,128)(2,1)}, bf16[128,2048]{1,0:T(8,128)(2,1)}, u32[]{:S(2)}, u32[]{:S(2)}) collective-permute-start(bf16[128,2048]{1,0:T(8,128)(2,1)} %collective-permute-done.31.refs_3_), channel_id=1, source_target_pairs={{0,1},{1,0},{2,3},{3,2},{4,5},{5,4},{6,7},{7,6},{8,9},{9,8},{10,11... | collective-permute-start | bytes 1572872 | tf_op jit(solution)/shard_map/ppermute | solution.py:136
  256.0 23.7 %collective-permute-start.47 = (bf16[128,2048]{1,0:T(8,128)(2,1)}, bf16[128,2048]{1,0:T(8,128)(2,1)}, u32[]{:S(2)}, u32[]{:S(2)}) collective-permute-start(bf16[128,2048]{1,0:T(8,128)(2,1)} %collective-permute-done.32.refs_4_), channel_id=1, source_target_pairs={{0,1},{1,0},{2,3},{3,2},{4,5},{5,4},{6,7},{7,6},{8,9},{9,8},{10,11... | collective-permute-start | bytes 1572872 | tf_op jit(solution)/shard_map/ppermute | solution.py:136
  256.5 28.9 %collective-permute-start.43 = (bf16[256,2048]{1,0:T(8,128)(2,1)S(1)}, bf16[256,2048]{1,0:T(8,128)(2,1)}, u32[]{:S(2)}, u32[]{:S(2)}) collective-permute-start(bf16[256,2048]{1,0:T(8,128)(2,1)S(1)} %bitcast.389), channel_id=1, source_target_pairs={{0,1},{1,0},{2,3},{3,2},{4,5},{5,4},{6,7},{7,6},{8,9},{9,8},{10,11... | collective-permute-start | bytes 3145736 | tf_op jit(solution)/shard_map/ppermute | solution.py:136
  267.8 17.6 %collective-permute-start.44 = (bf16[256,2048]{1,0:T(8,128)(2,1)S(1)}, bf16[256,2048]{1,0:T(8,128)(2,1)}, u32[]{:S(2)}, u32[]{:S(2)}) collective-permute-start(bf16[256,2048]{1,0:T(8,128)(2,1)S(1)} %collective-permute-done.26.refs_1_), channel_id=1, source_target_pairs={{0,1},{1,0},{2,3},{3,2},{4,5},{5,4},{6,7},{7,6},{8,9},{9,8},{10,11... | collective-permute-start | bytes 3145736 | tf_op jit(solution)/shard_map/ppermute | solution.py:136
  269.0 16.4 %collective-permute-start.45 = (bf16[256,2048]{1,0:T(8,128)(2,1)S(1)}, bf16[256,2048]{1,0:T(8,128)(2,1)}, u32[]{:S(2)}, u32[]{:S(2)}) collective-permute-start(bf16[256,2048]{1,0:T(8,128)(2,1)S(1)} %collective-permute-done.27.refs_2_), channel_id=1, source_target_pairs={{0,1},{1,0},{2,3},{3,2},{4,5},{5,4},{6,7},{7,6},{8,9},{9,8},{10,11... | collective-permute-start | bytes 3145736 | tf_op jit(solution)/shard_map/ppermute | solution.py:136
  278.2 25.5 %collective-permute-start.42 = (bf16[256,2048]{1,0:T(8,128)(2,1)}, bf16[256,2048]{1,0:T(8,128)(2,1)}, u32[]{:S(2)}, u32[]{:S(2)}) collective-permute-start(bf16[256,2048]{1,0:T(8,128)(2,1)} %multiply_convert_fusion.2.refs_0_), channel_id=1, source_target_pairs={{0,16},{8,24},{16,0},{24,8},{1,17},{9,25},{17,1},{25,9},{2,18},{10... | collective-permute-start | bytes 3145736 | tf_op jit(solution)/shard_map/ppermute | solution.py:133
  279.7 25.1 %collective-permute-start.41 = (bf16[256,2048]{1,0:T(8,128)(2,1)}, bf16[256,2048]{1,0:T(8,128)(2,1)}, u32[]{:S(2)}, u32[]{:S(2)}) collective-permute-start(bf16[256,2048]{1,0:T(8,128)(2,1)} %multiply_convert_fusion.2.refs_0_), channel_id=1, source_target_pairs={{0,8},{8,0},{16,24},{24,16},{1,9},{9,1},{17,25},{25,17},{2,10},{10... | collective-permute-start | bytes 3145736 | tf_op jit(solution)/shard_map/ppermute | solution.py:133
  309.2 17.9 %collective-permute-start.50 = (bf16[256,2048]{1,0:T(8,128)(2,1)}, bf16[256,2048]{1,0:T(8,128)(2,1)S(1)}, u32[]{:S(2)}, u32[]{:S(2)}) collective-permute-start(bf16[256,2048]{1,0:T(8,128)(2,1)} %multiply_convert_fusion.2.refs_0_), channel_id=1, source_target_pairs={{0,1},{1,0},{2,3},{3,2},{4,5},{5,4},{6,7},{7,6},{8,9},{9,8},{10,11... | collective-permute-start | bytes 3145736 | tf_op jit(solution)/shard_map/ppermute | solution.py:136
  309.2 18.0 %collective-permute-start.51 = (bf16[256,2048]{1,0:T(8,128)(2,1)}, bf16[256,2048]{1,0:T(8,128)(2,1)S(1)}, u32[]{:S(2)}, u32[]{:S(2)}) collective-permute-start(bf16[256,2048]{1,0:T(8,128)(2,1)} %collective-permute-done.41.refs_1_), channel_id=1, source_target_pairs={{0,1},{1,0},{2,3},{3,2},{4,5},{5,4},{6,7},{7,6},{8,9},{9,8},{10,11... | collective-permute-start | bytes 3145736 | tf_op jit(solution)/shard_map/ppermute | solution.py:136
  309.7 17.5 %collective-permute-start.52 = (bf16[256,2048]{1,0:T(8,128)(2,1)}, bf16[256,2048]{1,0:T(8,128)(2,1)}, u32[]{:S(2)}, u32[]{:S(2)}) collective-permute-start(bf16[256,2048]{1,0:T(8,128)(2,1)} %collective-permute-done.42.refs_2_), channel_id=1, source_target_pairs={{0,1},{1,0},{2,3},{3,2},{4,5},{5,4},{6,7},{7,6},{8,9},{9,8},{10,11... | collective-permute-start | bytes 3145736 | tf_op jit(solution)/shard_map/ppermute | solution.py:136
  390.6 25.6 %collective-permute-start.56 = (bf16[2,256,1024]{2,1,0:T(8,128)(2,1)}, bf16[2,256,1024]{2,1,0:T(8,128)(2,1)S(1)}, u32[]{:S(2)}, u32[]{:S(2)}) collective-permute-start(bf16[2,256,1024]{2,1,0:T(8,128)(2,1)} %get-tuple-element.349), channel_id=1, source_target_pairs={{0,8},{8,0},{16,24},{24,16},{1,9},{9,1},{17,25},{25,17},{2,10},{10... | collective-permute-start | bytes 3145736 | tf_op jit(solution)/shard_map/ppermute | solution.py:133
  392.1 25.4 %collective-permute-start.57 = (bf16[2,256,1024]{2,1,0:T(8,128)(2,1)}, bf16[2,256,1024]{2,1,0:T(8,128)(2,1)S(1)}, u32[]{:S(2)}, u32[]{:S(2)}) collective-permute-start(bf16[2,256,1024]{2,1,0:T(8,128)(2,1)} %get-tuple-element.350), channel_id=1, source_target_pairs={{0,16},{8,24},{16,0},{24,8},{1,17},{9,25},{17,1},{25,9},{2,18},{10... | collective-permute-start | bytes 3145736 | tf_op jit(solution)/shard_map/ppermute | solution.py:133
  417.5 247.6 %reduce-scatter.9.cloned.1.call-start = ((), (), s32[]{:S(2)}) async-start(), calls=%async_computation.11 | async-start | bytes 3932160 | tf_op jit(solution)/shard_map/reduce_scatter | solution.py:160
  425.1 36.9 %collective-permute-start.62 = (bf16[1024,2048]{1,0:T(8,128)(2,1)}, bf16[1024,2048]{1,0:T(8,128)(2,1)}, u32[]{:S(2)}, u32[]{:S(2)}) collective-permute-start(bf16[1024,2048]{1,0:T(8,128)(2,1)} %shard_map.313), channel_id=1, source_target_pairs={{0,1},{1,0},{2,3},{3,2},{4,5},{5,4},{6,7},{7,6},{8,9},{9,8},{10,11... | collective-permute-start | bytes 12582920 | tf_op jit(solution)/shard_map/ppermute | solution.py:136
  447.1 24.6 %collective-permute-start.61 = (bf16[256,2048]{1,0:T(8,128)(2,1)S(1)}, bf16[256,2048]{1,0:T(8,128)(2,1)S(1)}, u32[]{:S(2)}, u32[]{:S(2)}) collective-permute-start(bf16[256,2048]{1,0:T(8,128)(2,1)S(1)} %get-tuple-element.385.refs_0_), channel_id=1, source_target_pairs={{0,16},{8,24},{16,0},{24,8},{1,17},{9,25},{17,1},{25,9},{2,18},{10... | collective-permute-start | bytes 3145736 | tf_op jit(solution)/shard_map/ppermute | solution.py:133
  447.7 24.3 %collective-permute-start.60 = (bf16[256,2048]{1,0:T(8,128)(2,1)S(1)}, bf16[256,2048]{1,0:T(8,128)(2,1)S(1)}, u32[]{:S(2)}, u32[]{:S(2)}) collective-permute-start(bf16[256,2048]{1,0:T(8,128)(2,1)S(1)} %get-tuple-element.385.refs_0_), channel_id=1, source_target_pairs={{0,8},{8,0},{16,24},{24,16},{1,9},{9,1},{17,25},{25,17},{2,10},{10... | collective-permute-start | bytes 3145736 | tf_op jit(solution)/shard_map/ppermute | solution.py:133
  489.0 25.4 %collective-permute-start.70 = (bf16[2,256,1024]{2,1,0:T(8,128)(2,1)}, bf16[2,256,1024]{2,1,0:T(8,128)(2,1)S(1)}, u32[]{:S(2)}, u32[]{:S(2)}) collective-permute-start(bf16[2,256,1024]{2,1,0:T(8,128)(2,1)} %get-tuple-element.403), channel_id=1, source_target_pairs={{0,8},{8,0},{16,24},{24,16},{1,9},{9,1},{17,25},{25,17},{2,10},{10... | collective-permute-start | bytes 3145736 | tf_op jit(solution)/shard_map/ppermute | solution.py:133
  489.9 25.5 %collective-permute-start.71 = (bf16[2,256,1024]{2,1,0:T(8,128)(2,1)}, bf16[2,256,1024]{2,1,0:T(8,128)(2,1)}, u32[]{:S(2)}, u32[]{:S(2)}) collective-permute-start(bf16[2,256,1024]{2,1,0:T(8,128)(2,1)} %get-tuple-element.404), channel_id=1, source_target_pairs={{0,16},{8,24},{16,0},{24,8},{1,17},{9,25},{17,1},{25,9},{2,18},{10... | collective-permute-start | bytes 3145736 | tf_op jit(solution)/shard_map/ppermute | solution.py:133
  531.2 155.8 %reduce-scatter.11.cloned.1.call-start = ((), (), s32[]{:S(2)}) async-start(), calls=%async_computation.12 | async-start | bytes 2048000 | tf_op jit(solution)/shard_map/reduce_scatter | solution.py:160
  540.8 28.3 %collective-permute-start.78 = (f32[2,64,1536]{2,1,0:T(8,128)}, f32[2,64,1536]{2,1,0:T(8,128)S(1)}, u32[]{:S(2)}, u32[]{:S(2)}) collective-permute-start(f32[2,64,1536]{2,1,0:T(8,128)} %get-tuple-element.628), channel_id=1, source_target_pairs={{0,8},{8,0},{16,24},{24,16},{1,9},{9,1},{17,25},{25,17},{2,10},{10... | collective-permute-start | bytes 2359304 | tf_op jit(solution)/shard_map/ppermute | solution.py:133
  542.3 36.5 %collective-permute-start.77 = (f32[2,64,1536]{2,1,0:T(8,128)}, f32[2,64,1536]{2,1,0:T(8,128)}, u32[]{:S(2)}, u32[]{:S(2)}) collective-permute-start(f32[2,64,1536]{2,1,0:T(8,128)} %get-tuple-element.629), channel_id=1, source_target_pairs={{0,16},{8,24},{16,0},{24,8},{1,17},{9,25},{17,1},{25,9},{2,18},{10... | collective-permute-start | bytes 2359304 | tf_op jit(solution)/shard_map/ppermute | solution.py:133
  543.8 35.0 %collective-permute-start.76 = (f32[2,64,1536]{2,1,0:T(8,128)}, f32[2,64,1536]{2,1,0:T(8,128)}, u32[]{:S(2)}, u32[]{:S(2)}) collective-permute-start(f32[2,64,1536]{2,1,0:T(8,128)} %get-tuple-element.630), channel_id=1, source_target_pairs={{0,24},{8,16},{16,8},{24,0},{1,25},{9,17},{17,9},{25,1},{2,26},{10... | collective-permute-start | bytes 2359304 | tf_op jit(solution)/shard_map/ppermute | solution.py:133
  569.1 21.2 %collective-permute-start.80 = (bf16[2,80,2496]{2,1,0:T(8,128)(2,1)S(1)}, bf16[2,80,2496]{2,1,0:T(8,128)(2,1)S(1)}, u32[]{:S(2)}, u32[]{:S(2)}) collective-permute-start(bf16[2,80,2496]{2,1,0:T(8,128)(2,1)S(1)} %get-tuple-element.654), channel_id=1, source_target_pairs={{0,1},{1,0},{2,3},{3,2},{4,5},{5,4},{6,7},{7,6},{8,9},{9,8},{10,11... | collective-permute-start | bytes 2396168 | tf_op jit(solution)/shard_map/ppermute | solution.py:136
  594.3 93.9 %reduce-scatter.7.cloned.1.call-start = ((), (), s32[]{:S(2)}) async-start(), calls=%async_computation.10 | async-start | bytes 3276800 | tf_op jit(solution)/shard_map/reduce_scatter | solution.py:160
  637.8 26.1 %collective-permute-start.84 = (bf16[2,256,1024]{2,1,0:T(8,128)(2,1)}, bf16[2,256,1024]{2,1,0:T(8,128)(2,1)}, u32[]{:S(2)}, u32[]{:S(2)}) collective-permute-start(bf16[2,256,1024]{2,1,0:T(8,128)(2,1)} %get-tuple-element.454), channel_id=1, source_target_pairs={{0,8},{8,0},{16,24},{24,16},{1,9},{9,1},{17,25},{25,17},{2,10},{10... | collective-permute-start | bytes 3145736 | tf_op jit(solution)/shard_map/ppermute | solution.py:133
  639.4 25.7 %collective-permute-start.85 = (bf16[2,256,1024]{2,1,0:T(8,128)(2,1)}, bf16[2,256,1024]{2,1,0:T(8,128)(2,1)}, u32[]{:S(2)}, u32[]{:S(2)}) collective-permute-start(bf16[2,256,1024]{2,1,0:T(8,128)(2,1)} %get-tuple-element.455), channel_id=1, source_target_pairs={{0,16},{8,24},{16,0},{24,8},{1,17},{9,25},{17,1},{25,9},{2,18},{10... | collective-permute-start | bytes 3145736 | tf_op jit(solution)/shard_map/ppermute | solution.py:133
  699.7 16.0 %collective-permute-start.90 = (f32[2,64,640]{2,1,0:T(8,128)S(1)}, f32[2,64,640]{2,1,0:T(8,128)S(1)}, u32[]{:S(2)}, u32[]{:S(2)}) collective-permute-start(f32[2,64,640]{2,1,0:T(8,128)S(1)} %get-tuple-element.667), channel_id=1, source_target_pairs={{0,16},{8,24},{16,0},{24,8},{1,17},{9,25},{17,1},{25,9},{2,18},{10... | collective-permute-start | bytes 983048 | tf_op jit(solution)/shard_map/ppermute | solution.py:133
  701.2 14.5 %collective-permute-start.89 = (f32[2,64,640]{2,1,0:T(8,128)S(1)}, f32[2,64,640]{2,1,0:T(8,128)S(1)}, u32[]{:S(2)}, u32[]{:S(2)}) collective-permute-start(f32[2,64,640]{2,1,0:T(8,128)S(1)} %get-tuple-element.668), channel_id=1, source_target_pairs={{0,24},{8,16},{16,8},{24,0},{1,25},{9,17},{17,9},{25,1},{2,26},{10... | collective-permute-start | bytes 983048 | tf_op jit(solution)/shard_map/ppermute | solution.py:133
  (143 other events, 976.9 us)
Sparse Core Ops, SparseCore 0:
  25.3 37.3 all-gather.5
  64.9 53.6 all-gather.7
  121.8 63.6 all-gather.9
  200.9 62.5 all-gather.11
  265.0 62.1 all-gather.13
  417.6 110.2 reduce-scatter.4
  531.4 64.5 reduce-scatter.8
  598.2 36.3 reduce-scatter.10
  637.0 51.1 reduce-scatter.6

commit v5 on v4

--- a/solution.py
+++ b/solution.py
@@ -196,6 +196,13 @@
         for part in near + second:
             total = total + part.astype(wide)
         return total
+
+    def sum_z(self, array):
+        if self.z_count != 4:
+            return lax.psum(array, AXES, axis_index_groups=self.z_groups)
+        for flip in range(1, 3):
+            array = array + lax.ppermute(array, "seq", self.z_pairs([(z, z ^ flip) for z in range(4)]))
+        return array
 
     def gather_seq_small(self, array):
         if self.s_count != 8:
@@ -616,7 +623,7 @@
 
 def adjoint_kernel(
     rows, span, part_ref, run_ref, carry_ref, state_ref, start_ref, low_ref, gates_ref, params_ref,
-    masks_ref, in_ref, before_ref, grad_conv_ref, small_ref, gates_grad_ref, sums_ref, line, ends, tail,
+    masks_ref, in_ref, before_ref, grad_conv_ref, small_ref, vectors_ref, gates_grad_ref, sums_ref, line, ends, tail,
 ):
     step = pl.program_id(0)
     width = low_ref.shape[1]
@@ -672,13 +679,13 @@
 
     @pl.when(step == pl.num_programs(0) - 1)
     def _():
-        block = small_ref.shape[1] // 2 - 64
+        block = small_ref.shape[1] // 2
         for head in range(width // block):
             at = slice(head * block, (head + 1) * block)
             small_ref[at, :block] = gates_grad_ref[at, at].astype(low)
             then = slice(width + head * block, width + (head + 1) * block)
-            small_ref[at, block : 2 * block] = gates_grad_ref[at, then].astype(low)
-        small_ref[:, 2 * block :] = sums_ref[...].T[:width].astype(low)
+            small_ref[at, block:] = gates_grad_ref[at, then].astype(low)
+        vectors_ref[...] = sums_ref[...]
 
 
 def conv_back_kernel(rows, span, grad_ref, halo_ref, masks_ref, halo_masks_ref, branch_ref, params_ref, one_ref, line):
@@ -1227,7 +1234,7 @@
     mlp_pairs = at.exchange_core(summed(w2_sum).reshape(k_count, 2, d_own, 2 * f_slot))
     carry_in, mlp_pairs = together(carry_in, mlp_pairs)
     mlp_back = at.exchange_dp(mlp_pairs)
-    grad_conv, rec_small = kernel_call(
+    grad_conv, rec_small, vectors = kernel_call(
         functools.partial(adjoint_kernel, rows, span),
         steps,
         [
@@ -1243,16 +1250,18 @@
             (conv_in, tok),
             (conv_before, None),
         ],
-        [(flat16, tok), (shape((w_slot, 2 * BS + 128), low), None)],
+        [(flat16, tok), (shape((w_slot, 2 * BS), low), None), (shape((8, w_slot), wide), None)],
         [
             pltpu.VMEM((w_slot, 2 * w_slot), wide),
-            pltpu.VMEM((128, w_slot), wide),
+            pltpu.VMEM((8, w_slot), wide),
             pltpu.VMEM((span + 8, w_slot), wide),
             pltpu.VMEM(ends.shape, wide),
             pltpu.VMEM(ends.shape, wide),
         ],
     )
-    grad_conv, near_three, mlp_back = together(grad_conv, near_three, mlp_back)
+    grad_conv, near_three, mlp_back, rec_small, vectors = together(
+        grad_conv, near_three, mlp_back, rec_small, vectors
+    )
     block_out = (resid + at.far_product(near_three)).astype(low)
     head = at.to_z(grad_conv.reshape(2, rows, span, w_slot)[0, :, :16], -1).reshape(rows * 16, w_slot)
     rec_part = at.own_apart(by_owner(jnp.concatenate([grad_out.astype(low), rec_small], axis=1)), 0)
@@ -1276,7 +1285,13 @@
     mlp_whole = jax.ShapeDtypeStruct(mlp_gate.shape, wide)
     join = functools.partial(join_kernel, k_count, z_count)
     grad_gate_w, grad_up_w = in_vmem(join, (mlp_back,), (mlp_whole, mlp_whole))
-    near_one, grad_gate_w, grad_up_w, down_sum = together(near_one, grad_gate_w, grad_up_w, down_sum)
+    vectors = at.sum_z(vectors)
+    vectors = at.by_core(vectors, at.to_core(vectors))
+    near_one, grad_gate_w, grad_up_w, down_sum, vectors = together(
+        near_one, grad_gate_w, grad_up_w, down_sum, vectors
+    )
+    vectors = lax.dynamic_index_in_dim(vectors, at.s // z_count, 0, False)
+    grad_small = lax.dynamic_slice_in_dim(vectors, at.s % z_count * w_own, w_own, 1)
     grad_n1 = at.far_product(near_one)
     w1_sum, grad_n1, rec_sum = together(w1_sum, grad_n1, rec_sum)
     rec_pairs = at.exchange_core(summed(w1_sum).reshape(k_count, 2, d_own, 2 * w_slot))
@@ -1292,7 +1307,6 @@
     grad_out_w = rec_rows[:, :width_d]
     grad_rate_w = rec_rows[:, width_d : width_d + BS]
     grad_igate_w = rec_rows[:, width_d + BS : width_d + 2 * BS]
-    grad_small = rec_rows[:, width_d + 2 * BS : width_d + 2 * BS + taps + 4].T
     grad_down = summed(down_sum)
     rec_back = jnp.moveaxis(rec_back, 2, 0)
     grad_branch_w = rec_back[..., :w_slot].reshape(d_own, width_r)

time: 738 us -> 739 us (level)
  other arithmetic: 100 us -> 89.9 us
  waiting for transfers between devices: 217 us -> 226 us
    ppermute x34 -> x35, waiting for transfers between devices: 15.9 us -> 16.1 us  [to_core(): return lax.ppermute(array, 'seq', [(i, i ^ 1) for i in range(self.s_count)])]
    unnamed x187 -> x180, local copies, waits for them, and re-layouts: 17.1 us -> 17.2 us
  transfers between devices with their start and end apart: 101 -> 104, of which waited for: 45 -> 50; matrix products, arithmetic and copies ran while one was open for 20% -> 19% of each run, Pallas kernels for 25% -> 25%
where the time goes in v5:
time: 739 us; the launch traced here: 729 us
  Pallas kernels  234 us (32%)
  waiting for transfers between devices  226 us (31%)
  other arithmetic  89.9 us (12%)
  starting transfers between devices  85.3 us (12%)
  local copies, waits for them, and re-layouts  62.2 us (8%)
  between operations  16.3 us (2%)
  matrix products  15.7 us (2%)
    ppermute x48, waiting for transfers between devices, to_k(): lax.ppermute(array, 'dp', [(i, i ^ flip) for i in range(self.k_count)])  198 us
    pallas_call x3, Pallas kernels, gathered_call(): pl.pallas_call(functools.partial(gathered_kernel, kernel, len(own), steps...  82.7 us
    pallas_call x6, Pallas kernels, half_call(): pl.pallas_call(kernel, out_shape=[array for array, _, _ in outputs], grid...  59.3 us
    ppermute x48, starting transfers between devices, to_k(): lax.ppermute(array, 'dp', [(i, i ^ flip) for i in range(self.k_count)])  51.8 us
    pallas_call x3, Pallas kernels, kernel_call(): pl.pallas_call(kernel, out_shape=[array for array, _ in outputs], grid=(s...  38.6 us
    pallas_call x2, Pallas kernels, rows_call(): pl.pallas_call(rows_kernel, out_shape=[sent, kept], grid_spec=pltpu.Prefe...  33.9 us
    ppermute x9, starting transfers between devices, to_z(): return lax.ppermute(array, 'seq', pairs)  17.8 us
    unnamed x180, local copies, waits for them, and re-layouts  17.2 us
  transfers between devices with their start and end apart: 104, of which 50 were waited for; matrix products, arithmetic and copies ran while one was open for 19% of the time, Pallas kernels for 25%

profile of v5, /device:TPU:0, one launch (start us, length us, event | category | flops | bytes accessed | tf_op | source)
XLA Modules:
  0.0 729.0 jit_solution(11035166121251322655)
XLA Ops:
  11.2 4.5 collective-permute-start.1
  18.7 3.2 maximum_bitcast_fusion.1
  33.2 2.5 collective-permute-done.5
  35.7 3.8 collective-permute-done.4
  47.8 18.6 %collective-permute-done.7.refs_2_ = bf16[256,2176]{1,0:T(8,128)(2,1)} collective-permute-done((bf16[256,2176]{1,0:T(8,128)(2,1)}, bf16[256,2176]{1,0:T(8,128)(2,1)}, u32[]{:S(2)}, u32[]{:S(2)}) %collective-permute-start.7) | collective-permute-done | bytes 1114144 | tf_op jit(solution)/shard_map/ppermute | solution.py:133
  77.9 2.8 collective-permute-done.11
  88.4 9.7 %collective-permute-done.17.refs_4_ = bf16[128,2176]{1,0:T(8,128)(2,1)S(1)} collective-permute-done((bf16[128,2176]{1,0:T(8,128)(2,1)}, bf16[128,2176]{1,0:T(8,128)(2,1)S(1)}, u32[]{:S(2)}, u32[]{:S(2)}) %collective-permute-start.17) | collective-permute-done | bytes 557088 | tf_op jit(solution)/shard_map/ppermute | solution.py:133
  103.2 8.1 %collective-permute-done.25 = bf16[2,64,1536]{2,1,0:T(8,128)(2,1)S(1)} collective-permute-done((bf16[2,64,1536]{2,1,0:T(8,128)(2,1)S(1)}, bf16[2,64,1536]{2,1,0:T(8,128)(2,1)S(1)}, u32[]{:S(2)}, u32[]{:S(2)}) %collective-permute-start.25) | collective-permute-done | bytes 393248 | tf_op jit(solution)/shard_map/ppermute | solution.py:133
  111.3 5.1 collective-permute-done.24
  125.0 34.1 %shard_map.306 = (bf16[2048,2048]{1,0:T(8,128)(2,1)}, f32[2048,8]{1,0:T(8,128)}, f32[2048,320]{1,0:T(8,128)}, bf16[2048,320]{1,0:T(8,128)(2,1)}, bf16[2048,320]{...) custom-call(s32[1]{0:T(128)} %bitcast.core_ref.c_ref, ...), custom_call_target="tpu_custom_call" | custom-call | tf_op jit(solution)/shard_map/pallas_call | solution.py:947
  160.2 3.1 collective-permute-start.30
  177.5 8.3 %shard_map.307 = (f32[2048,320]{1,0:T(8,128)}, bf16[2048,320]{1,0:T(8,128)(2,1)}) custom-call(f32[2048,320]{1,0:T(8,128)} %get-tuple-element.291.part_ref, f32[2048,320]{1,0:T(8,128)} %get-tuple-element.292.run_ref, f32[64,320]{1,0:T(8,128)} %broadcast_bitcast_fusion.1.start_ref, f32[2048,320]{1,0:T(8,128)} %get-tuple-element.295.branch_ref.refs_11_), custom_call_target="tpu_custom_call" | custom-call | tf_op jit(solution)/shard_map/pallas_call | solution.py:875
  190.1 2.8 abs_reduce_fusion
  216.5 25.1 %collective-permute-done.37 = f16[2,256,1152]{2,1,0:T(8,128)(2,1)S(1)} collective-permute-done((f16[2,256,1152]{2,1,0:T(8,128)(2,1)S(1)}, f16[2,256,1152]{2,1,0:T(8,128)(2,1)S(1)}, u32[]{:S(2)}, u32[]{:S(2)}) %collective-permute-start.37) | collective-permute-done | bytes 1179680 | tf_op jit(solution)/shard_map/ppermute | solution.py:133
  256.6 11.3 %collective-permute-done.39 = f16[256,1152]{1,0:T(8,128)(2,1)} collective-permute-done((f16[256,1152]{1,0:T(8,128)(2,1)}, f16[256,1152]{1,0:T(8,128)(2,1)}, u32[]{:S(2)}, u32[]{:S(2)}) %collective-permute-start.39) | collective-permute-done | bytes 589856 | tf_op jit(solution)/shard_map/ppermute | solution.py:133
  282.5 3.0 pad_maximum_fusion.refs_11_.w_ref
  285.5 3.0 shard_map.308.refs_10_.cot_ref
  288.4 3.3 copy-done
  291.7 12.0 %collective-permute-done.42.refs_2_ = bf16[256,2048]{1,0:T(8,128)(2,1)} collective-permute-done((bf16[256,2048]{1,0:T(8,128)(2,1)}, bf16[256,2048]{1,0:T(8,128)(2,1)}, u32[]{:S(2)}, u32[]{:S(2)}) %collective-permute-start.42) | collective-permute-done | bytes 1048608 | tf_op jit(solution)/shard_map/ppermute | solution.py:133
  309.8 9.1 %collective-permute-done.49.refs_4_ = bf16[128,2048]{1,0:T(8,128)(2,1)} collective-permute-done((bf16[128,2048]{1,0:T(8,128)(2,1)S(1)}, bf16[128,2048]{1,0:T(8,128)(2,1)}, u32[]{:S(2)}, u32[]{:S(2)}) %collective-permute-start.49) | collective-permute-done | bytes 524320 | tf_op jit(solution)/shard_map/ppermute | solution.py:133
  320.4 6.8 all-gather.14.cloned.1.call-done.refs_12_.w_ref
  328.5 28.7 %shard_map.309 = (bf16[2048,2048]{1,0:T(8,128)(2,1)}, bf16[2048,768]{1,0:T(8,128)(2,1)}, bf16[2048,1536]{1,0:T(8,128)(2,1)}) custom-call(s32[1]{0:T(128)} %bitcast.core_ref.c_ref, bf16[256,2048]{1,0:T(8,128)(2,1)} %multiply_convert_fusion.2.refs_0_, bf16[256,2048]{1,0:T(8,128)(2,1)} %collective-permute-done.41.refs_1_, ...), custom_call_target="tpu_custom_call" | custom-call | tf_op jit(solution)/shard_map/pallas_call | solution.py:947
  357.2 11.4 %shard_map.310 = bf16[1024,2048]{1,0:T(8,128)(2,1)} custom-call(s32[1]{0:T(128)} %bitcast.81.core_ref, bf16[2048,1536]{1,0:T(8,128)(2,1)} %get-tuple-element.358.x_ref.grad_ref, bf16[2048,1536]{1,0:T(8,128)(2,1)} %pad_maximum_fusion.refs_11_.w_ref), custom_call_target="tpu_custom_call" | custom-call | tf_op jit(solution)/shard_map/pallas_call | solution.py:737
  369.7 7.1 collective-permute-done.55.got_ref
  376.8 13.8 %shard_map.311 = (f32[256,2048]{1,0:T(8,128)}, f32[256,1024]{1,0:T(8,128)}, f32[256,1024]{1,0:T(8,128)}, bf16[2,256,1024]{2,1,0:T(8,128)(2,1)}, bf16[2,256,1024]{2,1,0:T(8,128)(2,1)}) custom-call(s32[1]{0:T(128)} %bitcast.core_ref.c_ref, bf16[2048,1536]{1,0:T(8,128)(2,1)} %get-tuple-element.358.x_ref.grad_ref, ...), custom_call_target="tpu_custom_call" | custom-call | tf_op jit(solution)/shard_map/pallas_call | solution.py:737
  394.2 20.4 %shard_map.312 = (bf16[4,4,128,1536]{3,2,1,0:T(8,128)(2,1)}, f32[4,128,1536]{2,1,0:T(8,128)}) custom-call(s32[2]{0:T(128)} %pad_add_fusion.core_ref, bf16[2048,2048]{1,0:T(8,128)(2,1)} %get-tuple-element.357.x_ref, bf16[2048,1536]{1,0:T(8,128)(2,1)} %get-tuple-element.358.x_ref.grad_ref), custom_call_target="tpu_custom_call" | custom-call | tf_op jit(solution)/shard_map/pallas_call | solution.py:809
  417.7 7.4 %shard_map.313 = bf16[1024,2048]{1,0:T(8,128)(2,1)} custom-call(s32[1]{0:T(128)} %bitcast.81.core_ref, bf16[2048,768]{1,0:T(8,128)(2,1)} %get-tuple-element.373.x_ref.hidden_ref, bf16[768,2048]{1,0:T(8,128)(2,1)} %all-gather.14.cloned.1.call-done.refs_12_.w_ref), custom_call_target="tpu_custom_call" | custom-call | tf_op jit(solution)/shard_map/pallas_call | solution.py:737
  429.1 12.3 %collective-permute-done.58 = bf16[256,1024]{1,0:T(8,128)(2,1)S(1)} collective-permute-done((bf16[256,1024]{1,0:T(8,128)(2,1)S(1)}, bf16[256,1024]{1,0:T(8,128)(2,1)S(1)}, u32[]{:S(2)}, u32[]{:S(2)}) %collective-permute-start.58) | collective-permute-done | bytes 524320 | tf_op jit(solution)/shard_map/ppermute | solution.py:133
  448.3 13.7 %shard_map.315 = (bf16[4,192,2048]{2,1,0:T(8,128)(2,1)}, f32[192,2048]{1,0:T(8,128)}) custom-call(s32[1]{0:T(128)} %bitcast.82.core_ref, bf16[2048,768]{1,0:T(8,128)(2,1)} %get-tuple-element.373.x_ref.hidden_ref, bf16[2048,2048]{1,0:T(8,128)(2,1)} %copy-done), custom_call_target="tpu_custom_call" | custom-call | tf_op jit(solution)/shard_map/pallas_call | solution.py:851
  462.0 9.7 %shard_map.314 = (f32[256,2048]{1,0:T(8,128)}, f32[256,1024]{1,0:T(8,128)}, f32[256,1024]{1,0:T(8,128)}, bf16[2,256,1024]{2,1,0:T(8,128)(2,1)}, bf16[2,256,1024]{2,1,0:T(8,128)(2,1)}) custom-call(s32[1]{0:T(128)} %bitcast.core_ref.c_ref, bf16[2048,768]{1,0:T(8,128)(2,1)} %get-tuple-element.373.x_ref.hidden_ref, ...), custom_call_target="tpu_custom_call" | custom-call | tf_op jit(solution)/shard_map/pallas_call | solution.py:737
  475.5 9.2 %collective-permute-done.64.refs_4_ = bf16[128,2048]{1,0:T(8,128)(2,1)S(1)} collective-permute-done((bf16[128,2048]{1,0:T(8,128)(2,1)S(1)}, bf16[128,2048]{1,0:T(8,128)(2,1)S(1)}, u32[]{:S(2)}, u32[]{:S(2)}) %collective-permute-start.64) | collective-permute-done | bytes 524320 | tf_op jit(solution)/shard_map/ppermute | solution.py:133
  491.4 19.9 %shard_map.316 = (bf16[2048,2048]{1,0:T(8,128)(2,1)}, bf16[2048,320]{1,0:T(8,128)(2,1)}, f32[2048,320]{1,0:T(8,128)}, f32[2048,320]{1,0:T(8,128)}, f32[64,320]{1,0:T(8,128)}) custom-call(s32[1]{0:T(128)} %bitcast.core_ref.c_ref, bf16[256,2048]{1,0:T(8,128)(2,1)} %copy-done.22, bf16[256,2048]{1,0:T(8,128)(2,1)} %copy-done.29, bf16[256,2048]{1,0:T(8,128)(2,1)} %copy-done.28, ...), custom_call_target="tpu_custom_call" | custom-call | bytes 73400320 | tf_op jit(solution)/shard_map/pallas_call | solution.py:947
  519.4 8.0 %fusion.97 = bf16[320,2048]{1,0:T(8,128)(2,1)} fusion(bf16[2048,320]{1,0:T(8,128)(2,1)} %get-tuple-element.412, bf16[2048,2048]{1,0:T(8,128)(2,1)} %get-tuple-element.413), kind=kOutput, calls=%fused_computation.323 | convolution fusion | flops 2684354560 | bytes 11010048 | tf_op jit(solution)/shard_map/dot_general | solution.py:34
  531.4 3.1 collective-permute-done.75
  535.7 3.8 fusion.2
  545.3 22.2 %shard_map.317 = (bf16[2048,320]{1,0:T(8,128)(2,1)}, bf16[320,320]{1,0:T(8,128)(2,1)}, f32[8,320]{1,0:T(8,128)}) custom-call(f32[2048,320]{1,0:T(8,128)} %get-tuple-element.401.part_ref, f32[2048,320]{1,0:T(8,128)} %get-tuple-element.402.run_ref, f32[64,320]{1,0:T(8,128)} %broadcast_bitcast_fusion.carry_ref, ...), custom_call_target="tpu_custom_call" | custom-call | tf_op jit(solution)/shard_map/pallas_call | solution.py:875
  567.5 11.4 %collective-permute-done.77 = f32[2,64,1536]{2,1,0:T(8,128)} collective-permute-done((f32[2,64,1536]{2,1,0:T(8,128)}, f32[2,64,1536]{2,1,0:T(8,128)}, u32[]{:S(2)}, u32[]{:S(2)}) %collective-permute-start.77) | collective-permute-done | bytes 786464 | tf_op jit(solution)/shard_map/ppermute | solution.py:133
  596.2 8.4 %collective-permute-done.81 = bf16[256,1024]{1,0:T(8,128)(2,1)} collective-permute-done((bf16[256,1024]{1,0:T(8,128)(2,1)}, bf16[256,1024]{1,0:T(8,128)(2,1)}, u32[]{:S(2)}, u32[]{:S(2)}) %collective-permute-start.81) | collective-permute-done | bytes 524320 | tf_op jit(solution)/shard_map/ppermute | solution.py:133
  605.8 3.1 fusion.27
  610.2 8.1 %shard_map.318.x_ref.grad_ref = bf16[2048,640]{1,0:T(8,128)(2,1)} custom-call(bf16[2048,320]{1,0:T(8,128)(2,1)} %get-tuple-element.434.grad_ref, bf16[128,320]{1,0:T(8,128)(2,1)} %bitcast.109.halo_ref, f32[2048,8]{1,0:T(8,128)} %get-tuple-element.301.masks_ref, f32[128,8]{1,0:T(8,128)} %bitcast.442, bf16[2048,320]{1,0:T(8,128)(2,1)} %get-tuple-element.439.branch_ref, ...), custom_call_target="tpu_custom_call" | custom-call | tf_op jit(solution)/shard_map/pallas_call | solution.py:875
  618.3 7.2 shard_map.319
  625.5 13.5 %shard_map.320 = (bf16[4,4,128,640]{3,2,1,0:T(8,128)(2,1)}, f32[4,128,640]{2,1,0:T(8,128)}) custom-call(s32[2]{0:T(128)} %pad_add_fusion.core_ref, bf16[2048,2048]{1,0:T(8,128)(2,1)} %get-tuple-element.451.x_ref, bf16[2048,640]{1,0:T(8,128)(2,1)} %shard_map.318.x_ref.grad_ref), custom_call_target="tpu_custom_call" | custom-call | tf_op jit(solution)/shard_map/pallas_call | solution.py:809
  639.0 9.9 %shard_map.321 = (f32[256,2048]{1,0:T(8,128)}, f32[256,1024]{1,0:T(8,128)}, f32[256,1024]{1,0:T(8,128)}, bf16[2,256,1024]{2,1,0:T(8,128)(2,1)}, bf16[2,256,1024]{2,1,0:T(8,128)(2,1)}) custom-call(s32[1]{0:T(128)} %bitcast.core_ref.c_ref, bf16[2048,640]{1,0:T(8,128)(2,1)} %shard_map.318.x_ref.grad_ref, bf16[2048,640]{1,0:T(8,128)(2,1)} %bitcast.408, ...), custom_call_target="tpu_custom_call" | custom-call | tf_op jit(solution)/shard_map/pallas_call | solution.py:737
  658.8 2.8 collective-permute-done.87
  666.5 8.3 %collective-permute-done.84 = bf16[2,256,1024]{2,1,0:T(8,128)(2,1)} collective-permute-done((bf16[2,256,1024]{2,1,0:T(8,128)(2,1)}, bf16[2,256,1024]{2,1,0:T(8,128)(2,1)}, u32[]{:S(2)}, u32[]{:S(2)}) %collective-permute-start.84) | collective-permute-done | bytes 1048608 | tf_op jit(solution)/shard_map/ppermute | solution.py:133
  682.6 9.5 %collective-permute-done.89 = bf16[256,1024]{1,0:T(8,128)(2,1)S(1)} collective-permute-done((bf16[256,1024]{1,0:T(8,128)(2,1)S(1)}, bf16[256,1024]{1,0:T(8,128)(2,1)S(1)}, u32[]{:S(2)}, u32[]{:S(2)}) %collective-permute-start.89) | collective-permute-done | bytes 524320 | tf_op jit(solution)/shard_map/ppermute | solution.py:133
  707.7 3.4 collective-permute-done.94
  711.1 6.6 collective-permute-done.93
  (596 shorter events, 249.7 us)
Async XLA Ops:
  7.2 59.4 %all-gather.6.cloned.1.call-start = ((), (), s32[]{:S(2)}) async-start(), calls=%async_computation.4 | async-start | bytes 2048000 | tf_op jit(solution)/shard_map/all_gather | solution.py:146
  8.0 17.2 %collective-permute-start = (bf16[2,3]{1,0:T(2,128)(2,1)S(1)}, bf16[2,3]{1,0:T(2,128)(2,1)S(1)}, u32[]{:S(2)}, u32[]{:S(2)}) collective-permute-start(bf16[2,3]{1,0:T(2,128)(2,1)S(1)} %slice.340), channel_id=1, source_target_pairs={{0,1},{1,2},{2,3},{3,4},{4,5},{5,6},{6,7},{8,9},{9,10},{10,11},{11... | collective-permute-start | bytes 44 | tf_op jit(solution)/shard_map/ppermute | solution.py:1029
  25.2 99.8 %all-gather.8.cloned.1.call-start = ((), (), s32[]{:S(2)}) async-start(), calls=%async_computation.5 | async-start | bytes 3276800 | tf_op jit(solution)/shard_map/all_gather | solution.py:146
  40.5 25.8 %collective-permute-start.7 = (bf16[256,2176]{1,0:T(8,128)(2,1)}, bf16[256,2176]{1,0:T(8,128)(2,1)}, u32[]{:S(2)}, u32[]{:S(2)}) collective-permute-start(bf16[256,2176]{1,0:T(8,128)(2,1)} %pad_maximum_fusion.10.refs_0_), channel_id=1, source_target_pairs={{0,16},{8,24},{16,0},{24,8},{1,17},{9,25},{17,1},{25,9},{2,18},{10... | collective-permute-start | bytes 3342344 | tf_op jit(solution)/shard_map/ppermute | solution.py:133
  42.1 24.5 %collective-permute-start.6 = (bf16[256,2176]{1,0:T(8,128)(2,1)}, bf16[256,2176]{1,0:T(8,128)(2,1)}, u32[]{:S(2)}, u32[]{:S(2)}) collective-permute-start(bf16[256,2176]{1,0:T(8,128)(2,1)} %pad_maximum_fusion.10.refs_0_), channel_id=1, source_target_pairs={{0,8},{8,0},{16,24},{24,16},{1,9},{9,1},{17,25},{25,17},{2,10},{10... | collective-permute-start | bytes 3342344 | tf_op jit(solution)/shard_map/ppermute | solution.py:133
  46.0 144.0 %all-gather.10.cloned.1.call-start = ((), (), s32[]{:S(2)}) async-start(), calls=%async_computation.6 | async-start | bytes 3932160 | tf_op jit(solution)/shard_map/all_gather | solution.py:146
  100.2 16.2 %collective-permute-start.24 = (bf16[2,64,1536]{2,1,0:T(8,128)(2,1)S(1)}, bf16[2,64,1536]{2,1,0:T(8,128)(2,1)S(1)}, u32[]{:S(2)}, u32[]{:S(2)}) collective-permute-start(bf16[2,64,1536]{2,1,0:T(8,128)(2,1)S(1)} %get-tuple-element.543), channel_id=1, source_target_pairs={{0,16},{8,24},{16,0},{24,8},{1,17},{9,25},{17,1},{25,9},{2,18},{10... | collective-permute-start | bytes 1179656 | tf_op jit(solution)/shard_map/ppermute | solution.py:133
  100.7 15.7 %collective-permute-start.23 = (bf16[2,64,1536]{2,1,0:T(8,128)(2,1)S(1)}, bf16[2,64,1536]{2,1,0:T(8,128)(2,1)S(1)}, u32[]{:S(2)}, u32[]{:S(2)}) collective-permute-start(bf16[2,64,1536]{2,1,0:T(8,128)(2,1)S(1)} %get-tuple-element.544), channel_id=1, source_target_pairs={{0,24},{8,16},{16,8},{24,0},{1,25},{9,17},{17,9},{25,1},{2,26},{10... | collective-permute-start | bytes 1179656 | tf_op jit(solution)/shard_map/ppermute | solution.py:133
  102.7 16.6 %collective-permute-start.18 = (bf16[256,2176]{1,0:T(8,128)(2,1)}, bf16[256,2176]{1,0:T(8,128)(2,1)S(1)}, u32[]{:S(2)}, u32[]{:S(2)}) collective-permute-start(bf16[256,2176]{1,0:T(8,128)(2,1)} %pad_maximum_fusion.10.refs_0_), channel_id=1, source_target_pairs={{0,1},{1,0},{2,3},{3,2},{4,5},{5,4},{6,7},{7,6},{8,9},{9,8},{10,11... | collective-permute-start | bytes 3342344 | tf_op jit(solution)/shard_map/ppermute | solution.py:136
  102.7 16.6 %collective-permute-start.19 = (bf16[256,2176]{1,0:T(8,128)(2,1)}, bf16[256,2176]{1,0:T(8,128)(2,1)S(1)}, u32[]{:S(2)}, u32[]{:S(2)}) collective-permute-start(bf16[256,2176]{1,0:T(8,128)(2,1)} %collective-permute-done.6.refs_1_), channel_id=1, source_target_pairs={{0,1},{1,0},{2,3},{3,2},{4,5},{5,4},{6,7},{7,6},{8,9},{9,8},{10,11... | collective-permute-start | bytes 3342344 | tf_op jit(solution)/shard_map/ppermute | solution.py:136
  121.9 152.9 %all-gather.12.cloned.1.call-start = ((), (), s32[]{:S(2)}) async-start(), calls=%async_computation.7 | async-start | bytes 3932160 | tf_op jit(solution)/shard_map/all_gather | solution.py:146
  122.1 38.1 %collective-permute-start.27 = (bf16[256,2048]{1,0:T(8,128)(2,1)S(1)}, bf16[256,2048]{1,0:T(8,128)(2,1)S(1)}, u32[]{:S(2)}, u32[]{:S(2)}) collective-permute-start(bf16[256,2048]{1,0:T(8,128)(2,1)S(1)} %bitcast.396), channel_id=1, source_target_pairs={{0,16},{8,24},{16,0},{24,8},{1,17},{9,25},{17,1},{25,9},{2,18},{10... | collective-permute-start | bytes 3145736 | tf_op jit(solution)/shard_map/ppermute | solution.py:133
  122.3 37.9 %collective-permute-start.26 = (bf16[256,2048]{1,0:T(8,128)(2,1)S(1)}, bf16[256,2048]{1,0:T(8,128)(2,1)S(1)}, u32[]{:S(2)}, u32[]{:S(2)}) collective-permute-start(bf16[256,2048]{1,0:T(8,128)(2,1)S(1)} %bitcast.397), channel_id=1, source_target_pairs={{0,8},{8,0},{16,24},{24,16},{1,9},{9,1},{17,25},{25,17},{2,10},{10... | collective-permute-start | bytes 3145736 | tf_op jit(solution)/shard_map/ppermute | solution.py:133
  160.2 14.6 %collective-permute-start.30 = (f32[2,8,320]{2,1,0:T(8,128)S(1)}, f32[2,8,320]{2,1,0:T(8,128)S(1)}, u32[]{:S(2)}, u32[]{:S(2)}) collective-permute-start(f32[2,8,320]{2,1,0:T(8,128)S(1)} %bitcast.445), channel_id=1, source_target_pairs={{0,6},{1,7},{8,14},{9,15},{16,22},{17,23},{24,30},{25,31}} | collective-permute-start | bytes 61448 | tf_op jit(solution)/shard_map/ppermute | solution.py:140
  169.7 16.1 %collective-permute-start.34 = (bf16[2,80,2048]{2,1,0:T(8,128)(2,1)}, bf16[2,80,2048]{2,1,0:T(8,128)(2,1)}, u32[]{:S(2)}, u32[]{:S(2)}) collective-permute-start(bf16[2,80,2048]{2,1,0:T(8,128)(2,1)} %get-tuple-element.557), channel_id=1, source_target_pairs={{0,1},{1,0},{2,3},{3,2},{4,5},{5,4},{6,7},{7,6},{8,9},{9,8},{10,11... | collective-permute-start | bytes 1966088 | tf_op jit(solution)/shard_map/ppermute | solution.py:136
  170.9 17.9 %collective-permute-start.33 = (f32[8,16,8]{2,1,0:T(8,128)S(1)}, f32[8,16,8]{2,1,0:T(8,128)S(1)}, u32[]{:S(2)}, u32[]{:S(2)}) collective-permute-start(f32[8,16,8]{2,1,0:T(8,128)S(1)} %slice_bitcast_fusion.17), channel_id=1, source_target_pairs={{2,0},{3,1},{4,2},{5,3},{6,4},{7,5},{10,8},{11,9},{12,10},{13,11},... | collective-permute-start | bytes 12296 | tf_op jit(solution)/shard_map/ppermute | solution.py:140
  200.8 126.3 %all-gather.14.cloned.1.call-start = ((), (), s32[]{:S(2)}) async-start(), calls=%async_computation.8 | async-start | bytes 3932160 | tf_op jit(solution)/shard_map/all_gather | solution.py:146
  213.7 28.0 %collective-permute-start.37 = (f16[2,256,1152]{2,1,0:T(8,128)(2,1)S(1)}, f16[2,256,1152]{2,1,0:T(8,128)(2,1)S(1)}, u32[]{:S(2)}, u32[]{:S(2)}) collective-permute-start(f16[2,256,1152]{2,1,0:T(8,128)(2,1)S(1)} %pad_maximum_fusion.8), channel_id=1, source_target_pairs={{0,8},{8,0},{16,24},{24,16},{1,9},{9,1},{17,25},{25,17},{2,10},{10... | collective-permute-start | bytes 3538952 | tf_op jit(solution)/shard_map/ppermute | solution.py:133
  215.0 27.7 %collective-permute-start.38 = (f16[2,256,1152]{2,1,0:T(8,128)(2,1)S(1)}, f16[2,256,1152]{2,1,0:T(8,128)(2,1)S(1)}, u32[]{:S(2)}, u32[]{:S(2)}) collective-permute-start(f16[2,256,1152]{2,1,0:T(8,128)(2,1)S(1)} %pad_maximum_fusion.9), channel_id=1, source_target_pairs={{0,16},{8,24},{16,0},{24,8},{1,17},{9,25},{17,1},{25,9},{2,18},{10... | collective-permute-start | bytes 3538952 | tf_op jit(solution)/shard_map/ppermute | solution.py:133
  255.5 272.3 %reduce-scatter.5.cloned.1.call-start = ((), (), s32[]{:S(2)}) async-start(), calls=%async_computation.9 | async-start | bytes 7864320 | tf_op jit(solution)/shard_map/reduce_scatter | solution.py:160
  256.0 22.2 %collective-permute-start.46 = (bf16[128,2048]{1,0:T(8,128)(2,1)}, bf16[128,2048]{1,0:T(8,128)(2,1)}, u32[]{:S(2)}, u32[]{:S(2)}) collective-permute-start(bf16[128,2048]{1,0:T(8,128)(2,1)} %collective-permute-done.31.refs_3_), channel_id=1, source_target_pairs={{0,1},{1,0},{2,3},{3,2},{4,5},{5,4},{6,7},{7,6},{8,9},{9,8},{10,11... | collective-permute-start | bytes 1572872 | tf_op jit(solution)/shard_map/ppermute | solution.py:136
  256.0 23.7 %collective-permute-start.47 = (bf16[128,2048]{1,0:T(8,128)(2,1)}, bf16[128,2048]{1,0:T(8,128)(2,1)}, u32[]{:S(2)}, u32[]{:S(2)}) collective-permute-start(bf16[128,2048]{1,0:T(8,128)(2,1)} %collective-permute-done.32.refs_4_), channel_id=1, source_target_pairs={{0,1},{1,0},{2,3},{3,2},{4,5},{5,4},{6,7},{7,6},{8,9},{9,8},{10,11... | collective-permute-start | bytes 1572872 | tf_op jit(solution)/shard_map/ppermute | solution.py:136
  256.5 28.9 %collective-permute-start.43 = (bf16[256,2048]{1,0:T(8,128)(2,1)S(1)}, bf16[256,2048]{1,0:T(8,128)(2,1)}, u32[]{:S(2)}, u32[]{:S(2)}) collective-permute-start(bf16[256,2048]{1,0:T(8,128)(2,1)S(1)} %bitcast.398), channel_id=1, source_target_pairs={{0,1},{1,0},{2,3},{3,2},{4,5},{5,4},{6,7},{7,6},{8,9},{9,8},{10,11... | collective-permute-start | bytes 3145736 | tf_op jit(solution)/shard_map/ppermute | solution.py:136
  267.9 17.6 %collective-permute-start.44 = (bf16[256,2048]{1,0:T(8,128)(2,1)S(1)}, bf16[256,2048]{1,0:T(8,128)(2,1)}, u32[]{:S(2)}, u32[]{:S(2)}) collective-permute-start(bf16[256,2048]{1,0:T(8,128)(2,1)S(1)} %collective-permute-done.26.refs_1_), channel_id=1, source_target_pairs={{0,1},{1,0},{2,3},{3,2},{4,5},{5,4},{6,7},{7,6},{8,9},{9,8},{10,11... | collective-permute-start | bytes 3145736 | tf_op jit(solution)/shard_map/ppermute | solution.py:136
  269.1 16.4 %collective-permute-start.45 = (bf16[256,2048]{1,0:T(8,128)(2,1)S(1)}, bf16[256,2048]{1,0:T(8,128)(2,1)}, u32[]{:S(2)}, u32[]{:S(2)}) collective-permute-start(bf16[256,2048]{1,0:T(8,128)(2,1)S(1)} %collective-permute-done.27.refs_2_), channel_id=1, source_target_pairs={{0,1},{1,0},{2,3},{3,2},{4,5},{5,4},{6,7},{7,6},{8,9},{9,8},{10,11... | collective-permute-start | bytes 3145736 | tf_op jit(solution)/shard_map/ppermute | solution.py:136
  278.2 25.5 %collective-permute-start.42 = (bf16[256,2048]{1,0:T(8,128)(2,1)}, bf16[256,2048]{1,0:T(8,128)(2,1)}, u32[]{:S(2)}, u32[]{:S(2)}) collective-permute-start(bf16[256,2048]{1,0:T(8,128)(2,1)} %multiply_convert_fusion.2.refs_0_), channel_id=1, source_target_pairs={{0,16},{8,24},{16,0},{24,8},{1,17},{9,25},{17,1},{25,9},{2,18},{10... | collective-permute-start | bytes 3145736 | tf_op jit(solution)/shard_map/ppermute | solution.py:133
  279.8 25.1 %collective-permute-start.41 = (bf16[256,2048]{1,0:T(8,128)(2,1)}, bf16[256,2048]{1,0:T(8,128)(2,1)}, u32[]{:S(2)}, u32[]{:S(2)}) collective-permute-start(bf16[256,2048]{1,0:T(8,128)(2,1)} %multiply_convert_fusion.2.refs_0_), channel_id=1, source_target_pairs={{0,8},{8,0},{16,24},{24,16},{1,9},{9,1},{17,25},{25,17},{2,10},{10... | collective-permute-start | bytes 3145736 | tf_op jit(solution)/shard_map/ppermute | solution.py:133
  309.3 17.9 %collective-permute-start.50 = (bf16[256,2048]{1,0:T(8,128)(2,1)}, bf16[256,2048]{1,0:T(8,128)(2,1)S(1)}, u32[]{:S(2)}, u32[]{:S(2)}) collective-permute-start(bf16[256,2048]{1,0:T(8,128)(2,1)} %multiply_convert_fusion.2.refs_0_), channel_id=1, source_target_pairs={{0,1},{1,0},{2,3},{3,2},{4,5},{5,4},{6,7},{7,6},{8,9},{9,8},{10,11... | collective-permute-start | bytes 3145736 | tf_op jit(solution)/shard_map/ppermute | solution.py:136
  309.3 17.9 %collective-permute-start.51 = (bf16[256,2048]{1,0:T(8,128)(2,1)}, bf16[256,2048]{1,0:T(8,128)(2,1)S(1)}, u32[]{:S(2)}, u32[]{:S(2)}) collective-permute-start(bf16[256,2048]{1,0:T(8,128)(2,1)} %collective-permute-done.41.refs_1_), channel_id=1, source_target_pairs={{0,1},{1,0},{2,3},{3,2},{4,5},{5,4},{6,7},{7,6},{8,9},{9,8},{10,11... | collective-permute-start | bytes 3145736 | tf_op jit(solution)/shard_map/ppermute | solution.py:136
  309.8 17.4 %collective-permute-start.52 = (bf16[256,2048]{1,0:T(8,128)(2,1)}, bf16[256,2048]{1,0:T(8,128)(2,1)}, u32[]{:S(2)}, u32[]{:S(2)}) collective-permute-start(bf16[256,2048]{1,0:T(8,128)(2,1)} %collective-permute-done.42.refs_2_), channel_id=1, source_target_pairs={{0,1},{1,0},{2,3},{3,2},{4,5},{5,4},{6,7},{7,6},{8,9},{9,8},{10,11... | collective-permute-start | bytes 3145736 | tf_op jit(solution)/shard_map/ppermute | solution.py:136
  390.6 25.6 %collective-permute-start.56 = (bf16[2,256,1024]{2,1,0:T(8,128)(2,1)}, bf16[2,256,1024]{2,1,0:T(8,128)(2,1)S(1)}, u32[]{:S(2)}, u32[]{:S(2)}) collective-permute-start(bf16[2,256,1024]{2,1,0:T(8,128)(2,1)} %get-tuple-element.353), channel_id=1, source_target_pairs={{0,8},{8,0},{16,24},{24,16},{1,9},{9,1},{17,25},{25,17},{2,10},{10... | collective-permute-start | bytes 3145736 | tf_op jit(solution)/shard_map/ppermute | solution.py:133
  392.1 25.4 %collective-permute-start.57 = (bf16[2,256,1024]{2,1,0:T(8,128)(2,1)}, bf16[2,256,1024]{2,1,0:T(8,128)(2,1)S(1)}, u32[]{:S(2)}, u32[]{:S(2)}) collective-permute-start(bf16[2,256,1024]{2,1,0:T(8,128)(2,1)} %get-tuple-element.354), channel_id=1, source_target_pairs={{0,16},{8,24},{16,0},{24,8},{1,17},{9,25},{17,1},{25,9},{2,18},{10... | collective-permute-start | bytes 3145736 | tf_op jit(solution)/shard_map/ppermute | solution.py:133
  417.4 257.7 %reduce-scatter.9.cloned.1.call-start = ((), (), s32[]{:S(2)}) async-start(), calls=%async_computation.11 | async-start | bytes 3932160 | tf_op jit(solution)/shard_map/reduce_scatter | solution.py:160
  425.0 37.0 %collective-permute-start.62 = (bf16[1024,2048]{1,0:T(8,128)(2,1)}, bf16[1024,2048]{1,0:T(8,128)(2,1)}, u32[]{:S(2)}, u32[]{:S(2)}) collective-permute-start(bf16[1024,2048]{1,0:T(8,128)(2,1)} %shard_map.313), channel_id=1, source_target_pairs={{0,1},{1,0},{2,3},{3,2},{4,5},{5,4},{6,7},{7,6},{8,9},{9,8},{10,11... | collective-permute-start | bytes 12582920 | tf_op jit(solution)/shard_map/ppermute | solution.py:136
  447.2 24.6 %collective-permute-start.61 = (bf16[256,2048]{1,0:T(8,128)(2,1)S(1)}, bf16[256,2048]{1,0:T(8,128)(2,1)S(1)}, u32[]{:S(2)}, u32[]{:S(2)}) collective-permute-start(bf16[256,2048]{1,0:T(8,128)(2,1)S(1)} %get-tuple-element.389.refs_0_), channel_id=1, source_target_pairs={{0,16},{8,24},{16,0},{24,8},{1,17},{9,25},{17,1},{25,9},{2,18},{10... | collective-permute-start | bytes 3145736 | tf_op jit(solution)/shard_map/ppermute | solution.py:133
  447.7 24.5 %collective-permute-start.60 = (bf16[256,2048]{1,0:T(8,128)(2,1)S(1)}, bf16[256,2048]{1,0:T(8,128)(2,1)S(1)}, u32[]{:S(2)}, u32[]{:S(2)}) collective-permute-start(bf16[256,2048]{1,0:T(8,128)(2,1)S(1)} %get-tuple-element.389.refs_0_), channel_id=1, source_target_pairs={{0,8},{8,0},{16,24},{24,16},{1,9},{9,1},{17,25},{25,17},{2,10},{10... | collective-permute-start | bytes 3145736 | tf_op jit(solution)/shard_map/ppermute | solution.py:133
  489.0 25.4 %collective-permute-start.70 = (bf16[2,256,1024]{2,1,0:T(8,128)(2,1)}, bf16[2,256,1024]{2,1,0:T(8,128)(2,1)S(1)}, u32[]{:S(2)}, u32[]{:S(2)}) collective-permute-start(bf16[2,256,1024]{2,1,0:T(8,128)(2,1)} %get-tuple-element.407), channel_id=1, source_target_pairs={{0,8},{8,0},{16,24},{24,16},{1,9},{9,1},{17,25},{25,17},{2,10},{10... | collective-permute-start | bytes 3145736 | tf_op jit(solution)/shard_map/ppermute | solution.py:133
  489.9 25.5 %collective-permute-start.71 = (bf16[2,256,1024]{2,1,0:T(8,128)(2,1)}, bf16[2,256,1024]{2,1,0:T(8,128)(2,1)}, u32[]{:S(2)}, u32[]{:S(2)}) collective-permute-start(bf16[2,256,1024]{2,1,0:T(8,128)(2,1)} %get-tuple-element.408), channel_id=1, source_target_pairs={{0,16},{8,24},{16,0},{24,8},{1,17},{9,25},{17,1},{25,9},{2,18},{10... | collective-permute-start | bytes 3145736 | tf_op jit(solution)/shard_map/ppermute | solution.py:133
  531.2 162.9 %reduce-scatter.11.cloned.1.call-start = ((), (), s32[]{:S(2)}) async-start(), calls=%async_computation.12 | async-start | bytes 1945600 | tf_op jit(solution)/shard_map/reduce_scatter | solution.py:160
  541.0 26.5 %collective-permute-start.78 = (f32[2,64,1536]{2,1,0:T(8,128)}, f32[2,64,1536]{2,1,0:T(8,128)}, u32[]{:S(2)}, u32[]{:S(2)}) collective-permute-start(f32[2,64,1536]{2,1,0:T(8,128)} %get-tuple-element.513), channel_id=1, source_target_pairs={{0,8},{8,0},{16,24},{24,16},{1,9},{9,1},{17,25},{25,17},{2,10},{10... | collective-permute-start | bytes 2359304 | tf_op jit(solution)/shard_map/ppermute | solution.py:133
  542.4 36.5 %collective-permute-start.77 = (f32[2,64,1536]{2,1,0:T(8,128)}, f32[2,64,1536]{2,1,0:T(8,128)}, u32[]{:S(2)}, u32[]{:S(2)}) collective-permute-start(f32[2,64,1536]{2,1,0:T(8,128)} %get-tuple-element.514), channel_id=1, source_target_pairs={{0,16},{8,24},{16,0},{24,8},{1,17},{9,25},{17,1},{25,9},{2,18},{10... | collective-permute-start | bytes 2359304 | tf_op jit(solution)/shard_map/ppermute | solution.py:133
  543.9 35.0 %collective-permute-start.76 = (f32[2,64,1536]{2,1,0:T(8,128)}, f32[2,64,1536]{2,1,0:T(8,128)}, u32[]{:S(2)}, u32[]{:S(2)}) collective-permute-start(f32[2,64,1536]{2,1,0:T(8,128)} %get-tuple-element.515), channel_id=1, source_target_pairs={{0,24},{8,16},{16,8},{24,0},{1,25},{9,17},{17,9},{25,1},{2,26},{10... | collective-permute-start | bytes 2359304 | tf_op jit(solution)/shard_map/ppermute | solution.py:133
  590.1 14.6 %collective-permute-start.81 = (bf16[256,1024]{1,0:T(8,128)(2,1)}, bf16[256,1024]{1,0:T(8,128)(2,1)}, u32[]{:S(2)}, u32[]{:S(2)}) collective-permute-start(bf16[256,1024]{1,0:T(8,128)(2,1)} %fusion.25), channel_id=1, source_target_pairs={{0,16},{8,24},{16,0},{24,8},{1,17},{9,25},{17,1},{25,9},{2,18},{10... | collective-permute-start | bytes 1572872 | tf_op jit(solution)/shard_map/ppermute | solution.py:133
  596.2 97.9 %reduce-scatter.7.cloned.1.call-start = ((), (), s32[]{:S(2)}) async-start(), calls=%async_computation.10 | async-start | bytes 3276800 | tf_op jit(solution)/shard_map/reduce_scatter | solution.py:160
  648.9 26.0 %collective-permute-start.84 = (bf16[2,256,1024]{2,1,0:T(8,128)(2,1)}, bf16[2,256,1024]{2,1,0:T(8,128)(2,1)}, u32[]{:S(2)}, u32[]{:S(2)}) collective-permute-start(bf16[2,256,1024]{2,1,0:T(8,128)(2,1)} %get-tuple-element.460), channel_id=1, source_target_pairs={{0,8},{8,0},{16,24},{24,16},{1,9},{9,1},{17,25},{25,17},{2,10},{10... | collective-permute-start | bytes 3145736 | tf_op jit(solution)/shard_map/ppermute | solution.py:133
  649.5 25.6 %collective-permute-start.85 = (bf16[2,256,1024]{2,1,0:T(8,128)(2,1)}, bf16[2,256,1024]{2,1,0:T(8,128)(2,1)}, u32[]{:S(2)}, u32[]{:S(2)}) collective-permute-start(bf16[2,256,1024]{2,1,0:T(8,128)(2,1)} %get-tuple-element.461), channel_id=1, source_target_pairs={{0,16},{8,24},{16,0},{24,8},{1,17},{9,25},{17,1},{25,9},{2,18},{10... | collective-permute-start | bytes 3145736 | tf_op jit(solution)/shard_map/ppermute | solution.py:133
  701.7 16.0 %collective-permute-start.93 = (f32[2,64,640]{2,1,0:T(8,128)S(1)}, f32[2,64,640]{2,1,0:T(8,128)S(1)}, u32[]{:S(2)}, u32[]{:S(2)}) collective-permute-start(f32[2,64,640]{2,1,0:T(8,128)S(1)} %get-tuple-element.552), channel_id=1, source_target_pairs={{0,16},{8,24},{16,0},{24,8},{1,17},{9,25},{17,1},{25,9},{2,18},{10... | collective-permute-start | bytes 983048 | tf_op jit(solution)/shard_map/ppermute | solution.py:133
  703.2 14.5 %collective-permute-start.92 = (f32[2,64,640]{2,1,0:T(8,128)S(1)}, f32[2,64,640]{2,1,0:T(8,128)S(1)}, u32[]{:S(2)}, u32[]{:S(2)}) collective-permute-start(f32[2,64,640]{2,1,0:T(8,128)S(1)} %get-tuple-element.553), channel_id=1, source_target_pairs={{0,24},{8,16},{16,8},{24,0},{1,25},{9,17},{17,9},{25,1},{2,26},{10... | collective-permute-start | bytes 983048 | tf_op jit(solution)/shard_map/ppermute | solution.py:133
  (143 other events, 1001.8 us)
Sparse Core Ops, SparseCore 0:
  25.3 37.3 all-gather.5
  64.9 53.6 all-gather.7
  121.8 63.6 all-gather.9
  200.9 62.5 all-gather.11
  265.0 62.1 all-gather.13
  417.6 110.2 reduce-scatter.4
  531.3 62.7 reduce-scatter.8
  596.4 37.8 reduce-scatter.10
  639.1 54.7 reduce-scatter.6

commit v6 on v5

--- a/solution.py
+++ b/solution.py
@@ -1275,9 +1275,8 @@
         [pltpu.VMEM((span + 8, w_slot), wide)],
     )
 
-    grad_one, block_out = together(grad_one, block_out)
     other_one, got_one = at.chip_send(grad_one, w1, 1)
-    other_one, then = together(other_one, grad_one)
+    other_one, then, block_out = together(other_one, grad_one, block_out)
     w1_part = rows_apart(n1_all, then)
     then, w1_part = together(then, w1_part)
     near_one = at.near_parts(at.chip_own(then, w1, got_one, 1))

time: 739 us -> 742 us (level)
    unnamed x180 -> x176, local copies, waits for them, and re-layouts: 17.2 us -> 17.4 us
  transfers between devices with their start and end apart: 104 -> 104, of which waited for: 50 -> 51; matrix products, arithmetic and copies ran while one was open for 19% -> 18% of each run, Pallas kernels for 25% -> 25%
where the time goes in v6:
time: 742 us; the launch traced here: 733 us
  Pallas kernels  234 us (32%)
  waiting for transfers between devices  229 us (31%)
  other arithmetic  88.2 us (12%)
  starting transfers between devices  85.5 us (12%)
  local copies, waits for them, and re-layouts  63.5 us (9%)
  between operations  16.3 us (2%)
  matrix products  15.6 us (2%)
    ppermute x48, waiting for transfers between devices, to_k(): lax.ppermute(array, 'dp', [(i, i ^ flip) for i in range(self.k_count)])  201 us
    pallas_call x3, Pallas kernels, gathered_call(): pl.pallas_call(functools.partial(gathered_kernel, kernel, len(own), steps...  82.8 us
    pallas_call x6, Pallas kernels, half_call(): pl.pallas_call(kernel, out_shape=[array for array, _, _ in outputs], grid...  59.6 us
    ppermute x48, starting transfers between devices, to_k(): lax.ppermute(array, 'dp', [(i, i ^ flip) for i in range(self.k_count)])  51.9 us
    pallas_call x3, Pallas kernels, kernel_call(): pl.pallas_call(kernel, out_shape=[array for array, _ in outputs], grid=(s...  38.5 us
    pallas_call x2, Pallas kernels, rows_call(): pl.pallas_call(rows_kernel, out_shape=[sent, kept], grid_spec=pltpu.Prefe...  33.9 us
    ppermute x9, starting transfers between devices, to_z(): return lax.ppermute(array, 'seq', pairs)  17.7 us
    unnamed x176, local copies, waits for them, and re-layouts  17.4 us
  transfers between devices with their start and end apart: 104, of which 51 were waited for; matrix products, arithmetic and copies ran while one was open for 18% of the time, Pallas kernels for 25%

profile of v6, /device:TPU:0, one launch (start us, length us, event | category | flops | bytes accessed | tf_op | source)
XLA Modules:
  0.0 732.6 jit_solution(16361154508245352489)
XLA Ops:
  11.2 4.5 collective-permute-start.1
  18.7 3.2 maximum_bitcast_fusion.1
  33.3 2.5 collective-permute-done.5
  35.8 3.8 collective-permute-done.4
  47.9 18.6 %collective-permute-done.7.refs_2_ = bf16[256,2176]{1,0:T(8,128)(2,1)} collective-permute-done((bf16[256,2176]{1,0:T(8,128)(2,1)}, bf16[256,2176]{1,0:T(8,128)(2,1)}, u32[]{:S(2)}, u32[]{:S(2)}) %collective-permute-start.7) | collective-permute-done | bytes 1114144 | tf_op jit(solution)/shard_map/ppermute | solution.py:133
  78.0 2.8 collective-permute-done.11
  88.5 9.7 %collective-permute-done.17.refs_4_ = bf16[128,2176]{1,0:T(8,128)(2,1)S(1)} collective-permute-done((bf16[128,2176]{1,0:T(8,128)(2,1)}, bf16[128,2176]{1,0:T(8,128)(2,1)S(1)}, u32[]{:S(2)}, u32[]{:S(2)}) %collective-permute-start.17) | collective-permute-done | bytes 557088 | tf_op jit(solution)/shard_map/ppermute | solution.py:133
  103.3 8.1 %collective-permute-done.25 = bf16[2,64,1536]{2,1,0:T(8,128)(2,1)S(1)} collective-permute-done((bf16[2,64,1536]{2,1,0:T(8,128)(2,1)S(1)}, bf16[2,64,1536]{2,1,0:T(8,128)(2,1)S(1)}, u32[]{:S(2)}, u32[]{:S(2)}) %collective-permute-start.25) | collective-permute-done | bytes 393248 | tf_op jit(solution)/shard_map/ppermute | solution.py:133
  111.4 5.1 collective-permute-done.24
  125.2 34.1 %shard_map.306 = (bf16[2048,2048]{1,0:T(8,128)(2,1)}, f32[2048,8]{1,0:T(8,128)}, f32[2048,320]{1,0:T(8,128)}, bf16[2048,320]{1,0:T(8,128)(2,1)}, bf16[2048,320]{...) custom-call(s32[1]{0:T(128)} %bitcast.1.core_ref.c_ref, ...), custom_call_target="tpu_custom_call" | custom-call | tf_op jit(solution)/shard_map/pallas_call | solution.py:947
  160.3 3.1 collective-permute-start.30
  177.6 8.3 %shard_map.307 = (f32[2048,320]{1,0:T(8,128)}, bf16[2048,320]{1,0:T(8,128)(2,1)}) custom-call(f32[2048,320]{1,0:T(8,128)} %get-tuple-element.290.part_ref, f32[2048,320]{1,0:T(8,128)} %get-tuple-element.291.run_ref, f32[64,320]{1,0:T(8,128)} %broadcast_bitcast_fusion.1.start_ref, f32[2048,320]{1,0:T(8,128)} %get-tuple-element.294.branch_ref.refs_11_), custom_call_target="tpu_custom_call" | custom-call | tf_op jit(solution)/shard_map/pallas_call | solution.py:875
  190.2 2.8 abs_reduce_fusion
  216.6 25.1 %collective-permute-done.37 = f16[2,256,1152]{2,1,0:T(8,128)(2,1)S(1)} collective-permute-done((f16[2,256,1152]{2,1,0:T(8,128)(2,1)S(1)}, f16[2,256,1152]{2,1,0:T(8,128)(2,1)S(1)}, u32[]{:S(2)}, u32[]{:S(2)}) %collective-permute-start.37) | collective-permute-done | bytes 1179680 | tf_op jit(solution)/shard_map/ppermute | solution.py:133
  256.7 11.3 %collective-permute-done.39 = f16[256,1152]{1,0:T(8,128)(2,1)} collective-permute-done((f16[256,1152]{1,0:T(8,128)(2,1)}, f16[256,1152]{1,0:T(8,128)(2,1)}, u32[]{:S(2)}, u32[]{:S(2)}) %collective-permute-start.39) | collective-permute-done | bytes 589856 | tf_op jit(solution)/shard_map/ppermute | solution.py:133
  282.5 3.0 pad_maximum_fusion.refs_11_.w_ref
  285.5 3.0 shard_map.308.refs_10_.cot_ref
  288.5 3.3 copy-done
  291.8 12.0 %collective-permute-done.42.refs_2_ = bf16[256,2048]{1,0:T(8,128)(2,1)} collective-permute-done((bf16[256,2048]{1,0:T(8,128)(2,1)}, bf16[256,2048]{1,0:T(8,128)(2,1)}, u32[]{:S(2)}, u32[]{:S(2)}) %collective-permute-start.42) | collective-permute-done | bytes 1048608 | tf_op jit(solution)/shard_map/ppermute | solution.py:133
  309.9 9.1 %collective-permute-done.49.refs_4_ = bf16[128,2048]{1,0:T(8,128)(2,1)} collective-permute-done((bf16[128,2048]{1,0:T(8,128)(2,1)S(1)}, bf16[128,2048]{1,0:T(8,128)(2,1)}, u32[]{:S(2)}, u32[]{:S(2)}) %collective-permute-start.49) | collective-permute-done | bytes 524320 | tf_op jit(solution)/shard_map/ppermute | solution.py:133
  320.4 6.8 all-gather.14.cloned.1.call-done.refs_12_.w_ref
  328.6 28.8 %shard_map.309 = (bf16[2048,2048]{1,0:T(8,128)(2,1)}, bf16[2048,768]{1,0:T(8,128)(2,1)}, bf16[2048,1536]{1,0:T(8,128)(2,1)}) custom-call(s32[1]{0:T(128)} %bitcast.1.core_ref.c_ref, bf16[256,2048]{1,0:T(8,128)(2,1)} %multiply_convert_fusion.2.refs_0_, bf16[256,2048]{1,0:T(8,128)(2,1)} %collective-permute-done.41.refs_1_, ...), custom_call_target="tpu_custom_call" | custom-call | tf_op jit(solution)/shard_map/pallas_call | solution.py:947
  357.4 11.4 %shard_map.310 = bf16[1024,2048]{1,0:T(8,128)(2,1)} custom-call(s32[1]{0:T(128)} %bitcast.core_ref, bf16[2048,1536]{1,0:T(8,128)(2,1)} %get-tuple-element.357.x_ref.grad_ref, bf16[2048,1536]{1,0:T(8,128)(2,1)} %pad_maximum_fusion.refs_11_.w_ref), custom_call_target="tpu_custom_call" | custom-call | tf_op jit(solution)/shard_map/pallas_call | solution.py:737
  369.8 7.1 collective-permute-done.55.got_ref
  377.0 13.8 %shard_map.311 = (f32[256,2048]{1,0:T(8,128)}, f32[256,1024]{1,0:T(8,128)}, f32[256,1024]{1,0:T(8,128)}, bf16[2,256,1024]{2,1,0:T(8,128)(2,1)}, bf16[2,256,1024]{2,1,0:T(8,128)(2,1)}) custom-call(s32[1]{0:T(128)} %bitcast.1.core_ref.c_ref, bf16[2048,1536]{1,0:T(8,128)(2,1)} %get-tuple-element.357.x_ref.grad_ref, ...), custom_call_target="tpu_custom_call" | custom-call | tf_op jit(solution)/shard_map/pallas_call | solution.py:737
  394.5 20.4 %shard_map.312 = (bf16[4,4,128,1536]{3,2,1,0:T(8,128)(2,1)}, f32[4,128,1536]{2,1,0:T(8,128)}) custom-call(s32[2]{0:T(128)} %pad_add_fusion.core_ref, bf16[2048,2048]{1,0:T(8,128)(2,1)} %get-tuple-element.356.x_ref, bf16[2048,1536]{1,0:T(8,128)(2,1)} %get-tuple-element.357.x_ref.grad_ref), custom_call_target="tpu_custom_call" | custom-call | tf_op jit(solution)/shard_map/pallas_call | solution.py:809
  417.8 7.4 %shard_map.313 = bf16[1024,2048]{1,0:T(8,128)(2,1)} custom-call(s32[1]{0:T(128)} %bitcast.core_ref, bf16[2048,768]{1,0:T(8,128)(2,1)} %get-tuple-element.372.x_ref.hidden_ref, bf16[768,2048]{1,0:T(8,128)(2,1)} %all-gather.14.cloned.1.call-done.refs_12_.w_ref), custom_call_target="tpu_custom_call" | custom-call | tf_op jit(solution)/shard_map/pallas_call | solution.py:737
  429.3 12.3 %collective-permute-done.58 = bf16[256,1024]{1,0:T(8,128)(2,1)S(1)} collective-permute-done((bf16[256,1024]{1,0:T(8,128)(2,1)S(1)}, bf16[256,1024]{1,0:T(8,128)(2,1)S(1)}, u32[]{:S(2)}, u32[]{:S(2)}) %collective-permute-start.58) | collective-permute-done | bytes 524320 | tf_op jit(solution)/shard_map/ppermute | solution.py:133
  448.5 13.7 %shard_map.315 = (bf16[4,192,2048]{2,1,0:T(8,128)(2,1)}, f32[192,2048]{1,0:T(8,128)}) custom-call(s32[1]{0:T(128)} %bitcast.82.core_ref, bf16[2048,768]{1,0:T(8,128)(2,1)} %get-tuple-element.372.x_ref.hidden_ref, bf16[2048,2048]{1,0:T(8,128)(2,1)} %copy-done), custom_call_target="tpu_custom_call" | custom-call | tf_op jit(solution)/shard_map/pallas_call | solution.py:851
  462.2 9.7 %shard_map.314 = (f32[256,2048]{1,0:T(8,128)}, f32[256,1024]{1,0:T(8,128)}, f32[256,1024]{1,0:T(8,128)}, bf16[2,256,1024]{2,1,0:T(8,128)(2,1)}, bf16[2,256,1024]{2,1,0:T(8,128)(2,1)}) custom-call(s32[1]{0:T(128)} %bitcast.1.core_ref.c_ref, bf16[2048,768]{1,0:T(8,128)(2,1)} %get-tuple-element.372.x_ref.hidden_ref, ...), custom_call_target="tpu_custom_call" | custom-call | tf_op jit(solution)/shard_map/pallas_call | solution.py:737
  475.7 9.2 %collective-permute-done.64.refs_4_ = bf16[128,2048]{1,0:T(8,128)(2,1)S(1)} collective-permute-done((bf16[128,2048]{1,0:T(8,128)(2,1)S(1)}, bf16[128,2048]{1,0:T(8,128)(2,1)S(1)}, u32[]{:S(2)}, u32[]{:S(2)}) %collective-permute-start.64) | collective-permute-done | bytes 524320 | tf_op jit(solution)/shard_map/ppermute | solution.py:133
  491.7 19.9 %shard_map.316 = (bf16[2048,2048]{1,0:T(8,128)(2,1)}, bf16[2048,320]{1,0:T(8,128)(2,1)}, f32[2048,320]{1,0:T(8,128)}, f32[2048,320]{1,0:T(8,128)}, f32[64,320]{1,0:T(8,128)}) custom-call(s32[1]{0:T(128)} %bitcast.1.core_ref.c_ref, bf16[256,2048]{1,0:T(8,128)(2,1)} %copy-done.20, bf16[256,2048]{1,0:T(8,128)(2,1)} %copy-done.27, bf16[256,2048]{1,0:T(8,128)(2,1)} %copy-done.26, ...), custom_call_target="tpu_custom_call" | custom-call | bytes 73400320 | tf_op jit(solution)/shard_map/pallas_call | solution.py:947
  519.6 8.0 %fusion.97 = bf16[320,2048]{1,0:T(8,128)(2,1)} fusion(bf16[2048,320]{1,0:T(8,128)(2,1)} %get-tuple-element.411, bf16[2048,2048]{1,0:T(8,128)(2,1)} %get-tuple-element.412), kind=kOutput, calls=%fused_computation.323 | convolution fusion | flops 2684354560 | bytes 11010048 | tf_op jit(solution)/shard_map/dot_general | solution.py:34
  531.6 3.1 collective-permute-done.75
  535.8 3.6 fusion.2
  545.1 22.2 %shard_map.317 = (bf16[2048,320]{1,0:T(8,128)(2,1)}, bf16[320,320]{1,0:T(8,128)(2,1)}, f32[8,320]{1,0:T(8,128)}) custom-call(f32[2048,320]{1,0:T(8,128)} %get-tuple-element.400.part_ref, f32[2048,320]{1,0:T(8,128)} %get-tuple-element.401.run_ref, f32[64,320]{1,0:T(8,128)} %broadcast_bitcast_fusion.carry_ref, ...), custom_call_target="tpu_custom_call" | custom-call | tf_op jit(solution)/shard_map/pallas_call | solution.py:875
  567.3 11.6 %collective-permute-done.77 = f32[2,64,1536]{2,1,0:T(8,128)} collective-permute-done((f32[2,64,1536]{2,1,0:T(8,128)}, f32[2,64,1536]{2,1,0:T(8,128)}, u32[]{:S(2)}, u32[]{:S(2)}) %collective-permute-start.77) | collective-permute-done | bytes 786464 | tf_op jit(solution)/shard_map/ppermute | solution.py:133
  592.4 2.4 collective-permute-done.79
  594.8 8.1 %shard_map.318.x_ref.grad_ref = bf16[2048,640]{1,0:T(8,128)(2,1)} custom-call(bf16[2048,320]{1,0:T(8,128)(2,1)} %get-tuple-element.433.grad_ref, bf16[128,320]{1,0:T(8,128)(2,1)} %bitcast.109.halo_ref, f32[2048,8]{1,0:T(8,128)} %get-tuple-element.300.masks_ref, f32[128,8]{1,0:T(8,128)} %bitcast.441, bf16[2048,320]{1,0:T(8,128)(2,1)} %get-tuple-element.438.branch_ref, ...), custom_call_target="tpu_custom_call" | custom-call | tf_op jit(solution)/shard_map/pallas_call | solution.py:875
  602.9 7.3 shard_map.319
  616.6 11.6 %collective-permute-done.81 = bf16[256,1024]{1,0:T(8,128)(2,1)S(1)} collective-permute-done((bf16[256,1024]{1,0:T(8,128)(2,1)S(1)}, bf16[256,1024]{1,0:T(8,128)(2,1)S(1)}, u32[]{:S(2)}, u32[]{:S(2)}) %collective-permute-start.81) | collective-permute-done | bytes 524320 | tf_op jit(solution)/shard_map/ppermute | solution.py:133
  631.2 13.4 %shard_map.320 = (bf16[4,4,128,640]{3,2,1,0:T(8,128)(2,1)}, f32[4,128,640]{2,1,0:T(8,128)}) custom-call(s32[2]{0:T(128)} %pad_add_fusion.core_ref, bf16[2048,2048]{1,0:T(8,128)(2,1)} %get-tuple-element.449.x_ref, bf16[2048,640]{1,0:T(8,128)(2,1)} %shard_map.318.x_ref.grad_ref), custom_call_target="tpu_custom_call" | custom-call | tf_op jit(solution)/shard_map/pallas_call | solution.py:809
  644.7 9.9 %shard_map.321 = (f32[256,2048]{1,0:T(8,128)}, f32[256,1024]{1,0:T(8,128)}, f32[256,1024]{1,0:T(8,128)}, bf16[2,256,1024]{2,1,0:T(8,128)(2,1)}, bf16[2,256,1024]{2,1,0:T(8,128)(2,1)}) custom-call(s32[1]{0:T(128)} %bitcast.1.core_ref.c_ref, bf16[2048,640]{1,0:T(8,128)(2,1)} %shard_map.318.x_ref.grad_ref, bf16[2048,640]{1,0:T(8,128)(2,1)} %bitcast.408, ...), custom_call_target="tpu_custom_call" | custom-call | tf_op jit(solution)/shard_map/pallas_call | solution.py:737
  660.5 3.2 collective-permute-start.87
  670.7 8.8 %collective-permute-done.84 = bf16[2,256,1024]{2,1,0:T(8,128)(2,1)} collective-permute-done((bf16[2,256,1024]{2,1,0:T(8,128)(2,1)}, bf16[2,256,1024]{2,1,0:T(8,128)(2,1)}, u32[]{:S(2)}, u32[]{:S(2)}) %collective-permute-start.84) | collective-permute-done | bytes 1048608 | tf_op jit(solution)/shard_map/ppermute | solution.py:133
  687.5 8.7 %collective-permute-done.89 = bf16[256,1024]{1,0:T(8,128)(2,1)S(1)} collective-permute-done((bf16[256,1024]{1,0:T(8,128)(2,1)S(1)}, bf16[256,1024]{1,0:T(8,128)(2,1)S(1)}, u32[]{:S(2)}, u32[]{:S(2)}) %collective-permute-start.89) | collective-permute-done | bytes 524320 | tf_op jit(solution)/shard_map/ppermute | solution.py:133
  711.3 3.4 collective-permute-done.94
  714.7 6.6 collective-permute-done.93
  (592 shorter events, 250.8 us)
Async XLA Ops:
  7.2 59.5 %all-gather.6.cloned.1.call-start = ((), (), s32[]{:S(2)}) async-start(), calls=%async_computation.4 | async-start | bytes 2048000 | tf_op jit(solution)/shard_map/all_gather | solution.py:146
  8.0 17.2 %collective-permute-start = (bf16[2,3]{1,0:T(2,128)(2,1)S(1)}, bf16[2,3]{1,0:T(2,128)(2,1)S(1)}, u32[]{:S(2)}, u32[]{:S(2)}) collective-permute-start(bf16[2,3]{1,0:T(2,128)(2,1)S(1)} %slice.340), channel_id=1, source_target_pairs={{0,1},{1,2},{2,3},{3,4},{4,5},{5,6},{6,7},{8,9},{9,10},{10,11},{11... | collective-permute-start | bytes 44 | tf_op jit(solution)/shard_map/ppermute | solution.py:1029
  25.2 99.9 %all-gather.8.cloned.1.call-start = ((), (), s32[]{:S(2)}) async-start(), calls=%async_computation.5 | async-start | bytes 3276800 | tf_op jit(solution)/shard_map/all_gather | solution.py:146
  40.6 25.8 %collective-permute-start.7 = (bf16[256,2176]{1,0:T(8,128)(2,1)}, bf16[256,2176]{1,0:T(8,128)(2,1)}, u32[]{:S(2)}, u32[]{:S(2)}) collective-permute-start(bf16[256,2176]{1,0:T(8,128)(2,1)} %pad_maximum_fusion.10.refs_0_), channel_id=1, source_target_pairs={{0,16},{8,24},{16,0},{24,8},{1,17},{9,25},{17,1},{25,9},{2,18},{10... | collective-permute-start | bytes 3342344 | tf_op jit(solution)/shard_map/ppermute | solution.py:133
  42.1 24.5 %collective-permute-start.6 = (bf16[256,2176]{1,0:T(8,128)(2,1)}, bf16[256,2176]{1,0:T(8,128)(2,1)}, u32[]{:S(2)}, u32[]{:S(2)}) collective-permute-start(bf16[256,2176]{1,0:T(8,128)(2,1)} %pad_maximum_fusion.10.refs_0_), channel_id=1, source_target_pairs={{0,8},{8,0},{16,24},{24,16},{1,9},{9,1},{17,25},{25,17},{2,10},{10... | collective-permute-start | bytes 3342344 | tf_op jit(solution)/shard_map/ppermute | solution.py:133
  46.1 144.1 %all-gather.10.cloned.1.call-start = ((), (), s32[]{:S(2)}) async-start(), calls=%async_computation.6 | async-start | bytes 3932160 | tf_op jit(solution)/shard_map/all_gather | solution.py:146
  100.3 16.2 %collective-permute-start.24 = (bf16[2,64,1536]{2,1,0:T(8,128)(2,1)S(1)}, bf16[2,64,1536]{2,1,0:T(8,128)(2,1)S(1)}, u32[]{:S(2)}, u32[]{:S(2)}) collective-permute-start(bf16[2,64,1536]{2,1,0:T(8,128)(2,1)S(1)} %get-tuple-element.541), channel_id=1, source_target_pairs={{0,16},{8,24},{16,0},{24,8},{1,17},{9,25},{17,1},{25,9},{2,18},{10... | collective-permute-start | bytes 1179656 | tf_op jit(solution)/shard_map/ppermute | solution.py:133
  100.8 15.7 %collective-permute-start.23 = (bf16[2,64,1536]{2,1,0:T(8,128)(2,1)S(1)}, bf16[2,64,1536]{2,1,0:T(8,128)(2,1)S(1)}, u32[]{:S(2)}, u32[]{:S(2)}) collective-permute-start(bf16[2,64,1536]{2,1,0:T(8,128)(2,1)S(1)} %get-tuple-element.542), channel_id=1, source_target_pairs={{0,24},{8,16},{16,8},{24,0},{1,25},{9,17},{17,9},{25,1},{2,26},{10... | collective-permute-start | bytes 1179656 | tf_op jit(solution)/shard_map/ppermute | solution.py:133
  102.8 16.6 %collective-permute-start.18 = (bf16[256,2176]{1,0:T(8,128)(2,1)}, bf16[256,2176]{1,0:T(8,128)(2,1)S(1)}, u32[]{:S(2)}, u32[]{:S(2)}) collective-permute-start(bf16[256,2176]{1,0:T(8,128)(2,1)} %pad_maximum_fusion.10.refs_0_), channel_id=1, source_target_pairs={{0,1},{1,0},{2,3},{3,2},{4,5},{5,4},{6,7},{7,6},{8,9},{9,8},{10,11... | collective-permute-start | bytes 3342344 | tf_op jit(solution)/shard_map/ppermute | solution.py:136
  102.8 16.6 %collective-permute-start.19 = (bf16[256,2176]{1,0:T(8,128)(2,1)}, bf16[256,2176]{1,0:T(8,128)(2,1)S(1)}, u32[]{:S(2)}, u32[]{:S(2)}) collective-permute-start(bf16[256,2176]{1,0:T(8,128)(2,1)} %collective-permute-done.6.refs_1_), channel_id=1, source_target_pairs={{0,1},{1,0},{2,3},{3,2},{4,5},{5,4},{6,7},{7,6},{8,9},{9,8},{10,11... | collective-permute-start | bytes 3342344 | tf_op jit(solution)/shard_map/ppermute | solution.py:136
  122.0 152.9 %all-gather.12.cloned.1.call-start = ((), (), s32[]{:S(2)}) async-start(), calls=%async_computation.7 | async-start | bytes 3932160 | tf_op jit(solution)/shard_map/all_gather | solution.py:146
  122.1 38.1 %collective-permute-start.27 = (bf16[256,2048]{1,0:T(8,128)(2,1)S(1)}, bf16[256,2048]{1,0:T(8,128)(2,1)S(1)}, u32[]{:S(2)}, u32[]{:S(2)}) collective-permute-start(bf16[256,2048]{1,0:T(8,128)(2,1)S(1)} %bitcast.396), channel_id=1, source_target_pairs={{0,16},{8,24},{16,0},{24,8},{1,17},{9,25},{17,1},{25,9},{2,18},{10... | collective-permute-start | bytes 3145736 | tf_op jit(solution)/shard_map/ppermute | solution.py:133
  122.4 37.9 %collective-permute-start.26 = (bf16[256,2048]{1,0:T(8,128)(2,1)S(1)}, bf16[256,2048]{1,0:T(8,128)(2,1)S(1)}, u32[]{:S(2)}, u32[]{:S(2)}) collective-permute-start(bf16[256,2048]{1,0:T(8,128)(2,1)S(1)} %bitcast.397), channel_id=1, source_target_pairs={{0,8},{8,0},{16,24},{24,16},{1,9},{9,1},{17,25},{25,17},{2,10},{10... | collective-permute-start | bytes 3145736 | tf_op jit(solution)/shard_map/ppermute | solution.py:133
  160.3 14.6 %collective-permute-start.30 = (f32[2,8,320]{2,1,0:T(8,128)S(1)}, f32[2,8,320]{2,1,0:T(8,128)S(1)}, u32[]{:S(2)}, u32[]{:S(2)}) collective-permute-start(f32[2,8,320]{2,1,0:T(8,128)S(1)} %bitcast.444), channel_id=1, source_target_pairs={{0,6},{1,7},{8,14},{9,15},{16,22},{17,23},{24,30},{25,31}} | collective-permute-start | bytes 61448 | tf_op jit(solution)/shard_map/ppermute | solution.py:140
  169.8 16.1 %collective-permute-start.34 = (bf16[2,80,2048]{2,1,0:T(8,128)(2,1)}, bf16[2,80,2048]{2,1,0:T(8,128)(2,1)}, u32[]{:S(2)}, u32[]{:S(2)}) collective-permute-start(bf16[2,80,2048]{2,1,0:T(8,128)(2,1)} %get-tuple-element.555), channel_id=1, source_target_pairs={{0,1},{1,0},{2,3},{3,2},{4,5},{5,4},{6,7},{7,6},{8,9},{9,8},{10,11... | collective-permute-start | bytes 1966088 | tf_op jit(solution)/shard_map/ppermute | solution.py:136
  171.0 18.0 %collective-permute-start.33 = (f32[8,16,8]{2,1,0:T(8,128)S(1)}, f32[8,16,8]{2,1,0:T(8,128)S(1)}, u32[]{:S(2)}, u32[]{:S(2)}) collective-permute-start(f32[8,16,8]{2,1,0:T(8,128)S(1)} %slice_bitcast_fusion.17), channel_id=1, source_target_pairs={{2,0},{3,1},{4,2},{5,3},{6,4},{7,5},{10,8},{11,9},{12,10},{13,11},... | collective-permute-start | bytes 12296 | tf_op jit(solution)/shard_map/ppermute | solution.py:140
  200.9 126.3 %all-gather.14.cloned.1.call-start = ((), (), s32[]{:S(2)}) async-start(), calls=%async_computation.8 | async-start | bytes 3932160 | tf_op jit(solution)/shard_map/all_gather | solution.py:146
  213.8 28.0 %collective-permute-start.37 = (f16[2,256,1152]{2,1,0:T(8,128)(2,1)S(1)}, f16[2,256,1152]{2,1,0:T(8,128)(2,1)S(1)}, u32[]{:S(2)}, u32[]{:S(2)}) collective-permute-start(f16[2,256,1152]{2,1,0:T(8,128)(2,1)S(1)} %pad_maximum_fusion.8), channel_id=1, source_target_pairs={{0,8},{8,0},{16,24},{24,16},{1,9},{9,1},{17,25},{25,17},{2,10},{10... | collective-permute-start | bytes 3538952 | tf_op jit(solution)/shard_map/ppermute | solution.py:133
  215.1 27.7 %collective-permute-start.38 = (f16[2,256,1152]{2,1,0:T(8,128)(2,1)S(1)}, f16[2,256,1152]{2,1,0:T(8,128)(2,1)S(1)}, u32[]{:S(2)}, u32[]{:S(2)}) collective-permute-start(f16[2,256,1152]{2,1,0:T(8,128)(2,1)S(1)} %pad_maximum_fusion.9), channel_id=1, source_target_pairs={{0,16},{8,24},{16,0},{24,8},{1,17},{9,25},{17,1},{25,9},{2,18},{10... | collective-permute-start | bytes 3538952 | tf_op jit(solution)/shard_map/ppermute | solution.py:133
  255.6 272.4 %reduce-scatter.5.cloned.1.call-start = ((), (), s32[]{:S(2)}) async-start(), calls=%async_computation.9 | async-start | bytes 7864320 | tf_op jit(solution)/shard_map/reduce_scatter | solution.py:160
  256.1 22.2 %collective-permute-start.46 = (bf16[128,2048]{1,0:T(8,128)(2,1)}, bf16[128,2048]{1,0:T(8,128)(2,1)}, u32[]{:S(2)}, u32[]{:S(2)}) collective-permute-start(bf16[128,2048]{1,0:T(8,128)(2,1)} %collective-permute-done.31.refs_3_), channel_id=1, source_target_pairs={{0,1},{1,0},{2,3},{3,2},{4,5},{5,4},{6,7},{7,6},{8,9},{9,8},{10,11... | collective-permute-start | bytes 1572872 | tf_op jit(solution)/shard_map/ppermute | solution.py:136
  256.1 23.7 %collective-permute-start.47 = (bf16[128,2048]{1,0:T(8,128)(2,1)}, bf16[128,2048]{1,0:T(8,128)(2,1)}, u32[]{:S(2)}, u32[]{:S(2)}) collective-permute-start(bf16[128,2048]{1,0:T(8,128)(2,1)} %collective-permute-done.32.refs_4_), channel_id=1, source_target_pairs={{0,1},{1,0},{2,3},{3,2},{4,5},{5,4},{6,7},{7,6},{8,9},{9,8},{10,11... | collective-permute-start | bytes 1572872 | tf_op jit(solution)/shard_map/ppermute | solution.py:136
  256.6 28.9 %collective-permute-start.43 = (bf16[256,2048]{1,0:T(8,128)(2,1)S(1)}, bf16[256,2048]{1,0:T(8,128)(2,1)}, u32[]{:S(2)}, u32[]{:S(2)}) collective-permute-start(bf16[256,2048]{1,0:T(8,128)(2,1)S(1)} %bitcast.398), channel_id=1, source_target_pairs={{0,1},{1,0},{2,3},{3,2},{4,5},{5,4},{6,7},{7,6},{8,9},{9,8},{10,11... | collective-permute-start | bytes 3145736 | tf_op jit(solution)/shard_map/ppermute | solution.py:136
  268.0 17.6 %collective-permute-start.44 = (bf16[256,2048]{1,0:T(8,128)(2,1)S(1)}, bf16[256,2048]{1,0:T(8,128)(2,1)}, u32[]{:S(2)}, u32[]{:S(2)}) collective-permute-start(bf16[256,2048]{1,0:T(8,128)(2,1)S(1)} %collective-permute-done.26.refs_1_), channel_id=1, source_target_pairs={{0,1},{1,0},{2,3},{3,2},{4,5},{5,4},{6,7},{7,6},{8,9},{9,8},{10,11... | collective-permute-start | bytes 3145736 | tf_op jit(solution)/shard_map/ppermute | solution.py:136
  269.2 16.4 %collective-permute-start.45 = (bf16[256,2048]{1,0:T(8,128)(2,1)S(1)}, bf16[256,2048]{1,0:T(8,128)(2,1)}, u32[]{:S(2)}, u32[]{:S(2)}) collective-permute-start(bf16[256,2048]{1,0:T(8,128)(2,1)S(1)} %collective-permute-done.27.refs_2_), channel_id=1, source_target_pairs={{0,1},{1,0},{2,3},{3,2},{4,5},{5,4},{6,7},{7,6},{8,9},{9,8},{10,11... | collective-permute-start | bytes 3145736 | tf_op jit(solution)/shard_map/ppermute | solution.py:136
  278.3 25.5 %collective-permute-start.42 = (bf16[256,2048]{1,0:T(8,128)(2,1)}, bf16[256,2048]{1,0:T(8,128)(2,1)}, u32[]{:S(2)}, u32[]{:S(2)}) collective-permute-start(bf16[256,2048]{1,0:T(8,128)(2,1)} %multiply_convert_fusion.2.refs_0_), channel_id=1, source_target_pairs={{0,16},{8,24},{16,0},{24,8},{1,17},{9,25},{17,1},{25,9},{2,18},{10... | collective-permute-start | bytes 3145736 | tf_op jit(solution)/shard_map/ppermute | solution.py:133
  279.9 25.1 %collective-permute-start.41 = (bf16[256,2048]{1,0:T(8,128)(2,1)}, bf16[256,2048]{1,0:T(8,128)(2,1)}, u32[]{:S(2)}, u32[]{:S(2)}) collective-permute-start(bf16[256,2048]{1,0:T(8,128)(2,1)} %multiply_convert_fusion.2.refs_0_), channel_id=1, source_target_pairs={{0,8},{8,0},{16,24},{24,16},{1,9},{9,1},{17,25},{25,17},{2,10},{10... | collective-permute-start | bytes 3145736 | tf_op jit(solution)/shard_map/ppermute | solution.py:133
  309.3 17.9 %collective-permute-start.50 = (bf16[256,2048]{1,0:T(8,128)(2,1)}, bf16[256,2048]{1,0:T(8,128)(2,1)S(1)}, u32[]{:S(2)}, u32[]{:S(2)}) collective-permute-start(bf16[256,2048]{1,0:T(8,128)(2,1)} %multiply_convert_fusion.2.refs_0_), channel_id=1, source_target_pairs={{0,1},{1,0},{2,3},{3,2},{4,5},{5,4},{6,7},{7,6},{8,9},{9,8},{10,11... | collective-permute-start | bytes 3145736 | tf_op jit(solution)/shard_map/ppermute | solution.py:136
  309.4 17.9 %collective-permute-start.51 = (bf16[256,2048]{1,0:T(8,128)(2,1)}, bf16[256,2048]{1,0:T(8,128)(2,1)S(1)}, u32[]{:S(2)}, u32[]{:S(2)}) collective-permute-start(bf16[256,2048]{1,0:T(8,128)(2,1)} %collective-permute-done.41.refs_1_), channel_id=1, source_target_pairs={{0,1},{1,0},{2,3},{3,2},{4,5},{5,4},{6,7},{7,6},{8,9},{9,8},{10,11... | collective-permute-start | bytes 3145736 | tf_op jit(solution)/shard_map/ppermute | solution.py:136
  309.9 17.4 %collective-permute-start.52 = (bf16[256,2048]{1,0:T(8,128)(2,1)}, bf16[256,2048]{1,0:T(8,128)(2,1)}, u32[]{:S(2)}, u32[]{:S(2)}) collective-permute-start(bf16[256,2048]{1,0:T(8,128)(2,1)} %collective-permute-done.42.refs_2_), channel_id=1, source_target_pairs={{0,1},{1,0},{2,3},{3,2},{4,5},{5,4},{6,7},{7,6},{8,9},{9,8},{10,11... | collective-permute-start | bytes 3145736 | tf_op jit(solution)/shard_map/ppermute | solution.py:136
  390.7 25.6 %collective-permute-start.56 = (bf16[2,256,1024]{2,1,0:T(8,128)(2,1)}, bf16[2,256,1024]{2,1,0:T(8,128)(2,1)S(1)}, u32[]{:S(2)}, u32[]{:S(2)}) collective-permute-start(bf16[2,256,1024]{2,1,0:T(8,128)(2,1)} %get-tuple-element.352), channel_id=1, source_target_pairs={{0,8},{8,0},{16,24},{24,16},{1,9},{9,1},{17,25},{25,17},{2,10},{10... | collective-permute-start | bytes 3145736 | tf_op jit(solution)/shard_map/ppermute | solution.py:133
  392.2 25.4 %collective-permute-start.57 = (bf16[2,256,1024]{2,1,0:T(8,128)(2,1)}, bf16[2,256,1024]{2,1,0:T(8,128)(2,1)S(1)}, u32[]{:S(2)}, u32[]{:S(2)}) collective-permute-start(bf16[2,256,1024]{2,1,0:T(8,128)(2,1)} %get-tuple-element.353), channel_id=1, source_target_pairs={{0,16},{8,24},{16,0},{24,8},{1,17},{9,25},{17,1},{25,9},{2,18},{10... | collective-permute-start | bytes 3145736 | tf_op jit(solution)/shard_map/ppermute | solution.py:133
  417.6 262.9 %reduce-scatter.9.cloned.1.call-start = ((), (), s32[]{:S(2)}) async-start(), calls=%async_computation.11 | async-start | bytes 3932160 | tf_op jit(solution)/shard_map/reduce_scatter | solution.py:160
  425.2 37.0 %collective-permute-start.62 = (bf16[1024,2048]{1,0:T(8,128)(2,1)}, bf16[1024,2048]{1,0:T(8,128)(2,1)}, u32[]{:S(2)}, u32[]{:S(2)}) collective-permute-start(bf16[1024,2048]{1,0:T(8,128)(2,1)} %shard_map.313), channel_id=1, source_target_pairs={{0,1},{1,0},{2,3},{3,2},{4,5},{5,4},{6,7},{7,6},{8,9},{9,8},{10,11... | collective-permute-start | bytes 12582920 | tf_op jit(solution)/shard_map/ppermute | solution.py:136
  447.5 24.6 %collective-permute-start.61 = (bf16[256,2048]{1,0:T(8,128)(2,1)S(1)}, bf16[256,2048]{1,0:T(8,128)(2,1)S(1)}, u32[]{:S(2)}, u32[]{:S(2)}) collective-permute-start(bf16[256,2048]{1,0:T(8,128)(2,1)S(1)} %get-tuple-element.388.refs_0_), channel_id=1, source_target_pairs={{0,16},{8,24},{16,0},{24,8},{1,17},{9,25},{17,1},{25,9},{2,18},{10... | collective-permute-start | bytes 3145736 | tf_op jit(solution)/shard_map/ppermute | solution.py:133
  447.8 24.5 %collective-permute-start.60 = (bf16[256,2048]{1,0:T(8,128)(2,1)S(1)}, bf16[256,2048]{1,0:T(8,128)(2,1)S(1)}, u32[]{:S(2)}, u32[]{:S(2)}) collective-permute-start(bf16[256,2048]{1,0:T(8,128)(2,1)S(1)} %get-tuple-element.388.refs_0_), channel_id=1, source_target_pairs={{0,8},{8,0},{16,24},{24,16},{1,9},{9,1},{17,25},{25,17},{2,10},{10... | collective-permute-start | bytes 3145736 | tf_op jit(solution)/shard_map/ppermute | solution.py:133
  489.2 25.4 %collective-permute-start.70 = (bf16[2,256,1024]{2,1,0:T(8,128)(2,1)}, bf16[2,256,1024]{2,1,0:T(8,128)(2,1)S(1)}, u32[]{:S(2)}, u32[]{:S(2)}) collective-permute-start(bf16[2,256,1024]{2,1,0:T(8,128)(2,1)} %get-tuple-element.406), channel_id=1, source_target_pairs={{0,8},{8,0},{16,24},{24,16},{1,9},{9,1},{17,25},{25,17},{2,10},{10... | collective-permute-start | bytes 3145736 | tf_op jit(solution)/shard_map/ppermute | solution.py:133
  490.2 25.5 %collective-permute-start.71 = (bf16[2,256,1024]{2,1,0:T(8,128)(2,1)}, bf16[2,256,1024]{2,1,0:T(8,128)(2,1)}, u32[]{:S(2)}, u32[]{:S(2)}) collective-permute-start(bf16[2,256,1024]{2,1,0:T(8,128)(2,1)} %get-tuple-element.407), channel_id=1, source_target_pairs={{0,16},{8,24},{16,0},{24,8},{1,17},{9,25},{17,1},{25,9},{2,18},{10... | collective-permute-start | bytes 3145736 | tf_op jit(solution)/shard_map/ppermute | solution.py:133
  531.3 166.3 %reduce-scatter.11.cloned.1.call-start = ((), (), s32[]{:S(2)}) async-start(), calls=%async_computation.12 | async-start | bytes 1945600 | tf_op jit(solution)/shard_map/reduce_scatter | solution.py:160
  540.9 26.3 %collective-permute-start.78 = (f32[2,64,1536]{2,1,0:T(8,128)}, f32[2,64,1536]{2,1,0:T(8,128)S(1)}, u32[]{:S(2)}, u32[]{:S(2)}) collective-permute-start(f32[2,64,1536]{2,1,0:T(8,128)} %get-tuple-element.511), channel_id=1, source_target_pairs={{0,8},{8,0},{16,24},{24,16},{1,9},{9,1},{17,25},{25,17},{2,10},{10... | collective-permute-start | bytes 2359304 | tf_op jit(solution)/shard_map/ppermute | solution.py:133
  542.4 36.5 %collective-permute-start.77 = (f32[2,64,1536]{2,1,0:T(8,128)}, f32[2,64,1536]{2,1,0:T(8,128)}, u32[]{:S(2)}, u32[]{:S(2)}) collective-permute-start(f32[2,64,1536]{2,1,0:T(8,128)} %get-tuple-element.512), channel_id=1, source_target_pairs={{0,16},{8,24},{16,0},{24,8},{1,17},{9,25},{17,1},{25,9},{2,18},{10... | collective-permute-start | bytes 2359304 | tf_op jit(solution)/shard_map/ppermute | solution.py:133
  543.9 35.0 %collective-permute-start.76 = (f32[2,64,1536]{2,1,0:T(8,128)}, f32[2,64,1536]{2,1,0:T(8,128)}, u32[]{:S(2)}, u32[]{:S(2)}) collective-permute-start(f32[2,64,1536]{2,1,0:T(8,128)} %get-tuple-element.513), channel_id=1, source_target_pairs={{0,24},{8,16},{16,8},{24,0},{1,25},{9,17},{17,9},{25,1},{2,26},{10... | collective-permute-start | bytes 2359304 | tf_op jit(solution)/shard_map/ppermute | solution.py:133
  594.8 102.9 %reduce-scatter.7.cloned.1.call-start = ((), (), s32[]{:S(2)}) async-start(), calls=%async_computation.10 | async-start | bytes 3276800 | tf_op jit(solution)/shard_map/reduce_scatter | solution.py:160
  610.2 34.5 %collective-permute-start.83 = (bf16[1024,2048]{1,0:T(8,128)(2,1)}, bf16[1024,2048]{1,0:T(8,128)(2,1)}, u32[]{:S(2)}, u32[]{:S(2)}) collective-permute-start(bf16[1024,2048]{1,0:T(8,128)(2,1)} %shard_map.319), channel_id=1, source_target_pairs={{0,1},{1,0},{2,3},{3,2},{4,5},{5,4},{6,7},{7,6},{8,9},{9,8},{10,11... | collective-permute-start | bytes 12582920 | tf_op jit(solution)/shard_map/ppermute | solution.py:136
  654.6 24.9 %collective-permute-start.84 = (bf16[2,256,1024]{2,1,0:T(8,128)(2,1)}, bf16[2,256,1024]{2,1,0:T(8,128)(2,1)}, u32[]{:S(2)}, u32[]{:S(2)}) collective-permute-start(bf16[2,256,1024]{2,1,0:T(8,128)(2,1)} %get-tuple-element.458), channel_id=1, source_target_pairs={{0,8},{8,0},{16,24},{24,16},{1,9},{9,1},{17,25},{25,17},{2,10},{10... | collective-permute-start | bytes 3145736 | tf_op jit(solution)/shard_map/ppermute | solution.py:133
  656.0 24.5 %collective-permute-start.85 = (bf16[2,256,1024]{2,1,0:T(8,128)(2,1)}, bf16[2,256,1024]{2,1,0:T(8,128)(2,1)}, u32[]{:S(2)}, u32[]{:S(2)}) collective-permute-start(bf16[2,256,1024]{2,1,0:T(8,128)(2,1)} %get-tuple-element.459), channel_id=1, source_target_pairs={{0,16},{8,24},{16,0},{24,8},{1,17},{9,25},{17,1},{25,9},{2,18},{10... | collective-permute-start | bytes 3145736 | tf_op jit(solution)/shard_map/ppermute | solution.py:133
  705.3 16.0 %collective-permute-start.93 = (f32[2,64,640]{2,1,0:T(8,128)S(1)}, f32[2,64,640]{2,1,0:T(8,128)S(1)}, u32[]{:S(2)}, u32[]{:S(2)}) collective-permute-start(f32[2,64,640]{2,1,0:T(8,128)S(1)} %get-tuple-element.550), channel_id=1, source_target_pairs={{0,16},{8,24},{16,0},{24,8},{1,17},{9,25},{17,1},{25,9},{2,18},{10... | collective-permute-start | bytes 983048 | tf_op jit(solution)/shard_map/ppermute | solution.py:133
  706.7 14.6 %collective-permute-start.92 = (f32[2,64,640]{2,1,0:T(8,128)S(1)}, f32[2,64,640]{2,1,0:T(8,128)S(1)}, u32[]{:S(2)}, u32[]{:S(2)}) collective-permute-start(f32[2,64,640]{2,1,0:T(8,128)S(1)} %get-tuple-element.551), channel_id=1, source_target_pairs={{0,24},{8,16},{16,8},{24,0},{1,25},{9,17},{17,9},{25,1},{2,26},{10... | collective-permute-start | bytes 983048 | tf_op jit(solution)/shard_map/ppermute | solution.py:133
  (141 other events, 993.2 us)
Sparse Core Ops, SparseCore 0:
  25.4 37.3 all-gather.5
  64.9 53.6 all-gather.7
  121.9 63.6 all-gather.9
  201.0 62.5 all-gather.11
  265.1 62.1 all-gather.13
  417.7 110.2 reduce-scatter.4
  531.4 62.6 reduce-scatter.8
  596.4 37.2 reduce-scatter.10
  644.8 52.5 reduce-scatter.6
